TPU v7x, 32 devices: a whole 2x2x4 slice. The times are simulated.
32 devices in a mesh: fsdp: 8 (over z, x), tp: 4 (over y, core).
Axes of the slice: x: 2, y: 2, z: 4, core: 2. Of those that a mesh axis runs over, the one named last changes fastest.
Arguments:
- dec_query: bfloat16 [8, 2, 4096], P('fsdp'), may hold values from -200 to 200
- new_keys: bfloat16 [8, 2, 512], P('fsdp'), may hold values from -6 to 6
- new_values: bfloat16 [8, 2, 512], P('fsdp'), may hold values from -6 to 6
- cache_keys: bfloat16 [8, 2048, 512], P('fsdp', 'tp'), may hold values from -6 to 6
- cache_values: bfloat16 [8, 2048, 512], P('fsdp', 'tp'), may hold values from -6 to 6
- lengths: int32 [8], P('fsdp'), may hold values from 256 to 2048, as said below
- out_weight: bfloat16 [4096, 4096], P('fsdp', 'tp'), may hold values from -0.09375 to 0.09375
- train_attn: bfloat16 [1024, 4096], P('fsdp', 'tp'), may hold values from -0.5 to 0.5
- grad_out: bfloat16 [1024, 4096], P('fsdp'), may hold values from -6 to 6
Outputs:
- dec_out: bfloat16 [8, 2, 4096], P('fsdp', None, 'tp')
- grad_attn: bfloat16 [1024, 4096], P('fsdp', 'tp')
- grad_weight: float32 [4096, 4096], P('fsdp', 'tp')
Inputs may be any that keep to these rules, and one draw needn't show every extreme that they name: `lengths`: the length 2048 occurs.
All inputs are finite; a program needn't handle non-finite values.
Results may differ from a plain program's by a relative error of at most 0.0049.
Values may be sent and summed in bfloat16 or wider, within the bound.
No kernel may reach another device: no remote copies, remote signals or barrier semaphores. Data moves between devices by JAX's collectives and lax.ppermute only.
A program may use at most 64 MiB of HBM per device.

v0:
```python
import jax
import jax.numpy as jnp
from jax import lax
from jax.sharding import PartitionSpec as P

QH = 32
KVH = 4
HD = 128
GROUP = 8


NEG_FILL = -1e30


def combined_all(part, axis, combine):
    gathered = jax.tree.map(lambda a: lax.all_gather(a, axis), part)

    def take(source):
        return jax.tree.map(lambda a: lax.dynamic_index_in_dim(a, source, 0, False), gathered)

    return lax.fori_loop(
        1, lax.axis_size(axis), lambda source, state: combine(state, take(source)), take(0)
    )


def combine_pair(left_part, right_part):
    highest = jnp.maximum(left_part[0], right_part[0])
    scale_left = jnp.exp(left_part[0] - highest)
    scale_right = jnp.exp(right_part[0] - highest)
    totals = left_part[1] * scale_left + right_part[1] * scale_right
    weighted = left_part[2] * scale_left[..., None] + right_part[2] * scale_right[..., None]
    return (highest, totals, weighted)


def shards(
    dec_query,
    new_keys,
    new_values,
    cache_keys,
    cache_values,
    lengths,
    out_weight,
    train_attn,
    grad_out,
):
    row_count, step_count, _ = dec_query.shape
    cache_len = cache_keys.shape[1]
    tp_size = lax.axis_size("tp")
    tp_index = lax.axis_index("tp")
    heads_dev = QH // tp_size
    head_first = tp_index * heads_dev
    scaling = 1.0 / HD**0.5
    weights = lax.all_gather(out_weight, "fsdp", axis=0, tiled=True)
    key_cache = cache_keys.reshape(row_count, cache_len, KVH, HD)
    value_cache = cache_values.reshape(row_count, cache_len, KVH, HD).astype(jnp.float32)
    positions = tp_index * cache_len + jnp.arange(cache_len, dtype=jnp.int32)
    usable = positions[None, :] < lengths[:, None]
    key_heads = jnp.repeat(new_keys.reshape(row_count, step_count, KVH, HD), GROUP, axis=2)
    value_heads = jnp.repeat(new_values.reshape(row_count, step_count, KVH, HD), GROUP, axis=2)
    key_own = lax.dynamic_slice_in_dim(key_heads, head_first, heads_dev, 2)
    value_own = lax.dynamic_slice_in_dim(value_heads, head_first, heads_dev, 2).astype(jnp.float32)
    step_span = dec_query.shape[1]
    cache_step_span = dec_query.shape[1]
    grouped = dec_query.reshape(row_count, cache_step_span, KVH, GROUP, HD)
    scores = (
        jnp.einsum("rsgqd,rpgd->rsgqp", grouped, key_cache, preferred_element_type=jnp.float32)
        * scaling
    )
    allowed = usable[:, None, None, None, :]
    maxima = jnp.max(jnp.where(allowed, scores, NEG_FILL), axis=-1)
    exp_terms = jnp.where(allowed, jnp.exp(scores - maxima[..., None]), 0.0)
    totals = jnp.sum(exp_terms, axis=-1)
    weighted = jnp.einsum(
        "rsgqp,rpgd->rsgqd", exp_terms, value_cache, precision=lax.Precision.HIGHEST
    )
    maxima, totals, weighted = (
        maxima.reshape(row_count, cache_step_span, QH),
        totals.reshape(row_count, cache_step_span, QH),
        weighted.reshape(row_count, cache_step_span, QH, HD),
    )
    maxima, totals, weighted = combined_all((maxima, totals, weighted), "tp", combine_pair)
    maxima = lax.dynamic_slice_in_dim(maxima, head_first, heads_dev, 2)
    totals = lax.dynamic_slice_in_dim(totals, head_first, heads_dev, 2)
    weighted = lax.dynamic_slice_in_dim(weighted, head_first, heads_dev, 2)
    own_query = lax.dynamic_slice_in_dim(
        dec_query.reshape(row_count, step_span, QH, HD), head_first, heads_dev, 2
    )
    new_scores = (
        jnp.einsum("rshd,rjhd->rshj", own_query, key_own, preferred_element_type=jnp.float32)
        * scaling
    )
    step_allowed = (
        jnp.arange(step_count, dtype=jnp.int32)[None, :]
        <= jnp.array(list(range(step_count)), jnp.int32)[:, None]
    )
    allowed = step_allowed[None, :, None, :]
    new_maxima = jnp.max(jnp.where(allowed, new_scores, NEG_FILL), axis=-1)
    new_terms = jnp.where(allowed, jnp.exp(new_scores - new_maxima[..., None]), 0.0)
    new_totals = jnp.sum(new_terms, axis=-1)
    new_weighted = jnp.einsum(
        "rshj,rjhd->rshd", new_terms, value_own, precision=lax.Precision.HIGHEST
    )
    highest, totals_all, weighted_all = combine_pair(
        (maxima, totals, weighted), (new_maxima, new_totals, new_weighted)
    )
    attended = (
        (weighted_all / totals_all[..., None])
        .astype(jnp.bfloat16)
        .reshape(row_count, step_span, heads_dev * HD)
    )
    partial_out = lax.dot_general(
        attended, weights, (((2,), (1,)), ((), ())), preferred_element_type=jnp.float32
    )
    dec_out = lax.psum_scatter(partial_out, "tp", scatter_dimension=2, tiled=True).astype(
        jnp.bfloat16
    )
    grad_attn = jnp.dot(grad_out, weights, preferred_element_type=jnp.float32).astype(jnp.bfloat16)
    grad_weight = lax.psum_scatter(
        lax.dot_general(
            grad_out, train_attn, (((0,), (0,)), ((), ())), preferred_element_type=jnp.float32
        ),
        "fsdp",
        scatter_dimension=0,
        tiled=True,
    )
    return (dec_out, grad_attn, grad_weight)


def solution(mesh):
    return jax.shard_map(
        shards,
        mesh=mesh,
        in_specs=(
            P("fsdp", None, None),
            P("fsdp", None, None),
            P("fsdp", None, None),
            P("fsdp", "tp", None),
            P("fsdp", "tp", None),
            P("fsdp"),
            P("fsdp", "tp"),
            P("fsdp", "tp"),
            P("fsdp", None),
        ),
        out_specs=(P("fsdp", None, "tp"), P("fsdp", "tp"), P("fsdp", "tp")),
        check_vma=False,
    )
```

profile of v0, /device:TPU:17, one launch (start us, length us, event | category | flops | bytes accessed | tf_op | source)
XLA Modules:
  0.0 465.2 jit_solution(6505889980102203775)
XLA Ops:
  7.2 0.0 copy-start
  7.2 0.0 all-gather.2.cloned.1.call-start
  7.2 0.7 all-gather.2.cloned.1.call-update
  7.9 0.0 reduce-scatter.7.cloned.1.call-start
  8.6 0.7 broadcast_in_dim.67
  9.3 0.8 convolution_multiply_fusion.1
  10.1 0.1 copy.51
  10.2 0.1 fusion.21
  10.3 0.1 fusion.34
  10.4 0.1 copy.55
  10.5 1.2 reshape.157
  11.7 0.0 copy-start.1
  11.7 1.1 select_reduce_fusion
  12.8 0.2 fusion.14
  13.0 0.1 all_gather_reshape.10
  13.1 0.1 all_gather_reshape.9
  13.1 1.2 reshape.160
  14.3 0.4 convolution_bitcast_fusion.1
  14.7 5.6 %all_gather.13 = f32[4,1,2,32]{3,2,1,0:T(2,128)S(1)} all-gather(f32[1,1,2,32]{3,2,1,0:T(2,128)S(1)} %all_gather_reshape.10), channel_id=1, replica_groups=mesh['fsdp'=8,'tp'=4] {'tp'}, dimensions={0}, use_global_device_ids=true | all-gather | bytes 1280 | tf_op jit(solution)/shard_map/all_gather | solution.py:16
  20.3 5.1 %all_gather.12 = f32[4,1,2,32]{3,2,1,0:T(2,128)S(1)} all-gather(f32[1,1,2,32]{3,2,1,0:T(2,128)S(1)} %all_gather_reshape.9), channel_id=1, replica_groups=mesh['fsdp'=8,'tp'=4] {'tp'}, dimensions={0}, use_global_device_ids=true | all-gather | bytes 1280 | tf_op jit(solution)/shard_map/all_gather | solution.py:16
  25.3 5.4 %all_gather.14 = f32[4,1,2,32,128]{4,3,2,1,0:T(8,128)S(1)} all-gather(f32[1,1,2,32,128]{4,3,2,1,0:T(8,128)S(1)} %bitcast.145), channel_id=1, replica_groups=mesh['fsdp'=8,'tp'=4] {'tp'}, dimensions={0}, use_global_device_ids=true | all-gather | bytes 163840 | tf_op jit(solution)/shard_map/all_gather | solution.py:16
  30.8 0.5 while.19
  30.8 0.1 fusion.49
  31.0 0.1 fusion.49
  31.2 0.1 fusion.49
  31.3 0.1 fusion.33
  31.4 0.1 copy.52
  31.5 0.1 copy.57
  31.6 0.1 copy.56
  31.7 0.7 broadcast_in_dim.70
  32.4 0.2 fusion.10
  32.5 102.3 %all-gather.2.cloned.1.call-done = bf16[4096,1024]{1,0:T(8,128)(2,1)} async-done(((bf16[512,1024]{1,0:T(8,128)(2,1)}), bf16[4096,1024]{1,0:T(8,128)(2,1)}) %all-gather.2.cloned.1.call-update) | async-done | bytes 8388624 | tf_op jit(solution)/shard_map/all_gather | solution.py:53
  134.9 7.1 %convolution_bitcast_fusion = f32[4096,2]{1,0:T(8,128)} fusion(bf16[2,1024]{1,0:T(2,128)(2,1)S(1)} %fusion.10, bf16[4096,1024]{1,0:T(8,128)(2,1)} %all-gather.2.cloned.1.call-done), kind=kOutput, calls=%fused_computation.11 | convolution fusion | flops 16777216 | bytes 8425472 | tf_op jit(solution)/shard_map/dot_general | solution.py:111
  142.0 0.0 reduce-scatter.7.cloned.1.call-update
  142.0 0.0 reduce-scatter.5.cloned.1.call-start
  142.0 0.0 copy-done
  142.0 0.0 copy-done.1
  142.1 8.9 %fusion.36 = f32[4096,1024]{1,0:T(8,128)} fusion(bf16[128,4096]{1,0:T(8,128)(2,1)S(1)} %copy-done, bf16[128,1024]{1,0:T(8,128)(2,1)S(1)} %copy-done.1), kind=kOutput, calls=%fused_computation.65 | convolution fusion | flops 1073741824 | bytes 18087936 | tf_op jit(solution)/shard_map/dot_general | solution.py:119
  150.9 0.0 reduce-scatter.5.cloned.1.call-update
  150.9 5.5 %convolution_convert_fusion = bf16[128,1024]{1,0:T(8,128)(2,1)} fusion(bf16[128,4096]{1,0:T(8,128)(2,1)S(1)} %copy-done, bf16[4096,1024]{1,0:T(8,128)(2,1)} %all-gather.2.cloned.1.call-done), kind=kOutput, calls=%fused_computation.12 | convolution fusion | flops 1073872896 | bytes 9699328 | tf_op jit(solution)/shard_map/dot_general | solution.py:117
  156.4 16.7 %reduce-scatter.7.cloned.1.call-done = f32[1024,2]{1,0:T(8,128)} async-done(((f32[4096,2]{1,0:T(8,128)}), f32[1024,2]{1,0:T(8,128)}) %reduce-scatter.7.cloned.1.call-update) | async-done | bytes 8208
  173.1 1.8 copy.67
  174.8 283.8 %reduce-scatter.5.cloned.1.call-done = f32[512,1024]{1,0:T(8,128)} async-done(((f32[4096,1024]{1,0:T(8,128)}), f32[512,1024]{1,0:T(8,128)}) %reduce-scatter.5.cloned.1.call-update) | async-done | bytes 2097168 | tf_op jit(solution)/shard_map/reduce_scatter | solution.py:118
  (18 shorter events, 0.2 us)
Async XLA Ops:
  7.2 134.9 %copy-start = (bf16[128,4096]{1,0:T(8,128)(2,1)S(1)}, bf16[128,4096]{1,0:T(8,128)(2,1)}, u32[]{:S(2)}) copy-start(bf16[128,4096]{1,0:T(8,128)(2,1)} %param.20) | copy-start | bytes 3145732
  7.2 127.7 %all-gather.2.cloned.1.call-start = ((), (), s32[]{:S(2)}) async-start(), calls=%async_computation.2 | async-start | bytes 9437184 | tf_op jit(solution)/shard_map/all_gather | solution.py:53
  7.9 165.1 %reduce-scatter.7.cloned.1.call-start = ((), (), s32[]{:S(2)}) async-start(), calls=%async_computation.4 | async-start | bytes 2621440
  11.7 130.4 %copy-start.1 = (bf16[128,1024]{1,0:T(8,128)(2,1)S(1)}, bf16[128,1024]{1,0:T(8,128)(2,1)}, u32[]{:S(2)}) copy-start(bf16[128,1024]{1,0:T(8,128)(2,1)} %param.19) | copy-start | bytes 786436
  142.0 316.7 %reduce-scatter.5.cloned.1.call-start = ((), (), s32[]{:S(2)}) async-start(), calls=%async_computation.3 | async-start | bytes 18874368 | tf_op jit(solution)/shard_map/reduce_scatter | solution.py:118
Sparse Core Ops, SparseCore 0:
  10.1 124.6 all-gather.1
  142.1 30.9 reduce-scatter.6
  177.9 280.7 reduce-scatter.4
where the time goes:
time: 469 us; the launch traced here: 465 us
  waiting for transfers between devices  404 us (86%)
  matrix products  23.9 us (5%)
  blocking collectives  16 us (3%)
  between operations  14.5 us (3%)
  local copies, waits for them, and re-layouts  6.17 us (1%)
    reduce_scatter x1, waiting for transfers between devices, shards(): lax.psum_scatter(lax.dot_general(grad_out, train_attn, (((0,), (0,)), (()...  284 us
    all_gather x1, waiting for transfers between devices, shards(): weights = lax.all_gather(out_weight, 'fsdp', axis=0, tiled=True)  102 us
    unnamed x4, waiting for transfers between devices  17.4 us
    all_gather x3, blocking collectives, combined_all(): gathered = jax.tree.map(lambda a: lax.all_gather(a, axis), part)  16 us
  transfers between devices with their start and end apart: 3, of which 3 were waited for; matrix products, arithmetic and copies ran while one was open for 5% of the time, Pallas kernels for 0%

commit v1 on v0

v1 whole, which is shorter than its diff:
```python
import jax
import jax.numpy as jnp
from jax import lax
from jax.sharding import PartitionSpec as P

KVH = 4
HD = 128
NEG_FILL = -1e30
BF16 = jnp.bfloat16
F32 = jnp.float32


def flip(a, axis, bits):
    size = lax.axis_size(axis)
    return lax.ppermute(a, axis, [(i, i ^ bits) for i in range(size)])


def local_attention(query, keys, values, usable):
    steps, width = query.shape
    heads = width // HD
    group = heads // KVH
    rows = query.reshape(steps, heads, HD).transpose(1, 0, 2).reshape(heads * steps, HD)
    own = jnp.arange(heads * steps)[:, None] // (group * steps) == jnp.arange(KVH * HD)[None, :] // HD
    spread = jnp.where(own, jnp.tile(rows, (1, KVH)), jnp.zeros((), query.dtype))
    scores = lax.dot_general(spread, keys, (((1,), (1,)), ((), ())), preferred_element_type=F32)
    scores = scores * (1.0 / HD**0.5)
    maxima = jnp.max(jnp.where(usable, scores, NEG_FILL), axis=-1, keepdims=True)
    terms = jnp.where(usable, jnp.exp(scores - maxima), 0.0)
    totals = jnp.sum(terms, axis=-1, keepdims=True)
    upper = lax.reduce_precision(terms, 8, 7)
    both = jnp.concatenate([upper.astype(BF16), (terms - upper).astype(BF16)], axis=0)
    wide = jnp.dot(both, values, preferred_element_type=F32)
    wide = wide[: heads * steps] + wide[heads * steps :]
    wide = jnp.where(own, wide, 0.0)
    weighted = sum(wide[:, g * HD : (g + 1) * HD] for g in range(KVH))
    return weighted, maxima, totals


def decode(dec_query, new_keys, new_values, cache_keys, cache_values, lengths, out_weight):
    rows, steps, width = dec_query.shape
    tp_size = lax.axis_size("tp")
    tp_index = lax.axis_index("tp")
    fsdp_size = lax.axis_size("fsdp")
    fsdp_index = lax.axis_index("fsdp")
    cache_len = cache_keys.shape[1]
    heads = width // HD
    heads_dev = heads // tp_size
    group = heads // KVH
    positions = tp_index * cache_len + jnp.arange(cache_len, dtype=jnp.int32)
    packed = []
    for r in range(rows):
        usable = (positions < lengths[r])[None, :]
        weighted, maxima, totals = local_attention(dec_query[r], cache_keys[r], cache_values[r], usable)
        packed.append(
            jnp.concatenate(
                [weighted, jnp.broadcast_to(maxima, (heads * steps, HD // 2)), jnp.broadcast_to(totals, (heads * steps, HD // 2))],
                axis=1,
            ).reshape(tp_size, heads_dev, steps, 2 * HD)
        )
    packed = jnp.stack(packed, axis=1)
    parts = [lax.dynamic_index_in_dim(packed, tp_index, 0, False)]
    for k in range(1, tp_size):
        parts.append(flip(lax.dynamic_index_in_dim(packed, tp_index ^ k, 0, False), "tp", k))

    own_query = lax.dynamic_slice_in_dim(dec_query.reshape(rows, steps, heads, HD), tp_index * heads_dev, heads_dev, 2)
    key_own = lax.dynamic_slice_in_dim(
        jnp.repeat(new_keys.reshape(rows, steps, KVH, HD), group, axis=2), tp_index * heads_dev, heads_dev, 2
    )
    value_own = lax.dynamic_slice_in_dim(
        jnp.repeat(new_values.reshape(rows, steps, KVH, HD), group, axis=2), tp_index * heads_dev, heads_dev, 2
    ).astype(F32)
    new_scores = jnp.sum(own_query.astype(F32)[:, :, None] * key_own.astype(F32)[:, None], axis=-1) * (1.0 / HD**0.5)
    new_scores = new_scores.transpose(0, 3, 1, 2)
    allowed = jnp.arange(steps)[None, :] <= jnp.arange(steps)[:, None]
    highest = jnp.max(jnp.where(allowed, new_scores, NEG_FILL), axis=-1)
    for part in parts:
        highest = jnp.maximum(highest, part[..., HD])
    new_terms = jnp.where(allowed, jnp.exp(new_scores - highest[..., None]), 0.0)
    total = jnp.sum(new_terms, axis=-1)
    weighted = sum(new_terms[..., j, None] * value_own[:, j, :, None, :] for j in range(steps))
    for part in parts:
        scale = jnp.exp(part[..., HD] - highest)
        total = total + part[..., HD + HD // 2] * scale
        weighted = weighted + part[..., :HD] * scale[..., None]
    attended = (weighted / total[..., None]).astype(BF16)
    attended = attended.transpose(0, 2, 1, 3).reshape(rows * steps, heads_dev * HD)

    every = attended[None]
    reach = 1
    while reach < fsdp_size:
        other = flip(every, "fsdp", reach)
        low = (fsdp_index // reach) % 2 == 0
        every = jnp.where(low, jnp.concatenate([every, other]), jnp.concatenate([other, every]))
        reach *= 2
    every = every.reshape(fsdp_size * rows * steps, heads_dev * HD)
    partial = lax.dot_general(every, out_weight, (((1,), (1,)), ((), ())), preferred_element_type=F32)
    feats = partial.shape[1]
    share = fsdp_size // tp_size
    partial = partial.reshape(tp_size, share, rows * steps, feats)
    mine = lax.dynamic_index_in_dim(partial, tp_index, 0, False)
    for k in range(1, tp_size):
        mine = mine + flip(lax.dynamic_index_in_dim(partial, tp_index ^ k, 0, False), "tp", k)
    mine = mine.astype(BF16)
    out = jnp.zeros((share, rows * steps, feats), BF16)
    for j in range(share):
        perm = [
            (f * tp_size + q, (q * share + (f % share ^ j)) * tp_size + f // share)
            for f in range(fsdp_size)
            for q in range(tp_size)
        ]
        piece = lax.dynamic_index_in_dim(mine, fsdp_index % share ^ j, 0, False)
        got = lax.ppermute(piece, ("fsdp", "tp"), perm)
        out = lax.dynamic_update_index_in_dim(out, got, fsdp_index % share ^ j, 0)
    return out.transpose(1, 0, 2).reshape(rows, steps, share * feats)


def gradients(out_weight, train_attn, grad_out):
    inner = 2
    fsdp_size = lax.axis_size("fsdp")
    outer = fsdp_size // inner
    fsdp_index = lax.axis_index("fsdp")
    z, x = fsdp_index // inner, fsdp_index % inner
    core = lax.axis_index("tp") % 2
    tokens, dout = grad_out.shape
    feats = out_weight.shape[0]
    plane = feats * inner
    half = tokens // 2
    other_weight = flip(out_weight, "fsdp", 1)
    got = [
        flip(lax.dynamic_slice(grad_out, (core * half, (z ^ k) * plane), (half, plane)), "fsdp", k * inner)
        for k in range(1, outer)
    ]
    attn = [train_attn] + [flip(train_attn, "fsdp", k * inner) for k in range(1, outer)]
    got = jnp.stack(got)
    twin = flip(got, "tp", 1)
    cot = jnp.where(core == 0, jnp.concatenate([got, twin], axis=1), jnp.concatenate([twin, got], axis=1))
    own_cot = lax.dynamic_slice(grad_out, (0, z * plane), (tokens, plane))
    cots = jnp.concatenate([own_cot[None], cot]).reshape(outer * tokens, plane)
    cot_x = lax.dynamic_slice(cots, (0, x * feats), (outer * tokens, feats))
    cot_o = lax.dynamic_slice(cots, (0, (1 - x) * feats), (outer * tokens, feats))
    dot = lambda a, b: jnp.dot(a, b, preferred_element_type=F32)
    partial = (dot(cot_x, out_weight) + dot(cot_o, other_weight)).reshape(outer, tokens, -1)
    grad_attn = partial[0]
    sent = partial[1:].astype(BF16)
    for k in range(1, outer):
        grad_attn = grad_attn + flip(sent[k - 1], "fsdp", k * inner).astype(F32)
    attn = jnp.concatenate(attn)
    span = outer * half
    piece = flip(lax.dynamic_slice(cot_o, (core * span, 0), (span, feats)), "fsdp", 1)
    piece_twin = flip(piece, "tp", 1)
    cot_far = jnp.where(core == 0, jnp.concatenate([piece, piece_twin]), jnp.concatenate([piece_twin, piece]))
    attn_far = flip(attn, "fsdp", 1)
    over_tokens = lambda a, b: lax.dot_general(a, b, (((0,), (0,)), ((), ())), preferred_element_type=F32)
    grad_weight = over_tokens(cot_x, attn) + over_tokens(cot_far, attn_far)
    return grad_attn.astype(BF16), grad_weight


def shards(dec_query, new_keys, new_values, cache_keys, cache_values, lengths, out_weight, train_attn, grad_out):
    grad_attn, grad_weight = gradients(out_weight, train_attn, grad_out)
    dec_out = decode(dec_query, new_keys, new_values, cache_keys, cache_values, lengths, out_weight)
    return dec_out, grad_attn, grad_weight


def solution(mesh):
    return jax.shard_map(
        shards,
        mesh=mesh,
        in_specs=(
            P("fsdp", None, None),
            P("fsdp", None, None),
            P("fsdp", None, None),
            P("fsdp", "tp", None),
            P("fsdp", "tp", None),
            P("fsdp"),
            P("fsdp", "tp"),
            P("fsdp", "tp"),
            P("fsdp", None),
        ),
        out_specs=(P("fsdp", None, "tp"), P("fsdp", "tp"), P("fsdp", "tp")),
        check_vma=False,
    )
```

time: 469 us -> 137 us (0.29)
  the two profiles are of different devices: /device:TPU:17 before, /device:TPU:0 now
where the time goes in v1:
time: 137 us
  waiting for transfers between devices  60.2 us (44%)
  starting transfers between devices  51.5 us (38%)
  other arithmetic  8.06 us (6%)
  local copies, waits for them, and re-layouts  7.82 us (6%)
  matrix products  7.56 us (6%)
  between operations  1.86 us (1%)
    ppermute x23, waiting for transfers between devices, flip(): return lax.ppermute(a, axis, [(i, i ^ bits) for i in range(size)])  60.2 us
    ppermute x23, starting transfers between devices, flip(): return lax.ppermute(a, axis, [(i, i ^ bits) for i in range(size)])  49.3 us
    dot_general x2, matrix products, gradients(): lax.dot_general(a, b, (((0,), (0,)), ((), ())), preferred_element_type=F32)  2.81 us
  transfers between devices with their start and end apart: 25, of which 10 were waited for; matrix products, arithmetic and copies ran while one was open for 12% of the time, Pallas kernels for 0%

profile of v1, /device:TPU:0, one launch (start us, length us, event | category | flops | bytes accessed | tf_op | source)
XLA Modules:
  0.0 136.9 jit_solution(8987059537509614087)
XLA Ops:
  1.4 0.9 compare_select_fusion
  2.3 1.4 %select_reduce_fusion = (f32[64]{0:T(128)S(1)}, f32[64,512]{1,0:T(8,128)S(1)}) fusion(pred[512]{0:T(512)(128)(4,1)S(1)} %add_compare_fusion, bf16[1,512,512]{2,1,0:T(8,128)(2,1)} %param.12, bf16[8,8,4,128]{3,2,1,0:T(4,128)(2,1)S(1)} %bitcast.141), kind=kOutput, calls=%fused_computation.46 | convolution fusion | flops 33652672 | bytes 721664 | tf_op jit(solution)/shard_map/dot_general | solution.py:25
  4.8 2.5 %collective-permute-start.2 = (f32[1,8,2,256]{1,2,3,0:T(2,128)S(1)}, f32[1,8,2,256]{1,2,3,0:T(2,128)S(1)}, u32[]{:S(2)}, u32[]{:S(2)}) collective-permute-start(f32[1,8,2,256]{1,2,3,0:T(2,128)S(1)} %bitcast.138), channel_id=1, source_target_pairs={{0,3},{1,2},{2,1},{3,0},{4,7},{5,6},{6,5},{7,4},{8,11},{9,10},{10,... | collective-permute-start | bytes 49160 | tf_op jit(solution)/shard_map/ppermute | solution.py:15
  7.4 0.6 collective-permute-start.1
  9.1 4.8 %collective-permute-done.2 = f32[1,8,2,256]{1,2,3,0:T(2,128)S(1)} collective-permute-done((f32[1,8,2,256]{1,2,3,0:T(2,128)S(1)}, f32[1,8,2,256]{1,2,3,0:T(2,128)S(1)}, u32[]{:S(2)}, u32[]{:S(2)}) %collective-permute-start.2) | collective-permute-done | bytes 16416 | tf_op jit(solution)/shard_map/ppermute | solution.py:15
  14.0 5.8 %collective-permute-done.1 = f32[1,8,2,256]{1,2,3,0:T(2,128)S(1)} collective-permute-done((f32[1,8,2,256]{1,2,3,0:T(2,128)S(1)}, f32[1,8,2,256]{1,2,3,0:T(2,128)S(1)}, u32[]{:S(2)}, u32[]{:S(2)}) %collective-permute-start.1) | collective-permute-done | bytes 16416 | tf_op jit(solution)/shard_map/ppermute | solution.py:15
  19.8 0.7 fusion.60
  20.5 0.7 fusion.61
  21.2 1.1 fusion.33
  22.4 2.3 %collective-permute-start.3 = (bf16[1,2,1024]{2,1,0:T(2,128)(2,1)S(1)}, bf16[1,2,1024]{2,1,0:T(2,128)(2,1)S(1)}, u32[]{:S(2)}, u32[]{:S(2)}) collective-permute-start(bf16[1,2,1024]{2,1,0:T(2,128)(2,1)S(1)} %broadcast_in_dim_reshape.3), channel_id=1, source_target_pairs={{0,4},{4,0},{8,12},{12,8},{16,20},{20,16},{24,28},{28,24},{1,5},{5... | collective-permute-start | bytes 12296 | tf_op jit(solution)/shard_map/ppermute | solution.py:15
  24.7 1.6 %collective-permute-done.3 = bf16[1,2,1024]{2,1,0:T(2,128)(2,1)S(1)} collective-permute-done((bf16[1,2,1024]{2,1,0:T(2,128)(2,1)S(1)}, bf16[1,2,1024]{2,1,0:T(2,128)(2,1)S(1)}, u32[]{:S(2)}, u32[]{:S(2)}) %collective-permute-start.3) | collective-permute-done | bytes 4128 | tf_op jit(solution)/shard_map/ppermute | solution.py:15
  26.3 2.2 %collective-permute-start.4 = (bf16[2,2,1024]{2,1,0:T(2,128)(2,1)S(1)}, bf16[2,2,1024]{2,1,0:T(2,128)(2,1)S(1)}, u32[]{:S(2)}, u32[]{:S(2)}) collective-permute-start(bf16[2,2,1024]{2,1,0:T(2,128)(2,1)S(1)} %broadcast_select_fusion.2), channel_id=1, source_target_pairs={{0,8},{4,12},{8,0},{12,4},{16,24},{20,28},{24,16},{28,20},{1,9},{5... | collective-permute-start | bytes 24584 | tf_op jit(solution)/shard_map/ppermute | solution.py:15
  28.5 1.5 %collective-permute-start.15 = (bf16[512,1024]{1,0:T(8,128)(2,1)S(1)}, bf16[512,1024]{1,0:T(8,128)(2,1)}, u32[]{:S(2)}, u32[]{:S(2)}) collective-permute-start(bf16[512,1024]{1,0:T(8,128)(2,1)S(1)} %copy-done.1), channel_id=1, source_target_pairs={{0,4},{4,0},{8,12},{12,8},{16,20},{20,16},{24,28},{28,24},{1,5},{5... | collective-permute-start | bytes 3145736 | tf_op jit(solution)/shard_map/ppermute | solution.py:15
  30.0 0.4 collective-permute-start.19
  30.5 2.8 %collective-permute-start.5 = (bf16[4,2,1024]{2,1,0:T(2,128)(2,1)S(1)}, bf16[4,2,1024]{2,1,0:T(2,128)(2,1)S(1)}, u32[]{:S(2)}, u32[]{:S(2)}) collective-permute-start(bf16[4,2,1024]{2,1,0:T(2,128)(2,1)S(1)} %broadcast_select_fusion.1), channel_id=1, source_target_pairs={{0,16},{4,20},{8,24},{12,28},{16,0},{20,4},{24,8},{28,12},{1,17},{... | collective-permute-start | bytes 49160 | tf_op jit(solution)/shard_map/ppermute | solution.py:15
  33.3 1.7 %fusion.68 = (bf16[64,1024]{1,0:T(8,128)(2,1)S(1)}, bf16[64,1024]{1,0:T(8,128)(2,1)}, bf16[64,1024]{1,0:T(8,128)(2,1)S(1)}) fusion(bf16[128,4096]{1,0:T(8,128)(2,1)} %param.17, s32[]{:T(128)S(6)} %select_n.236, s32[]{:T(128)S(6)} %select_n.237, s32[]{:T(128)S(6)} %select_n.239, s32[]{:T(128)S(6)} %select_n.238), kind=kLoop, calls=%fused_computation.144 | loop fusion | bytes 786448 | tf_op jit(solution)/shard_map/dynamic_slice | solution.py:130
  35.9 1.7 %collective-permute-start.7 = (f32[2,2,512]{2,1,0:T(2,128)S(1)}, f32[2,2,512]{2,1,0:T(2,128)}, u32[]{:S(2)}, u32[]{:S(2)}) collective-permute-start(f32[2,2,512]{2,1,0:T(2,128)S(1)} %bitcast.148), channel_id=1, source_target_pairs={{0,2},{1,3},{2,0},{3,1},{4,6},{5,7},{6,4},{7,5},{8,10},{9,11},{10,... | collective-permute-start | bytes 24584 | tf_op jit(solution)/shard_map/ppermute | solution.py:15
  37.8 1.1 collective-permute-done.8
  39.0 3.8 %collective-permute-start.13 = (bf16[64,1024]{1,0:T(8,128)(2,1)}, bf16[64,1024]{1,0:T(8,128)(2,1)S(1)}, u32[]{:S(2)}, u32[]{:S(2)}) collective-permute-start(bf16[64,1024]{1,0:T(8,128)(2,1)} %get-tuple-element.11), channel_id=1, source_target_pairs={{0,24},{4,28},{8,16},{12,20},{16,8},{20,12},{24,0},{28,4},{1,25},{... | collective-permute-start | bytes 393224 | tf_op jit(solution)/shard_map/ppermute | solution.py:15
  42.8 1.9 %collective-permute-start.12 = (bf16[64,1024]{1,0:T(8,128)(2,1)S(1)}, bf16[64,1024]{1,0:T(8,128)(2,1)S(1)}, u32[]{:S(2)}, u32[]{:S(2)}) collective-permute-start(bf16[64,1024]{1,0:T(8,128)(2,1)S(1)} %get-tuple-element.12), channel_id=1, source_target_pairs={{0,16},{4,20},{8,24},{12,28},{16,0},{20,4},{24,8},{28,12},{1,17},{... | collective-permute-start | bytes 393224 | tf_op jit(solution)/shard_map/ppermute | solution.py:15
  44.6 0.7 fusion.37
  45.4 1.6 %collective-permute-done.13 = bf16[64,1024]{1,0:T(8,128)(2,1)S(1)} collective-permute-done((bf16[64,1024]{1,0:T(8,128)(2,1)}, bf16[64,1024]{1,0:T(8,128)(2,1)S(1)}, u32[]{:S(2)}, u32[]{:S(2)}) %collective-permute-start.13) | collective-permute-done | bytes 131104 | tf_op jit(solution)/shard_map/ppermute | solution.py:15
  47.0 7.8 %collective-permute-start.20 = (bf16[128,1024]{1,0:T(8,128)(2,1)S(1)}, bf16[128,1024]{1,0:T(8,128)(2,1)}, u32[]{:S(2)}, u32[]{:S(2)}) collective-permute-start(bf16[128,1024]{1,0:T(8,128)(2,1)S(1)} %copy-done.2), channel_id=1, source_target_pairs={{0,16},{4,20},{8,24},{12,28},{16,0},{20,4},{24,8},{28,12},{1,17},{... | collective-permute-start | bytes 786440 | tf_op jit(solution)/shard_map/ppermute | solution.py:15
  54.8 0.6 collective-permute-done.12
  55.4 0.7 collective-permute-start.9
  56.1 1.6 %collective-permute-start.10 = (bf16[2,512]{1,0:T(2,128)(2,1)S(1)}, bf16[2,512]{1,0:T(2,128)(2,1)S(1)}, u32[]{:S(2)}, u32[]{:S(2)}) collective-permute-start(bf16[2,512]{1,0:T(2,128)(2,1)S(1)} %get-tuple-element.30), channel_id=1, source_target_pairs={{0,4},{1,12},{2,20},{3,28},{4,0},{5,8},{6,16},{7,24},{8,5},{9,13},... | collective-permute-start | bytes 6152 | tf_op jit(solution)/shard_map/ppermute | solution.py:112
  57.6 0.8 pad_maximum_fusion.1
  58.4 7.8 %collective-permute-start.21 = (bf16[128,1024]{1,0:T(8,128)(2,1)S(1)}, bf16[128,1024]{1,0:T(8,128)(2,1)}, u32[]{:S(2)}, u32[]{:S(2)}) collective-permute-start(bf16[128,1024]{1,0:T(8,128)(2,1)S(1)} %copy-done.2), channel_id=1, source_target_pairs={{0,24},{4,28},{8,16},{12,20},{16,8},{20,12},{24,0},{28,4},{1,25},{... | collective-permute-start | bytes 786440 | tf_op jit(solution)/shard_map/ppermute | solution.py:15
  66.2 4.7 %collective-permute-start.14 = (bf16[3,64,1024]{2,1,0:T(8,128)(2,1)}, bf16[3,64,1024]{2,1,0:T(8,128)(2,1)}, u32[]{:S(2)}, u32[]{:S(2)}) collective-permute-start(bf16[3,64,1024]{2,1,0:T(8,128)(2,1)} %pad_maximum_fusion.1), channel_id=1, source_target_pairs={{0,1},{1,0},{2,3},{3,2},{4,5},{5,4},{6,7},{7,6},{8,9},{9,8},{10,11... | collective-permute-start | bytes 1179656 | tf_op jit(solution)/shard_map/ppermute | solution.py:15
  70.9 1.0 dynamic-slice_bitcast_fusion
  72.0 0.6 reshape.342
  72.6 1.0 constant_dynamic-update-slice_fusion.2
  73.6 1.0 constant_dynamic-update-slice_fusion.1
  74.6 1.0 constant_dynamic-update-slice_fusion
  75.6 0.8 collective-permute-start.24
  76.3 1.4 %maximum_select_fusion = bf16[3,128,1024]{2,1,0:T(8,128)(2,1)S(1)} fusion(bf16[3,64,1024]{2,1,0:T(8,128)(2,1)} %collective-permute-done.14, bf16[1,64,1024]{2,1,0:T(8,128)(2,1)S(1)} %bitcast.133, bf16[1,64,1024]{2,1,0:T(8,128)(2,1)S(1)} %bitcast.135, bf16[1,64,1024]{2,1,0:T(8,128)(2,1)S(1)} %bitcast.137, pred[]{:T(512)S(6)} %eq.60), kind=kLoop, calls=%fused_computation.6 | loop fusion | flops 6684672 | bytes 1572865 | tf_op jit(solution)/shard_map/jit(_where)/select_n | solution.py:136
  78.1 1.4 %collective-permute-start.22 = (bf16[256,512]{1,0:T(8,128)(2,1)S(1)}, bf16[256,512]{1,0:T(8,128)(2,1)S(1)}, u32[]{:S(2)}, u32[]{:S(2)}) collective-permute-start(bf16[256,512]{1,0:T(8,128)(2,1)S(1)} %dynamic_slice.76), channel_id=1, source_target_pairs={{0,4},{4,0},{8,12},{12,8},{16,20},{20,16},{24,28},{28,24},{1,5},{5... | collective-permute-start | bytes 786440 | tf_op jit(solution)/shard_map/ppermute | solution.py:15
  79.4 0.7 fusion.17
  80.2 26.4 %collective-permute-done.22 = bf16[256,512]{1,0:T(8,128)(2,1)S(1)} collective-permute-done((bf16[256,512]{1,0:T(8,128)(2,1)S(1)}, bf16[256,512]{1,0:T(8,128)(2,1)S(1)}, u32[]{:S(2)}, u32[]{:S(2)}) %collective-permute-start.22) | collective-permute-done | bytes 262176 | tf_op jit(solution)/shard_map/ppermute | solution.py:15
  106.6 2.0 %fusion.70 = (bf16[512,1024]{1,0:T(8,128)(2,1)S(1)}, f32[512,1024]{1,0:T(8,128)S(1)}) fusion(f32[512,1024]{1,0:T(8,128)S(1)} %fusion.17, bf16[512,1024]{1,0:T(8,128)(2,1)} %collective-permute-done.15, bf16[512,1024]{1,0:T(8,128)(2,1)S(1)} %bitcast.127, s32[]{:T(128)S(6)} %select_n.242), kind=kOutput, calls=%fused_computation.146 | convolution fusion | flops 537919488 | bytes 6815748 | tf_op jit(solution)/shard_map/dot_general | solution.py:141
  108.6 1.1 collective-permute-start.18
  109.7 5.3 %collective-permute-start.17 = (bf16[128,1024]{1,0:T(8,128)(2,1)S(1)}, bf16[128,1024]{1,0:T(8,128)(2,1)S(1)}, u32[]{:S(2)}, u32[]{:S(2)}) collective-permute-start(bf16[128,1024]{1,0:T(8,128)(2,1)S(1)} %get-tuple-element.9), channel_id=1, source_target_pairs={{0,16},{4,20},{8,24},{12,28},{16,0},{20,4},{24,8},{28,12},{1,17},{... | collective-permute-start | bytes 786440 | tf_op jit(solution)/shard_map/ppermute | solution.py:15
  114.9 0.5 collective-permute-start.16
  115.4 0.7 fusion.5
  116.2 2.1 %convolution_add_fusion = f32[512,1024]{1,0:T(8,128)} fusion(f32[512,1024]{1,0:T(8,128)S(1)} %fusion.5, bf16[512,1024]{1,0:T(8,128)(2,1)S(1)} %constant_dynamic-update-slice_fusion, bf16[512,1024]{1,0:T(8,128)(2,1)S(1)} %bitcast.128, s32[]{:T(128)S(6)} %select_n.241), kind=kOutput, calls=%fused_computation | convolution fusion | flops 537395200 | bytes 5767172 | tf_op jit(solution)/shard_map/dot_general | solution.py:153
  118.3 1.4 %collective-permute-done.18 = bf16[128,1024]{1,0:T(8,128)(2,1)S(1)} collective-permute-done((bf16[128,1024]{1,0:T(8,128)(2,1)S(1)}, bf16[128,1024]{1,0:T(8,128)(2,1)S(1)}, u32[]{:S(2)}, u32[]{:S(2)}) %collective-permute-start.18) | collective-permute-done | bytes 262176 | tf_op jit(solution)/shard_map/ppermute | solution.py:15
  119.7 16.4 %collective-permute-done.17 = bf16[128,1024]{1,0:T(8,128)(2,1)S(1)} collective-permute-done((bf16[128,1024]{1,0:T(8,128)(2,1)S(1)}, bf16[128,1024]{1,0:T(8,128)(2,1)S(1)}, u32[]{:S(2)}, u32[]{:S(2)}) %collective-permute-start.17) | collective-permute-done | bytes 262176 | tf_op jit(solution)/shard_map/ppermute | solution.py:15
  136.1 0.9 fusion.4
  (86 shorter events, 3.9 us)
Async XLA Ops:
  0.6 3.3 %copy-start = (bf16[1,512,512]{2,1,0:T(8,128)(2,1)S(1)}, bf16[1,512,512]{2,1,0:T(8,128)(2,1)}, u32[]{:S(2)}) copy-start(bf16[1,512,512]{2,1,0:T(8,128)(2,1)} %param.13) | copy-start | bytes 1572868
  3.7 4.7 %copy-start.4 = (bf16[1,2,512]{2,1,0:T(2,128)(2,1)S(1)}, bf16[1,2,512]{2,1,0:T(2,128)(2,1)}, u32[]{:S(2)}) copy-start(bf16[1,2,512]{2,1,0:T(2,128)(2,1)} %param.10) | copy-start | bytes 6148
  3.7 4.7 %copy-start.3 = (bf16[1,2,4096]{2,1,0:T(2,128)(2,1)S(1)}, bf16[1,2,4096]{2,1,0:T(2,128)(2,1)}, u32[]{:S(2)}) copy-start(bf16[1,2,4096]{2,1,0:T(2,128)(2,1)} %param.9) | copy-start | bytes 49156
  3.7 4.8 %copy-start.5 = (bf16[1,2,512]{2,1,0:T(2,128)(2,1)S(1)}, bf16[1,2,512]{2,1,0:T(2,128)(2,1)}, u32[]{:S(2)}) copy-start(bf16[1,2,512]{2,1,0:T(2,128)(2,1)} %param.11) | copy-start | bytes 6148
  4.3 24.3 %copy-start.1 = (bf16[512,1024]{1,0:T(8,128)(2,1)S(1)}, bf16[512,1024]{1,0:T(8,128)(2,1)}, u32[]{:S(2)}) copy-start(bf16[512,1024]{1,0:T(8,128)(2,1)} %param.15) | copy-start | bytes 3145732
  4.3 25.7 %copy-start.2 = (bf16[128,1024]{1,0:T(8,128)(2,1)S(1)}, bf16[128,1024]{1,0:T(8,128)(2,1)}, u32[]{:S(2)}) copy-start(bf16[128,1024]{1,0:T(8,128)(2,1)} %param.16) | copy-start | bytes 786436
  4.8 9.2 %collective-permute-start.2 = (f32[1,8,2,256]{1,2,3,0:T(2,128)S(1)}, f32[1,8,2,256]{1,2,3,0:T(2,128)S(1)}, u32[]{:S(2)}, u32[]{:S(2)}) collective-permute-start(f32[1,8,2,256]{1,2,3,0:T(2,128)S(1)} %bitcast.138), channel_id=1, source_target_pairs={{0,3},{1,2},{2,1},{3,0},{4,7},{5,6},{6,5},{7,4},{8,11},{9,10},{10,... | collective-permute-start | bytes 49160 | tf_op jit(solution)/shard_map/ppermute | solution.py:15
  7.4 12.3 %collective-permute-start.1 = (f32[1,8,2,256]{1,2,3,0:T(2,128)S(1)}, f32[1,8,2,256]{1,2,3,0:T(2,128)S(1)}, u32[]{:S(2)}, u32[]{:S(2)}) collective-permute-start(f32[1,8,2,256]{1,2,3,0:T(2,128)S(1)} %bitcast.139), channel_id=1, source_target_pairs={{0,2},{1,3},{2,0},{3,1},{4,6},{5,7},{6,4},{7,5},{8,10},{9,11},{10,... | collective-permute-start | bytes 49160 | tf_op jit(solution)/shard_map/ppermute | solution.py:15
  8.2 11.5 %collective-permute-start = (f32[1,8,2,256]{1,2,3,0:T(2,128)S(1)}, f32[1,8,2,256]{1,2,3,0:T(2,128)}, u32[]{:S(2)}, u32[]{:S(2)}) collective-permute-start(f32[1,8,2,256]{1,2,3,0:T(2,128)S(1)} %bitcast.140), channel_id=1, source_target_pairs={{0,1},{1,0},{2,3},{3,2},{4,5},{5,4},{6,7},{7,6},{8,9},{9,8},{10,11... | collective-permute-start | bytes 49160 | tf_op jit(solution)/shard_map/ppermute | solution.py:15
  22.4 3.9 %collective-permute-start.3 = (bf16[1,2,1024]{2,1,0:T(2,128)(2,1)S(1)}, bf16[1,2,1024]{2,1,0:T(2,128)(2,1)S(1)}, u32[]{:S(2)}, u32[]{:S(2)}) collective-permute-start(bf16[1,2,1024]{2,1,0:T(2,128)(2,1)S(1)} %broadcast_in_dim_reshape.3), channel_id=1, source_target_pairs={{0,4},{4,0},{8,12},{12,8},{16,20},{20,16},{24,28},{28,24},{1,5},{5... | collective-permute-start | bytes 12296 | tf_op jit(solution)/shard_map/ppermute | solution.py:15
  26.3 4.1 %collective-permute-start.4 = (bf16[2,2,1024]{2,1,0:T(2,128)(2,1)S(1)}, bf16[2,2,1024]{2,1,0:T(2,128)(2,1)S(1)}, u32[]{:S(2)}, u32[]{:S(2)}) collective-permute-start(bf16[2,2,1024]{2,1,0:T(2,128)(2,1)S(1)} %broadcast_select_fusion.2), channel_id=1, source_target_pairs={{0,8},{4,12},{8,0},{12,4},{16,24},{20,28},{24,16},{28,20},{1,9},{5... | collective-permute-start | bytes 24584 | tf_op jit(solution)/shard_map/ppermute | solution.py:15
  28.5 78.1 %collective-permute-start.15 = (bf16[512,1024]{1,0:T(8,128)(2,1)S(1)}, bf16[512,1024]{1,0:T(8,128)(2,1)}, u32[]{:S(2)}, u32[]{:S(2)}) collective-permute-start(bf16[512,1024]{1,0:T(8,128)(2,1)S(1)} %copy-done.1), channel_id=1, source_target_pairs={{0,4},{4,0},{8,12},{12,8},{16,20},{20,16},{24,28},{28,24},{1,5},{5... | collective-permute-start | bytes 3145736 | tf_op jit(solution)/shard_map/ppermute | solution.py:15
  30.0 42.6 %collective-permute-start.19 = (bf16[128,1024]{1,0:T(8,128)(2,1)S(1)}, bf16[128,1024]{1,0:T(8,128)(2,1)}, u32[]{:S(2)}, u32[]{:S(2)}) collective-permute-start(bf16[128,1024]{1,0:T(8,128)(2,1)S(1)} %copy-done.2), channel_id=1, source_target_pairs={{0,8},{4,12},{8,0},{12,4},{16,24},{20,28},{24,16},{28,20},{1,9},{5... | collective-permute-start | bytes 786440 | tf_op jit(solution)/shard_map/ppermute | solution.py:15
  30.5 4.8 %collective-permute-start.5 = (bf16[4,2,1024]{2,1,0:T(2,128)(2,1)S(1)}, bf16[4,2,1024]{2,1,0:T(2,128)(2,1)S(1)}, u32[]{:S(2)}, u32[]{:S(2)}) collective-permute-start(bf16[4,2,1024]{2,1,0:T(2,128)(2,1)S(1)} %broadcast_select_fusion.1), channel_id=1, source_target_pairs={{0,16},{4,20},{8,24},{12,28},{16,0},{20,4},{24,8},{28,12},{1,17},{... | collective-permute-start | bytes 49160 | tf_op jit(solution)/shard_map/ppermute | solution.py:15
  35.8 3.1 %collective-permute-start.8 = (f32[2,2,512]{2,1,0:T(2,128)S(1)}, f32[2,2,512]{2,1,0:T(2,128)S(1)}, u32[]{:S(2)}, u32[]{:S(2)}) collective-permute-start(f32[2,2,512]{2,1,0:T(2,128)S(1)} %bitcast.149), channel_id=1, source_target_pairs={{0,3},{1,2},{2,1},{3,0},{4,7},{5,6},{6,5},{7,4},{8,11},{9,10},{10,... | collective-permute-start | bytes 24584 | tf_op jit(solution)/shard_map/ppermute | solution.py:15
  35.9 6.9 %collective-permute-start.7 = (f32[2,2,512]{2,1,0:T(2,128)S(1)}, f32[2,2,512]{2,1,0:T(2,128)}, u32[]{:S(2)}, u32[]{:S(2)}) collective-permute-start(f32[2,2,512]{2,1,0:T(2,128)S(1)} %bitcast.148), channel_id=1, source_target_pairs={{0,2},{1,3},{2,0},{3,1},{4,6},{5,7},{6,4},{7,5},{8,10},{9,11},{10,... | collective-permute-start | bytes 24584 | tf_op jit(solution)/shard_map/ppermute | solution.py:15
  37.6 7.0 %collective-permute-start.6 = (f32[2,2,512]{2,1,0:T(2,128)S(1)}, f32[2,2,512]{2,1,0:T(2,128)}, u32[]{:S(2)}, u32[]{:S(2)}) collective-permute-start(f32[2,2,512]{2,1,0:T(2,128)S(1)} %bitcast.147), channel_id=1, source_target_pairs={{0,1},{1,0},{2,3},{3,2},{4,5},{5,4},{6,7},{7,6},{8,9},{9,8},{10,11... | collective-permute-start | bytes 24584 | tf_op jit(solution)/shard_map/ppermute | solution.py:15
  39.0 8.1 %collective-permute-start.13 = (bf16[64,1024]{1,0:T(8,128)(2,1)}, bf16[64,1024]{1,0:T(8,128)(2,1)S(1)}, u32[]{:S(2)}, u32[]{:S(2)}) collective-permute-start(bf16[64,1024]{1,0:T(8,128)(2,1)} %get-tuple-element.11), channel_id=1, source_target_pairs={{0,24},{4,28},{8,16},{12,20},{16,8},{20,12},{24,0},{28,4},{1,25},{... | collective-permute-start | bytes 393224 | tf_op jit(solution)/shard_map/ppermute | solution.py:15
  42.8 12.6 %collective-permute-start.12 = (bf16[64,1024]{1,0:T(8,128)(2,1)S(1)}, bf16[64,1024]{1,0:T(8,128)(2,1)S(1)}, u32[]{:S(2)}, u32[]{:S(2)}) collective-permute-start(bf16[64,1024]{1,0:T(8,128)(2,1)S(1)} %get-tuple-element.12), channel_id=1, source_target_pairs={{0,16},{4,20},{8,24},{12,28},{16,0},{20,4},{24,8},{28,12},{1,17},{... | collective-permute-start | bytes 393224 | tf_op jit(solution)/shard_map/ppermute | solution.py:15
  44.6 11.4 %collective-permute-start.11 = (bf16[64,1024]{1,0:T(8,128)(2,1)S(1)}, bf16[64,1024]{1,0:T(8,128)(2,1)S(1)}, u32[]{:S(2)}, u32[]{:S(2)}) collective-permute-start(bf16[64,1024]{1,0:T(8,128)(2,1)S(1)} %get-tuple-element.10), channel_id=1, source_target_pairs={{0,8},{4,12},{8,0},{12,4},{16,24},{20,28},{24,16},{28,20},{1,9},{5... | collective-permute-start | bytes 393224 | tf_op jit(solution)/shard_map/ppermute | solution.py:15
  47.0 26.6 %collective-permute-start.20 = (bf16[128,1024]{1,0:T(8,128)(2,1)S(1)}, bf16[128,1024]{1,0:T(8,128)(2,1)}, u32[]{:S(2)}, u32[]{:S(2)}) collective-permute-start(bf16[128,1024]{1,0:T(8,128)(2,1)S(1)} %copy-done.2), channel_id=1, source_target_pairs={{0,16},{4,20},{8,24},{12,28},{16,0},{20,4},{24,8},{28,12},{1,17},{... | collective-permute-start | bytes 786440 | tf_op jit(solution)/shard_map/ppermute | solution.py:15
  55.4 3.0 %collective-permute-start.9 = (bf16[2,512]{1,0:T(2,128)(2,1)S(1)}, bf16[2,512]{1,0:T(2,128)(2,1)S(1)}, u32[]{:S(2)}, u32[]{:S(2)}) collective-permute-start(bf16[2,512]{1,0:T(2,128)(2,1)S(1)} %get-tuple-element.31), channel_id=1, source_target_pairs={{0,0},{1,8},{2,16},{3,24},{4,4},{5,12},{6,20},{7,28},{8,1},{9,9},{... | collective-permute-start | bytes 6152 | tf_op jit(solution)/shard_map/ppermute | solution.py:112
  56.1 10.1 %collective-permute-start.10 = (bf16[2,512]{1,0:T(2,128)(2,1)S(1)}, bf16[2,512]{1,0:T(2,128)(2,1)S(1)}, u32[]{:S(2)}, u32[]{:S(2)}) collective-permute-start(bf16[2,512]{1,0:T(2,128)(2,1)S(1)} %get-tuple-element.30), channel_id=1, source_target_pairs={{0,4},{1,12},{2,20},{3,28},{4,0},{5,8},{6,16},{7,24},{8,5},{9,13},... | collective-permute-start | bytes 6152 | tf_op jit(solution)/shard_map/ppermute | solution.py:112
  58.4 16.2 %collective-permute-start.21 = (bf16[128,1024]{1,0:T(8,128)(2,1)S(1)}, bf16[128,1024]{1,0:T(8,128)(2,1)}, u32[]{:S(2)}, u32[]{:S(2)}) collective-permute-start(bf16[128,1024]{1,0:T(8,128)(2,1)S(1)} %copy-done.2), channel_id=1, source_target_pairs={{0,24},{4,28},{8,16},{12,20},{16,8},{20,12},{24,0},{28,4},{1,25},{... | collective-permute-start | bytes 786440 | tf_op jit(solution)/shard_map/ppermute | solution.py:15
  66.2 10.2 %collective-permute-start.14 = (bf16[3,64,1024]{2,1,0:T(8,128)(2,1)}, bf16[3,64,1024]{2,1,0:T(8,128)(2,1)}, u32[]{:S(2)}, u32[]{:S(2)}) collective-permute-start(bf16[3,64,1024]{2,1,0:T(8,128)(2,1)} %pad_maximum_fusion.1), channel_id=1, source_target_pairs={{0,1},{1,0},{2,3},{3,2},{4,5},{5,4},{6,7},{7,6},{8,9},{9,8},{10,11... | collective-permute-start | bytes 1179656 | tf_op jit(solution)/shard_map/ppermute | solution.py:15
  75.6 39.9 %collective-permute-start.24 = (bf16[512,1024]{1,0:T(8,128)(2,1)S(1)}, bf16[512,1024]{1,0:T(8,128)(2,1)S(1)}, u32[]{:S(2)}, u32[]{:S(2)}) collective-permute-start(bf16[512,1024]{1,0:T(8,128)(2,1)S(1)} %constant_dynamic-update-slice_fusion), channel_id=1, source_target_pairs={{0,4},{4,0},{8,12},{12,8},{16,20},{20,16},{24,28},{28,24},{1,5},{5... | collective-permute-start | bytes 3145736 | tf_op jit(solution)/shard_map/ppermute | solution.py:15
  78.1 28.5 %collective-permute-start.22 = (bf16[256,512]{1,0:T(8,128)(2,1)S(1)}, bf16[256,512]{1,0:T(8,128)(2,1)S(1)}, u32[]{:S(2)}, u32[]{:S(2)}) collective-permute-start(bf16[256,512]{1,0:T(8,128)(2,1)S(1)} %dynamic_slice.76), channel_id=1, source_target_pairs={{0,4},{4,0},{8,12},{12,8},{16,20},{20,16},{24,28},{28,24},{1,5},{5... | collective-permute-start | bytes 786440 | tf_op jit(solution)/shard_map/ppermute | solution.py:15
  106.6 8.9 %collective-permute-start.23 = (bf16[256,512]{1,0:T(8,128)(2,1)S(1)}, bf16[256,512]{1,0:T(8,128)(2,1)S(1)}, u32[]{:S(2)}, u32[]{:S(2)}) collective-permute-start(bf16[256,512]{1,0:T(8,128)(2,1)S(1)} %collective-permute-done.22), channel_id=1, source_target_pairs={{0,1},{1,0},{2,3},{3,2},{4,5},{5,4},{6,7},{7,6},{8,9},{9,8},{10,11... | collective-permute-start | bytes 786440 | tf_op jit(solution)/shard_map/ppermute | solution.py:15
  108.6 11.1 %collective-permute-start.18 = (bf16[128,1024]{1,0:T(8,128)(2,1)S(1)}, bf16[128,1024]{1,0:T(8,128)(2,1)S(1)}, u32[]{:S(2)}, u32[]{:S(2)}) collective-permute-start(bf16[128,1024]{1,0:T(8,128)(2,1)S(1)} %get-tuple-element.8), channel_id=1, source_target_pairs={{0,24},{4,28},{8,16},{12,20},{16,8},{20,12},{24,0},{28,4},{1,25},{... | collective-permute-start | bytes 786440 | tf_op jit(solution)/shard_map/ppermute | solution.py:15
  109.7 26.4 %collective-permute-start.17 = (bf16[128,1024]{1,0:T(8,128)(2,1)S(1)}, bf16[128,1024]{1,0:T(8,128)(2,1)S(1)}, u32[]{:S(2)}, u32[]{:S(2)}) collective-permute-start(bf16[128,1024]{1,0:T(8,128)(2,1)S(1)} %get-tuple-element.9), channel_id=1, source_target_pairs={{0,16},{4,20},{8,24},{12,28},{16,0},{20,4},{24,8},{28,12},{1,17},{... | collective-permute-start | bytes 786440 | tf_op jit(solution)/shard_map/ppermute | solution.py:15
  114.9 21.1 %collective-permute-start.16 = (bf16[128,1024]{1,0:T(8,128)(2,1)S(1)}, bf16[128,1024]{1,0:T(8,128)(2,1)S(1)}, u32[]{:S(2)}, u32[]{:S(2)}) collective-permute-start(bf16[128,1024]{1,0:T(8,128)(2,1)S(1)} %get-tuple-element.7), channel_id=1, source_target_pairs={{0,8},{4,12},{8,0},{12,4},{16,24},{20,28},{24,16},{28,20},{1,9},{5... | collective-permute-start | bytes 786440 | tf_op jit(solution)/shard_map/ppermute | solution.py:15

commit v2 on v0

v2 whole, which is shorter than its diff:
```python
import functools

import jax
import jax.numpy as jnp
from jax import lax
from jax.experimental import pallas as pl
from jax.experimental.pallas import tpu as pltpu
from jax.sharding import PartitionSpec as P

KVH = 4
HD = 128
NEG_FILL = -1e30
INNER = 2
PAD = 16
BF16 = jnp.bfloat16
F32 = jnp.float32


def flip(a, axis, bits, name):
    size = lax.axis_size(axis)
    with jax.named_scope(name):
        return lax.ppermute(a, axis, [(i, i ^ bits) for i in range(size)])


def dot(a, b):
    return jnp.dot(a, b, preferred_element_type=F32)


def over_features(a, b):
    return lax.dot_general(a, b, (((1,), (1,)), ((), ())), preferred_element_type=F32)


def over_tokens(a, b):
    return lax.dot_general(a, b, (((0,), (0,)), ((), ())), preferred_element_type=F32)


class Mover:
    def __init__(self, sems):
        self.sems, self.count, self.open = sems, 0, []

    def start(self, source, target):
        copy = pltpu.make_async_copy(source, target, self.sems.at[self.count])
        self.count += 1
        self.open.append(copy)
        copy.start()
        return copy

    def wait(self, *copies):
        for copy in copies:
            copy.wait()
            self.open = [other for other in self.open if other is not copy]

    def finish(self):
        self.wait(*list(self.open))


def places():
    fsdp_index, tp_index = lax.axis_index("fsdp"), lax.axis_index("tp")
    return tp_index, tp_index % 2, fsdp_index // INNER, fsdp_index % INNER, tp_index * KVH // lax.axis_size("tp")


def call(kernel, name, operands, out_shapes, scratch, waits=(), scalars=None, room=12):
    copies = 4 * (len(operands) + len(out_shapes))
    scalars = [] if scalars is None else [scalars]

    def body(*refs):
        front, refs = refs[: len(scalars)], refs[len(scalars) :]
        ins, refs = refs[: len(operands)], refs[len(operands) + len(waits) :]
        outs, refs = refs[: len(out_shapes)], refs[len(out_shapes) :]
        mover = Mover(refs[-1])
        kernel(mover, *front, ins, outs, refs[:-1])
        mover.finish()

    results = pl.pallas_call(
        body,
        out_shape=[jax.ShapeDtypeStruct(shape, dtype) for shape, dtype in out_shapes],
        in_specs=[pl.BlockSpec(memory_space=pltpu.SMEM)] * len(scalars)
        + [pl.BlockSpec(memory_space=pltpu.HBM)] * (len(operands) + len(waits)),
        out_specs=[pl.BlockSpec(memory_space=pltpu.HBM)] * len(out_shapes),
        scratch_shapes=[pltpu.VMEM(shape, dtype) for shape, dtype in scratch] + [pltpu.SemaphoreType.DMA((copies,))],
        compiler_params=pltpu.CompilerParams(vmem_limit_bytes=room << 20),
        cost_estimate=pl.CostEstimate(flops=0, bytes_accessed=0, transcendentals=0),
        name=name,
    )(*scalars, *operands, *waits)
    return list(results)


def shaped(*arrays):
    return [(a.shape, a.dtype) for a in arrays]


def attend_kernel(steps, mover, lengths_ref, ins, outs, scratch):
    query_hbm, keys_hbm, values_hbm, new_keys_hbm, new_values_hbm = ins
    query_ref, keys_ref, values_ref, new_keys_ref, new_values_ref, query_rows, out_rows, own_rows, own_ref = scratch
    tp_index, _, _, _, own_group = places()
    length = lengths_ref[0]
    own_out, *part_outs = outs
    tp_size = sum(out.shape[0] for out in part_outs)
    first = mover.start(query_hbm.at[0], query_ref)
    news = [mover.start(new_keys_hbm.at[0], new_keys_ref), mover.start(new_values_hbm.at[0], new_values_ref)]
    groups = [slice(g * HD, (g + 1) * HD) for g in range(KVH)]
    arrive = [
        (mover.start(keys_hbm.at[0, :, group], keys_ref.at[:, group]), mover.start(values_hbm.at[0, :, group], values_ref.at[:, group]))
        for group in groups
    ]
    width = query_ref.shape[1]
    cache_len = keys_ref.shape[0]
    rows = width // HD // KVH * steps
    mover.wait(first)
    for h in range(width // HD):
        query_rows[h * steps : (h + 1) * steps, :] = query_ref[:, h * HD : (h + 1) * HD].astype(F32)
    usable = lax.broadcasted_iota(jnp.int32, (rows, cache_len), 1) + tp_index * cache_len < length
    left = lax.broadcasted_iota(jnp.int32, (rows, HD), 1) < HD // 2
    for g in range(KVH):
        mover.wait(*arrive[g])
        query = query_rows[g * rows : (g + 1) * rows, :].astype(BF16)
        scores = over_features(query, keys_ref[:, g * HD : (g + 1) * HD]) * (1.0 / HD**0.5)
        maxima = jnp.max(jnp.where(usable, scores, NEG_FILL), axis=1, keepdims=True)
        terms = jnp.where(usable, jnp.exp(scores - maxima), 0.0)
        totals = jnp.sum(terms, axis=1, keepdims=True)
        upper = terms.astype(BF16)
        lower = (terms - upper.astype(F32)).astype(BF16)
        both = dot(jnp.concatenate([upper, lower], axis=0), values_ref[:, g * HD : (g + 1) * HD])
        out_rows[g * rows : (g + 1) * rows, :HD] = both[:rows] + both[rows:]
        out_rows[g * rows : (g + 1) * rows, HD:] = jnp.where(left, maxima, totals)
    count = own_rows.shape[1]
    for t in range(KVH * rows // count):
        for k in range(tp_size):

            @pl.when(tp_index ^ k == t)
            def _():
                own_rows[k] = out_rows[t * count : (t + 1) * count, :]

        @pl.when(tp_index == t)
        def _():
            own_ref[:count, :HD] = query_rows[t * count : (t + 1) * count, :]

    first = 0
    for part_out in part_outs:
        mover.start(own_rows.at[first : first + part_out.shape[0]], part_out)
        first += part_out.shape[0]
    mover.wait(*news)
    own_ref[:count, HD:] = jnp.zeros((count, HD), F32)
    for at, ref in ((0, new_keys_ref), (HD, new_values_ref)):
        chosen = ref[:, :HD].astype(F32)
        for g in range(1, KVH):
            chosen = jnp.where(own_group == g, ref[:, groups[g]].astype(F32), chosen)
        own_ref[count : count + steps, at : at + HD] = chosen
    mover.start(own_ref, own_out)


def combine_kernel(steps, own_ref, attn_ref, *refs):
    *part_refs, out_ref, rows_ref = refs
    tokens = attn_ref.shape[0]
    count = part_refs[0].shape[1]
    out_ref[:tokens, :] = attn_ref[...]
    rows_ref[...] = jnp.zeros_like(rows_ref)
    step = lax.broadcasted_iota(jnp.int32, (count, 1), 0) % steps
    query = own_ref[:count, :HD]
    keys, values = own_ref[count:, :HD], own_ref[count:, HD:]
    parts = [part_ref[part_ref.shape[0] - 1] for part_ref in part_refs]
    scores = []
    for j in range(steps):
        score = jnp.sum(query * keys[j : j + 1], axis=-1, keepdims=True) * (1.0 / HD**0.5)
        scores.append(jnp.where(step >= j, score, NEG_FILL))
    maxima = [part[:, HD : HD + 1] for part in parts]
    highest = functools.reduce(jnp.maximum, scores + maxima)
    total = jnp.zeros((count, 1), F32)
    weighted = jnp.zeros((count, HD), F32)
    for part, own in zip(parts, maxima):
        scale = jnp.exp(own - highest)
        total = total + part[:, HD + HD // 2 : HD + HD // 2 + 1] * scale
        weighted = weighted + part[:, :HD] * scale
    for j in range(steps):
        term = jnp.where(step >= j, jnp.exp(scores[j] - highest), 0.0)
        total = total + term
        weighted = weighted + term * values[j : j + 1]
    attended = weighted / total
    for row in range(count):
        h, s = row // steps, row % steps
        rows_ref[s : s + 1, h * HD : (h + 1) * HD] = attended[row : row + 1]
    out_ref[tokens:, :] = rows_ref[...].astype(BF16)


def middle_kernel(outer, mover, ins, outs, scratch):
    grad_hbm, weight_hbm, other_hbm, *cot_hbms = ins
    sent_outs, (total_out, cot_own_out, cot_far_out) = outs[: outer - 1], outs[outer - 1 :]
    cots_ref, weight_ref, other_ref, sent_ref, total_ref, cot_own_ref, cot_far_ref = scratch
    _, core, z, x, _ = places()
    tokens = grad_hbm.shape[0]
    plane = cots_ref.shape[1]
    feats = weight_ref.shape[0]
    half = tokens // 2
    weights = [mover.start(weight_hbm, weight_ref), mover.start(other_hbm, other_ref)]
    blocks = [[mover.start(grad_hbm.at[:, pl.ds(pl.multiple_of(z * plane, plane), plane)], cots_ref.at[:tokens])]]
    for k in range(1, outer):
        blocks.append([])
        for hbms, side in ((cot_hbms[:2], core), (cot_hbms[2:], 1 - core)):
            base = pl.multiple_of(k * tokens + side * half, half)
            for i, hbm in enumerate(hbms):
                size = hbm.shape[0]
                low, high = max((k - 1) * half, i * size), min(k * half, (i + 1) * size)
                if low < high:
                    source = hbm.at[low - i * size : high - i * size]
                    first = pl.multiple_of(base + (low - (k - 1) * half), half // 2)
                    blocks[k].append(mover.start(source, cots_ref.at[pl.ds(first, high - low)]))
    mover.wait(*weights)
    span = outer * half
    for k in reversed(range(outer)):
        mover.wait(*blocks[k])
        here = slice(k * tokens, (k + 1) * tokens)
        block = cots_ref[here, :]
        low, high = block[:, :feats], block[:, feats:]
        own = jnp.where(x == 0, low, high)
        other = jnp.where(x == 0, high, low)
        total = dot(own, weight_ref[...]) + dot(other, other_ref[...])
        if k == 0:
            total_ref[...] = total
            mover.start(total_ref, total_out)
        else:
            sent_ref[k - 1] = total.astype(BF16)
            mover.start(sent_ref.at[k - 1], sent_outs[k - 1])
        cot_own_ref[here, :] = own
        for side in range(2):
            if span * side <= k * tokens < span * (side + 1):

                @pl.when(core == side)
                def _():
                    cot_far_ref[k * tokens - span * side : (k + 1) * tokens - span * side, :] = other

    mover.start(cot_far_ref, cot_far_out)
    mover.start(cot_own_ref, cot_own_out)


def decode_kernel(steps, mover, ins, outs, scratch):
    weight_hbm, other_hbm, *load_hbms = ins
    pack_out, *part_outs = outs
    weight_ref, other_ref, loads_ref, rows_ref, by_row_ref, parts_ref = scratch
    q, _, z, x, _ = places()
    outer = len(load_hbms)
    tokens = load_hbms[0].shape[0] - PAD
    loads = [mover.start(hbm, loads_ref.at[k]) for k, hbm in enumerate(load_hbms)]
    weights = [mover.start(weight_hbm, weight_ref), mover.start(other_hbm, other_ref)]
    mover.wait(*loads)
    for k in range(outer):
        mover.start(loads_ref.at[k, :tokens], pack_out.at[k * tokens : (k + 1) * tokens])
    mover.wait(*weights)
    for k in range(outer):
        rows_ref[k * steps : (k + 1) * steps, :] = loads_ref[k, tokens:, :].astype(F32)[:steps]
    every = rows_ref[...].astype(BF16)
    own, other = over_features(every, weight_ref[...]), over_features(every, other_ref[...])
    wide = jnp.concatenate([jnp.where(x == 0, own, other), jnp.where(x == 0, other, own)], axis=1)
    for k in range(outer):
        by_row_ref[k] = wide[k * steps : (k + 1) * steps]
    share = parts_ref.shape[1]
    for k, out in enumerate(part_outs):
        for i in range(share):
            parts_ref[k, i] = by_row_ref[((q ^ k) * share + i) ^ z]
        mover.start(parts_ref.at[k], out)


def stack_kernel(mover, ins, outs, scratch):
    half, size = ins[0].shape[0], outs[0].shape[0]
    arrive = [mover.start(hbm, scratch[0].at[k * half : (k + 1) * half]) for k, hbm in enumerate(ins)]
    mover.wait(*arrive)
    for i, out in enumerate(outs):
        mover.start(scratch[0].at[i * size : (i + 1) * size], out)


def release_kernel(mover, ins, outs, scratch):
    arrive = [mover.start(hbm, scratch[0].at[k]) for k, hbm in enumerate(ins)]
    for k, copy in enumerate(arrive):
        mover.wait(copy)
        mover.start(scratch[0].at[k], outs[k])


def sum_kernel(mover, ins, outs, scratch):
    total_hbm, *part_hbms = ins
    total_ref, parts_ref, out_ref = scratch
    arrive = [mover.start(total_hbm, total_ref)]
    arrive += [mover.start(hbm, parts_ref.at[i]) for i, hbm in enumerate(part_hbms)]
    mover.wait(*arrive)
    total = total_ref[...]
    for i in range(len(part_hbms)):
        total = total + parts_ref[i].astype(F32)
    out_ref[...] = total.astype(BF16)
    mover.start(out_ref, outs[0])


def product_kernel(mover, ins, outs, scratch):
    cot_hbm, cot_twin_hbm, attn_hbm, total_hbm = ins
    cots_ref, attn_ref, total_ref, out_ref = scratch
    _, core, _, _, _ = places()
    span = cot_hbm.shape[0]
    arrive = [
        mover.start(cot_hbm, cots_ref.at[pl.ds(pl.multiple_of(core * span, span), span)]),
        mover.start(cot_twin_hbm, cots_ref.at[pl.ds(pl.multiple_of((1 - core) * span, span), span)]),
        mover.start(attn_hbm, attn_ref),
    ]
    pieces = 2
    step = out_ref.shape[0] // pieces
    totals = [mover.start(total_hbm.at[i * step : (i + 1) * step], total_ref.at[i * step : (i + 1) * step]) for i in range(pieces)]
    mover.wait(*arrive)
    for i in range(pieces):
        here = slice(i * step, (i + 1) * step)
        product = over_tokens(cots_ref[:, here], attn_ref[...])
        mover.wait(totals[i])
        out_ref[here, :] = total_ref[here, :] + product
        mover.start(out_ref.at[here], outs[0].at[here])


def shards(dec_query, new_keys, new_values, cache_keys, cache_values, lengths, out_weight, train_attn, grad_out):
    rows, steps, width = dec_query.shape
    assert rows == 1
    fsdp_size = lax.axis_size("fsdp")
    tp_size = lax.axis_size("tp")
    outer = fsdp_size // INNER
    share = outer // tp_size
    fsdp_index = lax.axis_index("fsdp")
    tp_index = lax.axis_index("tp")
    z, x = fsdp_index // INNER, fsdp_index % INNER
    tokens = grad_out.shape[0]
    feats, cols = out_weight.shape
    plane = feats * INNER
    slot = tp_index % 4
    heads = width // HD
    count = heads // tp_size * steps
    far = range(1, outer)
    others = range(1, tp_size)

    other_weight = flip(out_weight, "fsdp", 1, "weight_x")

    half = tokens // 2
    got = [
        flip(lax.dynamic_slice(grad_out, (tp_index % 2 * half, (z ^ k) * plane), (half, plane)), "fsdp", k * INNER, f"cot_z{k}")
        for k in far
    ]

    sizes = [1 << b for b in range(tp_size.bit_length() - 1)]
    own, part, *chunks = call(
        functools.partial(attend_kernel, steps),
        "attend",
        [dec_query, cache_keys, cache_values, new_keys, new_values],
        [((count + 8, 2 * HD), F32), ((1, count, 2 * HD), F32)] + [((size, count, 2 * HD), F32) for size in sizes],
        shaped(dec_query[0], cache_keys[0], cache_values[0], new_keys[0], new_values[0])
        + [((heads * steps, HD), F32), ((heads * steps, 2 * HD), F32), ((tp_size, count, 2 * HD), F32), ((count + 8, 2 * HD), F32)],
        scalars=lengths,
        room=63,
    )
    held = []
    for size, chunk in reversed(list(zip(sizes, chunks))):
        leaving = [chunk] + [a if size == 1 else a[size:] for a in held]
        held = [a if size == 1 else a[:size] for a in held]
        came = [flip(a, "tp", size, f"softmax_tp{size}") for a in leaving]
        held = [a[:1] if size == 1 and a.shape[0] > 1 else a for a in held] + came
    parts = [part, *held]
    load = pl.pallas_call(
        functools.partial(combine_kernel, steps),
        out_shape=jax.ShapeDtypeStruct((tokens + PAD, cols), BF16),
        in_specs=[pl.BlockSpec(memory_space=pltpu.VMEM)] * (len(parts) + 2),
        out_specs=pl.BlockSpec(memory_space=pltpu.VMEM),
        scratch_shapes=[pltpu.VMEM((PAD, cols), F32)],
        cost_estimate=pl.CostEstimate(flops=0, bytes_accessed=0, transcendentals=0),
        name="combine",
    )(own, train_attn, *parts)
    loads = [flip(load, "fsdp", k * INNER, f"attn_z{k}") for k in far]

    stacked = call(
        stack_kernel,
        "stack",
        got,
        [((len(far) * half // 2, plane), BF16)] * 2,
        [((len(far) * half, plane), BF16)],
        waits=[load],
    )
    twins = [flip(a, "tp", 1, "cot_core") for a in stacked]

    *sent, total, cot_own, cot_far = call(
        functools.partial(middle_kernel, outer),
        "middle",
        [grad_out, out_weight, other_weight, *stacked, *twins],
        [((tokens, cols), BF16)] * len(far)
        + [((tokens, cols), F32), ((outer * tokens, feats), BF16), ((outer * half, feats), BF16)],
        [
            ((outer * tokens, plane), BF16),
            ((feats, cols), BF16),
            ((feats, cols), BF16),
            ((len(far), tokens, cols), BF16),
            ((tokens, cols), F32),
            ((outer * tokens, feats), BF16),
            ((outer * half, feats), BF16),
        ],
    )
    cot_x = flip(cot_far, "fsdp", 1, "cot_x")
    pack, *dec = call(
        functools.partial(decode_kernel, steps),
        "decode",
        [out_weight, other_weight, load, *loads],
        [((outer * tokens, cols), BF16)] + [((share, steps, plane), F32)] * tp_size,
        [
            ((feats, cols), BF16),
            ((feats, cols), BF16),
            ((outer, tokens + PAD, cols), BF16),
            ((outer * steps, cols), F32),
            ((outer, steps, plane), F32),
            ((tp_size, share, steps, plane), F32),
        ],
        waits=[cot_x],
    )
    sums = [flip(sent[k - 1], "fsdp", k * INNER, f"sum_z{k}") for k in far]
    pack_x = flip(pack, "fsdp", 1, "attn_x")
    cot_x_twin = flip(cot_x, "tp", 1, "cot_x_core")

    dec = call(
        release_kernel, "release", dec, [((share, steps, plane), F32)] * tp_size, [((tp_size, share, steps, plane), F32)], waits=[cot_x_twin]
    )
    dec = (dec[0] + sum(flip(dec[k], "tp", k, f"dec_tp{k}") for k in others)).astype(BF16)
    pieces = []
    for j in range(share):
        perm = [
            ((a * INNER + b) * tp_size + q, ((q * share + (a % share ^ j)) * INNER + b) * tp_size + a // share)
            for a in range(outer)
            for b in range(INNER)
            for q in range(tp_size)
        ]
        with jax.named_scope("dec_place"):
            pieces.append(lax.ppermute(lax.dynamic_index_in_dim(dec, z % share ^ j, 0, False), ("fsdp", "tp"), perm))
    pieces = jnp.stack(pieces)
    dec_out = jnp.concatenate(
        [lax.dynamic_index_in_dim(pieces, (z % share) ^ s, 0, False) for s in range(share)], axis=1
    ).reshape(rows, steps, share * plane)

    (grad_attn,) = call(
        sum_kernel,
        "sum",
        [total, *sums],
        [((tokens, cols), BF16)],
        [((tokens, cols), F32), ((len(far), tokens, cols), BF16), ((tokens, cols), BF16)],
    )

    own_total = over_tokens(cot_own, pack)
    (grad_weight,) = call(
        product_kernel,
        "product",
        [cot_x, cot_x_twin, pack_x, own_total],
        [((feats, cols), F32)],
        [((outer * tokens, feats), BF16), ((outer * tokens, cols), BF16), ((feats, cols), F32), ((feats, cols), F32)],
        waits=[grad_attn],
    )
    return dec_out, grad_attn, grad_weight


def solution(mesh):
    return jax.shard_map(
        shards,
        mesh=mesh,
        in_specs=(
            P("fsdp", None, None),
            P("fsdp", None, None),
            P("fsdp", None, None),
            P("fsdp", "tp", None),
            P("fsdp", "tp", None),
            P("fsdp"),
            P("fsdp", "tp"),
            P("fsdp", "tp"),
            P("fsdp", None),
        ),
        out_specs=(P("fsdp", None, "tp"), P("fsdp", "tp"), P("fsdp", "tp")),
        check_vma=False,
    )
```

time: 469 us -> 90.3 us (0.19)
  waiting for transfers between devices: 404 us -> 40 us
  starting transfers between devices: 0.12 us -> 25.3 us
  matrix products: 23.9 us -> 0.73 us
  Pallas kernels: 0 us -> 17.2 us
  blocking collectives: 16 us -> 0 us
  between operations: 14.5 us -> 1.43 us
    reduce_scatter x1 -> x0, waiting for transfers between devices: 284 us -> none  [shards(): lax.psum_scatter(lax.dot_general(grad_out, train_attn, (((0,), (0,)), (()...]
    all_gather x1 -> x0, waiting for transfers between devices: 102 us -> none  [shards(): weights = lax.all_gather(out_weight, 'fsdp', axis=0, tiled=True)]
    ppermute x0 -> x22, waiting for transfers between devices: none -> 40 us  [the longest x21 39.8 us: flip(): return lax.ppermute(a, axis, [(i, i ^ bits) for i in range(size)])]
    ppermute x0 -> x22, starting transfers between devices: none -> 25.3 us  [the longest x21 21.5 us: flip(): return lax.ppermute(a, axis, [(i, i ^ bits) for i in range(size)])]
    dot_general x7 -> x1, matrix products: 23.9 us -> 0.73 us  [over_tokens(): lax.dot_general(a, b, (((0,), (0,)), ((), ())), preferred_element_type=F32)]
    unnamed x4 -> x0, waiting for transfers between devices: 17.4 us -> none
    pallas_call x0 -> x8, Pallas kernels: none -> 17.2 us  [the longest x7 15.2 us: call(): pl.pallas_call(body, out_shape=[jax.ShapeDtypeStruct(shape, dtype) for sh...]
    all_gather x3 -> x0, blocking collectives: 16 us -> none  [combined_all(): gathered = jax.tree.map(lambda a: lax.all_gather(a, axis), part)]
  transfers between devices with their start and end apart: 3 -> 22, of which waited for: 3 -> 10; matrix products, arithmetic and copies ran while one was open for 5% -> 3% of each run, Pallas kernels for 0% -> 13%
where the time goes in v2:
time: 90.3 us; the launch traced here: 89.7 us
  waiting for transfers between devices  40 us (44%)
  starting transfers between devices  25.3 us (28%)
  Pallas kernels  17.2 us (19%)
  local copies, waits for them, and re-layouts  5.05 us (6%)
  between operations  1.43 us (2%)
    ppermute x21, waiting for transfers between devices, flip(): return lax.ppermute(a, axis, [(i, i ^ bits) for i in range(size)])  39.8 us
    ppermute x21, starting transfers between devices, flip(): return lax.ppermute(a, axis, [(i, i ^ bits) for i in range(size)])  21.5 us
    pallas_call x7, Pallas kernels, call(): pl.pallas_call(body, out_shape=[jax.ShapeDtypeStruct(shape, dtype) for sh...  15.2 us
    ppermute x1, starting transfers between devices, shards(): lax.ppermute(lax.dynamic_index_in_dim(dec, z % share ^ j, 0, False), ('fs...  3.74 us
    unnamed x11, local copies, waits for them, and re-layouts  3.39 us
    pallas_call x1, Pallas kernels, shards(): pl.pallas_call(functools.partial(combine_kernel, steps), out_shape=jax.Sh...  1.95 us
  transfers between devices with their start and end apart: 22, of which 10 were waited for; matrix products, arithmetic and copies ran while one was open for 3% of the time, Pallas kernels for 13%

profile of v2, /device:TPU:17, one launch (start us, length us, event | category | flops | bytes accessed | tf_op | source)
XLA Modules:
  0.0 89.7 jit_solution(17193754681128834178)
XLA Ops:
  0.6 1.3 %collective-permute-start = (bf16[512,1024]{1,0:T(8,128)(2,1)}, bf16[512,1024]{1,0:T(8,128)(2,1)}, u32[]{:S(2)}, u32[]{:S(2)}) collective-permute-start(bf16[512,1024]{1,0:T(8,128)(2,1)} %refs_0_.4), channel_id=1, source_target_pairs={{0,4},{4,0},{8,12},{12,8},{16,20},{20,16},{24,28},{28,24},{1,5},{5... | collective-permute-start | bytes 3145736 | tf_op jit(solution)/shard_map/weight_x/ppermute | solution.py:22
  1.9 1.1 %fusion.1 = (bf16[64,1024]{1,0:T(8,128)(2,1)S(1)}, bf16[64,1024]{1,0:T(8,128)(2,1)S(1)}, bf16[64,1024]{1,0:T(8,128)(2,1)S(1)}) fusion(bf16[128,4096]{1,0:T(8,128)(2,1)} %refs_0_.3, s32[]{:T(128)S(6)} %select_n.37, s32[]{:T(128)S(6)} %select_n.41, s32[]{:T(128)S(6)} %select_n.40, s32[]{:T(128)S(6)} %select_n.39), kind=kLoop, calls=%fused_computation.2 | loop fusion | bytes 786448 | tf_op jit(solution)/shard_map/dynamic_slice | solution.py:335
  3.0 0.2 collective-permute-start.9
  3.2 3.2 %collective-permute-start.8 = (bf16[64,1024]{1,0:T(8,128)(2,1)S(1)}, bf16[64,1024]{1,0:T(8,128)(2,1)S(1)}, u32[]{:S(2)}, u32[]{:S(2)}) collective-permute-start(bf16[64,1024]{1,0:T(8,128)(2,1)S(1)} %get-tuple-element.46), channel_id=1, source_target_pairs={{0,16},{4,20},{8,24},{12,28},{16,0},{20,4},{24,8},{28,12},{1,17},{... | collective-permute-start | bytes 393224 | tf_op jit(solution)/shard_map/cot_z2/ppermute | solution.py:22
  6.4 0.0 collective-permute-start.7
  7.1 3.5 %attend.1 = (f32[24,256]{1,0:T(8,128)}, f32[1,16,256]{2,1,0:T(8,128)}, f32[1,16,256]{2,1,0:T(8,128)}, f32[2,16,256]{2,1,0:T(8,128)}) custom-call(s32[1]{0:T(128)S(6)} %copy.13.refs_0_, bf16[1,2,4096]{2,1,0:T(2,128)(2,1)} %refs_1_.2, bf16[1,512,512]{2,1,0:T(8,128)(2,1)} %refs_2_.1, bf16[1,512,512]{2,1,0:T(8,128)(2,1)} %refs_3_.1, bf16[1,2,512]{2,1,0:T(2,128)(2,1)} %refs_4_.1, ...), custom_call_target="tpu_custom_call" | custom-call | tf_op jit(solution)/shard_map/attend/pallas_call | solution.py:74
  10.6 0.0 copy-start
  10.6 1.6 %collective-permute-start.2 = (f32[1,16,256]{2,1,0:T(8,128)}, f32[1,16,256]{2,1,0:T(8,128)S(1)}, u32[]{:S(2)}, u32[]{:S(2)}) collective-permute-start(f32[1,16,256]{2,1,0:T(8,128)} %get-tuple-element.27), channel_id=1, source_target_pairs={{0,1},{1,0},{2,3},{3,2},{4,5},{5,4},{6,7},{7,6},{8,9},{9,8},{10,11... | collective-permute-start | bytes 49160 | tf_op jit(solution)/shard_map/softmax_tp1/ppermute | solution.py:22
  12.2 1.0 %collective-permute-done.2.refs_2_ = f32[1,16,256]{2,1,0:T(8,128)S(1)} collective-permute-done((f32[1,16,256]{2,1,0:T(8,128)}, f32[1,16,256]{2,1,0:T(8,128)S(1)}, u32[]{:S(2)}, u32[]{:S(2)}) %collective-permute-start.2) | collective-permute-done | bytes 16416 | tf_op jit(solution)/shard_map/softmax_tp1/ppermute | solution.py:22
  13.2 1.2 %collective-permute-start.1 = (f32[2,16,256]{2,1,0:T(8,128)}, f32[2,16,256]{2,1,0:T(8,128)S(1)}, u32[]{:S(2)}, u32[]{:S(2)}) collective-permute-start(f32[2,16,256]{2,1,0:T(8,128)} %get-tuple-element.26), channel_id=1, source_target_pairs={{0,2},{1,3},{2,0},{3,1},{4,6},{5,7},{6,4},{7,5},{8,10},{9,11},{10,... | collective-permute-start | bytes 98312 | tf_op jit(solution)/shard_map/softmax_tp2/ppermute | solution.py:22
  14.5 2.1 %collective-permute-done.1 = f32[2,16,256]{2,1,0:T(8,128)S(1)} collective-permute-done((f32[2,16,256]{2,1,0:T(8,128)}, f32[2,16,256]{2,1,0:T(8,128)S(1)}, u32[]{:S(2)}, u32[]{:S(2)}) %collective-permute-start.1) | collective-permute-done | bytes 32800 | tf_op jit(solution)/shard_map/softmax_tp2/ppermute | solution.py:22
  16.6 1.1 %collective-permute-start.3 = (f32[2,16,256]{2,1,0:T(8,128)S(1)}, f32[2,16,256]{2,1,0:T(8,128)S(1)}, u32[]{:S(2)}, u32[]{:S(2)}) collective-permute-start(f32[2,16,256]{2,1,0:T(8,128)S(1)} %collective-permute-done.1), channel_id=1, source_target_pairs={{0,1},{1,0},{2,3},{3,2},{4,5},{5,4},{6,7},{7,6},{8,9},{9,8},{10,11... | collective-permute-start | bytes 98312 | tf_op jit(solution)/shard_map/softmax_tp1/ppermute | solution.py:22
  17.7 0.6 slice.4.refs_1_
  18.3 0.3 collective-permute-done.3.refs_3_
  18.5 0.6 copy-done.3
  19.1 1.9 %combine.1.refs_3_.refs_2_ = bf16[144,1024]{1,0:T(8,128)(2,1)} custom-call(f32[24,256]{1,0:T(8,128)} %get-tuple-element.24.own_ref, bf16[128,1024]{1,0:T(8,128)(2,1)} %attn_ref.1, f32[1,16,256]{2,1,0:T(8,128)} %get-tuple-element.25.refs_0_, f32[1,16,256]{2,1,0:T(8,128)} %slice.4.refs_1_, f32[1,16,256]{2,1,0:T(8,128)} %copy-done.4, f32[2,16,256]{2,1,0:T(8,128)} %copy-done.3), custom_call_target="tpu_custom_call" | custom-call | tf_op jit(solution)/shard_map/combine/pallas_call | solution.py:357
  21.1 0.0 collective-permute-done.9.refs_2_
  21.1 1.2 %stack.2 = (bf16[96,1024]{1,0:T(8,128)(2,1)S(1)}, bf16[96,1024]{1,0:T(8,128)(2,1)S(1)}) custom-call(bf16[64,1024]{1,0:T(8,128)(2,1)S(1)} %collective-permute-done.7.refs_0_, bf16[64,1024]{1,0:T(8,128)(2,1)S(1)} %collective-permute-done.8.refs_1_, bf16[64,1024]{1,0:T(8,128)(2,1)S(1)} %collective-permute-done.9.refs_2_, bf16[144,1024]{1,0:T(8,128)(2,1)} %combine.1.refs_3_.refs_2_), custom_call_target="tpu_custom_call" | custom-call | tf_op jit(solution)/shard_map/stack/pallas_call | solution.py:74
  22.3 0.4 collective-permute-start.10
  22.7 0.2 collective-permute-start.11
  22.9 0.3 collective-permute-start.6
  23.2 3.5 %collective-permute-start.5 = (bf16[144,1024]{1,0:T(8,128)(2,1)}, bf16[144,1024]{1,0:T(8,128)(2,1)S(1)}, u32[]{:S(2)}, u32[]{:S(2)}) collective-permute-start(bf16[144,1024]{1,0:T(8,128)(2,1)} %combine.1.refs_3_.refs_2_), channel_id=1, source_target_pairs={{0,16},{4,20},{8,24},{12,28},{16,0},{20,4},{24,8},{28,12},{1,17},{... | collective-permute-start | bytes 884744 | tf_op jit(solution)/shard_map/attn_z2/ppermute | solution.py:22
  26.8 0.0 copy-start.1
  26.8 1.2 %copy-done.1 = bf16[128,4096]{1,0:T(8,128)(2,1)S(1)} copy-done((bf16[128,4096]{1,0:T(8,128)(2,1)S(1)}, bf16[128,4096]{1,0:T(8,128)(2,1)}, u32[]{:S(2)}) %copy-start.1) | copy-done | bytes 1048600
  28.0 3.8 %middle.1 = (bf16[128,1024]{1,0:T(8,128)(2,1)S(1)}, bf16[128,1024]{1,0:T(8,128)(2,1)S(1)}, bf16[128,1024]{1,0:T(8,128)(2,1)S(1)}, f32[128,1024]{1,0:T(8,128)S(1)...) custom-call(bf16[128,4096]{1,0:T(8,128)(2,1)S(1)} %copy-done.1, bf16[512,1024]{1,0:T(8,128)(2,1)S(1)} %copy-done, ...), custom_call_target="tpu_custom_call" | custom-call | tf_op jit(solution)/shard_map/middle/pallas_call | solution.py:74
  31.8 0.3 collective-permute-start.12
  32.1 11.9 %collective-permute-done.6.refs_5_ = bf16[144,1024]{1,0:T(8,128)(2,1)S(1)} collective-permute-done((bf16[144,1024]{1,0:T(8,128)(2,1)}, bf16[144,1024]{1,0:T(8,128)(2,1)S(1)}, u32[]{:S(2)}, u32[]{:S(2)}) %collective-permute-start.6) | collective-permute-done | bytes 294944 | tf_op jit(solution)/shard_map/attn_z3/ppermute | solution.py:22
  44.0 4.5 %collective-permute-done.5.refs_4_ = bf16[144,1024]{1,0:T(8,128)(2,1)S(1)} collective-permute-done((bf16[144,1024]{1,0:T(8,128)(2,1)}, bf16[144,1024]{1,0:T(8,128)(2,1)S(1)}, u32[]{:S(2)}, u32[]{:S(2)}) %collective-permute-start.5) | collective-permute-done | bytes 294944 | tf_op jit(solution)/shard_map/attn_z2/ppermute | solution.py:22
  48.5 2.6 %decode.1 = (bf16[512,1024]{1,0:T(8,128)(2,1)S(1)}, f32[1,2,1024]{2,1,0:T(2,128)S(1)}, f32[1,2,1024]{2,1,0:T(2,128)S(1)}, f32[1,2,1024]{2,1,0:T(2,128)S(1)}, f32[1,2,1024]{2,1,0:T(2,128)S(1)}) custom-call(bf16[512,1024]{1,0:T(8,128)(2,1)S(1)} %copy-done, bf16[512,1024]{1,0:T(8,128)(2,1)} %collective-permute-done.refs_2_.refs_1_, ...), custom_call_target="tpu_custom_call" | custom-call | tf_op jit(solution)/shard_map/decode/pallas_call | solution.py:74
  51.1 0.3 collective-permute-start.21
  51.4 1.5 %collective-permute-start.13 = (bf16[256,512]{1,0:T(8,128)(2,1)S(1)}, bf16[256,512]{1,0:T(8,128)(2,1)S(1)}, u32[]{:S(2)}, u32[]{:S(2)}) collective-permute-start(bf16[256,512]{1,0:T(8,128)(2,1)S(1)} %collective-permute-done.12.refs_6_.refs_0_), channel_id=1, source_target_pairs={{0,1},{1,0},{2,3},{3,2},{4,5},{5,4},{6,7},{7,6},{8,9},{9,8},{10,11... | collective-permute-start | bytes 786440 | tf_op jit(solution)/shard_map/cot_x_core/ppermute | solution.py:22
  52.9 1.2 %collective-permute-done.13.refs_4_.refs_1_ = bf16[256,512]{1,0:T(8,128)(2,1)S(1)} collective-permute-done((bf16[256,512]{1,0:T(8,128)(2,1)S(1)}, bf16[256,512]{1,0:T(8,128)(2,1)S(1)}, u32[]{:S(2)}, u32[]{:S(2)}) %collective-permute-start.13) | collective-permute-done | bytes 262176 | tf_op jit(solution)/shard_map/cot_x_core/ppermute | solution.py:22
  54.1 0.4 release.1
  54.4 0.4 collective-permute-start.14
  54.9 1.2 %collective-permute-start.15 = (f32[1,2,1024]{2,1,0:T(2,128)S(1)}, f32[1,2,1024]{2,1,0:T(2,128)S(1)}, u32[]{:S(2)}, u32[]{:S(2)}) collective-permute-start(f32[1,2,1024]{2,1,0:T(2,128)S(1)} %get-tuple-element.37), channel_id=1, source_target_pairs={{0,2},{1,3},{2,0},{3,1},{4,6},{5,7},{6,4},{7,5},{8,10},{9,11},{10,... | collective-permute-start | bytes 24584 | tf_op jit(solution)/shard_map/dec_tp2/ppermute | solution.py:22
  56.1 0.5 collective-permute-start.16
  56.6 3.0 %collective-permute-start.18 = (bf16[128,1024]{1,0:T(8,128)(2,1)S(1)}, bf16[128,1024]{1,0:T(8,128)(2,1)S(1)}, u32[]{:S(2)}, u32[]{:S(2)}) collective-permute-start(bf16[128,1024]{1,0:T(8,128)(2,1)S(1)} %get-tuple-element.40), channel_id=1, source_target_pairs={{0,8},{4,12},{8,0},{12,4},{16,24},{20,28},{24,16},{28,20},{1,9},{5... | collective-permute-start | bytes 786440 | tf_op jit(solution)/shard_map/sum_z1/ppermute | solution.py:22
  59.7 1.2 %collective-permute-start.20 = (bf16[128,1024]{1,0:T(8,128)(2,1)S(1)}, bf16[128,1024]{1,0:T(8,128)(2,1)S(1)}, u32[]{:S(2)}, u32[]{:S(2)}) collective-permute-start(bf16[128,1024]{1,0:T(8,128)(2,1)S(1)} %get-tuple-element.42), channel_id=1, source_target_pairs={{0,24},{4,28},{8,16},{12,20},{16,8},{20,12},{24,0},{28,4},{1,25},{... | collective-permute-start | bytes 786440 | tf_op jit(solution)/shard_map/sum_z3/ppermute | solution.py:22
  60.9 3.7 %collective-permute-start.17 = (bf16[2,1024]{1,0:T(2,128)(2,1)S(1)}, bf16[2,1024]{1,0:T(2,128)(2,1)S(1)}, u32[]{:S(2)}, u32[]{:S(2)}) collective-permute-start(bf16[2,1024]{1,0:T(2,128)(2,1)S(1)} %fusion), channel_id=1, source_target_pairs={{0,0},{1,8},{2,16},{3,24},{4,4},{5,12},{6,20},{7,28},{8,1},{9,9},{... | collective-permute-start | bytes 12296 | tf_op jit(solution)/shard_map/dec_place/ppermute | solution.py:427
  64.6 0.7 fusion.2.refs_3_
  65.3 4.4 %collective-permute-done.18.refs_1_ = bf16[128,1024]{1,0:T(8,128)(2,1)S(1)} collective-permute-done((bf16[128,1024]{1,0:T(8,128)(2,1)S(1)}, bf16[128,1024]{1,0:T(8,128)(2,1)S(1)}, u32[]{:S(2)}, u32[]{:S(2)}) %collective-permute-start.18) | collective-permute-done | bytes 262176 | tf_op jit(solution)/shard_map/sum_z1/ppermute | solution.py:22
  69.8 2.1 %collective-permute-done.19.refs_2_ = bf16[128,1024]{1,0:T(8,128)(2,1)S(1)} collective-permute-done((bf16[128,1024]{1,0:T(8,128)(2,1)S(1)}, bf16[128,1024]{1,0:T(8,128)(2,1)S(1)}, u32[]{:S(2)}, u32[]{:S(2)}) %collective-permute-start.19) | collective-permute-done | bytes 262176 | tf_op jit(solution)/shard_map/sum_z2/ppermute | solution.py:22
  71.9 12.2 %collective-permute-done.20.refs_3_ = bf16[128,1024]{1,0:T(8,128)(2,1)S(1)} collective-permute-done((bf16[128,1024]{1,0:T(8,128)(2,1)S(1)}, bf16[128,1024]{1,0:T(8,128)(2,1)S(1)}, u32[]{:S(2)}, u32[]{:S(2)}) %collective-permute-start.20) | collective-permute-done | bytes 262176 | tf_op jit(solution)/shard_map/sum_z3/ppermute | solution.py:22
  84.1 1.1 %sum.1.refs_4_ = bf16[128,1024]{1,0:T(8,128)(2,1)} custom-call(f32[128,1024]{1,0:T(8,128)S(1)} %get-tuple-element.39.refs_0_, bf16[128,1024]{1,0:T(8,128)(2,1)S(1)} %collective-permute-done.18.refs_1_, bf16[128,1024]{1,0:T(8,128)(2,1)S(1)} %collective-permute-done.19.refs_2_, bf16[128,1024]{1,0:T(8,128)(2,1)S(1)} %collective-permute-done.20.refs_3_), custom_call_target="tpu_custom_call" | custom-call | tf_op jit(solution)/shard_map/sum/pallas_call | solution.py:74
  85.2 0.2 collective-permute-done.17
  85.5 0.9 %copy-done.2 = bf16[128,1024]{1,0:T(8,128)(2,1)S(1)} copy-done((bf16[128,1024]{1,0:T(8,128)(2,1)S(1)}, bf16[128,1024]{1,0:T(8,128)(2,1)}, u32[]{:S(2)}) %copy-start.2) | copy-done | bytes 262168
  86.4 2.7 %product.1 = f32[512,1024]{1,0:T(8,128)} custom-call(bf16[256,512]{1,0:T(8,128)(2,1)S(1)} %collective-permute-done.12.refs_6_.refs_0_, bf16[256,512]{1,0:T(8,128)(2,1)S(1)} %collective-permute-done.13.refs_4_.refs_1_, bf16[512,1024]{1,0:T(8,128)(2,1)S(1)} %collective-permute-done.21.refs_2_, f32[512,1024]{1,0:T(8,128)S(1)} %fusion.2.refs_3_, ...), custom_call_target="tpu_custom_call" | custom-call | tf_op jit(solution)/shard_map/product/pallas_call | solution.py:74
  89.1 0.6 copy.14
  (19 shorter events, 0.1 us)
Async XLA Ops:
  0.6 26.1 %collective-permute-start = (bf16[512,1024]{1,0:T(8,128)(2,1)}, bf16[512,1024]{1,0:T(8,128)(2,1)}, u32[]{:S(2)}, u32[]{:S(2)}) collective-permute-start(bf16[512,1024]{1,0:T(8,128)(2,1)} %refs_0_.4), channel_id=1, source_target_pairs={{0,4},{4,0},{8,12},{12,8},{16,20},{20,16},{24,28},{28,24},{1,5},{5... | collective-permute-start | bytes 3145736 | tf_op jit(solution)/shard_map/weight_x/ppermute | solution.py:22
  3.0 18.1 %collective-permute-start.9 = (bf16[64,1024]{1,0:T(8,128)(2,1)S(1)}, bf16[64,1024]{1,0:T(8,128)(2,1)S(1)}, u32[]{:S(2)}, u32[]{:S(2)}) collective-permute-start(bf16[64,1024]{1,0:T(8,128)(2,1)S(1)} %get-tuple-element.45), channel_id=1, source_target_pairs={{0,24},{4,28},{8,16},{12,20},{16,8},{20,12},{24,0},{28,4},{1,25},{... | collective-permute-start | bytes 393224 | tf_op jit(solution)/shard_map/cot_z3/ppermute | solution.py:22
  3.2 17.9 %collective-permute-start.8 = (bf16[64,1024]{1,0:T(8,128)(2,1)S(1)}, bf16[64,1024]{1,0:T(8,128)(2,1)S(1)}, u32[]{:S(2)}, u32[]{:S(2)}) collective-permute-start(bf16[64,1024]{1,0:T(8,128)(2,1)S(1)} %get-tuple-element.46), channel_id=1, source_target_pairs={{0,16},{4,20},{8,24},{12,28},{16,0},{20,4},{24,8},{28,12},{1,17},{... | collective-permute-start | bytes 393224 | tf_op jit(solution)/shard_map/cot_z2/ppermute | solution.py:22
  6.4 14.7 %collective-permute-start.7 = (bf16[64,1024]{1,0:T(8,128)(2,1)S(1)}, bf16[64,1024]{1,0:T(8,128)(2,1)S(1)}, u32[]{:S(2)}, u32[]{:S(2)}) collective-permute-start(bf16[64,1024]{1,0:T(8,128)(2,1)S(1)} %get-tuple-element.47), channel_id=1, source_target_pairs={{0,8},{4,12},{8,0},{12,4},{16,24},{20,28},{24,16},{28,20},{1,9},{5... | collective-permute-start | bytes 393224 | tf_op jit(solution)/shard_map/cot_z1/ppermute | solution.py:22
  10.6 16.2 %copy-start = (bf16[512,1024]{1,0:T(8,128)(2,1)S(1)}, bf16[512,1024]{1,0:T(8,128)(2,1)}, u32[]{:S(2)}) copy-start(bf16[512,1024]{1,0:T(8,128)(2,1)} %refs_0_.4) | copy-start | bytes 3145732
  10.6 2.6 %collective-permute-start.2 = (f32[1,16,256]{2,1,0:T(8,128)}, f32[1,16,256]{2,1,0:T(8,128)S(1)}, u32[]{:S(2)}, u32[]{:S(2)}) collective-permute-start(f32[1,16,256]{2,1,0:T(8,128)} %get-tuple-element.27), channel_id=1, source_target_pairs={{0,1},{1,0},{2,3},{3,2},{4,5},{5,4},{6,7},{7,6},{8,9},{9,8},{10,11... | collective-permute-start | bytes 49160 | tf_op jit(solution)/shard_map/softmax_tp1/ppermute | solution.py:22
  13.2 5.3 %copy-start.4 = (f32[1,16,256]{2,1,0:T(8,128)}, f32[1,16,256]{2,1,0:T(8,128)S(1)}, u32[]{:S(2)}) copy-start(f32[1,16,256]{2,1,0:T(8,128)S(1)} %collective-permute-done.2.refs_2_) | copy-start | bytes 49156
  13.2 3.4 %collective-permute-start.1 = (f32[2,16,256]{2,1,0:T(8,128)}, f32[2,16,256]{2,1,0:T(8,128)S(1)}, u32[]{:S(2)}, u32[]{:S(2)}) collective-permute-start(f32[2,16,256]{2,1,0:T(8,128)} %get-tuple-element.26), channel_id=1, source_target_pairs={{0,2},{1,3},{2,0},{3,1},{4,6},{5,7},{6,4},{7,5},{8,10},{9,11},{10,... | collective-permute-start | bytes 98312 | tf_op jit(solution)/shard_map/softmax_tp2/ppermute | solution.py:22
  16.6 2.0 %collective-permute-start.3 = (f32[2,16,256]{2,1,0:T(8,128)S(1)}, f32[2,16,256]{2,1,0:T(8,128)S(1)}, u32[]{:S(2)}, u32[]{:S(2)}) collective-permute-start(f32[2,16,256]{2,1,0:T(8,128)S(1)} %collective-permute-done.1), channel_id=1, source_target_pairs={{0,1},{1,0},{2,3},{3,2},{4,5},{5,4},{6,7},{7,6},{8,9},{9,8},{10,11... | collective-permute-start | bytes 98312 | tf_op jit(solution)/shard_map/softmax_tp1/ppermute | solution.py:22
  18.5 0.6 copy-start.3
  22.3 4.4 %collective-permute-start.10 = (bf16[96,1024]{1,0:T(8,128)(2,1)S(1)}, bf16[96,1024]{1,0:T(8,128)(2,1)S(1)}, u32[]{:S(2)}, u32[]{:S(2)}) collective-permute-start(bf16[96,1024]{1,0:T(8,128)(2,1)S(1)} %get-tuple-element.28.refs_3_), channel_id=1, source_target_pairs={{0,1},{1,0},{2,3},{3,2},{4,5},{5,4},{6,7},{7,6},{8,9},{9,8},{10,11... | collective-permute-start | bytes 589832 | tf_op jit(solution)/shard_map/cot_core/ppermute | solution.py:22
  22.7 4.0 %collective-permute-start.11 = (bf16[96,1024]{1,0:T(8,128)(2,1)S(1)}, bf16[96,1024]{1,0:T(8,128)(2,1)S(1)}, u32[]{:S(2)}, u32[]{:S(2)}) collective-permute-start(bf16[96,1024]{1,0:T(8,128)(2,1)S(1)} %get-tuple-element.29.refs_4_), channel_id=1, source_target_pairs={{0,1},{1,0},{2,3},{3,2},{4,5},{5,4},{6,7},{7,6},{8,9},{9,8},{10,11... | collective-permute-start | bytes 589832 | tf_op jit(solution)/shard_map/cot_core/ppermute | solution.py:22
  22.9 21.1 %collective-permute-start.6 = (bf16[144,1024]{1,0:T(8,128)(2,1)}, bf16[144,1024]{1,0:T(8,128)(2,1)S(1)}, u32[]{:S(2)}, u32[]{:S(2)}) collective-permute-start(bf16[144,1024]{1,0:T(8,128)(2,1)} %combine.1.refs_3_.refs_2_), channel_id=1, source_target_pairs={{0,24},{4,28},{8,16},{12,20},{16,8},{20,12},{24,0},{28,4},{1,25},{... | collective-permute-start | bytes 884744 | tf_op jit(solution)/shard_map/attn_z3/ppermute | solution.py:22
  23.2 25.3 %collective-permute-start.5 = (bf16[144,1024]{1,0:T(8,128)(2,1)}, bf16[144,1024]{1,0:T(8,128)(2,1)S(1)}, u32[]{:S(2)}, u32[]{:S(2)}) collective-permute-start(bf16[144,1024]{1,0:T(8,128)(2,1)} %combine.1.refs_3_.refs_2_), channel_id=1, source_target_pairs={{0,16},{4,20},{8,24},{12,28},{16,0},{20,4},{24,8},{28,12},{1,17},{... | collective-permute-start | bytes 884744 | tf_op jit(solution)/shard_map/attn_z2/ppermute | solution.py:22
  26.7 21.8 %collective-permute-start.4 = (bf16[144,1024]{1,0:T(8,128)(2,1)}, bf16[144,1024]{1,0:T(8,128)(2,1)S(1)}, u32[]{:S(2)}, u32[]{:S(2)}) collective-permute-start(bf16[144,1024]{1,0:T(8,128)(2,1)} %combine.1.refs_3_.refs_2_), channel_id=1, source_target_pairs={{0,8},{4,12},{8,0},{12,4},{16,24},{20,28},{24,16},{28,20},{1,9},{5... | collective-permute-start | bytes 884744 | tf_op jit(solution)/shard_map/attn_z1/ppermute | solution.py:22
  26.8 1.2 %copy-start.1 = (bf16[128,4096]{1,0:T(8,128)(2,1)S(1)}, bf16[128,4096]{1,0:T(8,128)(2,1)}, u32[]{:S(2)}) copy-start(bf16[128,4096]{1,0:T(8,128)(2,1)} %refs_0_.3) | copy-start | bytes 3145732
  31.8 16.7 %collective-permute-start.12 = (bf16[256,512]{1,0:T(8,128)(2,1)S(1)}, bf16[256,512]{1,0:T(8,128)(2,1)S(1)}, u32[]{:S(2)}, u32[]{:S(2)}) collective-permute-start(bf16[256,512]{1,0:T(8,128)(2,1)S(1)} %get-tuple-element.30), channel_id=1, source_target_pairs={{0,4},{4,0},{8,12},{12,8},{16,20},{20,16},{24,28},{28,24},{1,5},{5... | collective-permute-start | bytes 786440 | tf_op jit(solution)/shard_map/cot_x/ppermute | solution.py:22
  51.1 34.3 %collective-permute-start.21 = (bf16[512,1024]{1,0:T(8,128)(2,1)S(1)}, bf16[512,1024]{1,0:T(8,128)(2,1)S(1)}, u32[]{:S(2)}, u32[]{:S(2)}) collective-permute-start(bf16[512,1024]{1,0:T(8,128)(2,1)S(1)} %get-tuple-element.43), channel_id=1, source_target_pairs={{0,4},{4,0},{8,12},{12,8},{16,20},{20,16},{24,28},{28,24},{1,5},{5... | collective-permute-start | bytes 3145736 | tf_op jit(solution)/shard_map/attn_x/ppermute | solution.py:22
  51.4 2.6 %collective-permute-start.13 = (bf16[256,512]{1,0:T(8,128)(2,1)S(1)}, bf16[256,512]{1,0:T(8,128)(2,1)S(1)}, u32[]{:S(2)}, u32[]{:S(2)}) collective-permute-start(bf16[256,512]{1,0:T(8,128)(2,1)S(1)} %collective-permute-done.12.refs_6_.refs_0_), channel_id=1, source_target_pairs={{0,1},{1,0},{2,3},{3,2},{4,5},{5,4},{6,7},{7,6},{8,9},{9,8},{10,11... | collective-permute-start | bytes 786440 | tf_op jit(solution)/shard_map/cot_x_core/ppermute | solution.py:22
  54.4 5.2 %collective-permute-start.14 = (f32[1,2,1024]{2,1,0:T(2,128)S(1)}, f32[1,2,1024]{2,1,0:T(2,128)S(1)}, u32[]{:S(2)}, u32[]{:S(2)}) collective-permute-start(f32[1,2,1024]{2,1,0:T(2,128)S(1)} %get-tuple-element.36), channel_id=1, source_target_pairs={{0,1},{1,0},{2,3},{3,2},{4,5},{5,4},{6,7},{7,6},{8,9},{9,8},{10,11... | collective-permute-start | bytes 24584 | tf_op jit(solution)/shard_map/dec_tp1/ppermute | solution.py:22
  54.9 4.8 %collective-permute-start.15 = (f32[1,2,1024]{2,1,0:T(2,128)S(1)}, f32[1,2,1024]{2,1,0:T(2,128)S(1)}, u32[]{:S(2)}, u32[]{:S(2)}) collective-permute-start(f32[1,2,1024]{2,1,0:T(2,128)S(1)} %get-tuple-element.37), channel_id=1, source_target_pairs={{0,2},{1,3},{2,0},{3,1},{4,6},{5,7},{6,4},{7,5},{8,10},{9,11},{10,... | collective-permute-start | bytes 24584 | tf_op jit(solution)/shard_map/dec_tp2/ppermute | solution.py:22
  56.1 4.7 %collective-permute-start.16 = (f32[1,2,1024]{2,1,0:T(2,128)S(1)}, f32[1,2,1024]{2,1,0:T(2,128)S(1)}, u32[]{:S(2)}, u32[]{:S(2)}) collective-permute-start(f32[1,2,1024]{2,1,0:T(2,128)S(1)} %get-tuple-element.38), channel_id=1, source_target_pairs={{0,3},{1,2},{2,1},{3,0},{4,7},{5,6},{6,5},{7,4},{8,11},{9,10},{10,... | collective-permute-start | bytes 24584 | tf_op jit(solution)/shard_map/dec_tp3/ppermute | solution.py:22
  56.6 13.1 %collective-permute-start.18 = (bf16[128,1024]{1,0:T(8,128)(2,1)S(1)}, bf16[128,1024]{1,0:T(8,128)(2,1)S(1)}, u32[]{:S(2)}, u32[]{:S(2)}) collective-permute-start(bf16[128,1024]{1,0:T(8,128)(2,1)S(1)} %get-tuple-element.40), channel_id=1, source_target_pairs={{0,8},{4,12},{8,0},{12,4},{16,24},{20,28},{24,16},{28,20},{1,9},{5... | collective-permute-start | bytes 786440 | tf_op jit(solution)/shard_map/sum_z1/ppermute | solution.py:22
  59.7 12.2 %collective-permute-start.19 = (bf16[128,1024]{1,0:T(8,128)(2,1)S(1)}, bf16[128,1024]{1,0:T(8,128)(2,1)S(1)}, u32[]{:S(2)}, u32[]{:S(2)}) collective-permute-start(bf16[128,1024]{1,0:T(8,128)(2,1)S(1)} %get-tuple-element.41), channel_id=1, source_target_pairs={{0,16},{4,20},{8,24},{12,28},{16,0},{20,4},{24,8},{28,12},{1,17},{... | collective-permute-start | bytes 786440 | tf_op jit(solution)/shard_map/sum_z2/ppermute | solution.py:22
  59.7 24.5 %collective-permute-start.20 = (bf16[128,1024]{1,0:T(8,128)(2,1)S(1)}, bf16[128,1024]{1,0:T(8,128)(2,1)S(1)}, u32[]{:S(2)}, u32[]{:S(2)}) collective-permute-start(bf16[128,1024]{1,0:T(8,128)(2,1)S(1)} %get-tuple-element.42), channel_id=1, source_target_pairs={{0,24},{4,28},{8,16},{12,20},{16,8},{20,12},{24,0},{28,4},{1,25},{... | collective-permute-start | bytes 786440 | tf_op jit(solution)/shard_map/sum_z3/ppermute | solution.py:22
  60.9 24.6 %collective-permute-start.17 = (bf16[2,1024]{1,0:T(2,128)(2,1)S(1)}, bf16[2,1024]{1,0:T(2,128)(2,1)S(1)}, u32[]{:S(2)}, u32[]{:S(2)}) collective-permute-start(bf16[2,1024]{1,0:T(2,128)(2,1)S(1)} %fusion), channel_id=1, source_target_pairs={{0,0},{1,8},{2,16},{3,24},{4,4},{5,12},{6,20},{7,28},{8,1},{9,9},{... | collective-permute-start | bytes 12296 | tf_op jit(solution)/shard_map/dec_place/ppermute | solution.py:427
  85.5 1.0 %copy-start.2 = (bf16[128,1024]{1,0:T(8,128)(2,1)S(1)}, bf16[128,1024]{1,0:T(8,128)(2,1)}, u32[]{:S(2)}) copy-start(bf16[128,1024]{1,0:T(8,128)(2,1)} %sum.1.refs_4_) | copy-start | bytes 786436

commit v3 on v2

v3 whole, which is shorter than its diff:
```python
import functools

import jax
import jax.numpy as jnp
from jax import lax
from jax.experimental import pallas as pl
from jax.experimental.pallas import tpu as pltpu
from jax.sharding import PartitionSpec as P

KVH = 4
HD = 128
NEG_FILL = -1e30
INNER = 2
PAD = 16
BF16 = jnp.bfloat16
F32 = jnp.float32


def flip(a, axis, bits, name):
    size = lax.axis_size(axis)
    with jax.named_scope(name):
        return lax.ppermute(a, axis, [(i, i ^ bits) for i in range(size)])


def turn(a, steps, name):
    outer = lax.axis_size("fsdp") // INNER
    with jax.named_scope(name):
        return lax.ppermute(
            a, "fsdp", [(z * INNER + x, (z + steps) % outer * INNER + x) for z in range(outer) for x in range(INNER)]
        )


def dot(a, b):
    return jnp.dot(a, b, preferred_element_type=F32)


def over_features(a, b):
    return lax.dot_general(a, b, (((1,), (1,)), ((), ())), preferred_element_type=F32)


def over_tokens(a, b):
    return lax.dot_general(a, b, (((0,), (0,)), ((), ())), preferred_element_type=F32)


class Mover:
    def __init__(self, sems):
        self.sems, self.count, self.open = sems, 0, []

    def start(self, source, target):
        copy = pltpu.make_async_copy(source, target, self.sems.at[self.count])
        self.count += 1
        self.open.append(copy)
        copy.start()
        return copy

    def wait(self, *copies):
        for copy in copies:
            copy.wait()
            self.open = [other for other in self.open if other is not copy]

    def finish(self):
        self.wait(*list(self.open))


def places():
    fsdp_index, tp_index = lax.axis_index("fsdp"), lax.axis_index("tp")
    return tp_index, tp_index % 2, fsdp_index // INNER, fsdp_index % INNER, tp_index * KVH // lax.axis_size("tp")


def call(kernel, name, operands, out_shapes, scratch, waits=(), scalars=None, room=12, fast=()):
    copies = 4 * (len(operands) + len(out_shapes))
    scalars = [] if scalars is None else [scalars]

    def body(*refs):
        front, refs = refs[: len(scalars)], refs[len(scalars) :]
        ins, refs = refs[: len(operands)], refs[len(operands) + len(waits) :]
        outs, refs = refs[: len(out_shapes)], refs[len(out_shapes) :]
        mover = Mover(refs[-1])
        kernel(mover, *front, ins, outs, refs[:-1])
        mover.finish()

    results = pl.pallas_call(
        body,
        out_shape=[jax.ShapeDtypeStruct(shape, dtype) for shape, dtype in out_shapes],
        in_specs=[pl.BlockSpec(memory_space=pltpu.SMEM)] * len(scalars)
        + [pl.BlockSpec(memory_space=pltpu.HBM)] * (len(operands) + len(waits)),
        out_specs=[
            pl.BlockSpec(memory_space=pltpu.VMEM if i in fast else pltpu.HBM) for i in range(len(out_shapes))
        ],
        scratch_shapes=[pltpu.VMEM(shape, dtype) for shape, dtype in scratch] + [pltpu.SemaphoreType.DMA((copies,))],
        compiler_params=pltpu.CompilerParams(vmem_limit_bytes=room << 20),
        cost_estimate=pl.CostEstimate(flops=0, bytes_accessed=0, transcendentals=0),
        name=name,
    )(*scalars, *operands, *waits)
    return list(results)


def shaped(*arrays):
    return [(a.shape, a.dtype) for a in arrays]


def attend_kernel(steps, mover, lengths_ref, ins, outs, scratch):
    query_hbm, keys_hbm, values_hbm, new_keys_hbm, new_values_hbm, attn_hbm = ins
    query_ref, keys_ref, values_ref, new_keys_ref, new_values_ref, query_rows, out_rows, attn_ref = scratch
    tp_index, _, _, _, own_group = places()
    length = lengths_ref[0]
    load_out, own_ref, *part_refs = outs
    tp_size = sum(ref.shape[0] for ref in part_refs)
    first = mover.start(query_hbm.at[0], query_ref)
    news = [mover.start(new_keys_hbm.at[0], new_keys_ref), mover.start(new_values_hbm.at[0], new_values_ref)]
    groups = [slice(g * HD, (g + 1) * HD) for g in range(KVH)]
    arrive = [
        (mover.start(keys_hbm.at[0, :, group], keys_ref.at[:, group]), mover.start(values_hbm.at[0, :, group], values_ref.at[:, group]))
        for group in groups
    ]
    attn = mover.start(attn_hbm, attn_ref)
    width = query_ref.shape[1]
    cache_len = keys_ref.shape[0]
    rows = width // HD // KVH * steps
    mover.wait(first)
    for h in range(width // HD):
        query_rows[h * steps : (h + 1) * steps, :] = query_ref[:, h * HD : (h + 1) * HD].astype(F32)
    usable = lax.broadcasted_iota(jnp.int32, (rows, cache_len), 1) + tp_index * cache_len < length
    left = lax.broadcasted_iota(jnp.int32, (rows, HD), 1) < HD // 2
    for g in range(KVH):
        if g == KVH - 1:
            mover.wait(attn)
            mover.start(attn_ref, load_out.at[: attn_ref.shape[0]])
        mover.wait(*arrive[g])
        query = query_rows[g * rows : (g + 1) * rows, :].astype(BF16)
        scores = over_features(query, keys_ref[:, g * HD : (g + 1) * HD]) * (1.0 / HD**0.5)
        maxima = jnp.max(jnp.where(usable, scores, NEG_FILL), axis=1, keepdims=True)
        terms = jnp.where(usable, jnp.exp(scores - maxima), 0.0)
        totals = jnp.sum(terms, axis=1, keepdims=True)
        upper = terms.astype(BF16)
        lower = (terms - upper.astype(F32)).astype(BF16)
        both = dot(jnp.concatenate([upper, lower], axis=0), values_ref[:, g * HD : (g + 1) * HD])
        out_rows[g * rows : (g + 1) * rows, :HD] = both[:rows] + both[rows:]
        out_rows[g * rows : (g + 1) * rows, HD:] = jnp.where(left, maxima, totals)
    count = part_refs[0].shape[1]
    for t in range(KVH * rows // count):
        for i, part_ref in enumerate(part_refs):
            for k in range(part_ref.shape[0]):

                @pl.when(tp_index ^ ((i and part_ref.shape[0]) + k) == t)
                def _():
                    part_ref[k] = out_rows[t * count : (t + 1) * count, :]

        @pl.when(tp_index == t)
        def _():
            own_ref[:count, :HD] = query_rows[t * count : (t + 1) * count, :]

    mover.wait(*news)
    own_ref[:count, HD:] = jnp.zeros((count, HD), F32)
    for at, ref in ((0, new_keys_ref), (HD, new_values_ref)):
        chosen = ref[:, :HD].astype(F32)
        for g in range(1, KVH):
            chosen = jnp.where(own_group == g, ref[:, groups[g]].astype(F32), chosen)
        own_ref[count : count + steps, at : at + HD] = chosen


def combine_kernel(steps, indices, load_ref, own_ref, *refs):
    *part_refs, out_ref, rows_ref, low_ref, sem = refs
    count = part_refs[0].shape[1]
    rows_ref[...] = jnp.zeros_like(rows_ref)
    step = lax.broadcasted_iota(jnp.int32, (count, 1), 0) % steps
    query = own_ref[:count, :HD]
    keys, values = own_ref[count:, :HD], own_ref[count:, HD:]
    parts = [part_ref[i] for i, part_ref in zip(indices, part_refs)]
    scores = []
    for j in range(steps):
        score = jnp.sum(query * keys[j : j + 1], axis=-1, keepdims=True) * (1.0 / HD**0.5)
        scores.append(jnp.where(step >= j, score, NEG_FILL))
    maxima = [part[:, HD : HD + 1] for part in parts]
    highest = functools.reduce(jnp.maximum, scores + maxima)
    total = jnp.zeros((count, 1), F32)
    weighted = jnp.zeros((count, HD), F32)
    for part, own in zip(parts, maxima):
        scale = jnp.exp(own - highest)
        total = total + part[:, HD + HD // 2 : HD + HD // 2 + 1] * scale
        weighted = weighted + part[:, :HD] * scale
    for j in range(steps):
        term = jnp.where(step >= j, jnp.exp(scores[j] - highest), 0.0)
        total = total + term
        weighted = weighted + term * values[j : j + 1]
    attended = weighted / total
    for row in range(count):
        h, s = row // steps, row % steps
        rows_ref[s : s + 1, h * HD : (h + 1) * HD] = attended[row : row + 1]
    low_ref[...] = rows_ref[...].astype(BF16)
    copy = pltpu.make_async_copy(low_ref, out_ref.at[out_ref.shape[0] - PAD :], sem)
    copy.start()
    copy.wait()


def middle_kernel(outer, mover, ins, outs, scratch):
    grad_hbm, weight_hbm, other_hbm, *cot_hbms = ins
    sent_outs, (total_out, cot_own_out, *cot_far_outs) = outs[: outer - 1], outs[outer - 1 :]
    cots_ref, weight_ref, other_ref, sent_ref, total_ref, cot_own_ref, cot_far_ref = scratch
    _, core, z, x, _ = places()
    tokens = grad_hbm.shape[0]
    plane = cots_ref.shape[1]
    feats = weight_ref.shape[0]
    half = tokens // 2
    weights = [mover.start(weight_hbm, weight_ref), mover.start(other_hbm, other_ref)]
    blocks = [[mover.start(grad_hbm.at[:, pl.ds(pl.multiple_of(z * plane, plane), plane)], cots_ref.at[:tokens])]]
    for k in range(1, outer):
        blocks.append([])
        for hbms, side in ((cot_hbms[:2], core), (cot_hbms[2:], 1 - core)):
            base = pl.multiple_of(k * tokens + side * half, half)
            for i, hbm in enumerate(hbms):
                size = hbm.shape[0]
                low, high = max((k - 1) * half, i * size), min(k * half, (i + 1) * size)
                if low < high:
                    source = hbm.at[low - i * size : high - i * size]
                    first = pl.multiple_of(base + (low - (k - 1) * half), half // 2)
                    blocks[k].append(mover.start(source, cots_ref.at[pl.ds(first, high - low)]))
    mover.wait(*weights)
    span = outer * half
    for k in reversed(range(outer)):
        mover.wait(*blocks[k])
        here = slice(k * tokens, (k + 1) * tokens)
        block = cots_ref[here, :]
        low, high = block[:, :feats], block[:, feats:]
        own = jnp.where(x == 0, low, high)
        other = jnp.where(x == 0, high, low)
        total = dot(own, weight_ref[...]) + dot(other, other_ref[...])
        if k == 0:
            total_ref[...] = total
            mover.start(total_ref, total_out)
        else:
            sent_ref[k - 1] = total.astype(BF16)
            mover.start(sent_ref.at[k - 1], sent_outs[k - 1])
        cot_own_ref[here, :] = own
        cot_far_ref[here, :] = other

    for i, out in enumerate(cot_far_outs):
        mover.start(cot_far_ref.at[i * span : (i + 1) * span], out)
    mover.start(cot_own_ref, cot_own_out)


def decode_kernel(steps, mover, ins, outs, scratch):
    weight_hbm, other_hbm, *load_hbms = ins
    weight_ref, other_ref, dec_ref, rows_ref, by_row_ref, parts_ref = scratch
    _, _, z, x, _ = places()
    tokens = load_hbms[0].shape[0] - PAD
    outer, share = len(load_hbms), outs[0].shape[1]
    arrive = [mover.start(hbm.at[tokens:], dec_ref.at[k]) for k, hbm in enumerate(load_hbms)]
    mover.wait(*arrive, mover.start(weight_hbm, weight_ref), mover.start(other_hbm, other_ref))
    for k in range(outer):
        rows_ref[k * steps : (k + 1) * steps, :] = dec_ref[k].astype(F32)[:steps]
    every = rows_ref[...].astype(BF16)
    own, other = over_features(every, weight_ref[...]), over_features(every, other_ref[...])
    wide = jnp.concatenate([jnp.where(x == 0, own, other), jnp.where(x == 0, other, own)], axis=1)
    for k in range(outer):
        by_row_ref[k] = wide[k * steps : (k + 1) * steps]
    for q in range(parts_ref.shape[0]):
        for i in range(share):
            parts_ref[q, i] = by_row_ref[(z - (q * share + i)) % outer]
    mover.start(parts_ref, outs[0])


def own_kernel(mover, ins, outs, scratch):
    cots_ref, attn_ref, out_ref = scratch
    mover.wait(mover.start(ins[0], cots_ref), mover.start(ins[1], attn_ref))
    pieces = 2
    step = out_ref.shape[0] // pieces
    for i in range(pieces):
        here = slice(i * step, (i + 1) * step)
        out_ref[here, :] = over_tokens(cots_ref[:, here], attn_ref[...])
        mover.start(out_ref.at[here], outs[0].at[here])


def last_kernel(outer, share, mover, ins, outs, scratch):
    total_hbm, own_hbm, attn_hbm, *rest = ins
    cot_hbms, part_hbms, piece_hbms = rest[:2], rest[2 : outer + 1], rest[outer + 1 :]
    total_ref, parts_ref, sum_ref, pieces_ref, cots_ref, attn_ref, own_ref, out_ref = scratch
    _, _, z, _, _ = places()
    plane = pieces_ref.shape[2]
    span = cot_hbms[0].shape[0]
    attn = mover.start(attn_hbm, attn_ref)
    cots = [mover.start(hbm, cots_ref.at[i * span : (i + 1) * span]) for i, hbm in enumerate(cot_hbms)]
    pieces = 2
    step = out_ref.shape[0] // pieces
    heres = [slice(i * step, (i + 1) * step) for i in range(pieces)]
    owns = [mover.start(own_hbm.at[here], own_ref.at[here]) for here in heres]
    arrive = [mover.start(total_hbm, total_ref)]
    arrive += [mover.start(hbm, parts_ref.at[i]) for i, hbm in enumerate(part_hbms)]
    places_in = [mover.start(hbm, pieces_ref.at[j]) for j, hbm in enumerate(piece_hbms)]
    mover.wait(attn, *cots)
    for here, own in zip(heres, owns):
        product = over_tokens(cots_ref[:, here], attn_ref[...])
        mover.wait(own)
        out_ref[here, :] = own_ref[here, :] + product
        mover.start(out_ref.at[here], outs[2].at[here])
    mover.wait(*arrive)
    total = total_ref[...]
    for i in range(outer - 1):
        total = total + parts_ref[i].astype(F32)
    sum_ref[...] = total.astype(BF16)
    mover.start(sum_ref, outs[1])
    mover.wait(*places_in)
    for j in range(share):
        mover.start(pieces_ref.at[j], outs[0].at[0, :, pl.ds(pl.multiple_of((z % share ^ j) * plane, plane), plane)])


def stack_kernel(mover, ins, outs, scratch):
    half, size = ins[0].shape[0], outs[0].shape[0]
    arrive = [mover.start(hbm, scratch[0].at[k * half : (k + 1) * half]) for k, hbm in enumerate(ins)]
    mover.wait(*arrive)
    for i, out in enumerate(outs):
        mover.start(scratch[0].at[i * size : (i + 1) * size], out)


def gate_kernel(count, wait_count, *refs):
    refs, (pack_out, pack_ref, in_sems, out_sems) = refs[count : -4 - count], refs[-4:]
    refs = refs[:len(refs) - wait_count]
    tokens = pack_out.shape[0] // len(refs)
    parts = [slice(k * tokens, (k + 1) * tokens) for k in range(len(refs))]
    arrive = [pltpu.make_async_copy(ref.at[:tokens], pack_ref.at[part], in_sems.at[k]) for k, (ref, part) in enumerate(zip(refs, parts))]
    leave = [pltpu.make_async_copy(pack_ref.at[part], pack_out.at[part], out_sems.at[k]) for k, part in enumerate(parts)]
    for copy in arrive:
        copy.start()
    for copy, follow in zip(arrive, leave):
        copy.wait()
        follow.start()
    for copy in leave:
        copy.wait()


def shards(dec_query, new_keys, new_values, cache_keys, cache_values, lengths, out_weight, train_attn, grad_out):
    rows, steps, width = dec_query.shape
    assert rows == 1
    fsdp_size = lax.axis_size("fsdp")
    tp_size = lax.axis_size("tp")
    outer = fsdp_size // INNER
    share = outer // tp_size
    fsdp_index = lax.axis_index("fsdp")
    tp_index = lax.axis_index("tp")
    z, x = fsdp_index // INNER, fsdp_index % INNER
    tokens = grad_out.shape[0]
    feats, cols = out_weight.shape
    plane = feats * INNER
    slot = tp_index % 4
    heads = width // HD
    count = heads // tp_size * steps
    far = range(1, outer)
    others = range(1, tp_size)

    other_weight = flip(out_weight, "fsdp", 1, "weight_x")

    half = tokens // 2

    first = tp_index % 2 * half
    got = [
        turn(lax.dynamic_slice(grad_out, (first, (z + k) % outer * plane), (half, plane)), k, f"cot_z{k}") for k in far
    ]

    sizes = [1 << b for b in range(tp_size.bit_length() - 1)]
    load, own, part, *chunks = call(
        functools.partial(attend_kernel, steps),
        "attend",
        [dec_query, cache_keys, cache_values, new_keys, new_values, train_attn],
        [((tokens + PAD, cols), BF16), ((count + 8, 2 * HD), F32), ((1, count, 2 * HD), F32)]
        + [((size, count, 2 * HD), F32) for size in sizes],
        shaped(dec_query[0], cache_keys[0], cache_values[0], new_keys[0], new_values[0])
        + [((heads * steps, HD), F32), ((heads * steps, 2 * HD), F32), ((tokens, cols), BF16)],
        scalars=lengths,
        room=63,
        fast=range(1, 3 + len(sizes)),
    )
    parts, indices, held = [part], [0], []
    for size, chunk in reversed(list(zip(sizes, chunks))):
        if size > 1:
            came = [flip(a, "tp", size, f"softmax_tp{size}") for a in [chunk] + [a[size:] for a in held]]
            held = [a[:size] for a in held] + came
        else:
            parts += held + [flip(a, "tp", size, f"softmax_tp{size}") for a in [chunk] + held]
            indices += [0] * len(held) + [0] + [1] * len(held)
    load = pl.pallas_call(
        functools.partial(combine_kernel, steps, indices),
        out_shape=jax.ShapeDtypeStruct((tokens + PAD, cols), BF16),
        in_specs=[pl.BlockSpec(memory_space=pltpu.HBM)] + [pl.BlockSpec(memory_space=pltpu.VMEM)] * (len(parts) + 1),
        out_specs=pl.BlockSpec(memory_space=pltpu.HBM),
        scratch_shapes=[pltpu.VMEM((PAD, cols), F32), pltpu.VMEM((PAD, cols), BF16), pltpu.SemaphoreType.DMA],
        input_output_aliases={0: 0},
        cost_estimate=pl.CostEstimate(flops=0, bytes_accessed=0, transcendentals=0),
        name="combine",
    )(load, own, *parts)
    loads = [turn(load, k, f"attn_z{k}") for k in far]

    stacked = call(
        stack_kernel,
        "stack",
        got,
        [((len(far) * half // 2, plane), BF16)] * 2,
        [((len(far) * half, plane), BF16)],
        waits=[load],
    )
    twins = [flip(a, "tp", 1, "cot_core") for a in stacked]

    *sent, total, cot_own, cot_low, cot_high = call(
        functools.partial(middle_kernel, outer),
        "middle",
        [grad_out, out_weight, other_weight, *stacked, *twins],
        [((tokens, cols), BF16)] * len(far)
        + [((tokens, cols), F32), ((outer * tokens, feats), BF16)] + [((outer * half, feats), BF16)] * 2,
        [
            ((outer * tokens, plane), BF16),
            ((feats, cols), BF16),
            ((feats, cols), BF16),
            ((len(far), tokens, cols), BF16),
            ((tokens, cols), F32),
            ((outer * tokens, feats), BF16),
            ((outer * tokens, feats), BF16),
        ],
        room=63,
    )
    cots_x = [flip(a, "fsdp", 1, "cot_x") for a in (cot_low, cot_high)]

    waits = cots_x
    results = pl.pallas_call(
        functools.partial(gate_kernel, len(sent), len(waits)),
        out_shape=[jax.ShapeDtypeStruct(a.shape, a.dtype) for a in sent]
        + [jax.ShapeDtypeStruct((outer * tokens, cols), BF16)],
        in_specs=[pl.BlockSpec(memory_space=pltpu.HBM)] * (len(sent) + outer + len(waits)),
        out_specs=[pl.BlockSpec(memory_space=pltpu.HBM)] * (len(sent) + 1),
        scratch_shapes=[
            pltpu.VMEM((outer * tokens, cols), BF16),
            pltpu.SemaphoreType.DMA((outer,)),
            pltpu.SemaphoreType.DMA((outer,)),
        ],
        input_output_aliases={i: i for i in range(len(sent))},
        compiler_params=pltpu.CompilerParams(vmem_limit_bytes=63 << 20),
        cost_estimate=pl.CostEstimate(flops=0, bytes_accessed=0, transcendentals=0),
        name="gate",
    )(*sent, load, *loads, *waits)
    sent, pack = results[:-1], results[-1]
    sums = [turn(sent[k - 1], outer - k, f"sum_z{k}") for k in far]
    pack_x = flip(pack, "fsdp", 1, "attn_x")
    (dec,) = call(
        functools.partial(decode_kernel, steps),
        "decode",
        [out_weight, other_weight, load, *loads],
        [((tp_size, share, steps, plane), F32)],
        [
            ((feats, cols), BF16),
            ((feats, cols), BF16),
            ((outer, PAD, cols), BF16),
            ((outer * steps, cols), F32),
            ((outer, steps, plane), F32),
            ((tp_size, share, steps, plane), F32),
        ],
        waits=[pack],
        room=63,
    )
    with jax.named_scope("dec_tp"):
        dec = lax.all_to_all(dec, "tp", 0, 0, tiled=True).sum(axis=0).astype(BF16)
    pieces = []
    for j in range(share):
        perm = [
            ((a * INNER + b) * tp_size + q, ((q * share + (a % share ^ j)) * INNER + b) * tp_size + a // share)
            for a in range(outer)
            for b in range(INNER)
            for q in range(tp_size)
        ]
        with jax.named_scope("dec_place"):
            pieces.append(lax.ppermute(lax.dynamic_index_in_dim(dec, z % share ^ j, 0, False), ("fsdp", "tp"), perm))
    (own_total,) = call(
        own_kernel,
        "own",
        [cot_own, pack],
        [((feats, cols), F32)],
        [((outer * tokens, feats), BF16), ((outer * tokens, cols), BF16), ((feats, cols), F32)],
        room=63,
    )
    dec_out, grad_attn, grad_weight = call(
        functools.partial(last_kernel, outer, share),
        "last",
        [total, own_total, pack_x, *cots_x, *sums, *pieces],
        [((rows, steps, share * plane), BF16), ((tokens, cols), BF16), ((feats, cols), F32)],
        [
            ((tokens, cols), F32),
            ((len(far), tokens, cols), BF16),
            ((tokens, cols), BF16),
            ((share, steps, plane), BF16),
            ((outer * tokens, feats), BF16),
            ((outer * tokens, cols), BF16),
            ((feats, cols), F32),
            ((feats, cols), F32),
        ],
        room=63,
    )
    return dec_out, grad_attn, grad_weight


def solution(mesh):
    return jax.shard_map(
        shards,
        mesh=mesh,
        in_specs=(
            P("fsdp", None, None),
            P("fsdp", None, None),
            P("fsdp", None, None),
            P("fsdp", "tp", None),
            P("fsdp", "tp", None),
            P("fsdp"),
            P("fsdp", "tp"),
            P("fsdp", "tp"),
            P("fsdp", None),
        ),
        out_specs=(P("fsdp", None, "tp"), P("fsdp", "tp"), P("fsdp", "tp")),
        check_vma=False,
    )
```

time: 90.3 us -> 87.8 us (0.972); the launches traced: 89.7 us -> 86.1 us
  waiting for transfers between devices: 40 us -> 27.9 us
  blocking collectives: 0 us -> 9.11 us
  Pallas kernels: 17.2 us -> 24.6 us
  starting transfers between devices: 25.3 us -> 19.1 us
  local copies, waits for them, and re-layouts: 5.05 us -> 4.02 us
    ppermute x21 -> x9, waiting for transfers between devices: 39.8 us -> 4.06 us  [flip(): return lax.ppermute(a, axis, [(i, i ^ bits) for i in range(size)])]
    ppermute x0 -> x9, waiting for transfers between devices: none -> 18 us  [turn(): lax.ppermute(a, 'fsdp', [(z * INNER + x, (z + steps) % outer * INNER + x)...]
    ppermute x21 -> x9, starting transfers between devices: 21.5 us -> 7.62 us  [flip(): return lax.ppermute(a, axis, [(i, i ^ bits) for i in range(size)])]
    ppermute x0 -> x9, starting transfers between devices: none -> 9.53 us  [turn(): lax.ppermute(a, 'fsdp', [(z * INNER + x, (z + steps) % outer * INNER + x)...]
    all_to_all x0 -> x1, blocking collectives: none -> 9.11 us  [shards(): dec = lax.all_to_all(dec, 'tp', 0, 0, tiled=True).sum(axis=0).astype(BF16)]
    pallas_call x7 -> x6, Pallas kernels: 15.2 us -> 20.9 us  [call(): pl.pallas_call(body, out_shape=[jax.ShapeDtypeStruct(shape, dtype) for sh...]
    ppermute x1, waiting for transfers between devices: 0.22 us -> 5.82 us  [shards(): lax.ppermute(lax.dynamic_index_in_dim(dec, z % share ^ j, 0, False), ('fs...]
    ppermute x1, starting transfers between devices: 3.74 us -> 1.92 us  [shards(): lax.ppermute(lax.dynamic_index_in_dim(dec, z % share ^ j, 0, False), ('fs...]
  transfers between devices with their start and end apart: 22 -> 19, of which waited for: 10 -> 6; matrix products, arithmetic and copies ran while one was open for 3% -> 1% of each run, Pallas kernels for 13% -> 21%
where the time goes in v3:
time: 87.8 us; the launch traced here: 86.1 us
  waiting for transfers between devices  27.9 us (32%)
  Pallas kernels  24.6 us (28%)
  starting transfers between devices  19.1 us (22%)
  blocking collectives  9.11 us (10%)
  local copies, waits for them, and re-layouts  4.02 us (5%)
  between operations  1.49 us (2%)
    pallas_call x6, Pallas kernels, call(): pl.pallas_call(body, out_shape=[jax.ShapeDtypeStruct(shape, dtype) for sh...  20.9 us
    ppermute x9, waiting for transfers between devices, turn(): lax.ppermute(a, 'fsdp', [(z * INNER + x, (z + steps) % outer * INNER + x)...  18 us
    ppermute x9, starting transfers between devices, turn(): lax.ppermute(a, 'fsdp', [(z * INNER + x, (z + steps) % outer * INNER + x)...  9.53 us
    all_to_all x1, blocking collectives, shards(): dec = lax.all_to_all(dec, 'tp', 0, 0, tiled=True).sum(axis=0).astype(BF16)  9.11 us
    ppermute x9, starting transfers between devices, flip(): return lax.ppermute(a, axis, [(i, i ^ bits) for i in range(size)])  7.62 us
    ppermute x1, waiting for transfers between devices, shards(): lax.ppermute(lax.dynamic_index_in_dim(dec, z % share ^ j, 0, False), ('fs...  5.82 us
    ppermute x9, waiting for transfers between devices, flip(): return lax.ppermute(a, axis, [(i, i ^ bits) for i in range(size)])  4.06 us
    unnamed x28, local copies, waits for them, and re-layouts  2.96 us
  transfers between devices with their start and end apart: 19, of which 6 were waited for; matrix products, arithmetic and copies ran while one was open for 1% of the time, Pallas kernels for 21%

profile of v3, /device:TPU:17, one launch (start us, length us, event | category | flops | bytes accessed | tf_op | source)
XLA Modules:
  0.0 86.1 jit_solution(18372643666340460222)
XLA Ops:
  0.6 1.3 %collective-permute-start = (bf16[512,1024]{1,0:T(8,128)(2,1)}, bf16[512,1024]{1,0:T(8,128)(2,1)}, u32[]{:S(2)}, u32[]{:S(2)}) collective-permute-start(bf16[512,1024]{1,0:T(8,128)(2,1)} %refs_0_.4), channel_id=1, source_target_pairs={{0,4},{4,0},{8,12},{12,8},{16,20},{20,16},{24,28},{28,24},{1,5},{5... | collective-permute-start | bytes 3145736 | tf_op jit(solution)/shard_map/weight_x/ppermute | solution.py:22
  1.9 1.1 %fusion = (bf16[64,1024]{1,0:T(8,128)(2,1)S(1)}, bf16[64,1024]{1,0:T(8,128)(2,1)S(1)}, bf16[64,1024]{1,0:T(8,128)(2,1)S(1)}) fusion(bf16[128,4096]{1,0:T(8,128)(2,1)} %refs_0_.3, s32[]{:T(128)S(6)} %select_n.42, s32[]{:T(128)S(6)} %select_n.49, s32[]{:T(128)S(6)} %select_n.47, s32[]{:T(128)S(6)} %select_n.45), kind=kLoop, calls=%fused_computation | loop fusion | bytes 786448 | tf_op jit(solution)/shard_map/dynamic_slice | solution.py:356
  3.0 0.2 collective-permute-start.3
  3.2 3.2 %collective-permute-start.2 = (bf16[64,1024]{1,0:T(8,128)(2,1)S(1)}, bf16[64,1024]{1,0:T(8,128)(2,1)S(1)}, u32[]{:S(2)}, u32[]{:S(2)}) collective-permute-start(bf16[64,1024]{1,0:T(8,128)(2,1)S(1)} %get-tuple-element.40), channel_id=1, source_target_pairs={{0,16},{4,20},{8,24},{12,28},{16,0},{20,4},{24,8},{28,12},{1,17},{... | collective-permute-start | bytes 393224 | tf_op jit(solution)/shard_map/cot_z2/ppermute | solution.py:28
  6.4 0.0 collective-permute-start.1
  7.1 3.9 %attend.1 = (bf16[144,1024]{1,0:T(8,128)(2,1)}, f32[24,256]{1,0:T(8,128)}, f32[1,16,256]{2,1,0:T(8,128)}, f32[1,16,256]{2,1,0:T(8,128)}, f32[2,16,256]{2,1,0:T(8,128)}) custom-call(s32[1]{0:T(128)S(6)} %copy.20.refs_0_, bf16[1,2,4096]{2,1,0:T(2,128)(2,1)} %refs_1_.2, bf16[1,512,512]{2,1,0:T(8,128)(2,1)} %refs_2_.1, bf16[1,512,512]{2,1,0:T(8,128)(2,1)} %refs_3_.1, ...), custom_call_target="tpu_custom_call" | custom-call | tf_op jit(solution)/shard_map/attend/pallas_call | solution.py:82
  10.9 1.6 %collective-permute-start.5 = (f32[1,16,256]{2,1,0:T(8,128)}, f32[1,16,256]{2,1,0:T(8,128)S(1)}, u32[]{:S(2)}, u32[]{:S(2)}) collective-permute-start(f32[1,16,256]{2,1,0:T(8,128)} %get-tuple-element.25), channel_id=1, source_target_pairs={{0,1},{1,0},{2,3},{3,2},{4,5},{5,4},{6,7},{7,6},{8,9},{9,8},{10,11... | collective-permute-start | bytes 49160 | tf_op jit(solution)/shard_map/softmax_tp1/ppermute | solution.py:22
  12.5 1.0 %collective-permute-done.5.refs_2_ = f32[1,16,256]{2,1,0:T(8,128)S(1)} collective-permute-done((f32[1,16,256]{2,1,0:T(8,128)}, f32[1,16,256]{2,1,0:T(8,128)S(1)}, u32[]{:S(2)}, u32[]{:S(2)}) %collective-permute-start.5) | collective-permute-done | bytes 16416 | tf_op jit(solution)/shard_map/softmax_tp1/ppermute | solution.py:22
  13.5 1.2 %collective-permute-start.4 = (f32[2,16,256]{2,1,0:T(8,128)}, f32[2,16,256]{2,1,0:T(8,128)S(1)}, u32[]{:S(2)}, u32[]{:S(2)}) collective-permute-start(f32[2,16,256]{2,1,0:T(8,128)} %get-tuple-element.24), channel_id=1, source_target_pairs={{0,2},{1,3},{2,0},{3,1},{4,6},{5,7},{6,4},{7,5},{8,10},{9,11},{10,... | collective-permute-start | bytes 98312 | tf_op jit(solution)/shard_map/softmax_tp2/ppermute | solution.py:22
  14.8 2.1 %collective-permute-done.4.refs_1_ = f32[2,16,256]{2,1,0:T(8,128)S(1)} collective-permute-done((f32[2,16,256]{2,1,0:T(8,128)}, f32[2,16,256]{2,1,0:T(8,128)S(1)}, u32[]{:S(2)}, u32[]{:S(2)}) %collective-permute-start.4) | collective-permute-done | bytes 32800 | tf_op jit(solution)/shard_map/softmax_tp2/ppermute | solution.py:22
  16.9 1.1 %collective-permute-start.6 = (f32[2,16,256]{2,1,0:T(8,128)S(1)}, f32[2,16,256]{2,1,0:T(8,128)S(1)}, u32[]{:S(2)}, u32[]{:S(2)}) collective-permute-start(f32[2,16,256]{2,1,0:T(8,128)S(1)} %collective-permute-done.4.refs_1_), channel_id=1, source_target_pairs={{0,1},{1,0},{2,3},{3,2},{4,5},{5,4},{6,7},{7,6},{8,9},{9,8},{10,11... | collective-permute-start | bytes 98312 | tf_op jit(solution)/shard_map/softmax_tp1/ppermute | solution.py:22
  18.0 0.9 collective-permute-done.6.refs_3_
  18.9 0.6 copy-done.11
  19.5 1.7 %combine.1.refs_3_.refs_2_ = bf16[144,1024]{1,0:T(8,128)(2,1)} custom-call(bf16[144,1024]{1,0:T(8,128)(2,1)} %get-tuple-element.21.load_ref, f32[24,256]{1,0:T(8,128)} %get-tuple-element.22.own_ref, f32[1,16,256]{2,1,0:T(8,128)} %get-tuple-element.23.refs_0_, f32[2,16,256]{2,1,0:T(8,128)} %copy-done.10, ...), custom_call_target="tpu_custom_call", output_to_operand_aliasing={{}: (0, {})} | custom-call | tf_op jit(solution)/shard_map/combine/pallas_call | solution.py:380
  21.2 0.0 collective-permute-done.2.refs_1_
  21.2 0.0 collective-permute-done.1.refs_0_
  21.2 1.2 %stack.1 = (bf16[96,1024]{1,0:T(8,128)(2,1)S(1)}, bf16[96,1024]{1,0:T(8,128)(2,1)S(1)}) custom-call(bf16[64,1024]{1,0:T(8,128)(2,1)S(1)} %collective-permute-done.1.refs_0_, bf16[64,1024]{1,0:T(8,128)(2,1)S(1)} %collective-permute-done.2.refs_1_, bf16[64,1024]{1,0:T(8,128)(2,1)S(1)} %collective-permute-done.3.refs_2_, bf16[144,1024]{1,0:T(8,128)(2,1)} %combine.1.refs_3_.refs_2_), custom_call_target="tpu_custom_call" | custom-call | tf_op jit(solution)/shard_map/stack/pallas_call | solution.py:82
  22.5 0.4 collective-permute-start.7
  22.9 0.2 collective-permute-start.8
  23.0 1.7 %collective-permute-start.11 = (bf16[144,1024]{1,0:T(8,128)(2,1)}, bf16[144,1024]{1,0:T(8,128)(2,1)S(1)}, u32[]{:S(2)}, u32[]{:S(2)}) collective-permute-start(bf16[144,1024]{1,0:T(8,128)(2,1)} %combine.1.refs_3_.refs_2_), channel_id=1, source_target_pairs={{0,24},{4,28},{8,0},{12,4},{16,8},{20,12},{24,16},{28,20},{1,25},{... | collective-permute-start | bytes 884744 | tf_op jit(solution)/shard_map/attn_z3/ppermute | solution.py:28
  24.8 1.5 %collective-permute-start.10 = (bf16[144,1024]{1,0:T(8,128)(2,1)}, bf16[144,1024]{1,0:T(8,128)(2,1)}, u32[]{:S(2)}, u32[]{:S(2)}) collective-permute-start(bf16[144,1024]{1,0:T(8,128)(2,1)} %combine.1.refs_3_.refs_2_), channel_id=1, source_target_pairs={{0,16},{4,20},{8,24},{12,28},{16,0},{20,4},{24,8},{28,12},{1,17},{... | collective-permute-start | bytes 884744 | tf_op jit(solution)/shard_map/attn_z2/ppermute | solution.py:28
  26.3 0.0 collective-permute-done.7.refs_5_
  26.3 0.0 collective-permute-start.9
  26.3 0.7 copy-done.9
  27.0 0.0 copy-done.8
  27.1 5.3 %middle.1 = (bf16[128,1024]{1,0:T(8,128)(2,1)}, bf16[128,1024]{1,0:T(8,128)(2,1)}, bf16[128,1024]{1,0:T(8,128)(2,1)}, f32[128,1024]{1,0:T(8,128)}, bf16[512,512]...) custom-call(bf16[128,4096]{1,0:T(8,128)(2,1)} %refs_0_.3, bf16[512,1024]{1,0:T(8,128)(2,1)} %refs_0_.4, ...), custom_call_target="tpu_custom_call" | custom-call | tf_op jit(solution)/shard_map/middle/pallas_call | solution.py:82
  32.3 0.3 collective-permute-start.12
  32.7 1.2 %collective-permute-start.13 = (bf16[256,512]{1,0:T(8,128)(2,1)}, bf16[256,512]{1,0:T(8,128)(2,1)S(1)}, u32[]{:S(2)}, u32[]{:S(2)}) collective-permute-start(bf16[256,512]{1,0:T(8,128)(2,1)} %get-tuple-element.34), channel_id=1, source_target_pairs={{0,4},{4,0},{8,12},{12,8},{16,20},{20,16},{24,28},{28,24},{1,5},{5... | collective-permute-start | bytes 786440 | tf_op jit(solution)/shard_map/cot_x/ppermute | solution.py:22
  33.9 16.2 %collective-permute-done.10.refs_5_.refs_4_ = bf16[144,1024]{1,0:T(8,128)(2,1)} collective-permute-done((bf16[144,1024]{1,0:T(8,128)(2,1)}, bf16[144,1024]{1,0:T(8,128)(2,1)}, u32[]{:S(2)}, u32[]{:S(2)}) %collective-permute-start.10) | collective-permute-done | bytes 294944 | tf_op jit(solution)/shard_map/attn_z2/ppermute | solution.py:28
  50.1 1.7 %collective-permute-done.9.refs_4_.refs_3_ = bf16[144,1024]{1,0:T(8,128)(2,1)} collective-permute-done((bf16[144,1024]{1,0:T(8,128)(2,1)}, bf16[144,1024]{1,0:T(8,128)(2,1)}, u32[]{:S(2)}, u32[]{:S(2)}) %collective-permute-start.9) | collective-permute-done | bytes 294944 | tf_op jit(solution)/shard_map/attn_z1/ppermute | solution.py:28
  51.8 0.0 collective-permute-done.12.refs_7_.refs_3_
  51.8 0.0 collective-permute-done.13.refs_8_.refs_4_
  51.9 0.7 copy-done.3
  52.6 0.1 copy-done.4
  52.6 2.0 %gate.1 = (bf16[128,1024]{1,0:T(8,128)(2,1)}, bf16[128,1024]{1,0:T(8,128)(2,1)}, bf16[128,1024]{1,0:T(8,128)(2,1)}, bf16[512,1024]{1,0:T(8,128)(2,1)}) custom-call(bf16[128,1024]{1,0:T(8,128)(2,1)} %get-tuple-element.30.refs_0_, bf16[128,1024]{1,0:T(8,128)(2,1)} %get-tuple-element.31.refs_1_, ...), custom_call_target="tpu_custom_call", output_to_operand_aliasing={{0}: (0, {}), {1}: (1, {}), {2}: (2, {})} | custom-call | tf_op jit(solution)/shard_map/gate/pallas_call | solution.py:422
  54.6 0.3 collective-permute-start.14
  54.9 1.4 %collective-permute-start.16 = (bf16[128,1024]{1,0:T(8,128)(2,1)}, bf16[128,1024]{1,0:T(8,128)(2,1)S(1)}, u32[]{:S(2)}, u32[]{:S(2)}) collective-permute-start(bf16[128,1024]{1,0:T(8,128)(2,1)} %get-tuple-element.37), channel_id=1, source_target_pairs={{0,16},{4,20},{8,24},{12,28},{16,0},{20,4},{24,8},{28,12},{1,17},{... | collective-permute-start | bytes 786440 | tf_op jit(solution)/shard_map/sum_z2/ppermute | solution.py:28
  56.3 1.5 %collective-permute-start.17 = (bf16[128,1024]{1,0:T(8,128)(2,1)}, bf16[128,1024]{1,0:T(8,128)(2,1)S(1)}, u32[]{:S(2)}, u32[]{:S(2)}) collective-permute-start(bf16[128,1024]{1,0:T(8,128)(2,1)} %get-tuple-element.38), channel_id=1, source_target_pairs={{0,8},{4,12},{8,16},{12,20},{16,24},{20,28},{24,0},{28,4},{1,9},{5... | collective-permute-start | bytes 786440 | tf_op jit(solution)/shard_map/sum_z3/ppermute | solution.py:28
  57.8 3.1 %decode.1 = f32[4,1,2,1024]{3,2,1,0:T(2,128)} custom-call(bf16[512,1024]{1,0:T(8,128)(2,1)} %refs_0_.4, bf16[512,1024]{1,0:T(8,128)(2,1)} %collective-permute-done.refs_2_.refs_1_, bf16[144,1024]{1,0:T(8,128)(2,1)} %combine.1.refs_3_.refs_2_, bf16[144,1024]{1,0:T(8,128)(2,1)} %collective-permute-done.9.refs_4_.refs_3_, ...), custom_call_target="tpu_custom_call" | custom-call | tf_op jit(solution)/shard_map/decode/pallas_call | solution.py:82
  60.9 9.1 %all_to_all.5 = f32[4,1,2,1024]{3,2,1,0:T(2,128)S(1)} all-to-all(f32[4,1,2,1024]{3,2,1,0:T(2,128)} %decode.1), channel_id=1, replica_groups=mesh['fsdp'=8,'tp'=4] {'tp'}, dimensions={0} | all-to-all | bytes 65536 | tf_op jit(solution)/shard_map/dec_tp/all_to_all | solution.py:458
  70.1 1.9 %collective-permute-start.18 = (bf16[2,1024]{1,0:T(2,128)(2,1)S(1)}, bf16[2,1024]{1,0:T(2,128)(2,1)S(1)}, u32[]{:S(2)}, u32[]{:S(2)}) collective-permute-start(bf16[2,1024]{1,0:T(2,128)(2,1)S(1)} %reduce_sum.9), channel_id=1, source_target_pairs={{0,0},{1,8},{2,16},{3,24},{4,4},{5,12},{6,20},{7,28},{8,1},{9,9},{... | collective-permute-start | bytes 12296 | tf_op jit(solution)/shard_map/dec_place/ppermute | solution.py:468
  72.0 3.3 %own.1.refs_1_ = f32[512,1024]{1,0:T(8,128)} custom-call(bf16[512,512]{1,0:T(8,128)(2,1)} %get-tuple-element.29.refs_0_, bf16[512,1024]{1,0:T(8,128)(2,1)} %get-tuple-element.35.refs_1_.refs_6_), custom_call_target="tpu_custom_call" | custom-call | tf_op jit(solution)/shard_map/own/pallas_call | solution.py:82
  75.3 5.8 %collective-permute-done.18.refs_8_ = bf16[2,1024]{1,0:T(2,128)(2,1)S(1)} collective-permute-done((bf16[2,1024]{1,0:T(2,128)(2,1)S(1)}, bf16[2,1024]{1,0:T(2,128)(2,1)S(1)}, u32[]{:S(2)}, u32[]{:S(2)}) %collective-permute-start.18) | collective-permute-done | bytes 4128 | tf_op jit(solution)/shard_map/dec_place/ppermute | solution.py:468
  81.2 0.5 copy-done.13
  81.7 0.1 copy-done.5
  81.8 0.1 copy-done.6
  81.9 0.1 copy-done.7
  82.0 4.1 %last.1 = (bf16[1,2,1024]{2,1,0:T(2,128)(2,1)}, bf16[128,1024]{1,0:T(8,128)(2,1)}, f32[512,1024]{1,0:T(8,128)}) custom-call(f32[128,1024]{1,0:T(8,128)} %get-tuple-element.28.refs_0_, f32[512,1024]{1,0:T(8,128)} %own.1.refs_1_, bf16[512,1024]{1,0:T(8,128)(2,1)} %collective-permute-done.14.refs_2_, bf16[256,512]{1,0:T(8,128)(2,1)} %copy-done.3, ...), custom_call_target="tpu_custom_call" | custom-call | tf_op jit(solution)/shard_map/last/pallas_call | solution.py:82
  (29 shorter events, 0.1 us)
Async XLA Ops:
  0.6 26.4 %collective-permute-start = (bf16[512,1024]{1,0:T(8,128)(2,1)}, bf16[512,1024]{1,0:T(8,128)(2,1)}, u32[]{:S(2)}, u32[]{:S(2)}) collective-permute-start(bf16[512,1024]{1,0:T(8,128)(2,1)} %refs_0_.4), channel_id=1, source_target_pairs={{0,4},{4,0},{8,12},{12,8},{16,20},{20,16},{24,28},{28,24},{1,5},{5... | collective-permute-start | bytes 3145736 | tf_op jit(solution)/shard_map/weight_x/ppermute | solution.py:22
  3.0 18.2 %collective-permute-start.3 = (bf16[64,1024]{1,0:T(8,128)(2,1)S(1)}, bf16[64,1024]{1,0:T(8,128)(2,1)S(1)}, u32[]{:S(2)}, u32[]{:S(2)}) collective-permute-start(bf16[64,1024]{1,0:T(8,128)(2,1)S(1)} %get-tuple-element.39), channel_id=1, source_target_pairs={{0,24},{4,28},{8,0},{12,4},{16,8},{20,12},{24,16},{28,20},{1,25},{... | collective-permute-start | bytes 393224 | tf_op jit(solution)/shard_map/cot_z3/ppermute | solution.py:28
  3.2 18.0 %collective-permute-start.2 = (bf16[64,1024]{1,0:T(8,128)(2,1)S(1)}, bf16[64,1024]{1,0:T(8,128)(2,1)S(1)}, u32[]{:S(2)}, u32[]{:S(2)}) collective-permute-start(bf16[64,1024]{1,0:T(8,128)(2,1)S(1)} %get-tuple-element.40), channel_id=1, source_target_pairs={{0,16},{4,20},{8,24},{12,28},{16,0},{20,4},{24,8},{28,12},{1,17},{... | collective-permute-start | bytes 393224 | tf_op jit(solution)/shard_map/cot_z2/ppermute | solution.py:28
  6.4 14.8 %collective-permute-start.1 = (bf16[64,1024]{1,0:T(8,128)(2,1)S(1)}, bf16[64,1024]{1,0:T(8,128)(2,1)S(1)}, u32[]{:S(2)}, u32[]{:S(2)}) collective-permute-start(bf16[64,1024]{1,0:T(8,128)(2,1)S(1)} %get-tuple-element.41), channel_id=1, source_target_pairs={{0,8},{4,12},{8,16},{12,20},{16,24},{20,28},{24,0},{28,4},{1,9},{5... | collective-permute-start | bytes 393224 | tf_op jit(solution)/shard_map/cot_z1/ppermute | solution.py:28
  10.9 2.6 %collective-permute-start.5 = (f32[1,16,256]{2,1,0:T(8,128)}, f32[1,16,256]{2,1,0:T(8,128)S(1)}, u32[]{:S(2)}, u32[]{:S(2)}) collective-permute-start(f32[1,16,256]{2,1,0:T(8,128)} %get-tuple-element.25), channel_id=1, source_target_pairs={{0,1},{1,0},{2,3},{3,2},{4,5},{5,4},{6,7},{7,6},{8,9},{9,8},{10,11... | collective-permute-start | bytes 49160 | tf_op jit(solution)/shard_map/softmax_tp1/ppermute | solution.py:22
  13.5 5.3 %copy-start.12 = (f32[1,16,256]{2,1,0:T(8,128)}, f32[1,16,256]{2,1,0:T(8,128)S(1)}, u32[]{:S(2)}) copy-start(f32[1,16,256]{2,1,0:T(8,128)S(1)} %collective-permute-done.5.refs_2_) | copy-start | bytes 49156
  13.5 3.4 %collective-permute-start.4 = (f32[2,16,256]{2,1,0:T(8,128)}, f32[2,16,256]{2,1,0:T(8,128)S(1)}, u32[]{:S(2)}, u32[]{:S(2)}) collective-permute-start(f32[2,16,256]{2,1,0:T(8,128)} %get-tuple-element.24), channel_id=1, source_target_pairs={{0,2},{1,3},{2,0},{3,1},{4,6},{5,7},{6,4},{7,5},{8,10},{9,11},{10,... | collective-permute-start | bytes 98312 | tf_op jit(solution)/shard_map/softmax_tp2/ppermute | solution.py:22
  16.9 2.0 %copy-start.10 = (f32[2,16,256]{2,1,0:T(8,128)}, f32[2,16,256]{2,1,0:T(8,128)S(1)}, u32[]{:S(2)}) copy-start(f32[2,16,256]{2,1,0:T(8,128)S(1)} %collective-permute-done.4.refs_1_) | copy-start | bytes 98308
  16.9 2.0 %collective-permute-start.6 = (f32[2,16,256]{2,1,0:T(8,128)S(1)}, f32[2,16,256]{2,1,0:T(8,128)S(1)}, u32[]{:S(2)}, u32[]{:S(2)}) collective-permute-start(f32[2,16,256]{2,1,0:T(8,128)S(1)} %collective-permute-done.4.refs_1_), channel_id=1, source_target_pairs={{0,1},{1,0},{2,3},{3,2},{4,5},{5,4},{6,7},{7,6},{8,9},{9,8},{10,11... | collective-permute-start | bytes 98312 | tf_op jit(solution)/shard_map/softmax_tp1/ppermute | solution.py:22
  18.9 0.6 copy-start.11
  22.4 4.6 %copy-start = (bf16[96,1024]{1,0:T(8,128)(2,1)}, bf16[96,1024]{1,0:T(8,128)(2,1)S(1)}, u32[]{:S(2)}) copy-start(bf16[96,1024]{1,0:T(8,128)(2,1)S(1)} %get-tuple-element.26.refs_3_) | copy-start | bytes 589828
  22.5 4.6 %copy-start.1 = (bf16[96,1024]{1,0:T(8,128)(2,1)}, bf16[96,1024]{1,0:T(8,128)(2,1)S(1)}, u32[]{:S(2)}) copy-start(bf16[96,1024]{1,0:T(8,128)(2,1)S(1)} %get-tuple-element.27.refs_4_) | copy-start | bytes 589828
  22.5 3.8 %collective-permute-start.7 = (bf16[96,1024]{1,0:T(8,128)(2,1)S(1)}, bf16[96,1024]{1,0:T(8,128)(2,1)S(1)}, u32[]{:S(2)}, u32[]{:S(2)}) collective-permute-start(bf16[96,1024]{1,0:T(8,128)(2,1)S(1)} %get-tuple-element.26.refs_3_), channel_id=1, source_target_pairs={{0,1},{1,0},{2,3},{3,2},{4,5},{5,4},{6,7},{7,6},{8,9},{9,8},{10,11... | collective-permute-start | bytes 589832 | tf_op jit(solution)/shard_map/cot_core/ppermute | solution.py:22
  22.9 3.4 %collective-permute-start.8 = (bf16[96,1024]{1,0:T(8,128)(2,1)S(1)}, bf16[96,1024]{1,0:T(8,128)(2,1)S(1)}, u32[]{:S(2)}, u32[]{:S(2)}) collective-permute-start(bf16[96,1024]{1,0:T(8,128)(2,1)S(1)} %get-tuple-element.27.refs_4_), channel_id=1, source_target_pairs={{0,1},{1,0},{2,3},{3,2},{4,5},{5,4},{6,7},{7,6},{8,9},{9,8},{10,11... | collective-permute-start | bytes 589832 | tf_op jit(solution)/shard_map/cot_core/ppermute | solution.py:22
  23.0 10.8 %collective-permute-start.11 = (bf16[144,1024]{1,0:T(8,128)(2,1)}, bf16[144,1024]{1,0:T(8,128)(2,1)S(1)}, u32[]{:S(2)}, u32[]{:S(2)}) collective-permute-start(bf16[144,1024]{1,0:T(8,128)(2,1)} %combine.1.refs_3_.refs_2_), channel_id=1, source_target_pairs={{0,24},{4,28},{8,0},{12,4},{16,8},{20,12},{24,16},{28,20},{1,25},{... | collective-permute-start | bytes 884744 | tf_op jit(solution)/shard_map/attn_z3/ppermute | solution.py:28
  24.8 25.3 %collective-permute-start.10 = (bf16[144,1024]{1,0:T(8,128)(2,1)}, bf16[144,1024]{1,0:T(8,128)(2,1)}, u32[]{:S(2)}, u32[]{:S(2)}) collective-permute-start(bf16[144,1024]{1,0:T(8,128)(2,1)} %combine.1.refs_3_.refs_2_), channel_id=1, source_target_pairs={{0,16},{4,20},{8,24},{12,28},{16,0},{20,4},{24,8},{28,12},{1,17},{... | collective-permute-start | bytes 884744 | tf_op jit(solution)/shard_map/attn_z2/ppermute | solution.py:28
  26.3 0.7 copy-start.8
  26.3 25.5 %collective-permute-start.9 = (bf16[144,1024]{1,0:T(8,128)(2,1)}, bf16[144,1024]{1,0:T(8,128)(2,1)}, u32[]{:S(2)}, u32[]{:S(2)}) collective-permute-start(bf16[144,1024]{1,0:T(8,128)(2,1)} %combine.1.refs_3_.refs_2_), channel_id=1, source_target_pairs={{0,8},{4,12},{8,16},{12,20},{16,24},{20,28},{24,0},{28,4},{1,9},{5... | collective-permute-start | bytes 884744 | tf_op jit(solution)/shard_map/attn_z1/ppermute | solution.py:28
  26.3 0.7 copy-start.9
  32.3 19.5 %collective-permute-start.12 = (bf16[256,512]{1,0:T(8,128)(2,1)}, bf16[256,512]{1,0:T(8,128)(2,1)S(1)}, u32[]{:S(2)}, u32[]{:S(2)}) collective-permute-start(bf16[256,512]{1,0:T(8,128)(2,1)} %get-tuple-element.33), channel_id=1, source_target_pairs={{0,4},{4,0},{8,12},{12,8},{16,20},{20,16},{24,28},{28,24},{1,5},{5... | collective-permute-start | bytes 786440 | tf_op jit(solution)/shard_map/cot_x/ppermute | solution.py:22
  32.7 19.2 %collective-permute-start.13 = (bf16[256,512]{1,0:T(8,128)(2,1)}, bf16[256,512]{1,0:T(8,128)(2,1)S(1)}, u32[]{:S(2)}, u32[]{:S(2)}) collective-permute-start(bf16[256,512]{1,0:T(8,128)(2,1)} %get-tuple-element.34), channel_id=1, source_target_pairs={{0,4},{4,0},{8,12},{12,8},{16,20},{20,16},{24,28},{28,24},{1,5},{5... | collective-permute-start | bytes 786440 | tf_op jit(solution)/shard_map/cot_x/ppermute | solution.py:22
  33.9 18.0 %copy-start.2 = (bf16[144,1024]{1,0:T(8,128)(2,1)}, bf16[144,1024]{1,0:T(8,128)(2,1)S(1)}, u32[]{:S(2)}) copy-start(bf16[144,1024]{1,0:T(8,128)(2,1)S(1)} %collective-permute-done.11.refs_6_.refs_5_) | copy-start | bytes 884740
  51.8 0.7 copy-start.3
  51.9 0.8 copy-start.4
  54.6 26.5 %collective-permute-start.14 = (bf16[512,1024]{1,0:T(8,128)(2,1)}, bf16[512,1024]{1,0:T(8,128)(2,1)}, u32[]{:S(2)}, u32[]{:S(2)}) collective-permute-start(bf16[512,1024]{1,0:T(8,128)(2,1)} %get-tuple-element.35.refs_1_.refs_6_), channel_id=1, source_target_pairs={{0,4},{4,0},{8,12},{12,8},{16,20},{20,16},{24,28},{28,24},{1,5},{5... | collective-permute-start | bytes 3145736 | tf_op jit(solution)/shard_map/attn_x/ppermute | solution.py:22
  54.9 26.2 %collective-permute-start.15 = (bf16[128,1024]{1,0:T(8,128)(2,1)}, bf16[128,1024]{1,0:T(8,128)(2,1)S(1)}, u32[]{:S(2)}, u32[]{:S(2)}) collective-permute-start(bf16[128,1024]{1,0:T(8,128)(2,1)} %get-tuple-element.36), channel_id=1, source_target_pairs={{0,24},{4,28},{8,0},{12,4},{16,8},{20,12},{24,16},{28,20},{1,25},{... | collective-permute-start | bytes 786440 | tf_op jit(solution)/shard_map/sum_z1/ppermute | solution.py:28
  54.9 26.2 %collective-permute-start.16 = (bf16[128,1024]{1,0:T(8,128)(2,1)}, bf16[128,1024]{1,0:T(8,128)(2,1)S(1)}, u32[]{:S(2)}, u32[]{:S(2)}) collective-permute-start(bf16[128,1024]{1,0:T(8,128)(2,1)} %get-tuple-element.37), channel_id=1, source_target_pairs={{0,16},{4,20},{8,24},{12,28},{16,0},{20,4},{24,8},{28,12},{1,17},{... | collective-permute-start | bytes 786440 | tf_op jit(solution)/shard_map/sum_z2/ppermute | solution.py:28
  56.3 24.8 %collective-permute-start.17 = (bf16[128,1024]{1,0:T(8,128)(2,1)}, bf16[128,1024]{1,0:T(8,128)(2,1)S(1)}, u32[]{:S(2)}, u32[]{:S(2)}) collective-permute-start(bf16[128,1024]{1,0:T(8,128)(2,1)} %get-tuple-element.38), channel_id=1, source_target_pairs={{0,8},{4,12},{8,16},{12,20},{16,24},{20,28},{24,0},{28,4},{1,9},{5... | collective-permute-start | bytes 786440 | tf_op jit(solution)/shard_map/sum_z3/ppermute | solution.py:28
  70.1 11.1 %collective-permute-start.18 = (bf16[2,1024]{1,0:T(2,128)(2,1)S(1)}, bf16[2,1024]{1,0:T(2,128)(2,1)S(1)}, u32[]{:S(2)}, u32[]{:S(2)}) collective-permute-start(bf16[2,1024]{1,0:T(2,128)(2,1)S(1)} %reduce_sum.9), channel_id=1, source_target_pairs={{0,0},{1,8},{2,16},{3,24},{4,4},{5,12},{6,20},{7,28},{8,1},{9,9},{... | collective-permute-start | bytes 12296 | tf_op jit(solution)/shard_map/dec_place/ppermute | solution.py:468
  81.1 0.6 copy-start.13
  81.1 0.7 copy-start.5
  81.1 0.8 copy-start.6
  81.1 0.9 %copy-start.7 = (bf16[128,1024]{1,0:T(8,128)(2,1)}, bf16[128,1024]{1,0:T(8,128)(2,1)S(1)}, u32[]{:S(2)}) copy-start(bf16[128,1024]{1,0:T(8,128)(2,1)S(1)} %collective-permute-done.17.refs_7_) | copy-start | bytes 786436

commit v4 on v3

--- a/solution.py
+++ b/solution.py
@@ -67,7 +67,7 @@
     return tp_index, tp_index % 2, fsdp_index // INNER, fsdp_index % INNER, tp_index * KVH // lax.axis_size("tp")
 
 
-def call(kernel, name, operands, out_shapes, scratch, waits=(), scalars=None, room=12, fast=()):
+def call(kernel, name, operands, out_shapes, scratch, waits=(), scalars=None, room=12, fast=(), near=()):
     copies = 4 * (len(operands) + len(out_shapes))
     scalars = [] if scalars is None else [scalars]
 
@@ -83,7 +83,8 @@
         body,
         out_shape=[jax.ShapeDtypeStruct(shape, dtype) for shape, dtype in out_shapes],
         in_specs=[pl.BlockSpec(memory_space=pltpu.SMEM)] * len(scalars)
-        + [pl.BlockSpec(memory_space=pltpu.HBM)] * (len(operands) + len(waits)),
+        + [pl.BlockSpec(memory_space=pltpu.VMEM if i in near else pltpu.HBM) for i in range(len(operands))]
+        + [pl.BlockSpec(memory_space=pltpu.HBM)] * len(waits),
         out_specs=[
             pl.BlockSpec(memory_space=pltpu.VMEM if i in fast else pltpu.HBM) for i in range(len(out_shapes))
         ],
@@ -95,17 +96,31 @@
     return list(results)
 
 
+def kept(arrays, waits, name):
+    count = len(arrays)
+    results = pl.pallas_call(
+        lambda *refs: None,
+        out_shape=[jax.ShapeDtypeStruct(a.shape, a.dtype) for a in arrays],
+        in_specs=[pl.BlockSpec(memory_space=pltpu.HBM)] * (count + len(waits)),
+        out_specs=[pl.BlockSpec(memory_space=pltpu.HBM)] * count,
+        input_output_aliases={i: i for i in range(count)},
+        compiler_params=pltpu.CompilerParams(vmem_limit_bytes=12 << 20),
+        cost_estimate=pl.CostEstimate(flops=0, bytes_accessed=0, transcendentals=0),
+        name=name,
+    )(*arrays, *waits)
+    return list(results)
+
+
 def shaped(*arrays):
     return [(a.shape, a.dtype) for a in arrays]
 
 
 def attend_kernel(steps, mover, lengths_ref, ins, outs, scratch):
-    query_hbm, keys_hbm, values_hbm, new_keys_hbm, new_values_hbm, attn_hbm = ins
-    query_ref, keys_ref, values_ref, new_keys_ref, new_values_ref, query_rows, out_rows, attn_ref = scratch
+    query_hbm, keys_hbm, values_hbm, new_keys_hbm, new_values_hbm = ins
+    query_ref, keys_ref, values_ref, new_keys_ref, new_values_ref, query_rows, out_rows = scratch
     tp_index, _, _, _, own_group = places()
     length = lengths_ref[0]
-    load_out, own_ref, *part_refs = outs
-    tp_size = sum(ref.shape[0] for ref in part_refs)
+    own_ref, *chunk_refs = outs
     first = mover.start(query_hbm.at[0], query_ref)
     news = [mover.start(new_keys_hbm.at[0], new_keys_ref), mover.start(new_values_hbm.at[0], new_values_ref)]
     groups = [slice(g * HD, (g + 1) * HD) for g in range(KVH)]
@@ -113,7 +128,6 @@
         (mover.start(keys_hbm.at[0, :, group], keys_ref.at[:, group]), mover.start(values_hbm.at[0, :, group], values_ref.at[:, group]))
         for group in groups
     ]
-    attn = mover.start(attn_hbm, attn_ref)
     width = query_ref.shape[1]
     cache_len = keys_ref.shape[0]
     rows = width // HD // KVH * steps
@@ -123,9 +137,6 @@
     usable = lax.broadcasted_iota(jnp.int32, (rows, cache_len), 1) + tp_index * cache_len < length
     left = lax.broadcasted_iota(jnp.int32, (rows, HD), 1) < HD // 2
     for g in range(KVH):
-        if g == KVH - 1:
-            mover.wait(attn)
-            mover.start(attn_ref, load_out.at[: attn_ref.shape[0]])
         mover.wait(*arrive[g])
         query = query_rows[g * rows : (g + 1) * rows, :].astype(BF16)
         scores = over_features(query, keys_ref[:, g * HD : (g + 1) * HD]) * (1.0 / HD**0.5)
@@ -137,36 +148,41 @@
         both = dot(jnp.concatenate([upper, lower], axis=0), values_ref[:, g * HD : (g + 1) * HD])
         out_rows[g * rows : (g + 1) * rows, :HD] = both[:rows] + both[rows:]
         out_rows[g * rows : (g + 1) * rows, HD:] = jnp.where(left, maxima, totals)
-    count = part_refs[0].shape[1]
+    count = chunk_refs[0].shape[1]
     for t in range(KVH * rows // count):
-        for i, part_ref in enumerate(part_refs):
-            for k in range(part_ref.shape[0]):
-
-                @pl.when(tp_index ^ ((i and part_ref.shape[0]) + k) == t)
+        for chunk_ref in chunk_refs:
+            for k in range(chunk_ref.shape[0]):
+
+                @pl.when(tp_index ^ (chunk_ref.shape[0] + k) == t)
                 def _():
-                    part_ref[k] = out_rows[t * count : (t + 1) * count, :]
+                    chunk_ref[k] = out_rows[t * count : (t + 1) * count, :]
 
         @pl.when(tp_index == t)
         def _():
-            own_ref[:count, :HD] = query_rows[t * count : (t + 1) * count, :]
+            own_ref[:count, :] = out_rows[t * count : (t + 1) * count, :]
+            own_ref[count : 2 * count, :HD] = query_rows[t * count : (t + 1) * count, :]
 
     mover.wait(*news)
-    own_ref[:count, HD:] = jnp.zeros((count, HD), F32)
+    own_ref[count : 2 * count, HD:] = jnp.zeros((count, HD), F32)
     for at, ref in ((0, new_keys_ref), (HD, new_values_ref)):
         chosen = ref[:, :HD].astype(F32)
         for g in range(1, KVH):
             chosen = jnp.where(own_group == g, ref[:, groups[g]].astype(F32), chosen)
-        own_ref[count : count + steps, at : at + HD] = chosen
-
-
-def combine_kernel(steps, indices, load_ref, own_ref, *refs):
-    *part_refs, out_ref, rows_ref, low_ref, sem = refs
+        own_ref[2 * count : 2 * count + steps, at : at + HD] = chosen
+
+
+def combine_kernel(steps, sent, indices, attn_hbm, own_ref, *refs):
+    *part_refs, out_hbm, rows_ref, load_ref, sems = refs
+    rest = attn_hbm.shape[0] - sent
+    arrive = pltpu.make_async_copy(attn_hbm.at[sent:], load_ref.at[:rest], sems.at[0])
+    arrive.start()
     count = part_refs[0].shape[1]
+    own = own_ref[...]
     rows_ref[...] = jnp.zeros_like(rows_ref)
     step = lax.broadcasted_iota(jnp.int32, (count, 1), 0) % steps
-    query = own_ref[:count, :HD]
-    keys, values = own_ref[count:, :HD], own_ref[count:, HD:]
-    parts = [part_ref[i] for i, part_ref in zip(indices, part_refs)]
+    query = own[count : 2 * count, :HD]
+    keys, values = own[2 * count :, :HD], own[2 * count :, HD:]
+    parts = [own[:count]] + [part_ref[i] for i, part_ref in zip(indices, part_refs)]
     scores = []
     for j in range(steps):
         score = jnp.sum(query * keys[j : j + 1], axis=-1, keepdims=True) * (1.0 / HD**0.5)
@@ -187,10 +203,26 @@
     for row in range(count):
         h, s = row // steps, row % steps
         rows_ref[s : s + 1, h * HD : (h + 1) * HD] = attended[row : row + 1]
-    low_ref[...] = rows_ref[...].astype(BF16)
-    copy = pltpu.make_async_copy(low_ref, out_ref.at[out_ref.shape[0] - PAD :], sem)
-    copy.start()
-    copy.wait()
+    load_ref[rest:, :] = rows_ref[...].astype(BF16)
+    arrive.wait()
+    leave = pltpu.make_async_copy(load_ref, out_hbm, sems.at[1])
+    leave.start()
+    leave.wait()
+
+
+def cut_kernel(outer, half, early, mover, ins, outs, scratch):
+    grad_hbm, attn_hbm = ins
+    plane = outs[0].shape[1]
+    _, core, z, _, _ = places()
+    rows = pl.ds(pl.multiple_of(core * half, half), half)
+    for k in range(1, outer):
+        columns = pl.ds(pl.multiple_of((z + k) % outer * plane, plane), plane)
+        mover.start(grad_hbm.at[rows, columns], scratch[0].at[k - 1, :half])
+        mover.start(attn_hbm.at[:early], scratch[0].at[k - 1, half:])
+    arrive = list(mover.open)
+    for k in range(1, outer):
+        mover.wait(*arrive[2 * k - 2 : 2 * k])
+        mover.start(scratch[0].at[k - 1], outs[k - 1])
 
 
 def middle_kernel(outer, mover, ins, outs, scratch):
@@ -206,15 +238,9 @@
     blocks = [[mover.start(grad_hbm.at[:, pl.ds(pl.multiple_of(z * plane, plane), plane)], cots_ref.at[:tokens])]]
     for k in range(1, outer):
         blocks.append([])
-        for hbms, side in ((cot_hbms[:2], core), (cot_hbms[2:], 1 - core)):
-            base = pl.multiple_of(k * tokens + side * half, half)
-            for i, hbm in enumerate(hbms):
-                size = hbm.shape[0]
-                low, high = max((k - 1) * half, i * size), min(k * half, (i + 1) * size)
-                if low < high:
-                    source = hbm.at[low - i * size : high - i * size]
-                    first = pl.multiple_of(base + (low - (k - 1) * half), half // 2)
-                    blocks[k].append(mover.start(source, cots_ref.at[pl.ds(first, high - low)]))
+        for hbm, side in ((cot_hbms[k - 1], core), (cot_hbms[outer + k - 2], 1 - core)):
+            first = pl.multiple_of(k * tokens + side * half, half)
+            blocks[k].append(mover.start(hbm.at[:half], cots_ref.at[pl.ds(first, half)]))
     mover.wait(*weights)
     span = outer * half
     for k in reversed(range(outer)):
@@ -234,8 +260,10 @@
         cot_own_ref[here, :] = own
         cot_far_ref[here, :] = other
 
+    size = cot_far_outs[0].shape[0]
     for i, out in enumerate(cot_far_outs):
-        mover.start(cot_far_ref.at[i * span : (i + 1) * span], out)
+        first = pl.multiple_of(core * span + i * size, size)
+        mover.start(cot_far_ref.at[pl.ds(first, size)], out)
     mover.start(cot_own_ref, cot_own_out)
 
 
@@ -261,64 +289,57 @@
 
 
 def own_kernel(mover, ins, outs, scratch):
-    cots_ref, attn_ref, out_ref = scratch
+    cots_ref, attn_ref = scratch
     mover.wait(mover.start(ins[0], cots_ref), mover.start(ins[1], attn_ref))
+    outs[0][...] = over_tokens(cots_ref[...], attn_ref[...])
+
+
+def last_kernel(outer, share, mover, ins, outs, scratch):
+    total_ref, own_ref, attn_ref, *rest = ins
+    cot_refs, part_refs, piece_refs = rest[:2], rest[2 : outer + 1], rest[outer + 1 :]
+    sum_ref, cots_ref, out_ref = scratch
+    _, core, z, _, _ = places()
+    plane = piece_refs[0].shape[1]
+    size = cot_refs[0].shape[0]
+    for j in range(share):
+        mover.start(piece_refs[j], outs[0].at[0, :, pl.ds(pl.multiple_of((z % share ^ j) * plane, plane), plane)])
+    for i, ref in enumerate(cot_refs):
+        first = pl.multiple_of((core ^ i) * size, size)
+        cots_ref[pl.ds(first, size), :] = ref[...]
     pieces = 2
     step = out_ref.shape[0] // pieces
     for i in range(pieces):
         here = slice(i * step, (i + 1) * step)
-        out_ref[here, :] = over_tokens(cots_ref[:, here], attn_ref[...])
-        mover.start(out_ref.at[here], outs[0].at[here])
-
-
-def last_kernel(outer, share, mover, ins, outs, scratch):
-    total_hbm, own_hbm, attn_hbm, *rest = ins
-    cot_hbms, part_hbms, piece_hbms = rest[:2], rest[2 : outer + 1], rest[outer + 1 :]
-    total_ref, parts_ref, sum_ref, pieces_ref, cots_ref, attn_ref, own_ref, out_ref = scratch
-    _, _, z, _, _ = places()
-    plane = pieces_ref.shape[2]
-    span = cot_hbms[0].shape[0]
-    attn = mover.start(attn_hbm, attn_ref)
-    cots = [mover.start(hbm, cots_ref.at[i * span : (i + 1) * span]) for i, hbm in enumerate(cot_hbms)]
-    pieces = 2
-    step = out_ref.shape[0] // pieces
-    heres = [slice(i * step, (i + 1) * step) for i in range(pieces)]
-    owns = [mover.start(own_hbm.at[here], own_ref.at[here]) for here in heres]
-    arrive = [mover.start(total_hbm, total_ref)]
-    arrive += [mover.start(hbm, parts_ref.at[i]) for i, hbm in enumerate(part_hbms)]
-    places_in = [mover.start(hbm, pieces_ref.at[j]) for j, hbm in enumerate(piece_hbms)]
-    mover.wait(attn, *cots)
-    for here, own in zip(heres, owns):
-        product = over_tokens(cots_ref[:, here], attn_ref[...])
-        mover.wait(own)
-        out_ref[here, :] = own_ref[here, :] + product
+        out_ref[here, :] = own_ref[here, :] + over_tokens(cots_ref[:, here], attn_ref[...])
         mover.start(out_ref.at[here], outs[2].at[here])
-    mover.wait(*arrive)
     total = total_ref[...]
-    for i in range(outer - 1):
-        total = total + parts_ref[i].astype(F32)
+    for part_ref in part_refs:
+        total = total + part_ref[...].astype(F32)
     sum_ref[...] = total.astype(BF16)
     mover.start(sum_ref, outs[1])
-    mover.wait(*places_in)
-    for j in range(share):
-        mover.start(pieces_ref.at[j], outs[0].at[0, :, pl.ds(pl.multiple_of((z % share ^ j) * plane, plane), plane)])
-
-
-def stack_kernel(mover, ins, outs, scratch):
-    half, size = ins[0].shape[0], outs[0].shape[0]
-    arrive = [mover.start(hbm, scratch[0].at[k * half : (k + 1) * half]) for k, hbm in enumerate(ins)]
-    mover.wait(*arrive)
-    for i, out in enumerate(outs):
-        mover.start(scratch[0].at[i * size : (i + 1) * size], out)
-
-
-def gate_kernel(count, wait_count, *refs):
-    refs, (pack_out, pack_ref, in_sems, out_sems) = refs[count : -4 - count], refs[-4:]
-    refs = refs[:len(refs) - wait_count]
-    tokens = pack_out.shape[0] // len(refs)
-    parts = [slice(k * tokens, (k + 1) * tokens) for k in range(len(refs))]
-    arrive = [pltpu.make_async_copy(ref.at[:tokens], pack_ref.at[part], in_sems.at[k]) for k, (ref, part) in enumerate(zip(refs, parts))]
-    leave = [pltpu.make_async_copy(pack_ref.at[part], pack_out.at[part], out_sems.at[k]) for k, part in enumerate(parts)]
+
+
+def pack_kernel(early, skip, mover, ins, outs, scratch):
+    low_hbm, high_hbm, own_hbm, *first_hbms = ins
+    cots_ref, attn_ref = scratch
+    tokens, size = own_hbm.shape[0], low_hbm.shape[0]
+    parts = [(low_hbm, cots_ref, outs[0], 0, size), (high_hbm, cots_ref, outs[0], size, size), (own_hbm, attn_ref, outs[1], 0, tokens)]
+    parts += [(hbm.at[skip:], attn_ref, outs[1], (k + 1) * tokens, early) for k, hbm in enumerate(first_hbms)]
+    arrive = [mover.start(source, ref.at[at : at + rows]) for source, ref, _, at, rows in parts]
+    for copy, (_, ref, out, at, rows) in zip(arrive, parts):
+        mover.wait(copy)
+        mover.start(ref.at[at : at + rows], out.at[at : at + rows])
+
+
+def gate_kernel(count, early, *refs):
+    refs, pack_out, (last_ref, in_sems, out_sems) = refs[count + 2 : -4 - count], refs[-4], refs[-3:]
+    rest = refs[0].shape[0] - PAD
+    tokens = rest + early
+    arrive, leave = [], []
+    for k, ref in enumerate(refs):
+        arrive.append(pltpu.make_async_copy(ref.at[:rest], last_ref.at[k], in_sems.at[k]))
+        target = pack_out.at[(k + 1) * tokens + early : (k + 2) * tokens]
+        leave.append(pltpu.make_async_copy(last_ref.at[k], target, out_sems.at[k]))
     for copy in arrive:
         copy.start()
     for copy, follow in zip(arrive, leave):
@@ -351,25 +372,54 @@
 
     half = tokens // 2
 
-    first = tp_index % 2 * half
-    got = [
-        turn(lax.dynamic_slice(grad_out, (first, (z + k) % outer * plane), (half, plane)), k, f"cot_z{k}") for k in far
-    ]
+    early = tokens // 4
+    cot_rows = half * plane // cols
+    if plane == cols:
+        cuts = call(
+            functools.partial(cut_kernel, outer, half, early),
+            "cut",
+            [grad_out, train_attn],
+            [((half + early, cols), BF16)] * len(far),
+            [((len(far), half + early, cols), BF16)],
+            room=63,
+        )
+    else:
+        first = tp_index % 2 * half
+        cuts = [
+            jnp.concatenate(
+                [
+                    lax.dynamic_slice(grad_out, (first, (z + k) % outer * plane), (half, plane)).reshape(cot_rows, cols),
+                    train_attn[:early],
+                ]
+            )
+            for k in far
+        ]
+    firsts = [turn(cuts[k - 1], k, f"first_z{k}") for k in far]
+    got = firsts if plane == cols else [a[:cot_rows].reshape(half, plane) for a in firsts]
 
     sizes = [1 << b for b in range(tp_size.bit_length() - 1)]
-    load, own, part, *chunks = call(
+    own, *chunks = call(
         functools.partial(attend_kernel, steps),
         "attend",
-        [dec_query, cache_keys, cache_values, new_keys, new_values, train_attn],
-        [((tokens + PAD, cols), BF16), ((count + 8, 2 * HD), F32), ((1, count, 2 * HD), F32)]
+        [dec_query, cache_keys, cache_values, new_keys, new_values],
+        [((2 * count + 8, 2 * HD), F32)]
         + [((size, count, 2 * HD), F32) for size in sizes],
         shaped(dec_query[0], cache_keys[0], cache_values[0], new_keys[0], new_values[0])
-        + [((heads * steps, HD), F32), ((heads * steps, 2 * HD), F32), ((tokens, cols), BF16)],
+        + [((heads * steps, HD), F32), ((heads * steps, 2 * HD), F32)],
         scalars=lengths,
         room=63,
-        fast=range(1, 3 + len(sizes)),
-    )
-    parts, indices, held = [part], [0], []
+        fast=range(1 + len(sizes)),
+    )
+    own = pl.pallas_call(
+        lambda in_ref, out_ref: out_ref.__setitem__(..., in_ref[...]),
+        out_shape=jax.ShapeDtypeStruct(own.shape, own.dtype),
+        in_specs=[pl.BlockSpec(memory_space=pltpu.VMEM)],
+        out_specs=pl.BlockSpec(memory_space=pltpu.VMEM),
+        compiler_params=pltpu.CompilerParams(vmem_limit_bytes=12 << 20),
+        cost_estimate=pl.CostEstimate(flops=0, bytes_accessed=0, transcendentals=0),
+        name="hold",
+    )(own)
+    parts, indices, held = [], [], []
     for size, chunk in reversed(list(zip(sizes, chunks))):
         if size > 1:
             came = [flip(a, "tp", size, f"softmax_tp{size}") for a in [chunk] + [a[size:] for a in held]]
@@ -377,34 +427,32 @@
         else:
             parts += held + [flip(a, "tp", size, f"softmax_tp{size}") for a in [chunk] + held]
             indices += [0] * len(held) + [0] + [1] * len(held)
-    load = pl.pallas_call(
-        functools.partial(combine_kernel, steps, indices),
-        out_shape=jax.ShapeDtypeStruct((tokens + PAD, cols), BF16),
+    last = pl.pallas_call(
+        functools.partial(combine_kernel, steps, early, indices),
+        out_shape=jax.ShapeDtypeStruct((tokens - early + PAD, cols), BF16),
         in_specs=[pl.BlockSpec(memory_space=pltpu.HBM)] + [pl.BlockSpec(memory_space=pltpu.VMEM)] * (len(parts) + 1),
         out_specs=pl.BlockSpec(memory_space=pltpu.HBM),
-        scratch_shapes=[pltpu.VMEM((PAD, cols), F32), pltpu.VMEM((PAD, cols), BF16), pltpu.SemaphoreType.DMA],
-        input_output_aliases={0: 0},
+        scratch_shapes=[
+            pltpu.VMEM((PAD, cols), F32),
+            pltpu.VMEM((tokens - early + PAD, cols), BF16),
+            pltpu.SemaphoreType.DMA((2,)),
+        ],
+        compiler_params=pltpu.CompilerParams(vmem_limit_bytes=12 << 20),
         cost_estimate=pl.CostEstimate(flops=0, bytes_accessed=0, transcendentals=0),
         name="combine",
-    )(load, own, *parts)
-    loads = [turn(load, k, f"attn_z{k}") for k in far]
-
-    stacked = call(
-        stack_kernel,
-        "stack",
-        got,
-        [((len(far) * half // 2, plane), BF16)] * 2,
-        [((len(far) * half, plane), BF16)],
-        waits=[load],
-    )
-    twins = [flip(a, "tp", 1, "cot_core") for a in stacked]
+    )(train_attn, own, *parts)
+
+    lasts = [last] + [turn(last, k, f"last_z{k}") for k in far]
+
+    got = kept(got, [last], "kept")
+    twins = [flip(a, "tp", 1, "cot_core") for a in got]
 
     *sent, total, cot_own, cot_low, cot_high = call(
         functools.partial(middle_kernel, outer),
         "middle",
-        [grad_out, out_weight, other_weight, *stacked, *twins],
+        [grad_out, out_weight, other_weight, *got, *twins],
         [((tokens, cols), BF16)] * len(far)
-        + [((tokens, cols), F32), ((outer * tokens, feats), BF16)] + [((outer * half, feats), BF16)] * 2,
+        + [((tokens, cols), F32), ((outer * tokens, feats), BF16)] + [((outer * half // 2, feats), BF16)] * 2,
         [
             ((outer * tokens, plane), BF16),
             ((feats, cols), BF16),
@@ -418,30 +466,39 @@
     )
     cots_x = [flip(a, "fsdp", 1, "cot_x") for a in (cot_low, cot_high)]
 
-    waits = cots_x
+    cots_x, pack = call(
+        functools.partial(pack_kernel, early, cot_rows),
+        "pack",
+        [*cots_x, train_attn, *(got if plane == cols else firsts)],
+        [((outer * half, feats), BF16), ((outer * tokens, cols), BF16)],
+        [((outer * half, feats), BF16), ((outer * tokens, cols), BF16)],
+        room=63,
+    )
+
     results = pl.pallas_call(
-        functools.partial(gate_kernel, len(sent), len(waits)),
-        out_shape=[jax.ShapeDtypeStruct(a.shape, a.dtype) for a in sent]
-        + [jax.ShapeDtypeStruct((outer * tokens, cols), BF16)],
-        in_specs=[pl.BlockSpec(memory_space=pltpu.HBM)] * (len(sent) + outer + len(waits)),
+        functools.partial(gate_kernel, len(sent), early),
+        out_shape=[jax.ShapeDtypeStruct(a.shape, a.dtype) for a in [*sent, pack]],
+        in_specs=[pl.BlockSpec(memory_space=pltpu.HBM)] * (len(sent) + 2 + len(far)),
         out_specs=[pl.BlockSpec(memory_space=pltpu.HBM)] * (len(sent) + 1),
         scratch_shapes=[
-            pltpu.VMEM((outer * tokens, cols), BF16),
-            pltpu.SemaphoreType.DMA((outer,)),
-            pltpu.SemaphoreType.DMA((outer,)),
+            pltpu.VMEM((len(far), tokens - early, cols), BF16),
+            pltpu.SemaphoreType.DMA((len(far),)),
+            pltpu.SemaphoreType.DMA((len(far),)),
         ],
-        input_output_aliases={i: i for i in range(len(sent))},
+        input_output_aliases={i: i for i in range(len(sent) + 1)},
         compiler_params=pltpu.CompilerParams(vmem_limit_bytes=63 << 20),
         cost_estimate=pl.CostEstimate(flops=0, bytes_accessed=0, transcendentals=0),
         name="gate",
-    )(*sent, load, *loads, *waits)
+    )(*sent, pack, cots_x, *lasts[1:])
     sent, pack = results[:-1], results[-1]
     sums = [turn(sent[k - 1], outer - k, f"sum_z{k}") for k in far]
     pack_x = flip(pack, "fsdp", 1, "attn_x")
+    twin_x = flip(cots_x, "tp", 1, "cot_x_core")
+
     (dec,) = call(
         functools.partial(decode_kernel, steps),
         "decode",
-        [out_weight, other_weight, load, *loads],
+        [out_weight, other_weight, *lasts],
         [((tp_size, share, steps, plane), F32)],
         [
             ((feats, cols), BF16),
@@ -471,25 +528,18 @@
         "own",
         [cot_own, pack],
         [((feats, cols), F32)],
-        [((outer * tokens, feats), BF16), ((outer * tokens, cols), BF16), ((feats, cols), F32)],
-        room=63,
-    )
+        [((outer * tokens, feats), BF16), ((outer * tokens, cols), BF16)],
+        waits=[twin_x],
+        fast=[0],
+    )
+    operands = [total, own_total, pack_x, cots_x, twin_x, *sums, *pieces]
     dec_out, grad_attn, grad_weight = call(
         functools.partial(last_kernel, outer, share),
         "last",
-        [total, own_total, pack_x, *cots_x, *sums, *pieces],
+        operands,
         [((rows, steps, share * plane), BF16), ((tokens, cols), BF16), ((feats, cols), F32)],
-        [
-            ((tokens, cols), F32),
-            ((len(far), tokens, cols), BF16),
-            ((tokens, cols), BF16),
-            ((share, steps, plane), BF16),
-            ((outer * tokens, feats), BF16),
-            ((outer * tokens, cols), BF16),
-            ((feats, cols), F32),
-            ((feats, cols), F32),
-        ],
-        room=63,
+        [((tokens, cols), BF16), ((outer * tokens, feats), BF16), ((feats, cols), F32)],
+        near=range(len(operands)),
     )
     return dec_out, grad_attn, grad_weight
 

time: 87.8 us -> 83.4 us (0.950)
  the two profiles are of different devices: /device:TPU:17 before, /device:TPU:0 now
where the time goes in v4:
time: 83.4 us; the launch traced here: 82.9 us
  starting transfers between devices  25.2 us (30%)
  Pallas kernels  23.3 us (28%)
  waiting for transfers between devices  21.3 us (26%)
  blocking collectives  7.19 us (9%)
  local copies, waits for them, and re-layouts  4.41 us (5%)
  between operations  1.53 us (2%)
    pallas_call x7, Pallas kernels, call(): pl.pallas_call(body, out_shape=[jax.ShapeDtypeStruct(shape, dtype) for sh...  20.6 us
    ppermute x9, starting transfers between devices, turn(): lax.ppermute(a, 'fsdp', [(z * INNER + x, (z + steps) % outer * INNER + x)...  16.5 us
    ppermute x9, waiting for transfers between devices, turn(): lax.ppermute(a, 'fsdp', [(z * INNER + x, (z + steps) % outer * INNER + x)...  10.9 us
    ppermute x11, waiting for transfers between devices, flip(): return lax.ppermute(a, axis, [(i, i ^ bits) for i in range(size)])  10.4 us
    ppermute x11, starting transfers between devices, flip(): return lax.ppermute(a, axis, [(i, i ^ bits) for i in range(size)])  8.03 us
    all_to_all x1, blocking collectives, shards(): dec = lax.all_to_all(dec, 'tp', 0, 0, tiled=True).sum(axis=0).astype(BF16)  7.19 us
    unnamed x26, local copies, waits for them, and re-layouts  4.41 us
    pallas_call x1, Pallas kernels, shards(): pl.pallas_call(functools.partial(gate_kernel, len(sent), early), out_shap...  1.84 us
  transfers between devices with their start and end apart: 21, of which 7 were waited for; matrix products, arithmetic and copies ran while one was open for 0% of the time, Pallas kernels for 21%

profile of v4, /device:TPU:0, one launch (start us, length us, event | category | flops | bytes accessed | tf_op | source)
XLA Modules:
  0.0 82.9 jit_solution(2428258279491393386)
XLA Ops:
  0.6 0.0 copy-start.1
  0.6 3.0 %collective-permute-start = (bf16[512,1024]{1,0:T(8,128)(2,1)}, bf16[512,1024]{1,0:T(8,128)(2,1)}, u32[]{:S(2)}, u32[]{:S(2)}) collective-permute-start(bf16[512,1024]{1,0:T(8,128)(2,1)} %refs_0_.6), channel_id=1, source_target_pairs={{0,4},{4,0},{8,12},{12,8},{16,20},{20,16},{24,28},{28,24},{1,5},{5... | collective-permute-start | bytes 3145736 | tf_op jit(solution)/shard_map/weight_x/ppermute | solution.py:22
  3.6 1.9 %cut.1 = (bf16[96,1024]{1,0:T(8,128)(2,1)}, bf16[96,1024]{1,0:T(8,128)(2,1)}, bf16[96,1024]{1,0:T(8,128)(2,1)}) custom-call(bf16[128,4096]{1,0:T(8,128)(2,1)} %refs_0_.5, bf16[128,1024]{1,0:T(8,128)(2,1)} %refs_2_.3), custom_call_target="tpu_custom_call" | custom-call | tf_op jit(solution)/shard_map/cut/pallas_call | solution.py:82
  5.6 1.6 %collective-permute-start.1 = (bf16[96,1024]{1,0:T(8,128)(2,1)}, bf16[96,1024]{1,0:T(8,128)(2,1)S(1)}, u32[]{:S(2)}, u32[]{:S(2)}) collective-permute-start(bf16[96,1024]{1,0:T(8,128)(2,1)} %get-tuple-element.25), channel_id=1, source_target_pairs={{0,8},{4,12},{8,16},{12,20},{16,24},{20,28},{24,0},{28,4},{1,9},{5... | collective-permute-start | bytes 589832 | tf_op jit(solution)/shard_map/first_z1/ppermute | solution.py:28
  7.2 2.6 %collective-permute-start.2 = (bf16[96,1024]{1,0:T(8,128)(2,1)}, bf16[96,1024]{1,0:T(8,128)(2,1)S(1)}, u32[]{:S(2)}, u32[]{:S(2)}) collective-permute-start(bf16[96,1024]{1,0:T(8,128)(2,1)} %get-tuple-element.26), channel_id=1, source_target_pairs={{0,16},{4,20},{8,24},{12,28},{16,0},{20,4},{24,8},{28,12},{1,17},{... | collective-permute-start | bytes 589832 | tf_op jit(solution)/shard_map/first_z2/ppermute | solution.py:28
  9.8 1.3 %collective-permute-start.3 = (bf16[96,1024]{1,0:T(8,128)(2,1)}, bf16[96,1024]{1,0:T(8,128)(2,1)}, u32[]{:S(2)}, u32[]{:S(2)}) collective-permute-start(bf16[96,1024]{1,0:T(8,128)(2,1)} %get-tuple-element.27), channel_id=1, source_target_pairs={{0,24},{4,28},{8,0},{12,4},{16,8},{20,12},{24,16},{28,20},{1,25},{... | collective-permute-start | bytes 589832 | tf_op jit(solution)/shard_map/first_z3/ppermute | solution.py:28
  11.8 3.5 %attend.1 = (f32[40,256]{1,0:T(8,128)}, f32[1,16,256]{2,1,0:T(8,128)}, f32[2,16,256]{2,1,0:T(8,128)}) custom-call(s32[1]{0:T(128)S(6)} %copy.26.refs_0_, bf16[1,2,4096]{2,1,0:T(2,128)(2,1)} %refs_1_.4, bf16[1,512,512]{2,1,0:T(8,128)(2,1)} %refs_2_.2, bf16[1,512,512]{2,1,0:T(8,128)(2,1)} %refs_3_.1, bf16[1,2,512]{2,1,0:T(2,128)(2,1)} %refs_4_.1, ...), custom_call_target="tpu_custom_call" | custom-call | tf_op jit(solution)/shard_map/attend/pallas_call | solution.py:82
  15.3 0.1 collective-permute-start.5
  15.4 1.4 %collective-permute-done.5.refs_1_ = f32[1,16,256]{2,1,0:T(8,128)S(1)} collective-permute-done((f32[1,16,256]{2,1,0:T(8,128)}, f32[1,16,256]{2,1,0:T(8,128)S(1)}, u32[]{:S(2)}, u32[]{:S(2)}) %collective-permute-start.5) | collective-permute-done | bytes 16416 | tf_op jit(solution)/shard_map/softmax_tp1/ppermute | solution.py:22
  16.7 1.5 %collective-permute-start.4 = (f32[2,16,256]{2,1,0:T(8,128)}, f32[2,16,256]{2,1,0:T(8,128)S(1)}, u32[]{:S(2)}, u32[]{:S(2)}) collective-permute-start(f32[2,16,256]{2,1,0:T(8,128)} %get-tuple-element.29), channel_id=1, source_target_pairs={{0,2},{1,3},{2,0},{3,1},{4,6},{5,7},{6,4},{7,5},{8,10},{9,11},{10,... | collective-permute-start | bytes 98312 | tf_op jit(solution)/shard_map/softmax_tp2/ppermute | solution.py:22
  18.3 2.6 %collective-permute-done.4.refs_0_ = f32[2,16,256]{2,1,0:T(8,128)S(1)} collective-permute-done((f32[2,16,256]{2,1,0:T(8,128)}, f32[2,16,256]{2,1,0:T(8,128)S(1)}, u32[]{:S(2)}, u32[]{:S(2)}) %collective-permute-start.4) | collective-permute-done | bytes 32800 | tf_op jit(solution)/shard_map/softmax_tp2/ppermute | solution.py:22
  20.9 0.8 copy-done.8
  21.7 0.4 collective-permute-done.6.refs_2_
  22.1 0.8 combine.1.refs_3_.refs_2_
  22.9 0.0 collective-permute-done.1.refs_0_
  22.9 0.0 collective-permute-done.2.refs_1_
  23.0 0.2 collective-permute-start.7
  23.2 0.4 collective-permute-start.8
  23.6 0.2 collective-permute-start.9
  23.7 5.3 %collective-permute-start.14 = (bf16[112,1024]{1,0:T(8,128)(2,1)S(1)}, bf16[112,1024]{1,0:T(8,128)(2,1)}, u32[]{:S(2)}, u32[]{:S(2)}) collective-permute-start(bf16[112,1024]{1,0:T(8,128)(2,1)S(1)} %combine.1.refs_3_.refs_2_), channel_id=1, source_target_pairs={{0,24},{4,28},{8,0},{12,4},{16,8},{20,12},{24,16},{28,20},{1,25},{... | collective-permute-start | bytes 688136 | tf_op jit(solution)/shard_map/last_z3/ppermute | solution.py:28
  29.0 0.4 collective-permute-start.13
  29.5 0.0 collective-permute-done.8.refs_7_
  29.5 0.7 copy-done.10
  30.1 1.0 %collective-permute-start.12 = (bf16[112,1024]{1,0:T(8,128)(2,1)S(1)}, bf16[112,1024]{1,0:T(8,128)(2,1)}, u32[]{:S(2)}, u32[]{:S(2)}) collective-permute-start(bf16[112,1024]{1,0:T(8,128)(2,1)S(1)} %combine.1.refs_3_.refs_2_), channel_id=1, source_target_pairs={{0,8},{4,12},{8,16},{12,20},{16,24},{20,28},{24,0},{28,4},{1,9},{5... | collective-permute-start | bytes 688136 | tf_op jit(solution)/shard_map/last_z1/ppermute | solution.py:28
  31.1 0.0 collective-permute-done.9.refs_8_
  31.1 0.0 collective-permute-done.refs_2_.refs_1_
  31.2 5.3 %middle.1 = (bf16[128,1024]{1,0:T(8,128)(2,1)}, bf16[128,1024]{1,0:T(8,128)(2,1)}, bf16[128,1024]{1,0:T(8,128)(2,1)}, f32[128,1024]{1,0:T(8,128)}, bf16[512,512]...) custom-call(bf16[128,4096]{1,0:T(8,128)(2,1)} %refs_0_.5, bf16[512,1024]{1,0:T(8,128)(2,1)} %refs_0_.6, ...), custom_call_target="tpu_custom_call" | custom-call | tf_op jit(solution)/shard_map/middle/pallas_call | solution.py:82
  36.4 0.6 collective-permute-start.10
  37.0 1.5 %collective-permute-start.11 = (bf16[128,512]{1,0:T(8,128)(2,1)}, bf16[128,512]{1,0:T(8,128)(2,1)S(1)}, u32[]{:S(2)}, u32[]{:S(2)}) collective-permute-start(bf16[128,512]{1,0:T(8,128)(2,1)} %get-tuple-element.40), channel_id=1, source_target_pairs={{0,4},{4,0},{8,12},{12,8},{16,20},{20,16},{24,28},{28,24},{1,5},{5... | collective-permute-start | bytes 393224 | tf_op jit(solution)/shard_map/cot_x/ppermute | solution.py:22
  38.5 4.6 %collective-permute-done.10.refs_0_ = bf16[128,512]{1,0:T(8,128)(2,1)S(1)} collective-permute-done((bf16[128,512]{1,0:T(8,128)(2,1)}, bf16[128,512]{1,0:T(8,128)(2,1)S(1)}, u32[]{:S(2)}, u32[]{:S(2)}) %collective-permute-start.10) | collective-permute-done | bytes 131104 | tf_op jit(solution)/shard_map/cot_x/ppermute | solution.py:22
  43.1 1.4 %collective-permute-done.11.refs_1_ = bf16[128,512]{1,0:T(8,128)(2,1)S(1)} collective-permute-done((bf16[128,512]{1,0:T(8,128)(2,1)}, bf16[128,512]{1,0:T(8,128)(2,1)S(1)}, u32[]{:S(2)}, u32[]{:S(2)}) %collective-permute-start.11) | collective-permute-done | bytes 131104 | tf_op jit(solution)/shard_map/cot_x/ppermute | solution.py:22
  44.5 0.7 copy-done.12
  45.2 2.1 %pack.1 = (bf16[256,512]{1,0:T(8,128)(2,1)}, bf16[512,1024]{1,0:T(8,128)(2,1)}) custom-call(bf16[128,512]{1,0:T(8,128)(2,1)} %copy-done.11, bf16[128,512]{1,0:T(8,128)(2,1)} %copy-done.12, bf16[128,1024]{1,0:T(8,128)(2,1)} %refs_2_.3, bf16[96,1024]{1,0:T(8,128)(2,1)} %copy-done.3, bf16[96,1024]{1,0:T(8,128)(2,1)} %copy-done.4, ...), custom_call_target="tpu_custom_call" | custom-call | tf_op jit(solution)/shard_map/pack/pallas_call | solution.py:82
  47.3 2.9 %collective-permute-done.13.refs_6_.refs_4_ = bf16[112,1024]{1,0:T(8,128)(2,1)} collective-permute-done((bf16[112,1024]{1,0:T(8,128)(2,1)S(1)}, bf16[112,1024]{1,0:T(8,128)(2,1)}, u32[]{:S(2)}, u32[]{:S(2)}) %collective-permute-start.13) | collective-permute-done | bytes 229408 | tf_op jit(solution)/shard_map/last_z2/ppermute | solution.py:28
  50.2 1.8 %gate.1 = (bf16[128,1024]{1,0:T(8,128)(2,1)}, bf16[128,1024]{1,0:T(8,128)(2,1)}, bf16[128,1024]{1,0:T(8,128)(2,1)}, bf16[512,1024]{1,0:T(8,128)(2,1)}) custom-call(bf16[128,1024]{1,0:T(8,128)(2,1)} %get-tuple-element.36.refs_0_, ...), custom_call_target="tpu_custom_call", output_to_operand_aliasing={{0}: (0, {}), {1}: (1, {}), {2}: (2, {}), {3}: (3, {})} | custom-call | tf_op jit(solution)/shard_map/gate/pallas_call | solution.py:478
  52.1 0.6 collective-permute-start.16
  52.7 0.0 collective-permute-start.17
  52.7 2.3 %collective-permute-start.18 = (bf16[128,1024]{1,0:T(8,128)(2,1)}, bf16[128,1024]{1,0:T(8,128)(2,1)}, u32[]{:S(2)}, u32[]{:S(2)}) collective-permute-start(bf16[128,1024]{1,0:T(8,128)(2,1)} %get-tuple-element.45), channel_id=1, source_target_pairs={{0,16},{4,20},{8,24},{12,28},{16,0},{20,4},{24,8},{28,12},{1,17},{... | collective-permute-start | bytes 786440 | tf_op jit(solution)/shard_map/sum_z2/ppermute | solution.py:28
  54.9 2.0 %collective-permute-start.19 = (bf16[128,1024]{1,0:T(8,128)(2,1)}, bf16[128,1024]{1,0:T(8,128)(2,1)}, u32[]{:S(2)}, u32[]{:S(2)}) collective-permute-start(bf16[128,1024]{1,0:T(8,128)(2,1)} %get-tuple-element.46), channel_id=1, source_target_pairs={{0,8},{4,12},{8,16},{12,20},{16,24},{20,28},{24,0},{28,4},{1,9},{5... | collective-permute-start | bytes 786440 | tf_op jit(solution)/shard_map/sum_z3/ppermute | solution.py:28
  56.9 3.1 %decode.1 = f32[4,1,2,1024]{3,2,1,0:T(2,128)} custom-call(bf16[512,1024]{1,0:T(8,128)(2,1)} %refs_0_.6, bf16[512,1024]{1,0:T(8,128)(2,1)} %collective-permute-done.refs_2_.refs_1_, bf16[112,1024]{1,0:T(8,128)(2,1)} %copy-done.2, bf16[112,1024]{1,0:T(8,128)(2,1)} %collective-permute-done.12.refs_5_.refs_3_, ...), custom_call_target="tpu_custom_call" | custom-call | tf_op jit(solution)/shard_map/decode/pallas_call | solution.py:82
  60.1 7.2 %all_to_all.5 = f32[4,1,2,1024]{3,2,1,0:T(2,128)S(1)} all-to-all(f32[4,1,2,1024]{3,2,1,0:T(2,128)} %decode.1), channel_id=1, replica_groups=mesh['fsdp'=8,'tp'=4] {'tp'}, dimensions={0} | all-to-all | bytes 65536 | tf_op jit(solution)/shard_map/dec_tp/all_to_all | solution.py:515
  67.3 0.7 collective-permute-start.20
  67.9 0.0 copy-start
  68.0 1.2 %copy-done = bf16[512,1024]{1,0:T(8,128)(2,1)S(1)} copy-done((bf16[512,1024]{1,0:T(8,128)(2,1)S(1)}, bf16[512,1024]{1,0:T(8,128)(2,1)}, u32[]{:S(2)}) %copy-start) | copy-done | bytes 1048600
  69.2 1.0 %copy-done.6 = bf16[512,512]{1,0:T(8,128)(2,1)S(1)} copy-done((bf16[512,512]{1,0:T(8,128)(2,1)S(1)}, bf16[512,512]{1,0:T(8,128)(2,1)}, u32[]{:S(2)}) %copy-start.6) | copy-done | bytes 524312
  70.2 1.0 %own.1.refs_1_ = f32[512,1024]{1,0:T(8,128)S(1)} custom-call(bf16[512,512]{1,0:T(8,128)(2,1)S(1)} %copy-done.6, bf16[512,1024]{1,0:T(8,128)(2,1)S(1)} %copy-done, bf16[256,512]{1,0:T(8,128)(2,1)S(1)} %collective-permute-done.15.refs_2_.refs_4_), custom_call_target="tpu_custom_call" | custom-call | tf_op jit(solution)/shard_map/own/pallas_call | solution.py:82
  71.2 8.0 %collective-permute-done.18.refs_6_ = bf16[128,1024]{1,0:T(8,128)(2,1)} collective-permute-done((bf16[128,1024]{1,0:T(8,128)(2,1)}, bf16[128,1024]{1,0:T(8,128)(2,1)}, u32[]{:S(2)}, u32[]{:S(2)}) %collective-permute-start.18) | collective-permute-done | bytes 262176 | tf_op jit(solution)/shard_map/sum_z2/ppermute | solution.py:28
  79.2 3.7 %last.1 = (bf16[1,2,1024]{2,1,0:T(2,128)(2,1)}, bf16[128,1024]{1,0:T(8,128)(2,1)}, f32[512,1024]{1,0:T(8,128)}) custom-call(f32[128,1024]{1,0:T(8,128)S(1)} %copy-done.7, f32[512,1024]{1,0:T(8,128)S(1)} %own.1.refs_1_, bf16[512,1024]{1,0:T(8,128)(2,1)} %collective-permute-done.16.refs_2_, bf16[256,512]{1,0:T(8,128)(2,1)S(1)} %copy-done.5, ...), custom_call_target="tpu_custom_call" | custom-call | tf_op jit(solution)/shard_map/last/pallas_call | solution.py:82
  (33 shorter events, 0.1 us)
Async XLA Ops:
  0.6 21.5 %copy-start.1 = (bf16[128,1024]{1,0:T(8,128)(2,1)S(1)}, bf16[128,1024]{1,0:T(8,128)(2,1)}, u32[]{:S(2)}) copy-start(bf16[128,1024]{1,0:T(8,128)(2,1)} %refs_2_.3) | copy-start | bytes 786436
  0.6 30.5 %collective-permute-start = (bf16[512,1024]{1,0:T(8,128)(2,1)}, bf16[512,1024]{1,0:T(8,128)(2,1)}, u32[]{:S(2)}, u32[]{:S(2)}) collective-permute-start(bf16[512,1024]{1,0:T(8,128)(2,1)} %refs_0_.6), channel_id=1, source_target_pairs={{0,4},{4,0},{8,12},{12,8},{16,20},{20,16},{24,28},{28,24},{1,5},{5... | collective-permute-start | bytes 3145736 | tf_op jit(solution)/shard_map/weight_x/ppermute | solution.py:22
  5.6 17.3 %collective-permute-start.1 = (bf16[96,1024]{1,0:T(8,128)(2,1)}, bf16[96,1024]{1,0:T(8,128)(2,1)S(1)}, u32[]{:S(2)}, u32[]{:S(2)}) collective-permute-start(bf16[96,1024]{1,0:T(8,128)(2,1)} %get-tuple-element.25), channel_id=1, source_target_pairs={{0,8},{4,12},{8,16},{12,20},{16,24},{20,28},{24,0},{28,4},{1,9},{5... | collective-permute-start | bytes 589832 | tf_op jit(solution)/shard_map/first_z1/ppermute | solution.py:28
  7.2 15.7 %collective-permute-start.2 = (bf16[96,1024]{1,0:T(8,128)(2,1)}, bf16[96,1024]{1,0:T(8,128)(2,1)S(1)}, u32[]{:S(2)}, u32[]{:S(2)}) collective-permute-start(bf16[96,1024]{1,0:T(8,128)(2,1)} %get-tuple-element.26), channel_id=1, source_target_pairs={{0,16},{4,20},{8,24},{12,28},{16,0},{20,4},{24,8},{28,12},{1,17},{... | collective-permute-start | bytes 589832 | tf_op jit(solution)/shard_map/first_z2/ppermute | solution.py:28
  9.8 13.1 %collective-permute-start.3 = (bf16[96,1024]{1,0:T(8,128)(2,1)}, bf16[96,1024]{1,0:T(8,128)(2,1)}, u32[]{:S(2)}, u32[]{:S(2)}) collective-permute-start(bf16[96,1024]{1,0:T(8,128)(2,1)} %get-tuple-element.27), channel_id=1, source_target_pairs={{0,24},{4,28},{8,0},{12,4},{16,8},{20,12},{24,16},{28,20},{1,25},{... | collective-permute-start | bytes 589832 | tf_op jit(solution)/shard_map/first_z3/ppermute | solution.py:28
  15.3 1.5 %collective-permute-start.5 = (f32[1,16,256]{2,1,0:T(8,128)}, f32[1,16,256]{2,1,0:T(8,128)S(1)}, u32[]{:S(2)}, u32[]{:S(2)}) collective-permute-start(f32[1,16,256]{2,1,0:T(8,128)} %get-tuple-element.30), channel_id=1, source_target_pairs={{0,1},{1,0},{2,3},{3,2},{4,5},{5,4},{6,7},{7,6},{8,9},{9,8},{10,11... | collective-permute-start | bytes 49160 | tf_op jit(solution)/shard_map/softmax_tp1/ppermute | solution.py:22
  16.7 4.1 %collective-permute-start.4 = (f32[2,16,256]{2,1,0:T(8,128)}, f32[2,16,256]{2,1,0:T(8,128)S(1)}, u32[]{:S(2)}, u32[]{:S(2)}) collective-permute-start(f32[2,16,256]{2,1,0:T(8,128)} %get-tuple-element.29), channel_id=1, source_target_pairs={{0,2},{1,3},{2,0},{3,1},{4,6},{5,7},{6,4},{7,5},{8,10},{9,11},{10,... | collective-permute-start | bytes 98312 | tf_op jit(solution)/shard_map/softmax_tp2/ppermute | solution.py:22
  20.9 1.2 %collective-permute-start.6 = (f32[2,16,256]{2,1,0:T(8,128)S(1)}, f32[2,16,256]{2,1,0:T(8,128)S(1)}, u32[]{:S(2)}, u32[]{:S(2)}) collective-permute-start(f32[2,16,256]{2,1,0:T(8,128)S(1)} %collective-permute-done.4.refs_0_), channel_id=1, source_target_pairs={{0,1},{1,0},{2,3},{3,2},{4,5},{5,4},{6,7},{7,6},{8,9},{9,8},{10,11... | collective-permute-start | bytes 98312 | tf_op jit(solution)/shard_map/softmax_tp1/ppermute | solution.py:22
  20.9 0.8 copy-start.8
  22.9 13.5 %copy-start.2 = (bf16[112,1024]{1,0:T(8,128)(2,1)}, bf16[112,1024]{1,0:T(8,128)(2,1)S(1)}, u32[]{:S(2)}) copy-start(bf16[112,1024]{1,0:T(8,128)(2,1)S(1)} %combine.1.refs_3_.refs_2_) | copy-start | bytes 688132
  23.0 8.2 %copy-start.3 = (bf16[96,1024]{1,0:T(8,128)(2,1)}, bf16[96,1024]{1,0:T(8,128)(2,1)S(1)}, u32[]{:S(2)}) copy-start(bf16[96,1024]{1,0:T(8,128)(2,1)S(1)} %get-tuple-element.31.refs_3_) | copy-start | bytes 589828
  23.0 8.2 %copy-start.4 = (bf16[96,1024]{1,0:T(8,128)(2,1)}, bf16[96,1024]{1,0:T(8,128)(2,1)S(1)}, u32[]{:S(2)}) copy-start(bf16[96,1024]{1,0:T(8,128)(2,1)S(1)} %get-tuple-element.32.refs_4_) | copy-start | bytes 589828
  23.0 6.0 %collective-permute-start.7 = (bf16[96,1024]{1,0:T(8,128)(2,1)S(1)}, bf16[96,1024]{1,0:T(8,128)(2,1)S(1)}, u32[]{:S(2)}, u32[]{:S(2)}) collective-permute-start(bf16[96,1024]{1,0:T(8,128)(2,1)S(1)} %get-tuple-element.31.refs_3_), channel_id=1, source_target_pairs={{0,1},{1,0},{2,3},{3,2},{4,5},{5,4},{6,7},{7,6},{8,9},{9,8},{10,11... | collective-permute-start | bytes 589832 | tf_op jit(solution)/shard_map/cot_core/ppermute | solution.py:22
  23.2 6.2 %collective-permute-start.8 = (bf16[96,1024]{1,0:T(8,128)(2,1)S(1)}, bf16[96,1024]{1,0:T(8,128)(2,1)S(1)}, u32[]{:S(2)}, u32[]{:S(2)}) collective-permute-start(bf16[96,1024]{1,0:T(8,128)(2,1)S(1)} %get-tuple-element.32.refs_4_), channel_id=1, source_target_pairs={{0,1},{1,0},{2,3},{3,2},{4,5},{5,4},{6,7},{7,6},{8,9},{9,8},{10,11... | collective-permute-start | bytes 589832 | tf_op jit(solution)/shard_map/cot_core/ppermute | solution.py:22
  23.6 7.6 %collective-permute-start.9 = (bf16[96,1024]{1,0:T(8,128)(2,1)}, bf16[96,1024]{1,0:T(8,128)(2,1)}, u32[]{:S(2)}, u32[]{:S(2)}) collective-permute-start(bf16[96,1024]{1,0:T(8,128)(2,1)} %get-tuple-element.33.refs_5_), channel_id=1, source_target_pairs={{0,1},{1,0},{2,3},{3,2},{4,5},{5,4},{6,7},{7,6},{8,9},{9,8},{10,11... | collective-permute-start | bytes 589832 | tf_op jit(solution)/shard_map/cot_core/ppermute | solution.py:22
  23.7 23.6 %collective-permute-start.14 = (bf16[112,1024]{1,0:T(8,128)(2,1)S(1)}, bf16[112,1024]{1,0:T(8,128)(2,1)}, u32[]{:S(2)}, u32[]{:S(2)}) collective-permute-start(bf16[112,1024]{1,0:T(8,128)(2,1)S(1)} %combine.1.refs_3_.refs_2_), channel_id=1, source_target_pairs={{0,24},{4,28},{8,0},{12,4},{16,8},{20,12},{24,16},{28,20},{1,25},{... | collective-permute-start | bytes 688136 | tf_op jit(solution)/shard_map/last_z3/ppermute | solution.py:28
  29.0 2.1 %copy-start.9 = (bf16[96,1024]{1,0:T(8,128)(2,1)}, bf16[96,1024]{1,0:T(8,128)(2,1)S(1)}, u32[]{:S(2)}) copy-start(bf16[96,1024]{1,0:T(8,128)(2,1)S(1)} %collective-permute-done.7.refs_6_) | copy-start | bytes 589828
  29.0 21.2 %collective-permute-start.13 = (bf16[112,1024]{1,0:T(8,128)(2,1)S(1)}, bf16[112,1024]{1,0:T(8,128)(2,1)}, u32[]{:S(2)}, u32[]{:S(2)}) collective-permute-start(bf16[112,1024]{1,0:T(8,128)(2,1)S(1)} %combine.1.refs_3_.refs_2_), channel_id=1, source_target_pairs={{0,16},{4,20},{8,24},{12,28},{16,0},{20,4},{24,8},{28,12},{1,17},{... | collective-permute-start | bytes 688136 | tf_op jit(solution)/shard_map/last_z2/ppermute | solution.py:28
  29.5 0.7 copy-start.10
  30.1 20.1 %collective-permute-start.12 = (bf16[112,1024]{1,0:T(8,128)(2,1)S(1)}, bf16[112,1024]{1,0:T(8,128)(2,1)}, u32[]{:S(2)}, u32[]{:S(2)}) collective-permute-start(bf16[112,1024]{1,0:T(8,128)(2,1)S(1)} %combine.1.refs_3_.refs_2_), channel_id=1, source_target_pairs={{0,8},{4,12},{8,16},{12,20},{16,24},{20,28},{24,0},{28,4},{1,9},{5... | collective-permute-start | bytes 688136 | tf_op jit(solution)/shard_map/last_z1/ppermute | solution.py:28
  36.4 6.6 %collective-permute-start.10 = (bf16[128,512]{1,0:T(8,128)(2,1)}, bf16[128,512]{1,0:T(8,128)(2,1)S(1)}, u32[]{:S(2)}, u32[]{:S(2)}) collective-permute-start(bf16[128,512]{1,0:T(8,128)(2,1)} %get-tuple-element.39), channel_id=1, source_target_pairs={{0,4},{4,0},{8,12},{12,8},{16,20},{20,16},{24,28},{28,24},{1,5},{5... | collective-permute-start | bytes 393224 | tf_op jit(solution)/shard_map/cot_x/ppermute | solution.py:22
  37.0 7.5 %collective-permute-start.11 = (bf16[128,512]{1,0:T(8,128)(2,1)}, bf16[128,512]{1,0:T(8,128)(2,1)S(1)}, u32[]{:S(2)}, u32[]{:S(2)}) collective-permute-start(bf16[128,512]{1,0:T(8,128)(2,1)} %get-tuple-element.40), channel_id=1, source_target_pairs={{0,4},{4,0},{8,12},{12,8},{16,20},{20,16},{24,28},{28,24},{1,5},{5... | collective-permute-start | bytes 393224 | tf_op jit(solution)/shard_map/cot_x/ppermute | solution.py:22
  43.1 1.4 %copy-start.11 = (bf16[128,512]{1,0:T(8,128)(2,1)}, bf16[128,512]{1,0:T(8,128)(2,1)S(1)}, u32[]{:S(2)}) copy-start(bf16[128,512]{1,0:T(8,128)(2,1)S(1)} %collective-permute-done.10.refs_0_) | copy-start | bytes 393220
  44.5 0.7 copy-start.12
  47.3 5.4 %copy-start.5 = (bf16[256,512]{1,0:T(8,128)(2,1)S(1)}, bf16[256,512]{1,0:T(8,128)(2,1)}, u32[]{:S(2)}) copy-start(bf16[256,512]{1,0:T(8,128)(2,1)} %get-tuple-element.42.refs_4_.refs_3_) | copy-start | bytes 786436
  52.1 27.1 %collective-permute-start.16 = (bf16[512,1024]{1,0:T(8,128)(2,1)}, bf16[512,1024]{1,0:T(8,128)(2,1)}, u32[]{:S(2)}, u32[]{:S(2)}) collective-permute-start(bf16[512,1024]{1,0:T(8,128)(2,1)} %get-tuple-element.43.refs_1_.refs_6_), channel_id=1, source_target_pairs={{0,4},{4,0},{8,12},{12,8},{16,20},{20,16},{24,28},{28,24},{1,5},{5... | collective-permute-start | bytes 3145736 | tf_op jit(solution)/shard_map/attn_x/ppermute | solution.py:22
  52.7 14.6 %collective-permute-start.15 = (bf16[256,512]{1,0:T(8,128)(2,1)S(1)}, bf16[256,512]{1,0:T(8,128)(2,1)S(1)}, u32[]{:S(2)}, u32[]{:S(2)}) collective-permute-start(bf16[256,512]{1,0:T(8,128)(2,1)S(1)} %copy-done.5), channel_id=1, source_target_pairs={{0,1},{1,0},{2,3},{3,2},{4,5},{5,4},{6,7},{7,6},{8,9},{9,8},{10,11... | collective-permute-start | bytes 786440 | tf_op jit(solution)/shard_map/cot_x_core/ppermute | solution.py:22
  52.7 18.5 %collective-permute-start.17 = (bf16[128,1024]{1,0:T(8,128)(2,1)}, bf16[128,1024]{1,0:T(8,128)(2,1)S(1)}, u32[]{:S(2)}, u32[]{:S(2)}) collective-permute-start(bf16[128,1024]{1,0:T(8,128)(2,1)} %get-tuple-element.44), channel_id=1, source_target_pairs={{0,24},{4,28},{8,0},{12,4},{16,8},{20,12},{24,16},{28,20},{1,25},{... | collective-permute-start | bytes 786440 | tf_op jit(solution)/shard_map/sum_z1/ppermute | solution.py:28
  52.7 26.5 %collective-permute-start.18 = (bf16[128,1024]{1,0:T(8,128)(2,1)}, bf16[128,1024]{1,0:T(8,128)(2,1)}, u32[]{:S(2)}, u32[]{:S(2)}) collective-permute-start(bf16[128,1024]{1,0:T(8,128)(2,1)} %get-tuple-element.45), channel_id=1, source_target_pairs={{0,16},{4,20},{8,24},{12,28},{16,0},{20,4},{24,8},{28,12},{1,17},{... | collective-permute-start | bytes 786440 | tf_op jit(solution)/shard_map/sum_z2/ppermute | solution.py:28
  54.9 24.2 %collective-permute-start.19 = (bf16[128,1024]{1,0:T(8,128)(2,1)}, bf16[128,1024]{1,0:T(8,128)(2,1)}, u32[]{:S(2)}, u32[]{:S(2)}) collective-permute-start(bf16[128,1024]{1,0:T(8,128)(2,1)} %get-tuple-element.46), channel_id=1, source_target_pairs={{0,8},{4,12},{8,16},{12,20},{16,24},{20,28},{24,0},{28,4},{1,9},{5... | collective-permute-start | bytes 786440 | tf_op jit(solution)/shard_map/sum_z3/ppermute | solution.py:28
  67.3 3.9 %collective-permute-start.20 = (bf16[2,1024]{1,0:T(2,128)(2,1)S(1)}, bf16[2,1024]{1,0:T(2,128)(2,1)S(1)}, u32[]{:S(2)}, u32[]{:S(2)}) collective-permute-start(bf16[2,1024]{1,0:T(2,128)(2,1)S(1)} %reduce_sum.9), channel_id=1, source_target_pairs={{0,0},{1,8},{2,16},{3,24},{4,4},{5,12},{6,20},{7,28},{8,1},{9,9},{... | collective-permute-start | bytes 12296 | tf_op jit(solution)/shard_map/dec_place/ppermute | solution.py:525
  67.9 1.2 %copy-start = (bf16[512,1024]{1,0:T(8,128)(2,1)S(1)}, bf16[512,1024]{1,0:T(8,128)(2,1)}, u32[]{:S(2)}) copy-start(bf16[512,1024]{1,0:T(8,128)(2,1)} %get-tuple-element.43.refs_1_.refs_6_) | copy-start | bytes 3145732
  69.2 1.0 %copy-start.6 = (bf16[512,512]{1,0:T(8,128)(2,1)S(1)}, bf16[512,512]{1,0:T(8,128)(2,1)}, u32[]{:S(2)}) copy-start(bf16[512,512]{1,0:T(8,128)(2,1)} %get-tuple-element.35.refs_0_) | copy-start | bytes 1572868
  70.2 8.9 %copy-start.7 = (f32[128,1024]{1,0:T(8,128)S(1)}, f32[128,1024]{1,0:T(8,128)}, u32[]{:S(2)}) copy-start(f32[128,1024]{1,0:T(8,128)} %get-tuple-element.34.refs_0_) | copy-start | bytes 1572868

commit v5 on v4

--- a/solution.py
+++ b/solution.py
@@ -11,7 +11,7 @@
 HD = 128
 NEG_FILL = -1e30
 INNER = 2
-PAD = 16
+PAD = 8
 BF16 = jnp.bfloat16
 F32 = jnp.float32
 
@@ -273,10 +273,10 @@
     _, _, z, x, _ = places()
     tokens = load_hbms[0].shape[0] - PAD
     outer, share = len(load_hbms), outs[0].shape[1]
-    arrive = [mover.start(hbm.at[tokens:], dec_ref.at[k]) for k, hbm in enumerate(load_hbms)]
+    arrive = [mover.start(hbm, dec_ref.at[k]) for k, hbm in enumerate(load_hbms)]
     mover.wait(*arrive, mover.start(weight_hbm, weight_ref), mover.start(other_hbm, other_ref))
     for k in range(outer):
-        rows_ref[k * steps : (k + 1) * steps, :] = dec_ref[k].astype(F32)[:steps]
+        rows_ref[k * steps : (k + 1) * steps, :] = dec_ref[k, tokens:, :].astype(F32)[:steps]
     every = rows_ref[...].astype(BF16)
     own, other = over_features(every, weight_ref[...]), over_features(every, other_ref[...])
     wide = jnp.concatenate([jnp.where(x == 0, own, other), jnp.where(x == 0, other, own)], axis=1)
@@ -294,15 +294,11 @@
     outs[0][...] = over_tokens(cots_ref[...], attn_ref[...])
 
 
-def last_kernel(outer, share, mover, ins, outs, scratch):
-    total_ref, own_ref, attn_ref, *rest = ins
-    cot_refs, part_refs, piece_refs = rest[:2], rest[2 : outer + 1], rest[outer + 1 :]
-    sum_ref, cots_ref, out_ref = scratch
-    _, core, z, _, _ = places()
-    plane = piece_refs[0].shape[1]
+def product_kernel(mover, ins, outs, scratch):
+    own_ref, attn_ref, *cot_refs = ins
+    cots_ref, out_ref = scratch
+    _, core, _, _, _ = places()
     size = cot_refs[0].shape[0]
-    for j in range(share):
-        mover.start(piece_refs[j], outs[0].at[0, :, pl.ds(pl.multiple_of((z % share ^ j) * plane, plane), plane)])
     for i, ref in enumerate(cot_refs):
         first = pl.multiple_of((core ^ i) * size, size)
         cots_ref[pl.ds(first, size), :] = ref[...]
@@ -311,10 +307,23 @@
     for i in range(pieces):
         here = slice(i * step, (i + 1) * step)
         out_ref[here, :] = own_ref[here, :] + over_tokens(cots_ref[:, here], attn_ref[...])
-        mover.start(out_ref.at[here], outs[2].at[here])
+        mover.start(out_ref.at[here], outs[0].at[here])
+    outs[1][...] = jnp.zeros(outs[1].shape, F32)
+
+
+def sum_kernel(outer, share, mover, ins, outs, scratch):
+    total_ref, *rest = ins
+    part_hbms, piece_refs = rest[: outer - 1], rest[outer - 1 :]
+    parts_ref, sum_ref = scratch
+    _, _, z, _, _ = places()
+    plane = piece_refs[0].shape[1]
+    arrive = [mover.start(hbm, parts_ref.at[i]) for i, hbm in enumerate(part_hbms)]
+    for j in range(share):
+        mover.start(piece_refs[j], outs[0].at[0, :, pl.ds(pl.multiple_of((z % share ^ j) * plane, plane), plane)])
+    mover.wait(*arrive)
     total = total_ref[...]
-    for part_ref in part_refs:
-        total = total + part_ref[...].astype(F32)
+    for i in range(outer - 1):
+        total = total + parts_ref[i].astype(F32)
     sum_ref[...] = total.astype(BF16)
     mover.start(sum_ref, outs[1])
 
@@ -372,7 +381,7 @@
 
     half = tokens // 2
 
-    early = tokens // 4
+    early = tokens // 8
     cot_rows = half * plane // cols
     if plane == cols:
         cuts = call(
@@ -503,7 +512,7 @@
         [
             ((feats, cols), BF16),
             ((feats, cols), BF16),
-            ((outer, PAD, cols), BF16),
+            ((outer, tokens - early + PAD, cols), BF16),
             ((outer * steps, cols), F32),
             ((outer, steps, plane), F32),
             ((tp_size, share, steps, plane), F32),
@@ -532,14 +541,24 @@
         waits=[twin_x],
         fast=[0],
     )
-    operands = [total, own_total, pack_x, cots_x, twin_x, *sums, *pieces]
-    dec_out, grad_attn, grad_weight = call(
-        functools.partial(last_kernel, outer, share),
-        "last",
+    grad_weight, mark = call(
+        product_kernel,
+        "product",
+        [own_total, pack_x, cots_x, twin_x],
+        [((feats, cols), F32), ((8, HD), F32)],
+        [((outer * tokens, feats), BF16), ((feats, cols), F32)],
+        near=range(4),
+        fast=[1],
+    )
+    operands = [total, *sums, *pieces]
+    dec_out, grad_attn = call(
+        functools.partial(sum_kernel, outer, share),
+        "sum",
         operands,
-        [((rows, steps, share * plane), BF16), ((tokens, cols), BF16), ((feats, cols), F32)],
-        [((tokens, cols), BF16), ((outer * tokens, feats), BF16), ((feats, cols), F32)],
-        near=range(len(operands)),
+        [((rows, steps, share * plane), BF16), ((tokens, cols), BF16)],
+        [((len(far), tokens, cols), BF16), ((tokens, cols), BF16)],
+        waits=[mark],
+        near=[0, *range(outer, len(operands))],
     )
     return dec_out, grad_attn, grad_weight
 

time: 83.4 us -> 81.8 us (0.981)
  starting transfers between devices: 25.2 us -> 22.2 us
  Pallas kernels: 23.3 us -> 25.3 us
    ppermute x9, waiting for transfers between devices: 10.9 us -> 5.11 us  [turn(): lax.ppermute(a, 'fsdp', [(z * INNER + x, (z + steps) % outer * INNER + x)...]
    ppermute x11, waiting for transfers between devices: 10.4 us -> 16 us  [flip(): return lax.ppermute(a, axis, [(i, i ^ bits) for i in range(size)])]
    ppermute x9, starting transfers between devices: 16.5 us -> 13.5 us  [turn(): lax.ppermute(a, 'fsdp', [(z * INNER + x, (z + steps) % outer * INNER + x)...]
    pallas_call x7 -> x8, Pallas kernels: 20.6 us -> 22.6 us  [call(): pl.pallas_call(body, out_shape=[jax.ShapeDtypeStruct(shape, dtype) for sh...]
  transfers between devices with their start and end apart: 21 -> 21, of which waited for: 7 -> 7; matrix products, arithmetic and copies ran while one was open for 0% -> 0% of each run, Pallas kernels for 21% -> 26%
where the time goes in v5:
time: 81.8 us; the launch traced here: 81.3 us
  Pallas kernels  25.3 us (31%)
  starting transfers between devices  22.2 us (27%)
  waiting for transfers between devices  21.2 us (26%)
  blocking collectives  7.19 us (9%)
  local copies, waits for them, and re-layouts  3.73 us (5%)
  between operations  1.57 us (2%)
    pallas_call x8, Pallas kernels, call(): pl.pallas_call(body, out_shape=[jax.ShapeDtypeStruct(shape, dtype) for sh...  22.6 us
    ppermute x11, waiting for transfers between devices, flip(): return lax.ppermute(a, axis, [(i, i ^ bits) for i in range(size)])  16 us
    ppermute x9, starting transfers between devices, turn(): lax.ppermute(a, 'fsdp', [(z * INNER + x, (z + steps) % outer * INNER + x)...  13.5 us
    ppermute x11, starting transfers between devices, flip(): return lax.ppermute(a, axis, [(i, i ^ bits) for i in range(size)])  8.03 us
    all_to_all x1, blocking collectives, shards(): dec = lax.all_to_all(dec, 'tp', 0, 0, tiled=True).sum(axis=0).astype(BF16)  7.19 us
    ppermute x9, waiting for transfers between devices, turn(): lax.ppermute(a, 'fsdp', [(z * INNER + x, (z + steps) % outer * INNER + x)...  5.11 us
    unnamed x26, local copies, waits for them, and re-layouts  3.73 us
    pallas_call x1, Pallas kernels, shards(): pl.pallas_call(functools.partial(gate_kernel, len(sent), early), out_shap...  1.9 us
  transfers between devices with their start and end apart: 21, of which 7 were waited for; matrix products, arithmetic and copies ran while one was open for 0% of the time, Pallas kernels for 26%

profile of v5, /device:TPU:0, one launch (start us, length us, event | category | flops | bytes accessed | tf_op | source)
XLA Modules:
  0.0 81.3 jit_solution(17416867996510032340)
XLA Ops:
  0.6 0.0 copy-start.1
  0.6 3.0 %collective-permute-start = (bf16[512,1024]{1,0:T(8,128)(2,1)}, bf16[512,1024]{1,0:T(8,128)(2,1)}, u32[]{:S(2)}, u32[]{:S(2)}) collective-permute-start(bf16[512,1024]{1,0:T(8,128)(2,1)} %refs_0_.6), channel_id=1, source_target_pairs={{0,4},{4,0},{8,12},{12,8},{16,20},{20,16},{24,28},{28,24},{1,5},{5... | collective-permute-start | bytes 3145736 | tf_op jit(solution)/shard_map/weight_x/ppermute | solution.py:22
  3.6 1.9 %cut.1 = (bf16[80,1024]{1,0:T(8,128)(2,1)}, bf16[80,1024]{1,0:T(8,128)(2,1)}, bf16[80,1024]{1,0:T(8,128)(2,1)}) custom-call(bf16[128,4096]{1,0:T(8,128)(2,1)} %refs_0_.5, bf16[128,1024]{1,0:T(8,128)(2,1)} %refs_2_.3), custom_call_target="tpu_custom_call" | custom-call | tf_op jit(solution)/shard_map/cut/pallas_call | solution.py:82
  5.6 1.6 %collective-permute-start.1 = (bf16[80,1024]{1,0:T(8,128)(2,1)}, bf16[80,1024]{1,0:T(8,128)(2,1)S(1)}, u32[]{:S(2)}, u32[]{:S(2)}) collective-permute-start(bf16[80,1024]{1,0:T(8,128)(2,1)} %get-tuple-element.29), channel_id=1, source_target_pairs={{0,8},{4,12},{8,16},{12,20},{16,24},{20,28},{24,0},{28,4},{1,9},{5... | collective-permute-start | bytes 491528 | tf_op jit(solution)/shard_map/first_z1/ppermute | solution.py:28
  7.2 2.6 %collective-permute-start.2 = (bf16[80,1024]{1,0:T(8,128)(2,1)}, bf16[80,1024]{1,0:T(8,128)(2,1)S(1)}, u32[]{:S(2)}, u32[]{:S(2)}) collective-permute-start(bf16[80,1024]{1,0:T(8,128)(2,1)} %get-tuple-element.30), channel_id=1, source_target_pairs={{0,16},{4,20},{8,24},{12,28},{16,0},{20,4},{24,8},{28,12},{1,17},{... | collective-permute-start | bytes 491528 | tf_op jit(solution)/shard_map/first_z2/ppermute | solution.py:28
  9.8 1.3 %collective-permute-start.3 = (bf16[80,1024]{1,0:T(8,128)(2,1)}, bf16[80,1024]{1,0:T(8,128)(2,1)}, u32[]{:S(2)}, u32[]{:S(2)}) collective-permute-start(bf16[80,1024]{1,0:T(8,128)(2,1)} %get-tuple-element.31), channel_id=1, source_target_pairs={{0,24},{4,28},{8,0},{12,4},{16,8},{20,12},{24,16},{28,20},{1,25},{... | collective-permute-start | bytes 491528 | tf_op jit(solution)/shard_map/first_z3/ppermute | solution.py:28
  11.8 3.5 %attend.1 = (f32[40,256]{1,0:T(8,128)}, f32[1,16,256]{2,1,0:T(8,128)}, f32[2,16,256]{2,1,0:T(8,128)}) custom-call(s32[1]{0:T(128)S(6)} %copy.26.refs_0_, bf16[1,2,4096]{2,1,0:T(2,128)(2,1)} %refs_1_.4, bf16[1,512,512]{2,1,0:T(8,128)(2,1)} %refs_2_.2, bf16[1,512,512]{2,1,0:T(8,128)(2,1)} %refs_3_.1, bf16[1,2,512]{2,1,0:T(2,128)(2,1)} %refs_4_.1, ...), custom_call_target="tpu_custom_call" | custom-call | tf_op jit(solution)/shard_map/attend/pallas_call | solution.py:82
  15.2 0.1 collective-permute-start.5
  15.3 1.4 %collective-permute-done.5.refs_1_ = f32[1,16,256]{2,1,0:T(8,128)S(1)} collective-permute-done((f32[1,16,256]{2,1,0:T(8,128)}, f32[1,16,256]{2,1,0:T(8,128)S(1)}, u32[]{:S(2)}, u32[]{:S(2)}) %collective-permute-start.5) | collective-permute-done | bytes 16416 | tf_op jit(solution)/shard_map/softmax_tp1/ppermute | solution.py:22
  16.7 1.5 %collective-permute-start.4 = (f32[2,16,256]{2,1,0:T(8,128)}, f32[2,16,256]{2,1,0:T(8,128)S(1)}, u32[]{:S(2)}, u32[]{:S(2)}) collective-permute-start(f32[2,16,256]{2,1,0:T(8,128)} %get-tuple-element.33), channel_id=1, source_target_pairs={{0,2},{1,3},{2,0},{3,1},{4,6},{5,7},{6,4},{7,5},{8,10},{9,11},{10,... | collective-permute-start | bytes 98312 | tf_op jit(solution)/shard_map/softmax_tp2/ppermute | solution.py:22
  18.2 2.6 %collective-permute-done.4.refs_0_ = f32[2,16,256]{2,1,0:T(8,128)S(1)} collective-permute-done((f32[2,16,256]{2,1,0:T(8,128)}, f32[2,16,256]{2,1,0:T(8,128)S(1)}, u32[]{:S(2)}, u32[]{:S(2)}) %collective-permute-start.4) | collective-permute-done | bytes 32800 | tf_op jit(solution)/shard_map/softmax_tp2/ppermute | solution.py:22
  20.8 0.0 collective-permute-start.6
  20.8 0.8 copy-done.8
  21.6 0.4 collective-permute-done.6.refs_2_
  22.0 0.9 %combine.1.refs_3_.refs_2_ = bf16[120,1024]{1,0:T(8,128)(2,1)S(1)} custom-call(bf16[128,1024]{1,0:T(8,128)(2,1)S(1)} %copy-done.1, f32[40,256]{1,0:T(8,128)S(1)} %hold.1.own_ref, f32[2,16,256]{2,1,0:T(8,128)S(1)} %collective-permute-done.4.refs_0_, f32[1,16,256]{2,1,0:T(8,128)S(1)} %collective-permute-done.5.refs_1_, ...), custom_call_target="tpu_custom_call" | custom-call | tf_op jit(solution)/shard_map/combine/pallas_call | solution.py:439
  22.9 0.0 collective-permute-done.1.refs_0_
  23.0 0.0 collective-permute-done.3.refs_2_
  23.0 0.2 collective-permute-start.7
  23.2 0.4 collective-permute-start.8
  23.6 0.2 collective-permute-start.9
  23.7 2.4 %collective-permute-start.14 = (bf16[120,1024]{1,0:T(8,128)(2,1)S(1)}, bf16[120,1024]{1,0:T(8,128)(2,1)}, u32[]{:S(2)}, u32[]{:S(2)}) collective-permute-start(bf16[120,1024]{1,0:T(8,128)(2,1)S(1)} %combine.1.refs_3_.refs_2_), channel_id=1, source_target_pairs={{0,24},{4,28},{8,0},{12,4},{16,8},{20,12},{24,16},{28,20},{1,25},{... | collective-permute-start | bytes 737288 | tf_op jit(solution)/shard_map/last_z3/ppermute | solution.py:28
  26.2 0.4 collective-permute-start.13
  26.6 0.9 %collective-permute-start.12 = (bf16[120,1024]{1,0:T(8,128)(2,1)S(1)}, bf16[120,1024]{1,0:T(8,128)(2,1)}, u32[]{:S(2)}, u32[]{:S(2)}) collective-permute-start(bf16[120,1024]{1,0:T(8,128)(2,1)S(1)} %combine.1.refs_3_.refs_2_), channel_id=1, source_target_pairs={{0,8},{4,12},{8,16},{12,20},{16,24},{20,28},{24,0},{28,4},{1,9},{5... | collective-permute-start | bytes 737288 | tf_op jit(solution)/shard_map/last_z1/ppermute | solution.py:28
  27.6 0.0 collective-permute-done.refs_2_.refs_1_
  27.6 5.2 %middle.1 = (bf16[128,1024]{1,0:T(8,128)(2,1)}, bf16[128,1024]{1,0:T(8,128)(2,1)}, bf16[128,1024]{1,0:T(8,128)(2,1)}, f32[128,1024]{1,0:T(8,128)}, bf16[512,512]...) custom-call(bf16[128,4096]{1,0:T(8,128)(2,1)} %refs_0_.5, bf16[512,1024]{1,0:T(8,128)(2,1)} %refs_0_.6, ...), custom_call_target="tpu_custom_call" | custom-call | tf_op jit(solution)/shard_map/middle/pallas_call | solution.py:82
  32.9 1.4 %collective-permute-start.10 = (bf16[128,512]{1,0:T(8,128)(2,1)}, bf16[128,512]{1,0:T(8,128)(2,1)S(1)}, u32[]{:S(2)}, u32[]{:S(2)}) collective-permute-start(bf16[128,512]{1,0:T(8,128)(2,1)} %get-tuple-element.42), channel_id=1, source_target_pairs={{0,4},{4,0},{8,12},{12,8},{16,20},{20,16},{24,28},{28,24},{1,5},{5... | collective-permute-start | bytes 393224 | tf_op jit(solution)/shard_map/cot_x/ppermute | solution.py:22
  34.2 0.7 collective-permute-start.11
  34.9 4.6 %collective-permute-done.10.refs_0_ = bf16[128,512]{1,0:T(8,128)(2,1)S(1)} collective-permute-done((bf16[128,512]{1,0:T(8,128)(2,1)}, bf16[128,512]{1,0:T(8,128)(2,1)S(1)}, u32[]{:S(2)}, u32[]{:S(2)}) %collective-permute-start.10) | collective-permute-done | bytes 131104 | tf_op jit(solution)/shard_map/cot_x/ppermute | solution.py:22
  39.5 1.4 %collective-permute-done.11.refs_1_ = bf16[128,512]{1,0:T(8,128)(2,1)S(1)} collective-permute-done((bf16[128,512]{1,0:T(8,128)(2,1)}, bf16[128,512]{1,0:T(8,128)(2,1)S(1)}, u32[]{:S(2)}, u32[]{:S(2)}) %collective-permute-start.11) | collective-permute-done | bytes 131104 | tf_op jit(solution)/shard_map/cot_x/ppermute | solution.py:22
  40.9 0.6 copy-done.12
  41.6 2.1 %pack.1 = (bf16[256,512]{1,0:T(8,128)(2,1)}, bf16[512,1024]{1,0:T(8,128)(2,1)}) custom-call(bf16[128,512]{1,0:T(8,128)(2,1)} %copy-done.11, bf16[128,512]{1,0:T(8,128)(2,1)} %copy-done.12, bf16[128,1024]{1,0:T(8,128)(2,1)} %refs_2_.3, bf16[80,1024]{1,0:T(8,128)(2,1)} %copy-done.3, bf16[80,1024]{1,0:T(8,128)(2,1)} %copy-done.4, ...), custom_call_target="tpu_custom_call" | custom-call | tf_op jit(solution)/shard_map/pack/pallas_call | solution.py:82
  43.7 5.1 %collective-permute-done.13.refs_6_.refs_4_ = bf16[120,1024]{1,0:T(8,128)(2,1)} collective-permute-done((bf16[120,1024]{1,0:T(8,128)(2,1)S(1)}, bf16[120,1024]{1,0:T(8,128)(2,1)}, u32[]{:S(2)}, u32[]{:S(2)}) %collective-permute-start.13) | collective-permute-done | bytes 245792 | tf_op jit(solution)/shard_map/last_z2/ppermute | solution.py:28
  48.8 0.0 collective-permute-done.12.refs_5_.refs_3_
  48.8 1.9 %gate.1 = (bf16[128,1024]{1,0:T(8,128)(2,1)}, bf16[128,1024]{1,0:T(8,128)(2,1)}, bf16[128,1024]{1,0:T(8,128)(2,1)}, bf16[512,1024]{1,0:T(8,128)(2,1)}) custom-call(bf16[128,1024]{1,0:T(8,128)(2,1)} %get-tuple-element.39.refs_0_, ...), custom_call_target="tpu_custom_call", output_to_operand_aliasing={{0}: (0, {}), {1}: (1, {}), {2}: (2, {}), {3}: (3, {})} | custom-call | tf_op jit(solution)/shard_map/gate/pallas_call | solution.py:487
  50.7 0.6 collective-permute-start.20
  51.3 0.0 collective-permute-start.19
  51.3 2.2 %collective-permute-start.16 = (bf16[128,1024]{1,0:T(8,128)(2,1)}, bf16[128,1024]{1,0:T(8,128)(2,1)}, u32[]{:S(2)}, u32[]{:S(2)}) collective-permute-start(bf16[128,1024]{1,0:T(8,128)(2,1)} %get-tuple-element.47), channel_id=1, source_target_pairs={{0,16},{4,20},{8,24},{12,28},{16,0},{20,4},{24,8},{28,12},{1,17},{... | collective-permute-start | bytes 786440 | tf_op jit(solution)/shard_map/sum_z2/ppermute | solution.py:28
  53.5 2.0 %collective-permute-start.17 = (bf16[128,1024]{1,0:T(8,128)(2,1)}, bf16[128,1024]{1,0:T(8,128)(2,1)}, u32[]{:S(2)}, u32[]{:S(2)}) collective-permute-start(bf16[128,1024]{1,0:T(8,128)(2,1)} %get-tuple-element.48), channel_id=1, source_target_pairs={{0,8},{4,12},{8,16},{12,20},{16,24},{20,28},{24,0},{28,4},{1,9},{5... | collective-permute-start | bytes 786440 | tf_op jit(solution)/shard_map/sum_z3/ppermute | solution.py:28
  55.5 3.5 %decode.1 = f32[4,1,2,1024]{3,2,1,0:T(2,128)} custom-call(bf16[512,1024]{1,0:T(8,128)(2,1)} %refs_0_.6, bf16[512,1024]{1,0:T(8,128)(2,1)} %collective-permute-done.refs_2_.refs_1_, bf16[120,1024]{1,0:T(8,128)(2,1)} %copy-done.2, bf16[120,1024]{1,0:T(8,128)(2,1)} %collective-permute-done.12.refs_5_.refs_3_, ...), custom_call_target="tpu_custom_call" | custom-call | tf_op jit(solution)/shard_map/decode/pallas_call | solution.py:82
  59.0 7.2 %all_to_all.5 = f32[4,1,2,1024]{3,2,1,0:T(2,128)S(1)} all-to-all(f32[4,1,2,1024]{3,2,1,0:T(2,128)} %decode.1), channel_id=1, replica_groups=mesh['fsdp'=8,'tp'=4] {'tp'}, dimensions={0} | all-to-all | bytes 65536 | tf_op jit(solution)/shard_map/dec_tp/all_to_all | solution.py:524
  66.2 0.7 collective-permute-start.18
  66.9 0.0 copy-start
  66.9 1.2 %copy-done = bf16[512,1024]{1,0:T(8,128)(2,1)S(1)} copy-done((bf16[512,1024]{1,0:T(8,128)(2,1)S(1)}, bf16[512,1024]{1,0:T(8,128)(2,1)}, u32[]{:S(2)}) %copy-start) | copy-done | bytes 1048600
  68.1 1.0 %copy-done.6 = bf16[512,512]{1,0:T(8,128)(2,1)S(1)} copy-done((bf16[512,512]{1,0:T(8,128)(2,1)S(1)}, bf16[512,512]{1,0:T(8,128)(2,1)}, u32[]{:S(2)}) %copy-start.6) | copy-done | bytes 524312
  69.1 1.0 %own.1.refs_0_ = f32[512,1024]{1,0:T(8,128)S(1)} custom-call(bf16[512,512]{1,0:T(8,128)(2,1)S(1)} %copy-done.6, bf16[512,1024]{1,0:T(8,128)(2,1)S(1)} %copy-done, bf16[256,512]{1,0:T(8,128)(2,1)S(1)} %collective-permute-done.19.refs_2_.refs_3_), custom_call_target="tpu_custom_call" | custom-call | tf_op jit(solution)/shard_map/own/pallas_call | solution.py:82
  70.1 5.7 %collective-permute-done.20.refs_1_ = bf16[512,1024]{1,0:T(8,128)(2,1)} collective-permute-done((bf16[512,1024]{1,0:T(8,128)(2,1)}, bf16[512,1024]{1,0:T(8,128)(2,1)}, u32[]{:S(2)}, u32[]{:S(2)}) %collective-permute-start.20) | collective-permute-done | bytes 1048608 | tf_op jit(solution)/shard_map/attn_x/ppermute | solution.py:22
  75.8 3.3 %product.1 = (f32[512,1024]{1,0:T(8,128)}, f32[8,128]{1,0:T(8,128)S(1)}) custom-call(f32[512,1024]{1,0:T(8,128)S(1)} %own.1.refs_0_, bf16[512,1024]{1,0:T(8,128)(2,1)} %collective-permute-done.20.refs_1_, bf16[256,512]{1,0:T(8,128)(2,1)S(1)} %copy-done.5, bf16[256,512]{1,0:T(8,128)(2,1)S(1)} %collective-permute-done.19.refs_2_.refs_3_), custom_call_target="tpu_custom_call" | custom-call | tf_op jit(solution)/shard_map/product/pallas_call | solution.py:82
  79.1 2.1 %sum.1 = (bf16[1,2,1024]{2,1,0:T(2,128)(2,1)}, bf16[128,1024]{1,0:T(8,128)(2,1)}) custom-call(f32[128,1024]{1,0:T(8,128)S(1)} %copy-done.7, bf16[128,1024]{1,0:T(8,128)(2,1)S(1)} %collective-permute-done.15.refs_1_, bf16[128,1024]{1,0:T(8,128)(2,1)} %collective-permute-done.16.refs_2_, bf16[128,1024]{1,0:T(8,128)(2,1)} %collective-permute-done.17.refs_3_, ...), custom_call_target="tpu_custom_call" | custom-call | tf_op jit(solution)/shard_map/sum/pallas_call | solution.py:82
  (34 shorter events, 0.1 us)
Async XLA Ops:
  0.6 21.4 %copy-start.1 = (bf16[128,1024]{1,0:T(8,128)(2,1)S(1)}, bf16[128,1024]{1,0:T(8,128)(2,1)}, u32[]{:S(2)}) copy-start(bf16[128,1024]{1,0:T(8,128)(2,1)} %refs_2_.3) | copy-start | bytes 786436
  0.6 26.9 %collective-permute-start = (bf16[512,1024]{1,0:T(8,128)(2,1)}, bf16[512,1024]{1,0:T(8,128)(2,1)}, u32[]{:S(2)}, u32[]{:S(2)}) collective-permute-start(bf16[512,1024]{1,0:T(8,128)(2,1)} %refs_0_.6), channel_id=1, source_target_pairs={{0,4},{4,0},{8,12},{12,8},{16,20},{20,16},{24,28},{28,24},{1,5},{5... | collective-permute-start | bytes 3145736 | tf_op jit(solution)/shard_map/weight_x/ppermute | solution.py:22
  5.6 17.4 %collective-permute-start.1 = (bf16[80,1024]{1,0:T(8,128)(2,1)}, bf16[80,1024]{1,0:T(8,128)(2,1)S(1)}, u32[]{:S(2)}, u32[]{:S(2)}) collective-permute-start(bf16[80,1024]{1,0:T(8,128)(2,1)} %get-tuple-element.29), channel_id=1, source_target_pairs={{0,8},{4,12},{8,16},{12,20},{16,24},{20,28},{24,0},{28,4},{1,9},{5... | collective-permute-start | bytes 491528 | tf_op jit(solution)/shard_map/first_z1/ppermute | solution.py:28
  7.2 15.8 %collective-permute-start.2 = (bf16[80,1024]{1,0:T(8,128)(2,1)}, bf16[80,1024]{1,0:T(8,128)(2,1)S(1)}, u32[]{:S(2)}, u32[]{:S(2)}) collective-permute-start(bf16[80,1024]{1,0:T(8,128)(2,1)} %get-tuple-element.30), channel_id=1, source_target_pairs={{0,16},{4,20},{8,24},{12,28},{16,0},{20,4},{24,8},{28,12},{1,17},{... | collective-permute-start | bytes 491528 | tf_op jit(solution)/shard_map/first_z2/ppermute | solution.py:28
  9.8 13.2 %collective-permute-start.3 = (bf16[80,1024]{1,0:T(8,128)(2,1)}, bf16[80,1024]{1,0:T(8,128)(2,1)}, u32[]{:S(2)}, u32[]{:S(2)}) collective-permute-start(bf16[80,1024]{1,0:T(8,128)(2,1)} %get-tuple-element.31), channel_id=1, source_target_pairs={{0,24},{4,28},{8,0},{12,4},{16,8},{20,12},{24,16},{28,20},{1,25},{... | collective-permute-start | bytes 491528 | tf_op jit(solution)/shard_map/first_z3/ppermute | solution.py:28
  15.2 1.5 %collective-permute-start.5 = (f32[1,16,256]{2,1,0:T(8,128)}, f32[1,16,256]{2,1,0:T(8,128)S(1)}, u32[]{:S(2)}, u32[]{:S(2)}) collective-permute-start(f32[1,16,256]{2,1,0:T(8,128)} %get-tuple-element.34), channel_id=1, source_target_pairs={{0,1},{1,0},{2,3},{3,2},{4,5},{5,4},{6,7},{7,6},{8,9},{9,8},{10,11... | collective-permute-start | bytes 49160 | tf_op jit(solution)/shard_map/softmax_tp1/ppermute | solution.py:22
  16.7 4.1 %collective-permute-start.4 = (f32[2,16,256]{2,1,0:T(8,128)}, f32[2,16,256]{2,1,0:T(8,128)S(1)}, u32[]{:S(2)}, u32[]{:S(2)}) collective-permute-start(f32[2,16,256]{2,1,0:T(8,128)} %get-tuple-element.33), channel_id=1, source_target_pairs={{0,2},{1,3},{2,0},{3,1},{4,6},{5,7},{6,4},{7,5},{8,10},{9,11},{10,... | collective-permute-start | bytes 98312 | tf_op jit(solution)/shard_map/softmax_tp2/ppermute | solution.py:22
  20.8 1.2 %collective-permute-start.6 = (f32[2,16,256]{2,1,0:T(8,128)S(1)}, f32[2,16,256]{2,1,0:T(8,128)S(1)}, u32[]{:S(2)}, u32[]{:S(2)}) collective-permute-start(f32[2,16,256]{2,1,0:T(8,128)S(1)} %collective-permute-done.4.refs_0_), channel_id=1, source_target_pairs={{0,1},{1,0},{2,3},{3,2},{4,5},{5,4},{6,7},{7,6},{8,9},{9,8},{10,11... | collective-permute-start | bytes 98312 | tf_op jit(solution)/shard_map/softmax_tp1/ppermute | solution.py:22
  20.8 0.8 copy-start.8
  22.9 9.9 %copy-start.2 = (bf16[120,1024]{1,0:T(8,128)(2,1)}, bf16[120,1024]{1,0:T(8,128)(2,1)S(1)}, u32[]{:S(2)}) copy-start(bf16[120,1024]{1,0:T(8,128)(2,1)S(1)} %combine.1.refs_3_.refs_2_) | copy-start | bytes 737284
  23.0 4.6 %copy-start.3 = (bf16[80,1024]{1,0:T(8,128)(2,1)}, bf16[80,1024]{1,0:T(8,128)(2,1)S(1)}, u32[]{:S(2)}) copy-start(bf16[80,1024]{1,0:T(8,128)(2,1)S(1)} %get-tuple-element.35.refs_3_) | copy-start | bytes 491524
  23.0 4.6 %copy-start.4 = (bf16[80,1024]{1,0:T(8,128)(2,1)}, bf16[80,1024]{1,0:T(8,128)(2,1)S(1)}, u32[]{:S(2)}) copy-start(bf16[80,1024]{1,0:T(8,128)(2,1)S(1)} %get-tuple-element.36.refs_4_) | copy-start | bytes 491524
  23.0 3.2 %collective-permute-start.7 = (bf16[80,1024]{1,0:T(8,128)(2,1)S(1)}, bf16[80,1024]{1,0:T(8,128)(2,1)S(1)}, u32[]{:S(2)}, u32[]{:S(2)}) collective-permute-start(bf16[80,1024]{1,0:T(8,128)(2,1)S(1)} %get-tuple-element.35.refs_3_), channel_id=1, source_target_pairs={{0,1},{1,0},{2,3},{3,2},{4,5},{5,4},{6,7},{7,6},{8,9},{9,8},{10,11... | collective-permute-start | bytes 491528 | tf_op jit(solution)/shard_map/cot_core/ppermute | solution.py:22
  23.2 3.4 %collective-permute-start.8 = (bf16[80,1024]{1,0:T(8,128)(2,1)S(1)}, bf16[80,1024]{1,0:T(8,128)(2,1)S(1)}, u32[]{:S(2)}, u32[]{:S(2)}) collective-permute-start(bf16[80,1024]{1,0:T(8,128)(2,1)S(1)} %get-tuple-element.36.refs_4_), channel_id=1, source_target_pairs={{0,1},{1,0},{2,3},{3,2},{4,5},{5,4},{6,7},{7,6},{8,9},{9,8},{10,11... | collective-permute-start | bytes 491528 | tf_op jit(solution)/shard_map/cot_core/ppermute | solution.py:22
  23.6 4.0 %collective-permute-start.9 = (bf16[80,1024]{1,0:T(8,128)(2,1)}, bf16[80,1024]{1,0:T(8,128)(2,1)}, u32[]{:S(2)}, u32[]{:S(2)}) collective-permute-start(bf16[80,1024]{1,0:T(8,128)(2,1)} %get-tuple-element.37.refs_5_), channel_id=1, source_target_pairs={{0,1},{1,0},{2,3},{3,2},{4,5},{5,4},{6,7},{7,6},{8,9},{9,8},{10,11... | collective-permute-start | bytes 491528 | tf_op jit(solution)/shard_map/cot_core/ppermute | solution.py:22
  23.7 19.9 %collective-permute-start.14 = (bf16[120,1024]{1,0:T(8,128)(2,1)S(1)}, bf16[120,1024]{1,0:T(8,128)(2,1)}, u32[]{:S(2)}, u32[]{:S(2)}) collective-permute-start(bf16[120,1024]{1,0:T(8,128)(2,1)S(1)} %combine.1.refs_3_.refs_2_), channel_id=1, source_target_pairs={{0,24},{4,28},{8,0},{12,4},{16,8},{20,12},{24,16},{28,20},{1,25},{... | collective-permute-start | bytes 737288 | tf_op jit(solution)/shard_map/last_z3/ppermute | solution.py:28
  26.2 1.4 %copy-start.9 = (bf16[80,1024]{1,0:T(8,128)(2,1)}, bf16[80,1024]{1,0:T(8,128)(2,1)S(1)}, u32[]{:S(2)}) copy-start(bf16[80,1024]{1,0:T(8,128)(2,1)S(1)} %collective-permute-done.7.refs_6_) | copy-start | bytes 491524
  26.2 22.6 %collective-permute-start.13 = (bf16[120,1024]{1,0:T(8,128)(2,1)S(1)}, bf16[120,1024]{1,0:T(8,128)(2,1)}, u32[]{:S(2)}, u32[]{:S(2)}) collective-permute-start(bf16[120,1024]{1,0:T(8,128)(2,1)S(1)} %combine.1.refs_3_.refs_2_), channel_id=1, source_target_pairs={{0,16},{4,20},{8,24},{12,28},{16,0},{20,4},{24,8},{28,12},{1,17},{... | collective-permute-start | bytes 737288 | tf_op jit(solution)/shard_map/last_z2/ppermute | solution.py:28
  26.6 1.0 %copy-start.10 = (bf16[80,1024]{1,0:T(8,128)(2,1)}, bf16[80,1024]{1,0:T(8,128)(2,1)S(1)}, u32[]{:S(2)}) copy-start(bf16[80,1024]{1,0:T(8,128)(2,1)S(1)} %collective-permute-done.8.refs_7_) | copy-start | bytes 491524
  26.6 22.2 %collective-permute-start.12 = (bf16[120,1024]{1,0:T(8,128)(2,1)S(1)}, bf16[120,1024]{1,0:T(8,128)(2,1)}, u32[]{:S(2)}, u32[]{:S(2)}) collective-permute-start(bf16[120,1024]{1,0:T(8,128)(2,1)S(1)} %combine.1.refs_3_.refs_2_), channel_id=1, source_target_pairs={{0,8},{4,12},{8,16},{12,20},{16,24},{20,28},{24,0},{28,4},{1,9},{5... | collective-permute-start | bytes 737288 | tf_op jit(solution)/shard_map/last_z1/ppermute | solution.py:28
  32.9 6.7 %collective-permute-start.10 = (bf16[128,512]{1,0:T(8,128)(2,1)}, bf16[128,512]{1,0:T(8,128)(2,1)S(1)}, u32[]{:S(2)}, u32[]{:S(2)}) collective-permute-start(bf16[128,512]{1,0:T(8,128)(2,1)} %get-tuple-element.42), channel_id=1, source_target_pairs={{0,4},{4,0},{8,12},{12,8},{16,20},{20,16},{24,28},{28,24},{1,5},{5... | collective-permute-start | bytes 393224 | tf_op jit(solution)/shard_map/cot_x/ppermute | solution.py:22
  34.2 6.7 %collective-permute-start.11 = (bf16[128,512]{1,0:T(8,128)(2,1)}, bf16[128,512]{1,0:T(8,128)(2,1)S(1)}, u32[]{:S(2)}, u32[]{:S(2)}) collective-permute-start(bf16[128,512]{1,0:T(8,128)(2,1)} %get-tuple-element.43), channel_id=1, source_target_pairs={{0,4},{4,0},{8,12},{12,8},{16,20},{20,16},{24,28},{28,24},{1,5},{5... | collective-permute-start | bytes 393224 | tf_op jit(solution)/shard_map/cot_x/ppermute | solution.py:22
  39.5 1.4 %copy-start.11 = (bf16[128,512]{1,0:T(8,128)(2,1)}, bf16[128,512]{1,0:T(8,128)(2,1)S(1)}, u32[]{:S(2)}) copy-start(bf16[128,512]{1,0:T(8,128)(2,1)S(1)} %collective-permute-done.10.refs_0_) | copy-start | bytes 393220
  40.9 0.6 copy-start.12
  43.7 7.6 %copy-start.5 = (bf16[256,512]{1,0:T(8,128)(2,1)S(1)}, bf16[256,512]{1,0:T(8,128)(2,1)}, u32[]{:S(2)}) copy-start(bf16[256,512]{1,0:T(8,128)(2,1)} %get-tuple-element.45.refs_4_.refs_2_) | copy-start | bytes 786436
  50.7 25.1 %collective-permute-start.20 = (bf16[512,1024]{1,0:T(8,128)(2,1)}, bf16[512,1024]{1,0:T(8,128)(2,1)}, u32[]{:S(2)}, u32[]{:S(2)}) collective-permute-start(bf16[512,1024]{1,0:T(8,128)(2,1)} %get-tuple-element.49.refs_6_.refs_1_), channel_id=1, source_target_pairs={{0,4},{4,0},{8,12},{12,8},{16,20},{20,16},{24,28},{28,24},{1,5},{5... | collective-permute-start | bytes 3145736 | tf_op jit(solution)/shard_map/attn_x/ppermute | solution.py:22
  51.3 14.9 %collective-permute-start.19 = (bf16[256,512]{1,0:T(8,128)(2,1)S(1)}, bf16[256,512]{1,0:T(8,128)(2,1)S(1)}, u32[]{:S(2)}, u32[]{:S(2)}) collective-permute-start(bf16[256,512]{1,0:T(8,128)(2,1)S(1)} %copy-done.5), channel_id=1, source_target_pairs={{0,1},{1,0},{2,3},{3,2},{4,5},{5,4},{6,7},{7,6},{8,9},{9,8},{10,11... | collective-permute-start | bytes 786440 | tf_op jit(solution)/shard_map/cot_x_core/ppermute | solution.py:22
  51.3 27.8 %collective-permute-start.15 = (bf16[128,1024]{1,0:T(8,128)(2,1)}, bf16[128,1024]{1,0:T(8,128)(2,1)S(1)}, u32[]{:S(2)}, u32[]{:S(2)}) collective-permute-start(bf16[128,1024]{1,0:T(8,128)(2,1)} %get-tuple-element.46), channel_id=1, source_target_pairs={{0,24},{4,28},{8,0},{12,4},{16,8},{20,12},{24,16},{28,20},{1,25},{... | collective-permute-start | bytes 786440 | tf_op jit(solution)/shard_map/sum_z1/ppermute | solution.py:28
  51.3 27.8 %collective-permute-start.16 = (bf16[128,1024]{1,0:T(8,128)(2,1)}, bf16[128,1024]{1,0:T(8,128)(2,1)}, u32[]{:S(2)}, u32[]{:S(2)}) collective-permute-start(bf16[128,1024]{1,0:T(8,128)(2,1)} %get-tuple-element.47), channel_id=1, source_target_pairs={{0,16},{4,20},{8,24},{12,28},{16,0},{20,4},{24,8},{28,12},{1,17},{... | collective-permute-start | bytes 786440 | tf_op jit(solution)/shard_map/sum_z2/ppermute | solution.py:28
  53.5 25.6 %collective-permute-start.17 = (bf16[128,1024]{1,0:T(8,128)(2,1)}, bf16[128,1024]{1,0:T(8,128)(2,1)}, u32[]{:S(2)}, u32[]{:S(2)}) collective-permute-start(bf16[128,1024]{1,0:T(8,128)(2,1)} %get-tuple-element.48), channel_id=1, source_target_pairs={{0,8},{4,12},{8,16},{12,20},{16,24},{20,28},{24,0},{28,4},{1,9},{5... | collective-permute-start | bytes 786440 | tf_op jit(solution)/shard_map/sum_z3/ppermute | solution.py:28
  66.2 12.9 %collective-permute-start.18 = (bf16[2,1024]{1,0:T(2,128)(2,1)S(1)}, bf16[2,1024]{1,0:T(2,128)(2,1)S(1)}, u32[]{:S(2)}, u32[]{:S(2)}) collective-permute-start(bf16[2,1024]{1,0:T(2,128)(2,1)S(1)} %reduce_sum.9), channel_id=1, source_target_pairs={{0,0},{1,8},{2,16},{3,24},{4,4},{5,12},{6,20},{7,28},{8,1},{9,9},{... | collective-permute-start | bytes 12296 | tf_op jit(solution)/shard_map/dec_place/ppermute | solution.py:534
  66.9 1.2 %copy-start = (bf16[512,1024]{1,0:T(8,128)(2,1)S(1)}, bf16[512,1024]{1,0:T(8,128)(2,1)}, u32[]{:S(2)}) copy-start(bf16[512,1024]{1,0:T(8,128)(2,1)} %get-tuple-element.49.refs_6_.refs_1_) | copy-start | bytes 3145732
  68.1 1.0 %copy-start.6 = (bf16[512,512]{1,0:T(8,128)(2,1)S(1)}, bf16[512,512]{1,0:T(8,128)(2,1)}, u32[]{:S(2)}) copy-start(bf16[512,512]{1,0:T(8,128)(2,1)} %get-tuple-element.50.refs_0_) | copy-start | bytes 1572868
  70.1 9.0 %copy-start.7 = (f32[128,1024]{1,0:T(8,128)S(1)}, f32[128,1024]{1,0:T(8,128)}, u32[]{:S(2)}) copy-start(f32[128,1024]{1,0:T(8,128)} %get-tuple-element.38.refs_0_) | copy-start | bytes 1572868

commit v6 on v5

--- a/solution.py
+++ b/solution.py
@@ -345,7 +345,7 @@
     rest = refs[0].shape[0] - PAD
     tokens = rest + early
     arrive, leave = [], []
-    for k, ref in enumerate(refs):
+    for k, ref in enumerate(refs[::-1]):
         arrive.append(pltpu.make_async_copy(ref.at[:rest], last_ref.at[k], in_sems.at[k]))
         target = pack_out.at[(k + 1) * tokens + early : (k + 2) * tokens]
         leave.append(pltpu.make_async_copy(last_ref.at[k], target, out_sems.at[k]))
@@ -498,7 +498,7 @@
         compiler_params=pltpu.CompilerParams(vmem_limit_bytes=63 << 20),
         cost_estimate=pl.CostEstimate(flops=0, bytes_accessed=0, transcendentals=0),
         name="gate",
-    )(*sent, pack, cots_x, *lasts[1:])
+    )(*sent, pack, cots_x, *lasts[:0:-1])
     sent, pack = results[:-1], results[-1]
     sums = [turn(sent[k - 1], outer - k, f"sum_z{k}") for k in far]
     pack_x = flip(pack, "fsdp", 1, "attn_x")
@@ -518,7 +518,7 @@
             ((tp_size, share, steps, plane), F32),
         ],
         waits=[pack],
-        room=63,
+        room=12,
     )
     with jax.named_scope("dec_tp"):
         dec = lax.all_to_all(dec, "tp", 0, 0, tiled=True).sum(axis=0).astype(BF16)
@@ -550,7 +550,7 @@
         near=range(4),
         fast=[1],
     )
-    operands = [total, *sums, *pieces]
+    operands = [total, *sums[::-1], *pieces]
     dec_out, grad_attn = call(
         functools.partial(sum_kernel, outer, share),
         "sum",

time: 81.8 us -> 79.3 us (0.969)
  the two profiles are of different devices: /device:TPU:0 before, /device:TPU:12 now
where the time goes in v6:
time: 79.3 us; the launch traced here: 78.8 us
  waiting for transfers between devices  23.6 us (30%)
  Pallas kernels  23.5 us (30%)
  starting transfers between devices  19.5 us (25%)
  local copies, waits for them, and re-layouts  5.6 us (7%)
  blocking collectives  5.02 us (6%)
  between operations  1.53 us (2%)
    pallas_call x8, Pallas kernels, call(): pl.pallas_call(body, out_shape=[jax.ShapeDtypeStruct(shape, dtype) for sh...  20.7 us
    ppermute x11, waiting for transfers between devices, flip(): return lax.ppermute(a, axis, [(i, i ^ bits) for i in range(size)])  18 us
    ppermute x9, starting transfers between devices, turn(): lax.ppermute(a, 'fsdp', [(z * INNER + x, (z + steps) % outer * INNER + x)...  9.73 us
    ppermute x9, waiting for transfers between devices, turn(): lax.ppermute(a, 'fsdp', [(z * INNER + x, (z + steps) % outer * INNER + x)...  5.61 us
    unnamed x28, local copies, waits for them, and re-layouts  5.6 us
    ppermute x11, starting transfers between devices, flip(): return lax.ppermute(a, axis, [(i, i ^ bits) for i in range(size)])  5.4 us
    all_to_all x1, blocking collectives, shards(): dec = lax.all_to_all(dec, 'tp', 0, 0, tiled=True).sum(axis=0).astype(BF16)  5.02 us
    ppermute x1, starting transfers between devices, shards(): lax.ppermute(lax.dynamic_index_in_dim(dec, z % share ^ j, 0, False), ('fs...  4.33 us
  transfers between devices with their start and end apart: 21, of which 10 were waited for; matrix products, arithmetic and copies ran while one was open for 0% of the time, Pallas kernels for 25%

profile of v6, /device:TPU:12, one launch (start us, length us, event | category | flops | bytes accessed | tf_op | source)
XLA Modules:
  0.0 78.8 jit_solution(16496318639049307060)
XLA Ops:
  0.6 0.0 copy-start.3
  0.6 1.6 %collective-permute-start = (bf16[512,1024]{1,0:T(8,128)(2,1)}, bf16[512,1024]{1,0:T(8,128)(2,1)}, u32[]{:S(2)}, u32[]{:S(2)}) collective-permute-start(bf16[512,1024]{1,0:T(8,128)(2,1)} %refs_0_.6), channel_id=1, source_target_pairs={{0,4},{4,0},{8,12},{12,8},{16,20},{20,16},{24,28},{28,24},{1,5},{5... | collective-permute-start | bytes 3145736 | tf_op jit(solution)/shard_map/weight_x/ppermute | solution.py:22
  2.2 1.9 %cut.1 = (bf16[80,1024]{1,0:T(8,128)(2,1)}, bf16[80,1024]{1,0:T(8,128)(2,1)}, bf16[80,1024]{1,0:T(8,128)(2,1)}) custom-call(bf16[128,4096]{1,0:T(8,128)(2,1)} %refs_0_.5, bf16[128,1024]{1,0:T(8,128)(2,1)} %refs_2_.3), custom_call_target="tpu_custom_call" | custom-call | tf_op jit(solution)/shard_map/cut/pallas_call | solution.py:82
  4.1 1.6 %collective-permute-start.1 = (bf16[80,1024]{1,0:T(8,128)(2,1)}, bf16[80,1024]{1,0:T(8,128)(2,1)S(1)}, u32[]{:S(2)}, u32[]{:S(2)}) collective-permute-start(bf16[80,1024]{1,0:T(8,128)(2,1)} %get-tuple-element.29), channel_id=1, source_target_pairs={{0,8},{4,12},{8,16},{12,20},{16,24},{20,28},{24,0},{28,4},{1,9},{5... | collective-permute-start | bytes 491528 | tf_op jit(solution)/shard_map/first_z1/ppermute | solution.py:28
  5.8 1.2 %collective-permute-start.2 = (bf16[80,1024]{1,0:T(8,128)(2,1)}, bf16[80,1024]{1,0:T(8,128)(2,1)S(1)}, u32[]{:S(2)}, u32[]{:S(2)}) collective-permute-start(bf16[80,1024]{1,0:T(8,128)(2,1)} %get-tuple-element.30), channel_id=1, source_target_pairs={{0,16},{4,20},{8,24},{12,28},{16,0},{20,4},{24,8},{28,12},{1,17},{... | collective-permute-start | bytes 491528 | tf_op jit(solution)/shard_map/first_z2/ppermute | solution.py:28
  7.0 1.8 %collective-permute-start.3 = (bf16[80,1024]{1,0:T(8,128)(2,1)}, bf16[80,1024]{1,0:T(8,128)(2,1)}, u32[]{:S(2)}, u32[]{:S(2)}) collective-permute-start(bf16[80,1024]{1,0:T(8,128)(2,1)} %get-tuple-element.31), channel_id=1, source_target_pairs={{0,24},{4,28},{8,0},{12,4},{16,8},{20,12},{24,16},{28,20},{1,25},{... | collective-permute-start | bytes 491528 | tf_op jit(solution)/shard_map/first_z3/ppermute | solution.py:28
  9.4 3.5 %attend.1 = (f32[40,256]{1,0:T(8,128)}, f32[1,16,256]{2,1,0:T(8,128)}, f32[2,16,256]{2,1,0:T(8,128)}) custom-call(s32[1]{0:T(128)S(6)} %copy.26.refs_0_, bf16[1,2,4096]{2,1,0:T(2,128)(2,1)} %refs_1_.4, bf16[1,512,512]{2,1,0:T(8,128)(2,1)} %refs_2_.2, bf16[1,512,512]{2,1,0:T(8,128)(2,1)} %refs_3_.1, bf16[1,2,512]{2,1,0:T(2,128)(2,1)} %refs_4_.1, ...), custom_call_target="tpu_custom_call" | custom-call | tf_op jit(solution)/shard_map/attend/pallas_call | solution.py:82
  12.9 0.1 collective-permute-start.5
  13.0 1.4 %collective-permute-done.5.refs_1_ = f32[1,16,256]{2,1,0:T(8,128)S(1)} collective-permute-done((f32[1,16,256]{2,1,0:T(8,128)}, f32[1,16,256]{2,1,0:T(8,128)S(1)}, u32[]{:S(2)}, u32[]{:S(2)}) %collective-permute-start.5) | collective-permute-done | bytes 16416 | tf_op jit(solution)/shard_map/softmax_tp1/ppermute | solution.py:22
  14.4 0.5 collective-permute-start.4
  14.9 3.6 %collective-permute-done.4.refs_0_ = f32[2,16,256]{2,1,0:T(8,128)S(1)} collective-permute-done((f32[2,16,256]{2,1,0:T(8,128)}, f32[2,16,256]{2,1,0:T(8,128)S(1)}, u32[]{:S(2)}, u32[]{:S(2)}) %collective-permute-start.4) | collective-permute-done | bytes 32800 | tf_op jit(solution)/shard_map/softmax_tp2/ppermute | solution.py:22
  18.5 0.8 copy-done.9
  19.3 0.4 collective-permute-done.6.refs_2_
  19.7 0.9 %combine.1.refs_3_.refs_2_ = bf16[120,1024]{1,0:T(8,128)(2,1)S(1)} custom-call(bf16[128,1024]{1,0:T(8,128)(2,1)S(1)} %copy-done.3, f32[40,256]{1,0:T(8,128)S(1)} %hold.1.own_ref, f32[2,16,256]{2,1,0:T(8,128)S(1)} %collective-permute-done.4.refs_0_, f32[1,16,256]{2,1,0:T(8,128)S(1)} %collective-permute-done.5.refs_1_, ...), custom_call_target="tpu_custom_call" | custom-call | tf_op jit(solution)/shard_map/combine/pallas_call | solution.py:439
  20.6 0.0 collective-permute-done.1.refs_0_
  20.6 0.0 collective-permute-done.2.refs_1_
  20.6 0.9 %collective-permute-done.3.refs_2_ = bf16[80,1024]{1,0:T(8,128)(2,1)} collective-permute-done((bf16[80,1024]{1,0:T(8,128)(2,1)}, bf16[80,1024]{1,0:T(8,128)(2,1)}, u32[]{:S(2)}, u32[]{:S(2)}) %collective-permute-start.3) | collective-permute-done | bytes 163872 | tf_op jit(solution)/shard_map/first_z3/ppermute | solution.py:28
  21.5 0.0 collective-permute-start.7
  21.5 0.5 collective-permute-start.8
  22.0 0.1 collective-permute-start.9
  22.1 0.8 %collective-permute-done.7.refs_6_ = bf16[80,1024]{1,0:T(8,128)(2,1)S(1)} collective-permute-done((bf16[80,1024]{1,0:T(8,128)(2,1)S(1)}, bf16[80,1024]{1,0:T(8,128)(2,1)S(1)}, u32[]{:S(2)}, u32[]{:S(2)}) %collective-permute-start.7) | collective-permute-done | bytes 163872 | tf_op jit(solution)/shard_map/cot_core/ppermute | solution.py:22
  22.9 2.2 %collective-permute-start.13 = (bf16[120,1024]{1,0:T(8,128)(2,1)S(1)}, bf16[120,1024]{1,0:T(8,128)(2,1)}, u32[]{:S(2)}, u32[]{:S(2)}) collective-permute-start(bf16[120,1024]{1,0:T(8,128)(2,1)S(1)} %combine.1.refs_3_.refs_2_), channel_id=1, source_target_pairs={{0,16},{4,20},{8,24},{12,28},{16,0},{20,4},{24,8},{28,12},{1,17},{... | collective-permute-start | bytes 737288 | tf_op jit(solution)/shard_map/last_z2/ppermute | solution.py:28
  25.1 0.0 collective-permute-done.8.refs_7_
  25.1 0.7 copy-done.11
  25.8 0.6 collective-permute-start.12
  26.5 5.3 %middle.1 = (bf16[128,1024]{1,0:T(8,128)(2,1)}, bf16[128,1024]{1,0:T(8,128)(2,1)}, bf16[128,1024]{1,0:T(8,128)(2,1)}, f32[128,1024]{1,0:T(8,128)}, bf16[512,512]...) custom-call(bf16[128,4096]{1,0:T(8,128)(2,1)} %refs_0_.5, bf16[512,1024]{1,0:T(8,128)(2,1)} %refs_0_.6, ...), custom_call_target="tpu_custom_call" | custom-call | tf_op jit(solution)/shard_map/middle/pallas_call | solution.py:82
  31.7 1.1 %collective-permute-start.10 = (bf16[128,512]{1,0:T(8,128)(2,1)}, bf16[128,512]{1,0:T(8,128)(2,1)S(1)}, u32[]{:S(2)}, u32[]{:S(2)}) collective-permute-start(bf16[128,512]{1,0:T(8,128)(2,1)} %get-tuple-element.42), channel_id=1, source_target_pairs={{0,4},{4,0},{8,12},{12,8},{16,20},{20,16},{24,28},{28,24},{1,5},{5... | collective-permute-start | bytes 393224 | tf_op jit(solution)/shard_map/cot_x/ppermute | solution.py:22
  32.8 1.0 %collective-permute-start.11 = (bf16[128,512]{1,0:T(8,128)(2,1)}, bf16[128,512]{1,0:T(8,128)(2,1)S(1)}, u32[]{:S(2)}, u32[]{:S(2)}) collective-permute-start(bf16[128,512]{1,0:T(8,128)(2,1)} %get-tuple-element.43), channel_id=1, source_target_pairs={{0,4},{4,0},{8,12},{12,8},{16,20},{20,16},{24,28},{28,24},{1,5},{5... | collective-permute-start | bytes 393224 | tf_op jit(solution)/shard_map/cot_x/ppermute | solution.py:22
  33.8 4.6 %collective-permute-done.10.refs_0_ = bf16[128,512]{1,0:T(8,128)(2,1)S(1)} collective-permute-done((bf16[128,512]{1,0:T(8,128)(2,1)}, bf16[128,512]{1,0:T(8,128)(2,1)S(1)}, u32[]{:S(2)}, u32[]{:S(2)}) %collective-permute-start.10) | collective-permute-done | bytes 131104 | tf_op jit(solution)/shard_map/cot_x/ppermute | solution.py:22
  38.4 1.4 %collective-permute-done.11.refs_1_ = bf16[128,512]{1,0:T(8,128)(2,1)S(1)} collective-permute-done((bf16[128,512]{1,0:T(8,128)(2,1)}, bf16[128,512]{1,0:T(8,128)(2,1)S(1)}, u32[]{:S(2)}, u32[]{:S(2)}) %collective-permute-start.11) | collective-permute-done | bytes 131104 | tf_op jit(solution)/shard_map/cot_x/ppermute | solution.py:22
  39.8 0.6 copy-done.13
  40.5 2.1 %pack.1 = (bf16[256,512]{1,0:T(8,128)(2,1)}, bf16[512,1024]{1,0:T(8,128)(2,1)}) custom-call(bf16[128,512]{1,0:T(8,128)(2,1)} %copy-done.12, bf16[128,512]{1,0:T(8,128)(2,1)} %copy-done.13, bf16[128,1024]{1,0:T(8,128)(2,1)} %refs_2_.3, bf16[80,1024]{1,0:T(8,128)(2,1)} %copy-done.4, bf16[80,1024]{1,0:T(8,128)(2,1)} %copy-done.5, ...), custom_call_target="tpu_custom_call" | custom-call | tf_op jit(solution)/shard_map/pack/pallas_call | solution.py:82
  42.6 1.4 %collective-permute-done.13.refs_6_.refs_4_ = bf16[120,1024]{1,0:T(8,128)(2,1)} collective-permute-done((bf16[120,1024]{1,0:T(8,128)(2,1)S(1)}, bf16[120,1024]{1,0:T(8,128)(2,1)}, u32[]{:S(2)}, u32[]{:S(2)}) %collective-permute-start.13) | collective-permute-done | bytes 245792 | tf_op jit(solution)/shard_map/last_z2/ppermute | solution.py:28
  44.0 3.2 %collective-permute-done.12.refs_5_ = bf16[120,1024]{1,0:T(8,128)(2,1)} collective-permute-done((bf16[120,1024]{1,0:T(8,128)(2,1)S(1)}, bf16[120,1024]{1,0:T(8,128)(2,1)}, u32[]{:S(2)}, u32[]{:S(2)}) %collective-permute-start.12) | collective-permute-done | bytes 245792 | tf_op jit(solution)/shard_map/last_z3/ppermute | solution.py:28
  47.3 1.9 %gate.1 = (bf16[128,1024]{1,0:T(8,128)(2,1)}, bf16[128,1024]{1,0:T(8,128)(2,1)}, bf16[128,1024]{1,0:T(8,128)(2,1)}, bf16[512,1024]{1,0:T(8,128)(2,1)}) custom-call(bf16[128,1024]{1,0:T(8,128)(2,1)} %get-tuple-element.39.refs_0_, ...), custom_call_target="tpu_custom_call", output_to_operand_aliasing={{0}: (0, {}), {1}: (1, {}), {2}: (2, {}), {3}: (3, {})} | custom-call | tf_op jit(solution)/shard_map/gate/pallas_call | solution.py:487
  49.2 0.6 collective-permute-start.20
  49.8 0.3 collective-permute-start.16
  50.1 2.0 %collective-permute-start.17 = (bf16[128,1024]{1,0:T(8,128)(2,1)}, bf16[128,1024]{1,0:T(8,128)(2,1)}, u32[]{:S(2)}, u32[]{:S(2)}) collective-permute-start(bf16[128,1024]{1,0:T(8,128)(2,1)} %get-tuple-element.48), channel_id=1, source_target_pairs={{0,24},{4,28},{8,0},{12,4},{16,8},{20,12},{24,16},{28,20},{1,25},{... | collective-permute-start | bytes 786440 | tf_op jit(solution)/shard_map/sum_z1/ppermute | solution.py:28
  52.0 1.2 %copy-done = bf16[512,1024]{1,0:T(8,128)(2,1)S(1)} copy-done((bf16[512,1024]{1,0:T(8,128)(2,1)S(1)}, bf16[512,1024]{1,0:T(8,128)(2,1)}, u32[]{:S(2)}) %copy-start) | copy-done | bytes 1048600
  53.3 1.2 %copy-done.2 = bf16[512,1024]{1,0:T(8,128)(2,1)S(1)} copy-done((bf16[512,1024]{1,0:T(8,128)(2,1)S(1)}, bf16[512,1024]{1,0:T(8,128)(2,1)}, u32[]{:S(2)}) %copy-start.2) | copy-done | bytes 1048600
  54.5 2.9 %decode.1 = f32[4,1,2,1024]{3,2,1,0:T(2,128)S(1)} custom-call(bf16[512,1024]{1,0:T(8,128)(2,1)S(1)} %copy-done.2, bf16[512,1024]{1,0:T(8,128)(2,1)} %collective-permute-done.refs_2_.refs_1_, bf16[120,1024]{1,0:T(8,128)(2,1)S(1)} %combine.1.refs_3_.refs_2_, bf16[120,1024]{1,0:T(8,128)(2,1)} %collective-permute-done.14.refs_7_.refs_3_, ...), custom_call_target="tpu_custom_call" | custom-call | tf_op jit(solution)/shard_map/decode/pallas_call | solution.py:82
  57.4 5.0 %all_to_all.5 = f32[4,1,2,1024]{3,2,1,0:T(2,128)S(1)} all-to-all(f32[4,1,2,1024]{3,2,1,0:T(2,128)S(1)} %decode.1), channel_id=1, replica_groups=mesh['fsdp'=8,'tp'=4] {'tp'}, dimensions={0} | all-to-all | bytes 65536 | tf_op jit(solution)/shard_map/dec_tp/all_to_all | solution.py:524
  62.4 4.3 %collective-permute-start.18 = (bf16[2,1024]{1,0:T(2,128)(2,1)S(1)}, bf16[2,1024]{1,0:T(2,128)(2,1)S(1)}, u32[]{:S(2)}, u32[]{:S(2)}) collective-permute-start(bf16[2,1024]{1,0:T(2,128)(2,1)S(1)} %reduce_sum.9), channel_id=1, source_target_pairs={{0,0},{1,8},{2,16},{3,24},{4,4},{5,12},{6,20},{7,28},{8,1},{9,9},{... | collective-permute-start | bytes 12296 | tf_op jit(solution)/shard_map/dec_place/ppermute | solution.py:534
  66.8 1.0 %copy-done.7 = bf16[512,512]{1,0:T(8,128)(2,1)S(1)} copy-done((bf16[512,512]{1,0:T(8,128)(2,1)S(1)}, bf16[512,512]{1,0:T(8,128)(2,1)}, u32[]{:S(2)}) %copy-start.7) | copy-done | bytes 524312
  67.8 1.0 %own.1.refs_0_ = f32[512,1024]{1,0:T(8,128)S(1)} custom-call(bf16[512,512]{1,0:T(8,128)(2,1)S(1)} %copy-done.7, bf16[512,1024]{1,0:T(8,128)(2,1)S(1)} %copy-done.1, bf16[256,512]{1,0:T(8,128)(2,1)S(1)} %collective-permute-done.19.refs_2_.refs_3_), custom_call_target="tpu_custom_call" | custom-call | tf_op jit(solution)/shard_map/own/pallas_call | solution.py:82
  68.8 5.7 %collective-permute-done.20.refs_1_ = bf16[512,1024]{1,0:T(8,128)(2,1)S(1)} collective-permute-done((bf16[512,1024]{1,0:T(8,128)(2,1)}, bf16[512,1024]{1,0:T(8,128)(2,1)S(1)}, u32[]{:S(2)}, u32[]{:S(2)}) %collective-permute-start.20) | collective-permute-done | bytes 1048608 | tf_op jit(solution)/shard_map/attn_x/ppermute | solution.py:22
  74.5 2.0 %product.1 = (f32[512,1024]{1,0:T(8,128)}, f32[8,128]{1,0:T(8,128)S(1)}) custom-call(f32[512,1024]{1,0:T(8,128)S(1)} %own.1.refs_0_, bf16[512,1024]{1,0:T(8,128)(2,1)S(1)} %collective-permute-done.20.refs_1_, bf16[256,512]{1,0:T(8,128)(2,1)S(1)} %copy-done.6, bf16[256,512]{1,0:T(8,128)(2,1)S(1)} %collective-permute-done.19.refs_2_.refs_3_), custom_call_target="tpu_custom_call" | custom-call | tf_op jit(solution)/shard_map/product/pallas_call | solution.py:82
  76.6 2.1 %sum.1 = (bf16[1,2,1024]{2,1,0:T(2,128)(2,1)}, bf16[128,1024]{1,0:T(8,128)(2,1)}) custom-call(f32[128,1024]{1,0:T(8,128)S(1)} %copy-done.8, bf16[128,1024]{1,0:T(8,128)(2,1)S(1)} %collective-permute-done.15.refs_1_, bf16[128,1024]{1,0:T(8,128)(2,1)} %collective-permute-done.16.refs_2_, bf16[128,1024]{1,0:T(8,128)(2,1)} %collective-permute-done.17.refs_3_, ...), custom_call_target="tpu_custom_call" | custom-call | tf_op jit(solution)/shard_map/sum/pallas_call | solution.py:82
  (36 shorter events, 0.1 us)
Async XLA Ops:
  0.6 19.1 %copy-start.3 = (bf16[128,1024]{1,0:T(8,128)(2,1)S(1)}, bf16[128,1024]{1,0:T(8,128)(2,1)}, u32[]{:S(2)}) copy-start(bf16[128,1024]{1,0:T(8,128)(2,1)} %refs_2_.3) | copy-start | bytes 786436
  0.6 25.8 %collective-permute-start = (bf16[512,1024]{1,0:T(8,128)(2,1)}, bf16[512,1024]{1,0:T(8,128)(2,1)}, u32[]{:S(2)}, u32[]{:S(2)}) collective-permute-start(bf16[512,1024]{1,0:T(8,128)(2,1)} %refs_0_.6), channel_id=1, source_target_pairs={{0,4},{4,0},{8,12},{12,8},{16,20},{20,16},{24,28},{28,24},{1,5},{5... | collective-permute-start | bytes 3145736 | tf_op jit(solution)/shard_map/weight_x/ppermute | solution.py:22
  4.1 16.5 %collective-permute-start.1 = (bf16[80,1024]{1,0:T(8,128)(2,1)}, bf16[80,1024]{1,0:T(8,128)(2,1)S(1)}, u32[]{:S(2)}, u32[]{:S(2)}) collective-permute-start(bf16[80,1024]{1,0:T(8,128)(2,1)} %get-tuple-element.29), channel_id=1, source_target_pairs={{0,8},{4,12},{8,16},{12,20},{16,24},{20,28},{24,0},{28,4},{1,9},{5... | collective-permute-start | bytes 491528 | tf_op jit(solution)/shard_map/first_z1/ppermute | solution.py:28
  5.8 14.8 %collective-permute-start.2 = (bf16[80,1024]{1,0:T(8,128)(2,1)}, bf16[80,1024]{1,0:T(8,128)(2,1)S(1)}, u32[]{:S(2)}, u32[]{:S(2)}) collective-permute-start(bf16[80,1024]{1,0:T(8,128)(2,1)} %get-tuple-element.30), channel_id=1, source_target_pairs={{0,16},{4,20},{8,24},{12,28},{16,0},{20,4},{24,8},{28,12},{1,17},{... | collective-permute-start | bytes 491528 | tf_op jit(solution)/shard_map/first_z2/ppermute | solution.py:28
  7.0 14.5 %collective-permute-start.3 = (bf16[80,1024]{1,0:T(8,128)(2,1)}, bf16[80,1024]{1,0:T(8,128)(2,1)}, u32[]{:S(2)}, u32[]{:S(2)}) collective-permute-start(bf16[80,1024]{1,0:T(8,128)(2,1)} %get-tuple-element.31), channel_id=1, source_target_pairs={{0,24},{4,28},{8,0},{12,4},{16,8},{20,12},{24,16},{28,20},{1,25},{... | collective-permute-start | bytes 491528 | tf_op jit(solution)/shard_map/first_z3/ppermute | solution.py:28
  12.9 1.5 %collective-permute-start.5 = (f32[1,16,256]{2,1,0:T(8,128)}, f32[1,16,256]{2,1,0:T(8,128)S(1)}, u32[]{:S(2)}, u32[]{:S(2)}) collective-permute-start(f32[1,16,256]{2,1,0:T(8,128)} %get-tuple-element.34), channel_id=1, source_target_pairs={{0,1},{1,0},{2,3},{3,2},{4,5},{5,4},{6,7},{7,6},{8,9},{9,8},{10,11... | collective-permute-start | bytes 49160 | tf_op jit(solution)/shard_map/softmax_tp1/ppermute | solution.py:22
  14.4 4.1 %collective-permute-start.4 = (f32[2,16,256]{2,1,0:T(8,128)}, f32[2,16,256]{2,1,0:T(8,128)S(1)}, u32[]{:S(2)}, u32[]{:S(2)}) collective-permute-start(f32[2,16,256]{2,1,0:T(8,128)} %get-tuple-element.33), channel_id=1, source_target_pairs={{0,2},{1,3},{2,0},{3,1},{4,6},{5,7},{6,4},{7,5},{8,10},{9,11},{10,... | collective-permute-start | bytes 98312 | tf_op jit(solution)/shard_map/softmax_tp2/ppermute | solution.py:22
  18.5 1.2 %collective-permute-start.6 = (f32[2,16,256]{2,1,0:T(8,128)S(1)}, f32[2,16,256]{2,1,0:T(8,128)S(1)}, u32[]{:S(2)}, u32[]{:S(2)}) collective-permute-start(f32[2,16,256]{2,1,0:T(8,128)S(1)} %collective-permute-done.4.refs_0_), channel_id=1, source_target_pairs={{0,1},{1,0},{2,3},{3,2},{4,5},{5,4},{6,7},{7,6},{8,9},{9,8},{10,11... | collective-permute-start | bytes 98312 | tf_op jit(solution)/shard_map/softmax_tp1/ppermute | solution.py:22
  18.5 0.8 copy-start.9
  21.5 4.9 %copy-start.4 = (bf16[80,1024]{1,0:T(8,128)(2,1)}, bf16[80,1024]{1,0:T(8,128)(2,1)S(1)}, u32[]{:S(2)}) copy-start(bf16[80,1024]{1,0:T(8,128)(2,1)S(1)} %get-tuple-element.35.refs_3_) | copy-start | bytes 491524
  21.5 4.9 %copy-start.5 = (bf16[80,1024]{1,0:T(8,128)(2,1)}, bf16[80,1024]{1,0:T(8,128)(2,1)S(1)}, u32[]{:S(2)}) copy-start(bf16[80,1024]{1,0:T(8,128)(2,1)S(1)} %get-tuple-element.36.refs_4_) | copy-start | bytes 491524
  21.5 1.4 %collective-permute-start.7 = (bf16[80,1024]{1,0:T(8,128)(2,1)S(1)}, bf16[80,1024]{1,0:T(8,128)(2,1)S(1)}, u32[]{:S(2)}, u32[]{:S(2)}) collective-permute-start(bf16[80,1024]{1,0:T(8,128)(2,1)S(1)} %get-tuple-element.35.refs_3_), channel_id=1, source_target_pairs={{0,1},{1,0},{2,3},{3,2},{4,5},{5,4},{6,7},{7,6},{8,9},{9,8},{10,11... | collective-permute-start | bytes 491528 | tf_op jit(solution)/shard_map/cot_core/ppermute | solution.py:22
  21.5 3.6 %collective-permute-start.8 = (bf16[80,1024]{1,0:T(8,128)(2,1)S(1)}, bf16[80,1024]{1,0:T(8,128)(2,1)S(1)}, u32[]{:S(2)}, u32[]{:S(2)}) collective-permute-start(bf16[80,1024]{1,0:T(8,128)(2,1)S(1)} %get-tuple-element.36.refs_4_), channel_id=1, source_target_pairs={{0,1},{1,0},{2,3},{3,2},{4,5},{5,4},{6,7},{7,6},{8,9},{9,8},{10,11... | collective-permute-start | bytes 491528 | tf_op jit(solution)/shard_map/cot_core/ppermute | solution.py:22
  22.0 4.4 %collective-permute-start.9 = (bf16[80,1024]{1,0:T(8,128)(2,1)}, bf16[80,1024]{1,0:T(8,128)(2,1)}, u32[]{:S(2)}, u32[]{:S(2)}) collective-permute-start(bf16[80,1024]{1,0:T(8,128)(2,1)} %get-tuple-element.37.refs_5_), channel_id=1, source_target_pairs={{0,1},{1,0},{2,3},{3,2},{4,5},{5,4},{6,7},{7,6},{8,9},{9,8},{10,11... | collective-permute-start | bytes 491528 | tf_op jit(solution)/shard_map/cot_core/ppermute | solution.py:22
  22.1 20.4 %collective-permute-start.14 = (bf16[120,1024]{1,0:T(8,128)(2,1)S(1)}, bf16[120,1024]{1,0:T(8,128)(2,1)}, u32[]{:S(2)}, u32[]{:S(2)}) collective-permute-start(bf16[120,1024]{1,0:T(8,128)(2,1)S(1)} %combine.1.refs_3_.refs_2_), channel_id=1, source_target_pairs={{0,8},{4,12},{8,16},{12,20},{16,24},{20,28},{24,0},{28,4},{1,9},{5... | collective-permute-start | bytes 737288 | tf_op jit(solution)/shard_map/last_z1/ppermute | solution.py:28
  22.9 3.5 %copy-start.10 = (bf16[80,1024]{1,0:T(8,128)(2,1)}, bf16[80,1024]{1,0:T(8,128)(2,1)S(1)}, u32[]{:S(2)}) copy-start(bf16[80,1024]{1,0:T(8,128)(2,1)S(1)} %collective-permute-done.7.refs_6_) | copy-start | bytes 491524
  22.9 21.1 %collective-permute-start.13 = (bf16[120,1024]{1,0:T(8,128)(2,1)S(1)}, bf16[120,1024]{1,0:T(8,128)(2,1)}, u32[]{:S(2)}, u32[]{:S(2)}) collective-permute-start(bf16[120,1024]{1,0:T(8,128)(2,1)S(1)} %combine.1.refs_3_.refs_2_), channel_id=1, source_target_pairs={{0,16},{4,20},{8,24},{12,28},{16,0},{20,4},{24,8},{28,12},{1,17},{... | collective-permute-start | bytes 737288 | tf_op jit(solution)/shard_map/last_z2/ppermute | solution.py:28
  25.1 0.7 copy-start.11
  25.8 21.5 %collective-permute-start.12 = (bf16[120,1024]{1,0:T(8,128)(2,1)S(1)}, bf16[120,1024]{1,0:T(8,128)(2,1)}, u32[]{:S(2)}, u32[]{:S(2)}) collective-permute-start(bf16[120,1024]{1,0:T(8,128)(2,1)S(1)} %combine.1.refs_3_.refs_2_), channel_id=1, source_target_pairs={{0,24},{4,28},{8,0},{12,4},{16,8},{20,12},{24,16},{28,20},{1,25},{... | collective-permute-start | bytes 737288 | tf_op jit(solution)/shard_map/last_z3/ppermute | solution.py:28
  31.7 6.7 %collective-permute-start.10 = (bf16[128,512]{1,0:T(8,128)(2,1)}, bf16[128,512]{1,0:T(8,128)(2,1)S(1)}, u32[]{:S(2)}, u32[]{:S(2)}) collective-permute-start(bf16[128,512]{1,0:T(8,128)(2,1)} %get-tuple-element.42), channel_id=1, source_target_pairs={{0,4},{4,0},{8,12},{12,8},{16,20},{20,16},{24,28},{28,24},{1,5},{5... | collective-permute-start | bytes 393224 | tf_op jit(solution)/shard_map/cot_x/ppermute | solution.py:22
  32.8 7.0 %collective-permute-start.11 = (bf16[128,512]{1,0:T(8,128)(2,1)}, bf16[128,512]{1,0:T(8,128)(2,1)S(1)}, u32[]{:S(2)}, u32[]{:S(2)}) collective-permute-start(bf16[128,512]{1,0:T(8,128)(2,1)} %get-tuple-element.43), channel_id=1, source_target_pairs={{0,4},{4,0},{8,12},{12,8},{16,20},{20,16},{24,28},{28,24},{1,5},{5... | collective-permute-start | bytes 393224 | tf_op jit(solution)/shard_map/cot_x/ppermute | solution.py:22
  38.4 1.4 %copy-start.12 = (bf16[128,512]{1,0:T(8,128)(2,1)}, bf16[128,512]{1,0:T(8,128)(2,1)S(1)}, u32[]{:S(2)}) copy-start(bf16[128,512]{1,0:T(8,128)(2,1)S(1)} %collective-permute-done.10.refs_0_) | copy-start | bytes 393220
  39.8 0.6 copy-start.13
  42.6 7.2 %copy-start.6 = (bf16[256,512]{1,0:T(8,128)(2,1)S(1)}, bf16[256,512]{1,0:T(8,128)(2,1)}, u32[]{:S(2)}) copy-start(bf16[256,512]{1,0:T(8,128)(2,1)} %get-tuple-element.45.refs_4_.refs_2_) | copy-start | bytes 786436
  49.2 25.4 %collective-permute-start.20 = (bf16[512,1024]{1,0:T(8,128)(2,1)}, bf16[512,1024]{1,0:T(8,128)(2,1)S(1)}, u32[]{:S(2)}, u32[]{:S(2)}) collective-permute-start(bf16[512,1024]{1,0:T(8,128)(2,1)} %get-tuple-element.49.refs_6_.refs_1_), channel_id=1, source_target_pairs={{0,4},{4,0},{8,12},{12,8},{16,20},{20,16},{24,28},{28,24},{1,5},{5... | collective-permute-start | bytes 3145736 | tf_op jit(solution)/shard_map/attn_x/ppermute | solution.py:22
  49.8 12.7 %collective-permute-start.19 = (bf16[256,512]{1,0:T(8,128)(2,1)S(1)}, bf16[256,512]{1,0:T(8,128)(2,1)S(1)}, u32[]{:S(2)}, u32[]{:S(2)}) collective-permute-start(bf16[256,512]{1,0:T(8,128)(2,1)S(1)} %copy-done.6), channel_id=1, source_target_pairs={{0,1},{1,0},{2,3},{3,2},{4,5},{5,4},{6,7},{7,6},{8,9},{9,8},{10,11... | collective-permute-start | bytes 786440 | tf_op jit(solution)/shard_map/cot_x_core/ppermute | solution.py:22
  49.8 26.8 %collective-permute-start.15 = (bf16[128,1024]{1,0:T(8,128)(2,1)}, bf16[128,1024]{1,0:T(8,128)(2,1)S(1)}, u32[]{:S(2)}, u32[]{:S(2)}) collective-permute-start(bf16[128,1024]{1,0:T(8,128)(2,1)} %get-tuple-element.46), channel_id=1, source_target_pairs={{0,8},{4,12},{8,16},{12,20},{16,24},{20,28},{24,0},{28,4},{1,9},{5... | collective-permute-start | bytes 786440 | tf_op jit(solution)/shard_map/sum_z3/ppermute | solution.py:28
  49.8 26.8 %collective-permute-start.16 = (bf16[128,1024]{1,0:T(8,128)(2,1)}, bf16[128,1024]{1,0:T(8,128)(2,1)}, u32[]{:S(2)}, u32[]{:S(2)}) collective-permute-start(bf16[128,1024]{1,0:T(8,128)(2,1)} %get-tuple-element.47), channel_id=1, source_target_pairs={{0,16},{4,20},{8,24},{12,28},{16,0},{20,4},{24,8},{28,12},{1,17},{... | collective-permute-start | bytes 786440 | tf_op jit(solution)/shard_map/sum_z2/ppermute | solution.py:28
  50.1 26.5 %collective-permute-start.17 = (bf16[128,1024]{1,0:T(8,128)(2,1)}, bf16[128,1024]{1,0:T(8,128)(2,1)}, u32[]{:S(2)}, u32[]{:S(2)}) collective-permute-start(bf16[128,1024]{1,0:T(8,128)(2,1)} %get-tuple-element.48), channel_id=1, source_target_pairs={{0,24},{4,28},{8,0},{12,4},{16,8},{20,12},{24,16},{28,20},{1,25},{... | collective-permute-start | bytes 786440 | tf_op jit(solution)/shard_map/sum_z1/ppermute | solution.py:28
  52.0 1.2 %copy-start = (bf16[512,1024]{1,0:T(8,128)(2,1)S(1)}, bf16[512,1024]{1,0:T(8,128)(2,1)}, u32[]{:S(2)}) copy-start(bf16[512,1024]{1,0:T(8,128)(2,1)} %get-tuple-element.49.refs_6_.refs_1_) | copy-start | bytes 3145732
  53.3 1.2 %copy-start.2 = (bf16[512,1024]{1,0:T(8,128)(2,1)S(1)}, bf16[512,1024]{1,0:T(8,128)(2,1)}, u32[]{:S(2)}) copy-start(bf16[512,1024]{1,0:T(8,128)(2,1)} %refs_0_.6) | copy-start | bytes 3145732
  54.5 12.3 %copy-start.1 = (bf16[512,1024]{1,0:T(8,128)(2,1)S(1)}, bf16[512,1024]{1,0:T(8,128)(2,1)}, u32[]{:S(2)}) copy-start(bf16[512,1024]{1,0:T(8,128)(2,1)} %get-tuple-element.49.refs_6_.refs_1_) | copy-start | bytes 3145732
  62.4 14.2 %collective-permute-start.18 = (bf16[2,1024]{1,0:T(2,128)(2,1)S(1)}, bf16[2,1024]{1,0:T(2,128)(2,1)S(1)}, u32[]{:S(2)}, u32[]{:S(2)}) collective-permute-start(bf16[2,1024]{1,0:T(2,128)(2,1)S(1)} %reduce_sum.9), channel_id=1, source_target_pairs={{0,0},{1,8},{2,16},{3,24},{4,4},{5,12},{6,20},{7,28},{8,1},{9,9},{... | collective-permute-start | bytes 12296 | tf_op jit(solution)/shard_map/dec_place/ppermute | solution.py:534
  66.8 1.0 %copy-start.7 = (bf16[512,512]{1,0:T(8,128)(2,1)S(1)}, bf16[512,512]{1,0:T(8,128)(2,1)}, u32[]{:S(2)}) copy-start(bf16[512,512]{1,0:T(8,128)(2,1)} %get-tuple-element.50.refs_0_) | copy-start | bytes 1572868
  68.8 7.8 %copy-start.8 = (f32[128,1024]{1,0:T(8,128)S(1)}, f32[128,1024]{1,0:T(8,128)}, u32[]{:S(2)}) copy-start(f32[128,1024]{1,0:T(8,128)} %get-tuple-element.38.refs_0_) | copy-start | bytes 1572868

commit v7 on v6

--- a/solution.py
+++ b/solution.py
@@ -289,24 +289,29 @@
 
 
 def own_kernel(mover, ins, outs, scratch):
-    cots_ref, attn_ref = scratch
-    mover.wait(mover.start(ins[0], cots_ref), mover.start(ins[1], attn_ref))
+    cot_hbm, attn_hbm, half_hbm, twin_hbm = ins
+    cots_ref, attn_ref, others_ref = scratch
+    _, core, _, _, _ = places()
+    size = half_hbm.shape[0]
+    arrive = [mover.start(cot_hbm, cots_ref), mover.start(attn_hbm, attn_ref)]
+    halves = [
+        mover.start(hbm, others_ref.at[pl.ds(pl.multiple_of((core ^ i) * size, size), size)])
+        for i, hbm in enumerate((half_hbm, twin_hbm))
+    ]
+    mover.wait(*arrive)
     outs[0][...] = over_tokens(cots_ref[...], attn_ref[...])
+    mover.wait(*halves)
+    outs[1][...] = others_ref[...].T
 
 
 def product_kernel(mover, ins, outs, scratch):
-    own_ref, attn_ref, *cot_refs = ins
-    cots_ref, out_ref = scratch
-    _, core, _, _, _ = places()
-    size = cot_refs[0].shape[0]
-    for i, ref in enumerate(cot_refs):
-        first = pl.multiple_of((core ^ i) * size, size)
-        cots_ref[pl.ds(first, size), :] = ref[...]
+    own_ref, attn_ref, turned_ref = ins
+    (out_ref,) = scratch
     pieces = 2
     step = out_ref.shape[0] // pieces
     for i in range(pieces):
         here = slice(i * step, (i + 1) * step)
-        out_ref[here, :] = own_ref[here, :] + over_tokens(cots_ref[:, here], attn_ref[...])
+        out_ref[here, :] = own_ref[here, :] + dot(turned_ref[here, :], attn_ref[...])
         mover.start(out_ref.at[here], outs[0].at[here])
     outs[1][...] = jnp.zeros(outs[1].shape, F32)
 
@@ -330,14 +335,16 @@
 
 def pack_kernel(early, skip, mover, ins, outs, scratch):
     low_hbm, high_hbm, own_hbm, *first_hbms = ins
-    cots_ref, attn_ref = scratch
+    cots_ref, attn_out = outs
+    (attn_ref,) = scratch
     tokens, size = own_hbm.shape[0], low_hbm.shape[0]
-    parts = [(low_hbm, cots_ref, outs[0], 0, size), (high_hbm, cots_ref, outs[0], size, size), (own_hbm, attn_ref, outs[1], 0, tokens)]
-    parts += [(hbm.at[skip:], attn_ref, outs[1], (k + 1) * tokens, early) for k, hbm in enumerate(first_hbms)]
-    arrive = [mover.start(source, ref.at[at : at + rows]) for source, ref, _, at, rows in parts]
-    for copy, (_, ref, out, at, rows) in zip(arrive, parts):
+    mover.start(low_hbm, cots_ref.at[:size])
+    mover.start(high_hbm, cots_ref.at[size:])
+    parts = [(own_hbm, 0, tokens)] + [(hbm.at[skip:], (k + 1) * tokens, early) for k, hbm in enumerate(first_hbms)]
+    arrive = [mover.start(source, attn_ref.at[at : at + rows]) for source, at, rows in parts]
+    for copy, (_, at, rows) in zip(arrive, parts):
         mover.wait(copy)
-        mover.start(ref.at[at : at + rows], out.at[at : at + rows])
+        mover.start(attn_ref.at[at : at + rows], attn_out.at[at : at + rows])
 
 
 def gate_kernel(count, early, *refs):
@@ -471,7 +478,7 @@
             ((outer * tokens, feats), BF16),
             ((outer * tokens, feats), BF16),
         ],
-        room=63,
+        room=12,
     )
     cots_x = [flip(a, "fsdp", 1, "cot_x") for a in (cot_low, cot_high)]
 
@@ -480,8 +487,8 @@
         "pack",
         [*cots_x, train_attn, *(got if plane == cols else firsts)],
         [((outer * half, feats), BF16), ((outer * tokens, cols), BF16)],
-        [((outer * half, feats), BF16), ((outer * tokens, cols), BF16)],
-        room=63,
+        [((outer * tokens, cols), BF16)],
+        fast=[0],
     )
 
     results = pl.pallas_call(
@@ -495,7 +502,7 @@
             pltpu.SemaphoreType.DMA((len(far),)),
         ],
         input_output_aliases={i: i for i in range(len(sent) + 1)},
-        compiler_params=pltpu.CompilerParams(vmem_limit_bytes=63 << 20),
+        compiler_params=pltpu.CompilerParams(vmem_limit_bytes=12 << 20),
         cost_estimate=pl.CostEstimate(flops=0, bytes_accessed=0, transcendentals=0),
         name="gate",
     )(*sent, pack, cots_x, *lasts[:0:-1])
@@ -532,22 +539,21 @@
         ]
         with jax.named_scope("dec_place"):
             pieces.append(lax.ppermute(lax.dynamic_index_in_dim(dec, z % share ^ j, 0, False), ("fsdp", "tp"), perm))
-    (own_total,) = call(
+    own_total, turned = call(
         own_kernel,
         "own",
-        [cot_own, pack],
-        [((feats, cols), F32)],
-        [((outer * tokens, feats), BF16), ((outer * tokens, cols), BF16)],
-        waits=[twin_x],
-        fast=[0],
+        [cot_own, pack, cots_x, twin_x],
+        [((feats, cols), F32), ((feats, outer * tokens), BF16)],
+        [((outer * tokens, feats), BF16), ((outer * tokens, cols), BF16), ((outer * tokens, feats), BF16)],
+        fast=[0, 1],
     )
     grad_weight, mark = call(
         product_kernel,
         "product",
-        [own_total, pack_x, cots_x, twin_x],
+        [own_total, pack_x, turned],
         [((feats, cols), F32), ((8, HD), F32)],
-        [((outer * tokens, feats), BF16), ((feats, cols), F32)],
-        near=range(4),
+        [((feats, cols), F32)],
+        near=range(3),
         fast=[1],
     )
     operands = [total, *sums[::-1], *pieces]

time: 79.3 us -> 77.7 us (0.980)
  the two profiles are of different devices: /device:TPU:12 before, /device:TPU:17 now
where the time goes in v7:
time: 77.7 us; the launch traced here: 76.3 us
  Pallas kernels  21.8 us (28%)
  starting transfers between devices  21.6 us (28%)
  waiting for transfers between devices  20.9 us (27%)
  blocking collectives  6.63 us (9%)
  local copies, waits for them, and re-layouts  3.83 us (5%)
  between operations  1.49 us (2%)
    pallas_call x8, Pallas kernels, call(): pl.pallas_call(body, out_shape=[jax.ShapeDtypeStruct(shape, dtype) for sh...  19.1 us
    ppermute x11, waiting for transfers between devices, flip(): return lax.ppermute(a, axis, [(i, i ^ bits) for i in range(size)])  13.2 us
    ppermute x9, starting transfers between devices, turn(): lax.ppermute(a, 'fsdp', [(z * INNER + x, (z + steps) % outer * INNER + x)...  10.5 us
    ppermute x11, starting transfers between devices, flip(): return lax.ppermute(a, axis, [(i, i ^ bits) for i in range(size)])  8.91 us
    all_to_all x1, blocking collectives, shards(): dec = lax.all_to_all(dec, 'tp', 0, 0, tiled=True).sum(axis=0).astype(BF16)  6.63 us
    ppermute x9, waiting for transfers between devices, turn(): lax.ppermute(a, 'fsdp', [(z * INNER + x, (z + steps) % outer * INNER + x)...  5.9 us
    unnamed x18, local copies, waits for them, and re-layouts  3.83 us
    ppermute x1, starting transfers between devices, shards(): lax.ppermute(lax.dynamic_index_in_dim(dec, z % share ^ j, 0, False), ('fs...  2.15 us
  transfers between devices with their start and end apart: 21, of which 10 were waited for; matrix products, arithmetic and copies ran while one was open for 0% of the time, Pallas kernels for 25%

profile of v7, /device:TPU:17, one launch (start us, length us, event | category | flops | bytes accessed | tf_op | source)
XLA Modules:
  0.0 76.3 jit_solution(11111027779544568877)
XLA Ops:
  0.6 1.3 %collective-permute-start = (bf16[512,1024]{1,0:T(8,128)(2,1)}, bf16[512,1024]{1,0:T(8,128)(2,1)}, u32[]{:S(2)}, u32[]{:S(2)}) collective-permute-start(bf16[512,1024]{1,0:T(8,128)(2,1)} %refs_0_.6), channel_id=1, source_target_pairs={{0,4},{4,0},{8,12},{12,8},{16,20},{20,16},{24,28},{28,24},{1,5},{5... | collective-permute-start | bytes 3145736 | tf_op jit(solution)/shard_map/weight_x/ppermute | solution.py:22
  1.9 1.9 %cut.1 = (bf16[80,1024]{1,0:T(8,128)(2,1)}, bf16[80,1024]{1,0:T(8,128)(2,1)}, bf16[80,1024]{1,0:T(8,128)(2,1)}) custom-call(bf16[128,4096]{1,0:T(8,128)(2,1)} %refs_0_.5, bf16[128,1024]{1,0:T(8,128)(2,1)} %refs_2_.3), custom_call_target="tpu_custom_call" | custom-call | tf_op jit(solution)/shard_map/cut/pallas_call | solution.py:82
  3.8 1.3 %collective-permute-start.1 = (bf16[80,1024]{1,0:T(8,128)(2,1)}, bf16[80,1024]{1,0:T(8,128)(2,1)S(1)}, u32[]{:S(2)}, u32[]{:S(2)}) collective-permute-start(bf16[80,1024]{1,0:T(8,128)(2,1)} %get-tuple-element.31), channel_id=1, source_target_pairs={{0,8},{4,12},{8,16},{12,20},{16,24},{20,28},{24,0},{28,4},{1,9},{5... | collective-permute-start | bytes 491528 | tf_op jit(solution)/shard_map/first_z1/ppermute | solution.py:28
  5.2 0.1 collective-permute-start.2
  5.2 1.2 %collective-permute-start.3 = (bf16[80,1024]{1,0:T(8,128)(2,1)}, bf16[80,1024]{1,0:T(8,128)(2,1)S(1)}, u32[]{:S(2)}, u32[]{:S(2)}) collective-permute-start(bf16[80,1024]{1,0:T(8,128)(2,1)} %get-tuple-element.33), channel_id=1, source_target_pairs={{0,24},{4,28},{8,0},{12,4},{16,8},{20,12},{24,16},{28,20},{1,25},{... | collective-permute-start | bytes 491528 | tf_op jit(solution)/shard_map/first_z3/ppermute | solution.py:28
  7.1 3.5 %attend.1 = (f32[40,256]{1,0:T(8,128)}, f32[1,16,256]{2,1,0:T(8,128)}, f32[2,16,256]{2,1,0:T(8,128)}) custom-call(s32[1]{0:T(128)S(6)} %copy.26.refs_0_, bf16[1,2,4096]{2,1,0:T(2,128)(2,1)} %refs_1_.4, bf16[1,512,512]{2,1,0:T(8,128)(2,1)} %refs_2_.2, bf16[1,512,512]{2,1,0:T(8,128)(2,1)} %refs_3_.1, bf16[1,2,512]{2,1,0:T(2,128)(2,1)} %refs_4_.1, ...), custom_call_target="tpu_custom_call" | custom-call | tf_op jit(solution)/shard_map/attend/pallas_call | solution.py:82
  10.6 0.0 copy-start
  10.6 1.7 %collective-permute-start.5 = (f32[1,16,256]{2,1,0:T(8,128)}, f32[1,16,256]{2,1,0:T(8,128)S(1)}, u32[]{:S(2)}, u32[]{:S(2)}) collective-permute-start(f32[1,16,256]{2,1,0:T(8,128)} %get-tuple-element.36), channel_id=1, source_target_pairs={{0,1},{1,0},{2,3},{3,2},{4,5},{5,4},{6,7},{7,6},{8,9},{9,8},{10,11... | collective-permute-start | bytes 49160 | tf_op jit(solution)/shard_map/softmax_tp1/ppermute | solution.py:22
  12.3 1.0 %collective-permute-done.5.refs_1_ = f32[1,16,256]{2,1,0:T(8,128)S(1)} collective-permute-done((f32[1,16,256]{2,1,0:T(8,128)}, f32[1,16,256]{2,1,0:T(8,128)S(1)}, u32[]{:S(2)}, u32[]{:S(2)}) %collective-permute-start.5) | collective-permute-done | bytes 16416 | tf_op jit(solution)/shard_map/softmax_tp1/ppermute | solution.py:22
  13.4 1.2 %collective-permute-start.4 = (f32[2,16,256]{2,1,0:T(8,128)}, f32[2,16,256]{2,1,0:T(8,128)S(1)}, u32[]{:S(2)}, u32[]{:S(2)}) collective-permute-start(f32[2,16,256]{2,1,0:T(8,128)} %get-tuple-element.35), channel_id=1, source_target_pairs={{0,2},{1,3},{2,0},{3,1},{4,6},{5,7},{6,4},{7,5},{8,10},{9,11},{10,... | collective-permute-start | bytes 98312 | tf_op jit(solution)/shard_map/softmax_tp2/ppermute | solution.py:22
  14.6 2.1 %collective-permute-done.4.refs_0_ = f32[2,16,256]{2,1,0:T(8,128)S(1)} collective-permute-done((f32[2,16,256]{2,1,0:T(8,128)}, f32[2,16,256]{2,1,0:T(8,128)S(1)}, u32[]{:S(2)}, u32[]{:S(2)}) %collective-permute-start.4) | collective-permute-done | bytes 32800 | tf_op jit(solution)/shard_map/softmax_tp2/ppermute | solution.py:22
  16.7 1.1 %collective-permute-start.6 = (f32[2,16,256]{2,1,0:T(8,128)S(1)}, f32[2,16,256]{2,1,0:T(8,128)S(1)}, u32[]{:S(2)}, u32[]{:S(2)}) collective-permute-start(f32[2,16,256]{2,1,0:T(8,128)S(1)} %collective-permute-done.4.refs_0_), channel_id=1, source_target_pairs={{0,1},{1,0},{2,3},{3,2},{4,5},{5,4},{6,7},{7,6},{8,9},{9,8},{10,11... | collective-permute-start | bytes 98312 | tf_op jit(solution)/shard_map/softmax_tp1/ppermute | solution.py:22
  17.8 0.8 %copy-done.8 = f32[40,256]{1,0:T(8,128)S(1)} copy-done((f32[40,256]{1,0:T(8,128)S(1)}, f32[40,256]{1,0:T(8,128)}, u32[]{:S(2)}) %copy-start.8) | copy-done | bytes 40984
  18.6 0.1 collective-permute-done.6.refs_2_
  18.7 0.9 %combine.1.refs_3_.refs_2_ = bf16[120,1024]{1,0:T(8,128)(2,1)S(1)} custom-call(bf16[128,1024]{1,0:T(8,128)(2,1)S(1)} %copy-done.3, f32[40,256]{1,0:T(8,128)S(1)} %hold.1.own_ref, f32[2,16,256]{2,1,0:T(8,128)S(1)} %collective-permute-done.4.refs_0_, f32[1,16,256]{2,1,0:T(8,128)S(1)} %collective-permute-done.5.refs_1_, ...), custom_call_target="tpu_custom_call" | custom-call | tf_op jit(solution)/shard_map/combine/pallas_call | solution.py:446
  19.6 0.1 collective-permute-done.3.refs_2_
  19.7 0.5 collective-permute-start.7
  20.2 0.0 collective-permute-start.8
  20.2 0.5 collective-permute-start.9
  20.7 2.3 %collective-permute-start.14 = (bf16[120,1024]{1,0:T(8,128)(2,1)S(1)}, bf16[120,1024]{1,0:T(8,128)(2,1)S(1)}, u32[]{:S(2)}, u32[]{:S(2)}) collective-permute-start(bf16[120,1024]{1,0:T(8,128)(2,1)S(1)} %combine.1.refs_3_.refs_2_), channel_id=1, source_target_pairs={{0,8},{4,12},{8,16},{12,20},{16,24},{20,28},{24,0},{28,4},{1,9},{5... | collective-permute-start | bytes 737288 | tf_op jit(solution)/shard_map/last_z1/ppermute | solution.py:28
  23.0 1.0 %collective-permute-start.13 = (bf16[120,1024]{1,0:T(8,128)(2,1)S(1)}, bf16[120,1024]{1,0:T(8,128)(2,1)S(1)}, u32[]{:S(2)}, u32[]{:S(2)}) collective-permute-start(bf16[120,1024]{1,0:T(8,128)(2,1)S(1)} %combine.1.refs_3_.refs_2_), channel_id=1, source_target_pairs={{0,16},{4,20},{8,24},{12,28},{16,0},{20,4},{24,8},{28,12},{1,17},{... | collective-permute-start | bytes 737288 | tf_op jit(solution)/shard_map/last_z2/ppermute | solution.py:28
  24.0 1.3 %collective-permute-start.12 = (bf16[120,1024]{1,0:T(8,128)(2,1)S(1)}, bf16[120,1024]{1,0:T(8,128)(2,1)S(1)}, u32[]{:S(2)}, u32[]{:S(2)}) collective-permute-start(bf16[120,1024]{1,0:T(8,128)(2,1)S(1)} %combine.1.refs_3_.refs_2_), channel_id=1, source_target_pairs={{0,24},{4,28},{8,0},{12,4},{16,8},{20,12},{24,16},{28,20},{1,25},{... | collective-permute-start | bytes 737288 | tf_op jit(solution)/shard_map/last_z3/ppermute | solution.py:28
  25.2 0.0 copy-start.1
  25.3 1.2 %copy-done.1 = bf16[512,1024]{1,0:T(8,128)(2,1)S(1)} copy-done((bf16[512,1024]{1,0:T(8,128)(2,1)S(1)}, bf16[512,1024]{1,0:T(8,128)(2,1)}, u32[]{:S(2)}) %copy-start.1) | copy-done | bytes 1048600
  26.5 4.1 %middle.1 = (bf16[128,1024]{1,0:T(8,128)(2,1)}, bf16[128,1024]{1,0:T(8,128)(2,1)}, bf16[128,1024]{1,0:T(8,128)(2,1)}, f32[128,1024]{1,0:T(8,128)S(1)}, bf16[512,...) custom-call(bf16[128,4096]{1,0:T(8,128)(2,1)S(1)} %copy-done, ...), custom_call_target="tpu_custom_call" | custom-call | tf_op jit(solution)/shard_map/middle/pallas_call | solution.py:82
  30.6 0.8 %copy-done.4 = f32[128,1024]{1,0:T(8,128)} copy-done((f32[128,1024]{1,0:T(8,128)}, f32[128,1024]{1,0:T(8,128)S(1)}, u32[]{:S(2)}) %copy-start.4) | copy-done | bytes 524312
  31.4 1.0 %collective-permute-start.10 = (bf16[128,512]{1,0:T(8,128)(2,1)S(1)}, bf16[128,512]{1,0:T(8,128)(2,1)S(1)}, u32[]{:S(2)}, u32[]{:S(2)}) collective-permute-start(bf16[128,512]{1,0:T(8,128)(2,1)S(1)} %get-tuple-element.44), channel_id=1, source_target_pairs={{0,4},{4,0},{8,12},{12,8},{16,20},{20,16},{24,28},{28,24},{1,5},{5... | collective-permute-start | bytes 393224 | tf_op jit(solution)/shard_map/cot_x/ppermute | solution.py:22
  32.4 0.5 collective-permute-start.11
  32.9 2.6 %collective-permute-done.10.refs_0_ = bf16[128,512]{1,0:T(8,128)(2,1)S(1)} collective-permute-done((bf16[128,512]{1,0:T(8,128)(2,1)S(1)}, bf16[128,512]{1,0:T(8,128)(2,1)S(1)}, u32[]{:S(2)}, u32[]{:S(2)}) %collective-permute-start.10) | collective-permute-done | bytes 131104 | tf_op jit(solution)/shard_map/cot_x/ppermute | solution.py:22
  35.5 2.3 %collective-permute-done.11.refs_1_ = bf16[128,512]{1,0:T(8,128)(2,1)S(1)} collective-permute-done((bf16[128,512]{1,0:T(8,128)(2,1)S(1)}, bf16[128,512]{1,0:T(8,128)(2,1)S(1)}, u32[]{:S(2)}, u32[]{:S(2)}) %collective-permute-start.11) | collective-permute-done | bytes 131104 | tf_op jit(solution)/shard_map/cot_x/ppermute | solution.py:22
  37.9 1.6 %pack.1 = (bf16[256,512]{1,0:T(8,128)(2,1)}, bf16[512,1024]{1,0:T(8,128)(2,1)S(1)}) custom-call(bf16[128,512]{1,0:T(8,128)(2,1)S(1)} %collective-permute-done.10.refs_0_, bf16[128,512]{1,0:T(8,128)(2,1)S(1)} %collective-permute-done.11.refs_1_, bf16[128,1024]{1,0:T(8,128)(2,1)S(1)} %copy-done.3, bf16[80,1024]{1,0:T(8,128)(2,1)S(1)} %get-tuple-element.37.refs_3_, ...), custom_call_target="tpu_custom_call" | custom-call | tf_op jit(solution)/shard_map/pack/pallas_call | solution.py:82
  39.5 0.5 collective-permute-done.13.refs_6_.refs_4_
  40.0 5.3 %collective-permute-done.12.refs_5_ = bf16[120,1024]{1,0:T(8,128)(2,1)S(1)} collective-permute-done((bf16[120,1024]{1,0:T(8,128)(2,1)S(1)}, bf16[120,1024]{1,0:T(8,128)(2,1)S(1)}, u32[]{:S(2)}, u32[]{:S(2)}) %collective-permute-start.12) | collective-permute-done | bytes 245792 | tf_op jit(solution)/shard_map/last_z3/ppermute | solution.py:28
  45.3 1.8 %gate.1 = (bf16[128,1024]{1,0:T(8,128)(2,1)}, bf16[128,1024]{1,0:T(8,128)(2,1)}, bf16[128,1024]{1,0:T(8,128)(2,1)}, bf16[512,1024]{1,0:T(8,128)(2,1)S(1)}) custom-call(bf16[128,1024]{1,0:T(8,128)(2,1)} %get-tuple-element.41.refs_0_, ...), custom_call_target="tpu_custom_call", output_to_operand_aliasing={{0}: (0, {}), {1}: (1, {}), {2}: (2, {}), {3}: (3, {})} | custom-call | tf_op jit(solution)/shard_map/gate/pallas_call | solution.py:494
  47.1 0.3 collective-permute-start.20
  47.4 0.8 collective-permute-start.19
  48.2 0.9 %collective-permute-start.15 = (bf16[128,1024]{1,0:T(8,128)(2,1)}, bf16[128,1024]{1,0:T(8,128)(2,1)S(1)}, u32[]{:S(2)}, u32[]{:S(2)}) collective-permute-start(bf16[128,1024]{1,0:T(8,128)(2,1)} %get-tuple-element.48), channel_id=1, source_target_pairs={{0,8},{4,12},{8,16},{12,20},{16,24},{20,28},{24,0},{28,4},{1,9},{5... | collective-permute-start | bytes 786440 | tf_op jit(solution)/shard_map/sum_z3/ppermute | solution.py:28
  49.1 2.5 %collective-permute-start.16 = (bf16[128,1024]{1,0:T(8,128)(2,1)}, bf16[128,1024]{1,0:T(8,128)(2,1)S(1)}, u32[]{:S(2)}, u32[]{:S(2)}) collective-permute-start(bf16[128,1024]{1,0:T(8,128)(2,1)} %get-tuple-element.49), channel_id=1, source_target_pairs={{0,16},{4,20},{8,24},{12,28},{16,0},{20,4},{24,8},{28,12},{1,17},{... | collective-permute-start | bytes 786440 | tf_op jit(solution)/shard_map/sum_z2/ppermute | solution.py:28
  51.6 3.5 %decode.1 = f32[4,1,2,1024]{3,2,1,0:T(2,128)S(1)} custom-call(bf16[512,1024]{1,0:T(8,128)(2,1)S(1)} %copy-done.2, bf16[512,1024]{1,0:T(8,128)(2,1)} %collective-permute-done.refs_2_.refs_1_, bf16[120,1024]{1,0:T(8,128)(2,1)S(1)} %combine.1.refs_3_.refs_2_, bf16[120,1024]{1,0:T(8,128)(2,1)S(1)} %collective-permute-done.14.refs_7_.refs_3_, ...), custom_call_target="tpu_custom_call" | custom-call | tf_op jit(solution)/shard_map/decode/pallas_call | solution.py:82
  55.1 6.6 %all_to_all.5 = f32[4,1,2,1024]{3,2,1,0:T(2,128)S(1)} all-to-all(f32[4,1,2,1024]{3,2,1,0:T(2,128)S(1)} %decode.1), channel_id=1, replica_groups=mesh['fsdp'=8,'tp'=4] {'tp'}, dimensions={0} | all-to-all | bytes 65536 | tf_op jit(solution)/shard_map/dec_tp/all_to_all | solution.py:531
  61.8 2.1 %collective-permute-start.18 = (bf16[2,1024]{1,0:T(2,128)(2,1)S(1)}, bf16[2,1024]{1,0:T(2,128)(2,1)S(1)}, u32[]{:S(2)}, u32[]{:S(2)}) collective-permute-start(bf16[2,1024]{1,0:T(2,128)(2,1)S(1)} %reduce_sum.9), channel_id=1, source_target_pairs={{0,0},{1,8},{2,16},{3,24},{4,4},{5,12},{6,20},{7,28},{8,1},{9,9},{... | collective-permute-start | bytes 12296 | tf_op jit(solution)/shard_map/dec_place/ppermute | solution.py:541
  63.9 0.0 copy-start.7
  63.9 1.0 %copy-done.7 = bf16[512,512]{1,0:T(8,128)(2,1)S(1)} copy-done((bf16[512,512]{1,0:T(8,128)(2,1)S(1)}, bf16[512,512]{1,0:T(8,128)(2,1)}, u32[]{:S(2)}) %copy-start.7) | copy-done | bytes 524312
  65.0 1.5 %own.1 = (f32[512,1024]{1,0:T(8,128)S(1)}, bf16[512,512]{1,0:T(8,128)(2,1)S(1)}) custom-call(bf16[512,512]{1,0:T(8,128)(2,1)S(1)} %copy-done.7, bf16[512,1024]{1,0:T(8,128)(2,1)S(1)} %get-tuple-element.51.refs_6_.refs_1_, bf16[256,512]{1,0:T(8,128)(2,1)} %get-tuple-element.47.refs_4_.refs_2_, bf16[256,512]{1,0:T(8,128)(2,1)S(1)} %collective-permute-done.19.refs_3_), custom_call_target="tpu_custom_call" | custom-call | tf_op jit(solution)/shard_map/own/pallas_call | solution.py:82
  66.4 5.0 %collective-permute-done.20.refs_1_ = bf16[512,1024]{1,0:T(8,128)(2,1)S(1)} collective-permute-done((bf16[512,1024]{1,0:T(8,128)(2,1)S(1)}, bf16[512,1024]{1,0:T(8,128)(2,1)S(1)}, u32[]{:S(2)}, u32[]{:S(2)}) %collective-permute-start.20) | collective-permute-done | bytes 1048608 | tf_op jit(solution)/shard_map/attn_x/ppermute | solution.py:22
  71.4 2.0 %product.1 = (f32[512,1024]{1,0:T(8,128)}, f32[8,128]{1,0:T(8,128)S(1)}) custom-call(f32[512,1024]{1,0:T(8,128)S(1)} %get-tuple-element.53.refs_0_, bf16[512,1024]{1,0:T(8,128)(2,1)S(1)} %collective-permute-done.20.refs_1_, bf16[512,512]{1,0:T(8,128)(2,1)S(1)} %get-tuple-element.54.refs_2_), custom_call_target="tpu_custom_call" | custom-call | tf_op jit(solution)/shard_map/product/pallas_call | solution.py:82
  73.4 1.8 %collective-permute-done.18.refs_4_ = bf16[2,1024]{1,0:T(2,128)(2,1)S(1)} collective-permute-done((bf16[2,1024]{1,0:T(2,128)(2,1)S(1)}, bf16[2,1024]{1,0:T(2,128)(2,1)S(1)}, u32[]{:S(2)}, u32[]{:S(2)}) %collective-permute-start.18) | collective-permute-done | bytes 4128 | tf_op jit(solution)/shard_map/dec_place/ppermute | solution.py:541
  75.2 1.1 %sum.1 = (bf16[1,2,1024]{2,1,0:T(2,128)(2,1)}, bf16[128,1024]{1,0:T(8,128)(2,1)}) custom-call(f32[128,1024]{1,0:T(8,128)S(1)} %copy-done.5, bf16[128,1024]{1,0:T(8,128)(2,1)S(1)} %collective-permute-done.15.refs_1_, bf16[128,1024]{1,0:T(8,128)(2,1)S(1)} %collective-permute-done.16.refs_2_, bf16[128,1024]{1,0:T(8,128)(2,1)S(1)} %collective-permute-done.17.refs_3_, ...), custom_call_target="tpu_custom_call" | custom-call | tf_op jit(solution)/shard_map/sum/pallas_call | solution.py:82
  (26 shorter events, 0.1 us)
Async XLA Ops:
  0.6 18.1 %copy-start.3 = (bf16[128,1024]{1,0:T(8,128)(2,1)S(1)}, bf16[128,1024]{1,0:T(8,128)(2,1)}, u32[]{:S(2)}) copy-start(bf16[128,1024]{1,0:T(8,128)(2,1)} %refs_2_.3) | copy-start | bytes 786436
  0.6 24.6 %collective-permute-start = (bf16[512,1024]{1,0:T(8,128)(2,1)}, bf16[512,1024]{1,0:T(8,128)(2,1)}, u32[]{:S(2)}, u32[]{:S(2)}) collective-permute-start(bf16[512,1024]{1,0:T(8,128)(2,1)} %refs_0_.6), channel_id=1, source_target_pairs={{0,4},{4,0},{8,12},{12,8},{16,20},{20,16},{24,28},{28,24},{1,5},{5... | collective-permute-start | bytes 3145736 | tf_op jit(solution)/shard_map/weight_x/ppermute | solution.py:22
  3.8 15.7 %collective-permute-start.1 = (bf16[80,1024]{1,0:T(8,128)(2,1)}, bf16[80,1024]{1,0:T(8,128)(2,1)S(1)}, u32[]{:S(2)}, u32[]{:S(2)}) collective-permute-start(bf16[80,1024]{1,0:T(8,128)(2,1)} %get-tuple-element.31), channel_id=1, source_target_pairs={{0,8},{4,12},{8,16},{12,20},{16,24},{20,28},{24,0},{28,4},{1,9},{5... | collective-permute-start | bytes 491528 | tf_op jit(solution)/shard_map/first_z1/ppermute | solution.py:28
  5.2 14.4 %collective-permute-start.2 = (bf16[80,1024]{1,0:T(8,128)(2,1)}, bf16[80,1024]{1,0:T(8,128)(2,1)S(1)}, u32[]{:S(2)}, u32[]{:S(2)}) collective-permute-start(bf16[80,1024]{1,0:T(8,128)(2,1)} %get-tuple-element.32), channel_id=1, source_target_pairs={{0,16},{4,20},{8,24},{12,28},{16,0},{20,4},{24,8},{28,12},{1,17},{... | collective-permute-start | bytes 491528 | tf_op jit(solution)/shard_map/first_z2/ppermute | solution.py:28
  5.2 14.4 %collective-permute-start.3 = (bf16[80,1024]{1,0:T(8,128)(2,1)}, bf16[80,1024]{1,0:T(8,128)(2,1)S(1)}, u32[]{:S(2)}, u32[]{:S(2)}) collective-permute-start(bf16[80,1024]{1,0:T(8,128)(2,1)} %get-tuple-element.33), channel_id=1, source_target_pairs={{0,24},{4,28},{8,0},{12,4},{16,8},{20,12},{24,16},{28,20},{1,25},{... | collective-permute-start | bytes 491528 | tf_op jit(solution)/shard_map/first_z3/ppermute | solution.py:28
  10.6 14.7 %copy-start = (bf16[128,4096]{1,0:T(8,128)(2,1)S(1)}, bf16[128,4096]{1,0:T(8,128)(2,1)}, u32[]{:S(2)}) copy-start(bf16[128,4096]{1,0:T(8,128)(2,1)} %refs_0_.5) | copy-start | bytes 3145732
  10.6 2.8 %collective-permute-start.5 = (f32[1,16,256]{2,1,0:T(8,128)}, f32[1,16,256]{2,1,0:T(8,128)S(1)}, u32[]{:S(2)}, u32[]{:S(2)}) collective-permute-start(f32[1,16,256]{2,1,0:T(8,128)} %get-tuple-element.36), channel_id=1, source_target_pairs={{0,1},{1,0},{2,3},{3,2},{4,5},{5,4},{6,7},{7,6},{8,9},{9,8},{10,11... | collective-permute-start | bytes 49160 | tf_op jit(solution)/shard_map/softmax_tp1/ppermute | solution.py:22
  13.4 3.4 %collective-permute-start.4 = (f32[2,16,256]{2,1,0:T(8,128)}, f32[2,16,256]{2,1,0:T(8,128)S(1)}, u32[]{:S(2)}, u32[]{:S(2)}) collective-permute-start(f32[2,16,256]{2,1,0:T(8,128)} %get-tuple-element.35), channel_id=1, source_target_pairs={{0,2},{1,3},{2,0},{3,1},{4,6},{5,7},{6,4},{7,5},{8,10},{9,11},{10,... | collective-permute-start | bytes 98312 | tf_op jit(solution)/shard_map/softmax_tp2/ppermute | solution.py:22
  16.7 2.0 %collective-permute-start.6 = (f32[2,16,256]{2,1,0:T(8,128)S(1)}, f32[2,16,256]{2,1,0:T(8,128)S(1)}, u32[]{:S(2)}, u32[]{:S(2)}) collective-permute-start(f32[2,16,256]{2,1,0:T(8,128)S(1)} %collective-permute-done.4.refs_0_), channel_id=1, source_target_pairs={{0,1},{1,0},{2,3},{3,2},{4,5},{5,4},{6,7},{7,6},{8,9},{9,8},{10,11... | collective-permute-start | bytes 98312 | tf_op jit(solution)/shard_map/softmax_tp1/ppermute | solution.py:22
  17.8 0.8 %copy-start.8 = (f32[40,256]{1,0:T(8,128)S(1)}, f32[40,256]{1,0:T(8,128)}, u32[]{:S(2)}) copy-start(f32[40,256]{1,0:T(8,128)} %get-tuple-element.34.in_ref) | copy-start | bytes 122884
  19.7 3.3 %collective-permute-start.7 = (bf16[80,1024]{1,0:T(8,128)(2,1)S(1)}, bf16[80,1024]{1,0:T(8,128)(2,1)S(1)}, u32[]{:S(2)}, u32[]{:S(2)}) collective-permute-start(bf16[80,1024]{1,0:T(8,128)(2,1)S(1)} %get-tuple-element.37.refs_3_), channel_id=1, source_target_pairs={{0,1},{1,0},{2,3},{3,2},{4,5},{5,4},{6,7},{7,6},{8,9},{9,8},{10,11... | collective-permute-start | bytes 491528 | tf_op jit(solution)/shard_map/cot_core/ppermute | solution.py:22
  20.2 3.8 %collective-permute-start.8 = (bf16[80,1024]{1,0:T(8,128)(2,1)S(1)}, bf16[80,1024]{1,0:T(8,128)(2,1)S(1)}, u32[]{:S(2)}, u32[]{:S(2)}) collective-permute-start(bf16[80,1024]{1,0:T(8,128)(2,1)S(1)} %get-tuple-element.38.refs_4_), channel_id=1, source_target_pairs={{0,1},{1,0},{2,3},{3,2},{4,5},{5,4},{6,7},{7,6},{8,9},{9,8},{10,11... | collective-permute-start | bytes 491528 | tf_op jit(solution)/shard_map/cot_core/ppermute | solution.py:22
  20.2 5.0 %collective-permute-start.9 = (bf16[80,1024]{1,0:T(8,128)(2,1)S(1)}, bf16[80,1024]{1,0:T(8,128)(2,1)S(1)}, u32[]{:S(2)}, u32[]{:S(2)}) collective-permute-start(bf16[80,1024]{1,0:T(8,128)(2,1)S(1)} %get-tuple-element.39.refs_5_), channel_id=1, source_target_pairs={{0,1},{1,0},{2,3},{3,2},{4,5},{5,4},{6,7},{7,6},{8,9},{9,8},{10,11... | collective-permute-start | bytes 491528 | tf_op jit(solution)/shard_map/cot_core/ppermute | solution.py:22
  20.7 18.8 %collective-permute-start.14 = (bf16[120,1024]{1,0:T(8,128)(2,1)S(1)}, bf16[120,1024]{1,0:T(8,128)(2,1)S(1)}, u32[]{:S(2)}, u32[]{:S(2)}) collective-permute-start(bf16[120,1024]{1,0:T(8,128)(2,1)S(1)} %combine.1.refs_3_.refs_2_), channel_id=1, source_target_pairs={{0,8},{4,12},{8,16},{12,20},{16,24},{20,28},{24,0},{28,4},{1,9},{5... | collective-permute-start | bytes 737288 | tf_op jit(solution)/shard_map/last_z1/ppermute | solution.py:28
  23.0 17.1 %collective-permute-start.13 = (bf16[120,1024]{1,0:T(8,128)(2,1)S(1)}, bf16[120,1024]{1,0:T(8,128)(2,1)S(1)}, u32[]{:S(2)}, u32[]{:S(2)}) collective-permute-start(bf16[120,1024]{1,0:T(8,128)(2,1)S(1)} %combine.1.refs_3_.refs_2_), channel_id=1, source_target_pairs={{0,16},{4,20},{8,24},{12,28},{16,0},{20,4},{24,8},{28,12},{1,17},{... | collective-permute-start | bytes 737288 | tf_op jit(solution)/shard_map/last_z2/ppermute | solution.py:28
  24.0 21.3 %collective-permute-start.12 = (bf16[120,1024]{1,0:T(8,128)(2,1)S(1)}, bf16[120,1024]{1,0:T(8,128)(2,1)S(1)}, u32[]{:S(2)}, u32[]{:S(2)}) collective-permute-start(bf16[120,1024]{1,0:T(8,128)(2,1)S(1)} %combine.1.refs_3_.refs_2_), channel_id=1, source_target_pairs={{0,24},{4,28},{8,0},{12,4},{16,8},{20,12},{24,16},{28,20},{1,25},{... | collective-permute-start | bytes 737288 | tf_op jit(solution)/shard_map/last_z3/ppermute | solution.py:28
  25.2 1.2 %copy-start.1 = (bf16[512,1024]{1,0:T(8,128)(2,1)S(1)}, bf16[512,1024]{1,0:T(8,128)(2,1)}, u32[]{:S(2)}) copy-start(bf16[512,1024]{1,0:T(8,128)(2,1)} %refs_0_.6) | copy-start | bytes 3145732
  30.6 0.8 %copy-start.4 = (f32[128,1024]{1,0:T(8,128)}, f32[128,1024]{1,0:T(8,128)S(1)}, u32[]{:S(2)}) copy-start(f32[128,1024]{1,0:T(8,128)S(1)} %get-tuple-element.40.refs_0_) | copy-start | bytes 1572868
  31.4 23.7 %copy-start.6 = (bf16[512,512]{1,0:T(8,128)(2,1)}, bf16[512,512]{1,0:T(8,128)(2,1)S(1)}, u32[]{:S(2)}) copy-start(bf16[512,512]{1,0:T(8,128)(2,1)S(1)} %get-tuple-element.52.refs_0_) | copy-start | bytes 1572868
  31.4 20.2 %copy-start.2 = (bf16[512,1024]{1,0:T(8,128)(2,1)S(1)}, bf16[512,1024]{1,0:T(8,128)(2,1)}, u32[]{:S(2)}) copy-start(bf16[512,1024]{1,0:T(8,128)(2,1)} %refs_0_.6) | copy-start | bytes 3145732
  31.4 4.1 %collective-permute-start.10 = (bf16[128,512]{1,0:T(8,128)(2,1)S(1)}, bf16[128,512]{1,0:T(8,128)(2,1)S(1)}, u32[]{:S(2)}, u32[]{:S(2)}) collective-permute-start(bf16[128,512]{1,0:T(8,128)(2,1)S(1)} %get-tuple-element.44), channel_id=1, source_target_pairs={{0,4},{4,0},{8,12},{12,8},{16,20},{20,16},{24,28},{28,24},{1,5},{5... | collective-permute-start | bytes 393224 | tf_op jit(solution)/shard_map/cot_x/ppermute | solution.py:22
  32.4 5.5 %collective-permute-start.11 = (bf16[128,512]{1,0:T(8,128)(2,1)S(1)}, bf16[128,512]{1,0:T(8,128)(2,1)S(1)}, u32[]{:S(2)}, u32[]{:S(2)}) collective-permute-start(bf16[128,512]{1,0:T(8,128)(2,1)S(1)} %get-tuple-element.45), channel_id=1, source_target_pairs={{0,4},{4,0},{8,12},{12,8},{16,20},{20,16},{24,28},{28,24},{1,5},{5... | collective-permute-start | bytes 393224 | tf_op jit(solution)/shard_map/cot_x/ppermute | solution.py:22
  47.1 24.3 %collective-permute-start.20 = (bf16[512,1024]{1,0:T(8,128)(2,1)S(1)}, bf16[512,1024]{1,0:T(8,128)(2,1)S(1)}, u32[]{:S(2)}, u32[]{:S(2)}) collective-permute-start(bf16[512,1024]{1,0:T(8,128)(2,1)S(1)} %get-tuple-element.51.refs_6_.refs_1_), channel_id=1, source_target_pairs={{0,4},{4,0},{8,12},{12,8},{16,20},{20,16},{24,28},{28,24},{1,5},{5... | collective-permute-start | bytes 3145736 | tf_op jit(solution)/shard_map/attn_x/ppermute | solution.py:22
  47.4 14.3 %collective-permute-start.19 = (bf16[256,512]{1,0:T(8,128)(2,1)}, bf16[256,512]{1,0:T(8,128)(2,1)S(1)}, u32[]{:S(2)}, u32[]{:S(2)}) collective-permute-start(bf16[256,512]{1,0:T(8,128)(2,1)} %get-tuple-element.47.refs_4_.refs_2_), channel_id=1, source_target_pairs={{0,1},{1,0},{2,3},{3,2},{4,5},{5,4},{6,7},{7,6},{8,9},{9,8},{10,11... | collective-permute-start | bytes 786440 | tf_op jit(solution)/shard_map/cot_x_core/ppermute | solution.py:22
  48.2 27.0 %collective-permute-start.15 = (bf16[128,1024]{1,0:T(8,128)(2,1)}, bf16[128,1024]{1,0:T(8,128)(2,1)S(1)}, u32[]{:S(2)}, u32[]{:S(2)}) collective-permute-start(bf16[128,1024]{1,0:T(8,128)(2,1)} %get-tuple-element.48), channel_id=1, source_target_pairs={{0,8},{4,12},{8,16},{12,20},{16,24},{20,28},{24,0},{28,4},{1,9},{5... | collective-permute-start | bytes 786440 | tf_op jit(solution)/shard_map/sum_z3/ppermute | solution.py:28
  49.1 26.1 %collective-permute-start.16 = (bf16[128,1024]{1,0:T(8,128)(2,1)}, bf16[128,1024]{1,0:T(8,128)(2,1)S(1)}, u32[]{:S(2)}, u32[]{:S(2)}) collective-permute-start(bf16[128,1024]{1,0:T(8,128)(2,1)} %get-tuple-element.49), channel_id=1, source_target_pairs={{0,16},{4,20},{8,24},{12,28},{16,0},{20,4},{24,8},{28,12},{1,17},{... | collective-permute-start | bytes 786440 | tf_op jit(solution)/shard_map/sum_z2/ppermute | solution.py:28
  51.6 23.6 %collective-permute-start.17 = (bf16[128,1024]{1,0:T(8,128)(2,1)}, bf16[128,1024]{1,0:T(8,128)(2,1)S(1)}, u32[]{:S(2)}, u32[]{:S(2)}) collective-permute-start(bf16[128,1024]{1,0:T(8,128)(2,1)} %get-tuple-element.50), channel_id=1, source_target_pairs={{0,24},{4,28},{8,0},{12,4},{16,8},{20,12},{24,16},{28,20},{1,25},{... | collective-permute-start | bytes 786440 | tf_op jit(solution)/shard_map/sum_z1/ppermute | solution.py:28
  61.8 13.4 %collective-permute-start.18 = (bf16[2,1024]{1,0:T(2,128)(2,1)S(1)}, bf16[2,1024]{1,0:T(2,128)(2,1)S(1)}, u32[]{:S(2)}, u32[]{:S(2)}) collective-permute-start(bf16[2,1024]{1,0:T(2,128)(2,1)S(1)} %reduce_sum.9), channel_id=1, source_target_pairs={{0,0},{1,8},{2,16},{3,24},{4,4},{5,12},{6,20},{7,28},{8,1},{9,9},{... | collective-permute-start | bytes 12296 | tf_op jit(solution)/shard_map/dec_place/ppermute | solution.py:541
  63.9 1.0 %copy-start.7 = (bf16[512,512]{1,0:T(8,128)(2,1)S(1)}, bf16[512,512]{1,0:T(8,128)(2,1)}, u32[]{:S(2)}) copy-start(bf16[512,512]{1,0:T(8,128)(2,1)} %copy-done.6) | copy-start | bytes 1572868
  66.4 8.8 %copy-start.5 = (f32[128,1024]{1,0:T(8,128)S(1)}, f32[128,1024]{1,0:T(8,128)}, u32[]{:S(2)}) copy-start(f32[128,1024]{1,0:T(8,128)} %copy-done.4) | copy-start | bytes 1572868

commit v8 on v7

--- a/solution.py
+++ b/solution.py
@@ -307,7 +307,7 @@
 def product_kernel(mover, ins, outs, scratch):
     own_ref, attn_ref, turned_ref = ins
     (out_ref,) = scratch
-    pieces = 2
+    pieces = 4
     step = out_ref.shape[0] // pieces
     for i in range(pieces):
         here = slice(i * step, (i + 1) * step)
@@ -388,7 +388,7 @@
 
     half = tokens // 2
 
-    early = tokens // 8
+    early = tokens // 4
     cot_rows = half * plane // cols
     if plane == cols:
         cuts = call(

time: 77.7 us -> 76.3 us (0.982)
  Pallas kernels: 21.8 us -> 20.8 us
    ppermute x1, starting transfers between devices: 2.15 us -> 3.25 us  [shards(): lax.ppermute(lax.dynamic_index_in_dim(dec, z % share ^ j, 0, False), ('fs...]
  transfers between devices with their start and end apart: 21 -> 21, of which waited for: 10 -> 9; matrix products, arithmetic and copies ran while one was open for 0% -> 0% of each run, Pallas kernels for 25% -> 24%
where the time goes in v8:
time: 76.3 us; the launch traced here: 75 us
  starting transfers between devices  22.2 us (29%)
  Pallas kernels  20.8 us (27%)
  waiting for transfers between devices  20.8 us (27%)
  blocking collectives  6.62 us (9%)
  local copies, waits for them, and re-layouts  3.07 us (4%)
  between operations  1.52 us (2%)
    pallas_call x8, Pallas kernels, call(): pl.pallas_call(body, out_shape=[jax.ShapeDtypeStruct(shape, dtype) for sh...  18.4 us
    ppermute x11, waiting for transfers between devices, flip(): return lax.ppermute(a, axis, [(i, i ^ bits) for i in range(size)])  12.7 us
    ppermute x9, starting transfers between devices, turn(): lax.ppermute(a, 'fsdp', [(z * INNER + x, (z + steps) % outer * INNER + x)...  10 us
    ppermute x11, starting transfers between devices, flip(): return lax.ppermute(a, axis, [(i, i ^ bits) for i in range(size)])  8.97 us
    all_to_all x1, blocking collectives, shards(): dec = lax.all_to_all(dec, 'tp', 0, 0, tiled=True).sum(axis=0).astype(BF16)  6.62 us
    ppermute x9, waiting for transfers between devices, turn(): lax.ppermute(a, 'fsdp', [(z * INNER + x, (z + steps) % outer * INNER + x)...  6.17 us
    ppermute x1, starting transfers between devices, shards(): lax.ppermute(lax.dynamic_index_in_dim(dec, z % share ^ j, 0, False), ('fs...  3.25 us
    unnamed x18, local copies, waits for them, and re-layouts  3.07 us
  transfers between devices with their start and end apart: 21, of which 9 were waited for; matrix products, arithmetic and copies ran while one was open for 0% of the time, Pallas kernels for 24%

profile of v8, /device:TPU:17, one launch (start us, length us, event | category | flops | bytes accessed | tf_op | source)
XLA Modules:
  0.0 75.0 jit_solution(18272522544934707556)
XLA Ops:
  0.6 1.3 %collective-permute-start = (bf16[512,1024]{1,0:T(8,128)(2,1)}, bf16[512,1024]{1,0:T(8,128)(2,1)}, u32[]{:S(2)}, u32[]{:S(2)}) collective-permute-start(bf16[512,1024]{1,0:T(8,128)(2,1)} %refs_0_.6), channel_id=1, source_target_pairs={{0,4},{4,0},{8,12},{12,8},{16,20},{20,16},{24,28},{28,24},{1,5},{5... | collective-permute-start | bytes 3145736 | tf_op jit(solution)/shard_map/weight_x/ppermute | solution.py:22
  1.9 2.0 %cut.1 = (bf16[96,1024]{1,0:T(8,128)(2,1)}, bf16[96,1024]{1,0:T(8,128)(2,1)}, bf16[96,1024]{1,0:T(8,128)(2,1)}) custom-call(bf16[128,4096]{1,0:T(8,128)(2,1)} %refs_0_.5, bf16[128,1024]{1,0:T(8,128)(2,1)} %refs_2_.3), custom_call_target="tpu_custom_call" | custom-call | tf_op jit(solution)/shard_map/cut/pallas_call | solution.py:82
  3.9 1.3 %collective-permute-start.1 = (bf16[96,1024]{1,0:T(8,128)(2,1)}, bf16[96,1024]{1,0:T(8,128)(2,1)S(1)}, u32[]{:S(2)}, u32[]{:S(2)}) collective-permute-start(bf16[96,1024]{1,0:T(8,128)(2,1)} %get-tuple-element.31), channel_id=1, source_target_pairs={{0,8},{4,12},{8,16},{12,20},{16,24},{20,28},{24,0},{28,4},{1,9},{5... | collective-permute-start | bytes 589832 | tf_op jit(solution)/shard_map/first_z1/ppermute | solution.py:28
  5.2 0.1 collective-permute-start.2
  5.3 1.2 %collective-permute-start.3 = (bf16[96,1024]{1,0:T(8,128)(2,1)}, bf16[96,1024]{1,0:T(8,128)(2,1)S(1)}, u32[]{:S(2)}, u32[]{:S(2)}) collective-permute-start(bf16[96,1024]{1,0:T(8,128)(2,1)} %get-tuple-element.33), channel_id=1, source_target_pairs={{0,24},{4,28},{8,0},{12,4},{16,8},{20,12},{24,16},{28,20},{1,25},{... | collective-permute-start | bytes 589832 | tf_op jit(solution)/shard_map/first_z3/ppermute | solution.py:28
  7.1 3.4 %attend.1 = (f32[40,256]{1,0:T(8,128)}, f32[1,16,256]{2,1,0:T(8,128)}, f32[2,16,256]{2,1,0:T(8,128)}) custom-call(s32[1]{0:T(128)S(6)} %copy.26.refs_0_, bf16[1,2,4096]{2,1,0:T(2,128)(2,1)} %refs_1_.4, bf16[1,512,512]{2,1,0:T(8,128)(2,1)} %refs_2_.2, bf16[1,512,512]{2,1,0:T(8,128)(2,1)} %refs_3_.1, bf16[1,2,512]{2,1,0:T(2,128)(2,1)} %refs_4_.1, ...), custom_call_target="tpu_custom_call" | custom-call | tf_op jit(solution)/shard_map/attend/pallas_call | solution.py:82
  10.6 0.0 copy-start
  10.6 1.7 %collective-permute-start.5 = (f32[1,16,256]{2,1,0:T(8,128)}, f32[1,16,256]{2,1,0:T(8,128)S(1)}, u32[]{:S(2)}, u32[]{:S(2)}) collective-permute-start(f32[1,16,256]{2,1,0:T(8,128)} %get-tuple-element.36), channel_id=1, source_target_pairs={{0,1},{1,0},{2,3},{3,2},{4,5},{5,4},{6,7},{7,6},{8,9},{9,8},{10,11... | collective-permute-start | bytes 49160 | tf_op jit(solution)/shard_map/softmax_tp1/ppermute | solution.py:22
  12.3 1.0 %collective-permute-done.5.refs_1_ = f32[1,16,256]{2,1,0:T(8,128)S(1)} collective-permute-done((f32[1,16,256]{2,1,0:T(8,128)}, f32[1,16,256]{2,1,0:T(8,128)S(1)}, u32[]{:S(2)}, u32[]{:S(2)}) %collective-permute-start.5) | collective-permute-done | bytes 16416 | tf_op jit(solution)/shard_map/softmax_tp1/ppermute | solution.py:22
  13.4 1.2 %collective-permute-start.4 = (f32[2,16,256]{2,1,0:T(8,128)}, f32[2,16,256]{2,1,0:T(8,128)S(1)}, u32[]{:S(2)}, u32[]{:S(2)}) collective-permute-start(f32[2,16,256]{2,1,0:T(8,128)} %get-tuple-element.35), channel_id=1, source_target_pairs={{0,2},{1,3},{2,0},{3,1},{4,6},{5,7},{6,4},{7,5},{8,10},{9,11},{10,... | collective-permute-start | bytes 98312 | tf_op jit(solution)/shard_map/softmax_tp2/ppermute | solution.py:22
  14.6 2.1 %collective-permute-done.4.refs_0_ = f32[2,16,256]{2,1,0:T(8,128)S(1)} collective-permute-done((f32[2,16,256]{2,1,0:T(8,128)}, f32[2,16,256]{2,1,0:T(8,128)S(1)}, u32[]{:S(2)}, u32[]{:S(2)}) %collective-permute-start.4) | collective-permute-done | bytes 32800 | tf_op jit(solution)/shard_map/softmax_tp2/ppermute | solution.py:22
  16.8 1.1 %collective-permute-start.6 = (f32[2,16,256]{2,1,0:T(8,128)S(1)}, f32[2,16,256]{2,1,0:T(8,128)S(1)}, u32[]{:S(2)}, u32[]{:S(2)}) collective-permute-start(f32[2,16,256]{2,1,0:T(8,128)S(1)} %collective-permute-done.4.refs_0_), channel_id=1, source_target_pairs={{0,1},{1,0},{2,3},{3,2},{4,5},{5,4},{6,7},{7,6},{8,9},{9,8},{10,11... | collective-permute-start | bytes 98312 | tf_op jit(solution)/shard_map/softmax_tp1/ppermute | solution.py:22
  17.9 0.8 %copy-done.8 = f32[40,256]{1,0:T(8,128)S(1)} copy-done((f32[40,256]{1,0:T(8,128)S(1)}, f32[40,256]{1,0:T(8,128)}, u32[]{:S(2)}) %copy-start.8) | copy-done | bytes 40984
  18.6 0.1 collective-permute-done.6.refs_2_
  18.7 0.8 %combine.1.refs_3_.refs_2_ = bf16[104,1024]{1,0:T(8,128)(2,1)S(1)} custom-call(bf16[128,1024]{1,0:T(8,128)(2,1)S(1)} %copy-done.3, f32[40,256]{1,0:T(8,128)S(1)} %hold.1.own_ref, f32[2,16,256]{2,1,0:T(8,128)S(1)} %collective-permute-done.4.refs_0_, f32[1,16,256]{2,1,0:T(8,128)S(1)} %collective-permute-done.5.refs_1_, ...), custom_call_target="tpu_custom_call" | custom-call | tf_op jit(solution)/shard_map/combine/pallas_call | solution.py:446
  19.5 3.0 %collective-permute-done.3.refs_2_ = bf16[96,1024]{1,0:T(8,128)(2,1)S(1)} collective-permute-done((bf16[96,1024]{1,0:T(8,128)(2,1)}, bf16[96,1024]{1,0:T(8,128)(2,1)S(1)}, u32[]{:S(2)}, u32[]{:S(2)}) %collective-permute-start.3) | collective-permute-done | bytes 196640 | tf_op jit(solution)/shard_map/first_z3/ppermute | solution.py:28
  22.5 0.5 collective-permute-start.7
  23.0 0.0 collective-permute-start.8
  23.0 0.5 collective-permute-start.9
  23.5 2.3 %collective-permute-start.14 = (bf16[104,1024]{1,0:T(8,128)(2,1)S(1)}, bf16[104,1024]{1,0:T(8,128)(2,1)S(1)}, u32[]{:S(2)}, u32[]{:S(2)}) collective-permute-start(bf16[104,1024]{1,0:T(8,128)(2,1)S(1)} %combine.1.refs_3_.refs_2_), channel_id=1, source_target_pairs={{0,8},{4,12},{8,16},{12,20},{16,24},{20,28},{24,0},{28,4},{1,9},{5... | collective-permute-start | bytes 638984 | tf_op jit(solution)/shard_map/last_z1/ppermute | solution.py:28
  25.8 1.0 %collective-permute-start.13 = (bf16[104,1024]{1,0:T(8,128)(2,1)S(1)}, bf16[104,1024]{1,0:T(8,128)(2,1)S(1)}, u32[]{:S(2)}, u32[]{:S(2)}) collective-permute-start(bf16[104,1024]{1,0:T(8,128)(2,1)S(1)} %combine.1.refs_3_.refs_2_), channel_id=1, source_target_pairs={{0,16},{4,20},{8,24},{12,28},{16,0},{20,4},{24,8},{28,12},{1,17},{... | collective-permute-start | bytes 638984 | tf_op jit(solution)/shard_map/last_z2/ppermute | solution.py:28
  26.8 0.7 collective-permute-start.12
  27.6 0.0 copy-start.1
  27.6 1.2 %copy-done.1 = bf16[512,1024]{1,0:T(8,128)(2,1)S(1)} copy-done((bf16[512,1024]{1,0:T(8,128)(2,1)S(1)}, bf16[512,1024]{1,0:T(8,128)(2,1)}, u32[]{:S(2)}) %copy-start.1) | copy-done | bytes 1048600
  28.8 4.1 %middle.1 = (bf16[128,1024]{1,0:T(8,128)(2,1)}, bf16[128,1024]{1,0:T(8,128)(2,1)}, bf16[128,1024]{1,0:T(8,128)(2,1)}, f32[128,1024]{1,0:T(8,128)S(1)}, bf16[512,...) custom-call(bf16[128,4096]{1,0:T(8,128)(2,1)S(1)} %copy-done, ...), custom_call_target="tpu_custom_call" | custom-call | tf_op jit(solution)/shard_map/middle/pallas_call | solution.py:82
  32.9 0.0 copy-start.6
  32.9 0.0 copy-start.2
  33.0 0.3 collective-permute-start.10
  33.2 1.2 %collective-permute-start.11 = (bf16[128,512]{1,0:T(8,128)(2,1)S(1)}, bf16[128,512]{1,0:T(8,128)(2,1)S(1)}, u32[]{:S(2)}, u32[]{:S(2)}) collective-permute-start(bf16[128,512]{1,0:T(8,128)(2,1)S(1)} %get-tuple-element.45), channel_id=1, source_target_pairs={{0,4},{4,0},{8,12},{12,8},{16,20},{20,16},{24,28},{28,24},{1,5},{5... | collective-permute-start | bytes 393224 | tf_op jit(solution)/shard_map/cot_x/ppermute | solution.py:22
  34.5 2.6 %collective-permute-done.10.refs_0_ = bf16[128,512]{1,0:T(8,128)(2,1)S(1)} collective-permute-done((bf16[128,512]{1,0:T(8,128)(2,1)S(1)}, bf16[128,512]{1,0:T(8,128)(2,1)S(1)}, u32[]{:S(2)}, u32[]{:S(2)}) %collective-permute-start.10) | collective-permute-done | bytes 131104 | tf_op jit(solution)/shard_map/cot_x/ppermute | solution.py:22
  37.1 2.8 %collective-permute-done.11.refs_1_ = bf16[128,512]{1,0:T(8,128)(2,1)S(1)} collective-permute-done((bf16[128,512]{1,0:T(8,128)(2,1)S(1)}, bf16[128,512]{1,0:T(8,128)(2,1)S(1)}, u32[]{:S(2)}, u32[]{:S(2)}) %collective-permute-start.11) | collective-permute-done | bytes 131104 | tf_op jit(solution)/shard_map/cot_x/ppermute | solution.py:22
  39.9 1.2 %pack.1 = (bf16[256,512]{1,0:T(8,128)(2,1)S(1)}, bf16[512,1024]{1,0:T(8,128)(2,1)S(1)}) custom-call(bf16[128,512]{1,0:T(8,128)(2,1)S(1)} %collective-permute-done.10.refs_0_, bf16[128,512]{1,0:T(8,128)(2,1)S(1)} %collective-permute-done.11.refs_1_, bf16[128,1024]{1,0:T(8,128)(2,1)S(1)} %copy-done.3, bf16[96,1024]{1,0:T(8,128)(2,1)S(1)} %get-tuple-element.37.refs_3_, ...), custom_call_target="tpu_custom_call" | custom-call | tf_op jit(solution)/shard_map/pack/pallas_call | solution.py:82
  41.1 3.2 %collective-permute-done.12.refs_5_ = bf16[104,1024]{1,0:T(8,128)(2,1)S(1)} collective-permute-done((bf16[104,1024]{1,0:T(8,128)(2,1)S(1)}, bf16[104,1024]{1,0:T(8,128)(2,1)S(1)}, u32[]{:S(2)}, u32[]{:S(2)}) %collective-permute-start.12) | collective-permute-done | bytes 213024 | tf_op jit(solution)/shard_map/last_z3/ppermute | solution.py:28
  44.2 1.5 %gate.1 = (bf16[128,1024]{1,0:T(8,128)(2,1)}, bf16[128,1024]{1,0:T(8,128)(2,1)}, bf16[128,1024]{1,0:T(8,128)(2,1)}, bf16[512,1024]{1,0:T(8,128)(2,1)S(1)}) custom-call(bf16[128,1024]{1,0:T(8,128)(2,1)} %get-tuple-element.41.refs_0_, ...), custom_call_target="tpu_custom_call", output_to_operand_aliasing={{0}: (0, {}), {1}: (1, {}), {2}: (2, {}), {3}: (3, {})} | custom-call | tf_op jit(solution)/shard_map/gate/pallas_call | solution.py:494
  45.8 0.3 collective-permute-start.20
  46.1 0.8 %collective-permute-start.19 = (bf16[256,512]{1,0:T(8,128)(2,1)S(1)}, bf16[256,512]{1,0:T(8,128)(2,1)}, u32[]{:S(2)}, u32[]{:S(2)}) collective-permute-start(bf16[256,512]{1,0:T(8,128)(2,1)S(1)} %get-tuple-element.47.refs_4_.refs_2_), channel_id=1, source_target_pairs={{0,1},{1,0},{2,3},{3,2},{4,5},{5,4},{6,7},{7,6},{8,9},{9,8},{10,11... | collective-permute-start | bytes 786440 | tf_op jit(solution)/shard_map/cot_x_core/ppermute | solution.py:22
  46.9 2.0 %collective-permute-start.15 = (bf16[128,1024]{1,0:T(8,128)(2,1)}, bf16[128,1024]{1,0:T(8,128)(2,1)S(1)}, u32[]{:S(2)}, u32[]{:S(2)}) collective-permute-start(bf16[128,1024]{1,0:T(8,128)(2,1)} %get-tuple-element.48), channel_id=1, source_target_pairs={{0,8},{4,12},{8,16},{12,20},{16,24},{20,28},{24,0},{28,4},{1,9},{5... | collective-permute-start | bytes 786440 | tf_op jit(solution)/shard_map/sum_z3/ppermute | solution.py:28
  48.9 1.4 %collective-permute-start.16 = (bf16[128,1024]{1,0:T(8,128)(2,1)}, bf16[128,1024]{1,0:T(8,128)(2,1)S(1)}, u32[]{:S(2)}, u32[]{:S(2)}) collective-permute-start(bf16[128,1024]{1,0:T(8,128)(2,1)} %get-tuple-element.49), channel_id=1, source_target_pairs={{0,16},{4,20},{8,24},{12,28},{16,0},{20,4},{24,8},{28,12},{1,17},{... | collective-permute-start | bytes 786440 | tf_op jit(solution)/shard_map/sum_z2/ppermute | solution.py:28
  50.3 3.3 %decode.1 = f32[4,1,2,1024]{3,2,1,0:T(2,128)S(1)} custom-call(bf16[512,1024]{1,0:T(8,128)(2,1)S(1)} %copy-done.2, bf16[512,1024]{1,0:T(8,128)(2,1)} %collective-permute-done.refs_2_.refs_1_, bf16[104,1024]{1,0:T(8,128)(2,1)S(1)} %combine.1.refs_3_.refs_2_, bf16[104,1024]{1,0:T(8,128)(2,1)S(1)} %collective-permute-done.14.refs_7_.refs_3_, ...), custom_call_target="tpu_custom_call" | custom-call | tf_op jit(solution)/shard_map/decode/pallas_call | solution.py:82
  53.6 6.6 %all_to_all.5 = f32[4,1,2,1024]{3,2,1,0:T(2,128)S(1)} all-to-all(f32[4,1,2,1024]{3,2,1,0:T(2,128)S(1)} %decode.1), channel_id=1, replica_groups=mesh['fsdp'=8,'tp'=4] {'tp'}, dimensions={0} | all-to-all | bytes 65536 | tf_op jit(solution)/shard_map/dec_tp/all_to_all | solution.py:531
  60.3 3.2 %collective-permute-start.18 = (bf16[2,1024]{1,0:T(2,128)(2,1)S(1)}, bf16[2,1024]{1,0:T(2,128)(2,1)S(1)}, u32[]{:S(2)}, u32[]{:S(2)}) collective-permute-start(bf16[2,1024]{1,0:T(2,128)(2,1)S(1)} %reduce_sum.9), channel_id=1, source_target_pairs={{0,0},{1,8},{2,16},{3,24},{4,4},{5,12},{6,20},{7,28},{8,1},{9,9},{... | collective-permute-start | bytes 12296 | tf_op jit(solution)/shard_map/dec_place/ppermute | solution.py:541
  63.5 0.0 copy-start.7
  63.6 1.0 %copy-done.7 = bf16[512,512]{1,0:T(8,128)(2,1)S(1)} copy-done((bf16[512,512]{1,0:T(8,128)(2,1)S(1)}, bf16[512,512]{1,0:T(8,128)(2,1)}, u32[]{:S(2)}) %copy-start.7) | copy-done | bytes 524312
  64.6 1.5 %own.1 = (f32[512,1024]{1,0:T(8,128)S(1)}, bf16[512,512]{1,0:T(8,128)(2,1)S(1)}) custom-call(bf16[512,512]{1,0:T(8,128)(2,1)S(1)} %copy-done.7, bf16[512,1024]{1,0:T(8,128)(2,1)S(1)} %get-tuple-element.51.refs_6_.refs_1_, bf16[256,512]{1,0:T(8,128)(2,1)S(1)} %get-tuple-element.47.refs_4_.refs_2_, bf16[256,512]{1,0:T(8,128)(2,1)} %collective-permute-done.19.refs_3_), custom_call_target="tpu_custom_call" | custom-call | tf_op jit(solution)/shard_map/own/pallas_call | solution.py:82
  66.1 4.0 %collective-permute-done.20.refs_1_ = bf16[512,1024]{1,0:T(8,128)(2,1)S(1)} collective-permute-done((bf16[512,1024]{1,0:T(8,128)(2,1)S(1)}, bf16[512,1024]{1,0:T(8,128)(2,1)S(1)}, u32[]{:S(2)}, u32[]{:S(2)}) %collective-permute-start.20) | collective-permute-done | bytes 1048608 | tf_op jit(solution)/shard_map/attn_x/ppermute | solution.py:22
  70.1 1.8 %product.1 = (f32[512,1024]{1,0:T(8,128)}, f32[8,128]{1,0:T(8,128)S(1)}) custom-call(f32[512,1024]{1,0:T(8,128)S(1)} %get-tuple-element.53.refs_0_, bf16[512,1024]{1,0:T(8,128)(2,1)S(1)} %collective-permute-done.20.refs_1_, bf16[512,512]{1,0:T(8,128)(2,1)S(1)} %get-tuple-element.54.refs_2_), custom_call_target="tpu_custom_call" | custom-call | tf_op jit(solution)/shard_map/product/pallas_call | solution.py:82
  71.9 1.9 %collective-permute-done.18.refs_4_ = bf16[2,1024]{1,0:T(2,128)(2,1)S(1)} collective-permute-done((bf16[2,1024]{1,0:T(2,128)(2,1)S(1)}, bf16[2,1024]{1,0:T(2,128)(2,1)S(1)}, u32[]{:S(2)}, u32[]{:S(2)}) %collective-permute-start.18) | collective-permute-done | bytes 4128 | tf_op jit(solution)/shard_map/dec_place/ppermute | solution.py:541
  73.9 1.1 %sum.1 = (bf16[1,2,1024]{2,1,0:T(2,128)(2,1)}, bf16[128,1024]{1,0:T(8,128)(2,1)}) custom-call(f32[128,1024]{1,0:T(8,128)S(1)} %copy-done.5, bf16[128,1024]{1,0:T(8,128)(2,1)S(1)} %collective-permute-done.15.refs_1_, bf16[128,1024]{1,0:T(8,128)(2,1)S(1)} %collective-permute-done.16.refs_2_, bf16[128,1024]{1,0:T(8,128)(2,1)S(1)} %collective-permute-done.17.refs_3_, ...), custom_call_target="tpu_custom_call" | custom-call | tf_op jit(solution)/shard_map/sum/pallas_call | solution.py:82
  (26 shorter events, 0.1 us)
Async XLA Ops:
  0.6 18.1 %copy-start.3 = (bf16[128,1024]{1,0:T(8,128)(2,1)S(1)}, bf16[128,1024]{1,0:T(8,128)(2,1)}, u32[]{:S(2)}) copy-start(bf16[128,1024]{1,0:T(8,128)(2,1)} %refs_2_.3) | copy-start | bytes 786436
  0.6 26.9 %collective-permute-start = (bf16[512,1024]{1,0:T(8,128)(2,1)}, bf16[512,1024]{1,0:T(8,128)(2,1)}, u32[]{:S(2)}, u32[]{:S(2)}) collective-permute-start(bf16[512,1024]{1,0:T(8,128)(2,1)} %refs_0_.6), channel_id=1, source_target_pairs={{0,4},{4,0},{8,12},{12,8},{16,20},{20,16},{24,28},{28,24},{1,5},{5... | collective-permute-start | bytes 3145736 | tf_op jit(solution)/shard_map/weight_x/ppermute | solution.py:22
  3.9 15.6 %collective-permute-start.1 = (bf16[96,1024]{1,0:T(8,128)(2,1)}, bf16[96,1024]{1,0:T(8,128)(2,1)S(1)}, u32[]{:S(2)}, u32[]{:S(2)}) collective-permute-start(bf16[96,1024]{1,0:T(8,128)(2,1)} %get-tuple-element.31), channel_id=1, source_target_pairs={{0,8},{4,12},{8,16},{12,20},{16,24},{20,28},{24,0},{28,4},{1,9},{5... | collective-permute-start | bytes 589832 | tf_op jit(solution)/shard_map/first_z1/ppermute | solution.py:28
  5.2 14.3 %collective-permute-start.2 = (bf16[96,1024]{1,0:T(8,128)(2,1)}, bf16[96,1024]{1,0:T(8,128)(2,1)S(1)}, u32[]{:S(2)}, u32[]{:S(2)}) collective-permute-start(bf16[96,1024]{1,0:T(8,128)(2,1)} %get-tuple-element.32), channel_id=1, source_target_pairs={{0,16},{4,20},{8,24},{12,28},{16,0},{20,4},{24,8},{28,12},{1,17},{... | collective-permute-start | bytes 589832 | tf_op jit(solution)/shard_map/first_z2/ppermute | solution.py:28
  5.3 17.2 %collective-permute-start.3 = (bf16[96,1024]{1,0:T(8,128)(2,1)}, bf16[96,1024]{1,0:T(8,128)(2,1)S(1)}, u32[]{:S(2)}, u32[]{:S(2)}) collective-permute-start(bf16[96,1024]{1,0:T(8,128)(2,1)} %get-tuple-element.33), channel_id=1, source_target_pairs={{0,24},{4,28},{8,0},{12,4},{16,8},{20,12},{24,16},{28,20},{1,25},{... | collective-permute-start | bytes 589832 | tf_op jit(solution)/shard_map/first_z3/ppermute | solution.py:28
  10.6 17.0 %copy-start = (bf16[128,4096]{1,0:T(8,128)(2,1)S(1)}, bf16[128,4096]{1,0:T(8,128)(2,1)}, u32[]{:S(2)}) copy-start(bf16[128,4096]{1,0:T(8,128)(2,1)} %refs_0_.5) | copy-start | bytes 3145732
  10.6 2.8 %collective-permute-start.5 = (f32[1,16,256]{2,1,0:T(8,128)}, f32[1,16,256]{2,1,0:T(8,128)S(1)}, u32[]{:S(2)}, u32[]{:S(2)}) collective-permute-start(f32[1,16,256]{2,1,0:T(8,128)} %get-tuple-element.36), channel_id=1, source_target_pairs={{0,1},{1,0},{2,3},{3,2},{4,5},{5,4},{6,7},{7,6},{8,9},{9,8},{10,11... | collective-permute-start | bytes 49160 | tf_op jit(solution)/shard_map/softmax_tp1/ppermute | solution.py:22
  13.4 3.4 %collective-permute-start.4 = (f32[2,16,256]{2,1,0:T(8,128)}, f32[2,16,256]{2,1,0:T(8,128)S(1)}, u32[]{:S(2)}, u32[]{:S(2)}) collective-permute-start(f32[2,16,256]{2,1,0:T(8,128)} %get-tuple-element.35), channel_id=1, source_target_pairs={{0,2},{1,3},{2,0},{3,1},{4,6},{5,7},{6,4},{7,5},{8,10},{9,11},{10,... | collective-permute-start | bytes 98312 | tf_op jit(solution)/shard_map/softmax_tp2/ppermute | solution.py:22
  16.8 2.0 %collective-permute-start.6 = (f32[2,16,256]{2,1,0:T(8,128)S(1)}, f32[2,16,256]{2,1,0:T(8,128)S(1)}, u32[]{:S(2)}, u32[]{:S(2)}) collective-permute-start(f32[2,16,256]{2,1,0:T(8,128)S(1)} %collective-permute-done.4.refs_0_), channel_id=1, source_target_pairs={{0,1},{1,0},{2,3},{3,2},{4,5},{5,4},{6,7},{7,6},{8,9},{9,8},{10,11... | collective-permute-start | bytes 98312 | tf_op jit(solution)/shard_map/softmax_tp1/ppermute | solution.py:22
  17.9 0.8 %copy-start.8 = (f32[40,256]{1,0:T(8,128)S(1)}, f32[40,256]{1,0:T(8,128)}, u32[]{:S(2)}) copy-start(f32[40,256]{1,0:T(8,128)} %get-tuple-element.34.in_ref) | copy-start | bytes 122884
  22.5 3.3 %collective-permute-start.7 = (bf16[96,1024]{1,0:T(8,128)(2,1)S(1)}, bf16[96,1024]{1,0:T(8,128)(2,1)S(1)}, u32[]{:S(2)}, u32[]{:S(2)}) collective-permute-start(bf16[96,1024]{1,0:T(8,128)(2,1)S(1)} %get-tuple-element.37.refs_3_), channel_id=1, source_target_pairs={{0,1},{1,0},{2,3},{3,2},{4,5},{5,4},{6,7},{7,6},{8,9},{9,8},{10,11... | collective-permute-start | bytes 589832 | tf_op jit(solution)/shard_map/cot_core/ppermute | solution.py:22
  23.0 3.8 %collective-permute-start.8 = (bf16[96,1024]{1,0:T(8,128)(2,1)S(1)}, bf16[96,1024]{1,0:T(8,128)(2,1)S(1)}, u32[]{:S(2)}, u32[]{:S(2)}) collective-permute-start(bf16[96,1024]{1,0:T(8,128)(2,1)S(1)} %get-tuple-element.38.refs_4_), channel_id=1, source_target_pairs={{0,1},{1,0},{2,3},{3,2},{4,5},{5,4},{6,7},{7,6},{8,9},{9,8},{10,11... | collective-permute-start | bytes 589832 | tf_op jit(solution)/shard_map/cot_core/ppermute | solution.py:22
  23.0 4.5 %collective-permute-start.9 = (bf16[96,1024]{1,0:T(8,128)(2,1)S(1)}, bf16[96,1024]{1,0:T(8,128)(2,1)S(1)}, u32[]{:S(2)}, u32[]{:S(2)}) collective-permute-start(bf16[96,1024]{1,0:T(8,128)(2,1)S(1)} %get-tuple-element.39.refs_5_), channel_id=1, source_target_pairs={{0,1},{1,0},{2,3},{3,2},{4,5},{5,4},{6,7},{7,6},{8,9},{9,8},{10,11... | collective-permute-start | bytes 589832 | tf_op jit(solution)/shard_map/cot_core/ppermute | solution.py:22
  23.5 17.5 %collective-permute-start.14 = (bf16[104,1024]{1,0:T(8,128)(2,1)S(1)}, bf16[104,1024]{1,0:T(8,128)(2,1)S(1)}, u32[]{:S(2)}, u32[]{:S(2)}) collective-permute-start(bf16[104,1024]{1,0:T(8,128)(2,1)S(1)} %combine.1.refs_3_.refs_2_), channel_id=1, source_target_pairs={{0,8},{4,12},{8,16},{12,20},{16,24},{20,28},{24,0},{28,4},{1,9},{5... | collective-permute-start | bytes 638984 | tf_op jit(solution)/shard_map/last_z1/ppermute | solution.py:28
  25.8 15.3 %collective-permute-start.13 = (bf16[104,1024]{1,0:T(8,128)(2,1)S(1)}, bf16[104,1024]{1,0:T(8,128)(2,1)S(1)}, u32[]{:S(2)}, u32[]{:S(2)}) collective-permute-start(bf16[104,1024]{1,0:T(8,128)(2,1)S(1)} %combine.1.refs_3_.refs_2_), channel_id=1, source_target_pairs={{0,16},{4,20},{8,24},{12,28},{16,0},{20,4},{24,8},{28,12},{1,17},{... | collective-permute-start | bytes 638984 | tf_op jit(solution)/shard_map/last_z2/ppermute | solution.py:28
  26.8 17.4 %collective-permute-start.12 = (bf16[104,1024]{1,0:T(8,128)(2,1)S(1)}, bf16[104,1024]{1,0:T(8,128)(2,1)S(1)}, u32[]{:S(2)}, u32[]{:S(2)}) collective-permute-start(bf16[104,1024]{1,0:T(8,128)(2,1)S(1)} %combine.1.refs_3_.refs_2_), channel_id=1, source_target_pairs={{0,24},{4,28},{8,0},{12,4},{16,8},{20,12},{24,16},{28,20},{1,25},{... | collective-permute-start | bytes 638984 | tf_op jit(solution)/shard_map/last_z3/ppermute | solution.py:28
  27.6 1.2 %copy-start.1 = (bf16[512,1024]{1,0:T(8,128)(2,1)S(1)}, bf16[512,1024]{1,0:T(8,128)(2,1)}, u32[]{:S(2)}) copy-start(bf16[512,1024]{1,0:T(8,128)(2,1)} %refs_0_.6) | copy-start | bytes 3145732
  32.9 20.7 %copy-start.4 = (f32[128,1024]{1,0:T(8,128)}, f32[128,1024]{1,0:T(8,128)S(1)}, u32[]{:S(2)}) copy-start(f32[128,1024]{1,0:T(8,128)S(1)} %get-tuple-element.40.refs_0_) | copy-start | bytes 1572868
  32.9 20.7 %copy-start.6 = (bf16[512,512]{1,0:T(8,128)(2,1)}, bf16[512,512]{1,0:T(8,128)(2,1)S(1)}, u32[]{:S(2)}) copy-start(bf16[512,512]{1,0:T(8,128)(2,1)S(1)} %get-tuple-element.52.refs_0_) | copy-start | bytes 1572868
  32.9 17.3 %copy-start.2 = (bf16[512,1024]{1,0:T(8,128)(2,1)S(1)}, bf16[512,1024]{1,0:T(8,128)(2,1)}, u32[]{:S(2)}) copy-start(bf16[512,1024]{1,0:T(8,128)(2,1)} %refs_0_.6) | copy-start | bytes 3145732
  33.0 4.2 %collective-permute-start.10 = (bf16[128,512]{1,0:T(8,128)(2,1)S(1)}, bf16[128,512]{1,0:T(8,128)(2,1)S(1)}, u32[]{:S(2)}, u32[]{:S(2)}) collective-permute-start(bf16[128,512]{1,0:T(8,128)(2,1)S(1)} %get-tuple-element.44), channel_id=1, source_target_pairs={{0,4},{4,0},{8,12},{12,8},{16,20},{20,16},{24,28},{28,24},{1,5},{5... | collective-permute-start | bytes 393224 | tf_op jit(solution)/shard_map/cot_x/ppermute | solution.py:22
  33.2 6.6 %collective-permute-start.11 = (bf16[128,512]{1,0:T(8,128)(2,1)S(1)}, bf16[128,512]{1,0:T(8,128)(2,1)S(1)}, u32[]{:S(2)}, u32[]{:S(2)}) collective-permute-start(bf16[128,512]{1,0:T(8,128)(2,1)S(1)} %get-tuple-element.45), channel_id=1, source_target_pairs={{0,4},{4,0},{8,12},{12,8},{16,20},{20,16},{24,28},{28,24},{1,5},{5... | collective-permute-start | bytes 393224 | tf_op jit(solution)/shard_map/cot_x/ppermute | solution.py:22
  45.8 24.3 %collective-permute-start.20 = (bf16[512,1024]{1,0:T(8,128)(2,1)S(1)}, bf16[512,1024]{1,0:T(8,128)(2,1)S(1)}, u32[]{:S(2)}, u32[]{:S(2)}) collective-permute-start(bf16[512,1024]{1,0:T(8,128)(2,1)S(1)} %get-tuple-element.51.refs_6_.refs_1_), channel_id=1, source_target_pairs={{0,4},{4,0},{8,12},{12,8},{16,20},{20,16},{24,28},{28,24},{1,5},{5... | collective-permute-start | bytes 3145736 | tf_op jit(solution)/shard_map/attn_x/ppermute | solution.py:22
  46.1 14.2 %collective-permute-start.19 = (bf16[256,512]{1,0:T(8,128)(2,1)S(1)}, bf16[256,512]{1,0:T(8,128)(2,1)}, u32[]{:S(2)}, u32[]{:S(2)}) collective-permute-start(bf16[256,512]{1,0:T(8,128)(2,1)S(1)} %get-tuple-element.47.refs_4_.refs_2_), channel_id=1, source_target_pairs={{0,1},{1,0},{2,3},{3,2},{4,5},{5,4},{6,7},{7,6},{8,9},{9,8},{10,11... | collective-permute-start | bytes 786440 | tf_op jit(solution)/shard_map/cot_x_core/ppermute | solution.py:22
  46.9 27.0 %collective-permute-start.15 = (bf16[128,1024]{1,0:T(8,128)(2,1)}, bf16[128,1024]{1,0:T(8,128)(2,1)S(1)}, u32[]{:S(2)}, u32[]{:S(2)}) collective-permute-start(bf16[128,1024]{1,0:T(8,128)(2,1)} %get-tuple-element.48), channel_id=1, source_target_pairs={{0,8},{4,12},{8,16},{12,20},{16,24},{20,28},{24,0},{28,4},{1,9},{5... | collective-permute-start | bytes 786440 | tf_op jit(solution)/shard_map/sum_z3/ppermute | solution.py:28
  48.9 25.0 %collective-permute-start.16 = (bf16[128,1024]{1,0:T(8,128)(2,1)}, bf16[128,1024]{1,0:T(8,128)(2,1)S(1)}, u32[]{:S(2)}, u32[]{:S(2)}) collective-permute-start(bf16[128,1024]{1,0:T(8,128)(2,1)} %get-tuple-element.49), channel_id=1, source_target_pairs={{0,16},{4,20},{8,24},{12,28},{16,0},{20,4},{24,8},{28,12},{1,17},{... | collective-permute-start | bytes 786440 | tf_op jit(solution)/shard_map/sum_z2/ppermute | solution.py:28
  50.3 23.6 %collective-permute-start.17 = (bf16[128,1024]{1,0:T(8,128)(2,1)}, bf16[128,1024]{1,0:T(8,128)(2,1)S(1)}, u32[]{:S(2)}, u32[]{:S(2)}) collective-permute-start(bf16[128,1024]{1,0:T(8,128)(2,1)} %get-tuple-element.50), channel_id=1, source_target_pairs={{0,24},{4,28},{8,0},{12,4},{16,8},{20,12},{24,16},{28,20},{1,25},{... | collective-permute-start | bytes 786440 | tf_op jit(solution)/shard_map/sum_z1/ppermute | solution.py:28
  60.3 13.6 %collective-permute-start.18 = (bf16[2,1024]{1,0:T(2,128)(2,1)S(1)}, bf16[2,1024]{1,0:T(2,128)(2,1)S(1)}, u32[]{:S(2)}, u32[]{:S(2)}) collective-permute-start(bf16[2,1024]{1,0:T(2,128)(2,1)S(1)} %reduce_sum.9), channel_id=1, source_target_pairs={{0,0},{1,8},{2,16},{3,24},{4,4},{5,12},{6,20},{7,28},{8,1},{9,9},{... | collective-permute-start | bytes 12296 | tf_op jit(solution)/shard_map/dec_place/ppermute | solution.py:541
  63.5 1.0 %copy-start.7 = (bf16[512,512]{1,0:T(8,128)(2,1)S(1)}, bf16[512,512]{1,0:T(8,128)(2,1)}, u32[]{:S(2)}) copy-start(bf16[512,512]{1,0:T(8,128)(2,1)} %copy-done.6) | copy-start | bytes 1572868
  66.1 7.8 %copy-start.5 = (f32[128,1024]{1,0:T(8,128)S(1)}, f32[128,1024]{1,0:T(8,128)}, u32[]{:S(2)}) copy-start(f32[128,1024]{1,0:T(8,128)} %copy-done.4) | copy-start | bytes 1572868

commit v9 on v8

--- a/solution.py
+++ b/solution.py
@@ -348,20 +348,16 @@
 
 
 def gate_kernel(count, early, *refs):
-    refs, pack_out, (last_ref, in_sems, out_sems) = refs[count + 2 : -4 - count], refs[-4], refs[-3:]
+    refs, pack_out, sems = refs[count + 2 : -2 - count], refs[-2], refs[-1]
     rest = refs[0].shape[0] - PAD
     tokens = rest + early
-    arrive, leave = [], []
+    copies = []
     for k, ref in enumerate(refs[::-1]):
-        arrive.append(pltpu.make_async_copy(ref.at[:rest], last_ref.at[k], in_sems.at[k]))
         target = pack_out.at[(k + 1) * tokens + early : (k + 2) * tokens]
-        leave.append(pltpu.make_async_copy(last_ref.at[k], target, out_sems.at[k]))
-    for copy in arrive:
+        copies.append(pltpu.make_async_copy(ref.at[:rest], target, sems.at[k]))
+    for copy in copies:
         copy.start()
-    for copy, follow in zip(arrive, leave):
-        copy.wait()
-        follow.start()
-    for copy in leave:
+    for copy in copies:
         copy.wait()
 
 
@@ -497,8 +493,6 @@
         in_specs=[pl.BlockSpec(memory_space=pltpu.HBM)] * (len(sent) + 2 + len(far)),
         out_specs=[pl.BlockSpec(memory_space=pltpu.HBM)] * (len(sent) + 1),
         scratch_shapes=[
-            pltpu.VMEM((len(far), tokens - early, cols), BF16),
-            pltpu.SemaphoreType.DMA((len(far),)),
             pltpu.SemaphoreType.DMA((len(far),)),
         ],
         input_output_aliases={i: i for i in range(len(sent) + 1)},

time: 76.3 us -> 75.6 us (level)
  Pallas kernels: 20.8 us -> 20 us
    pallas_call x1, Pallas kernels: 1.54 us -> 0.76 us  [shards(): pl.pallas_call(functools.partial(gate_kernel, len(sent), early), out_shap...]
where the time goes in v9:
time: 75.6 us; the launch traced here: 74.2 us
  starting transfers between devices  22.2 us (29%)
  waiting for transfers between devices  20.8 us (28%)
  Pallas kernels  20 us (26%)
  blocking collectives  6.62 us (9%)
  local copies, waits for them, and re-layouts  3.07 us (4%)
  between operations  1.52 us (2%)
    pallas_call x8, Pallas kernels, call(): pl.pallas_call(body, out_shape=[jax.ShapeDtypeStruct(shape, dtype) for sh...  18.4 us
    ppermute x11, waiting for transfers between devices, flip(): return lax.ppermute(a, axis, [(i, i ^ bits) for i in range(size)])  12.7 us
    ppermute x9, starting transfers between devices, turn(): lax.ppermute(a, 'fsdp', [(z * INNER + x, (z + steps) % outer * INNER + x)...  10 us
    ppermute x11, starting transfers between devices, flip(): return lax.ppermute(a, axis, [(i, i ^ bits) for i in range(size)])  8.97 us
    all_to_all x1, blocking collectives, shards(): dec = lax.all_to_all(dec, 'tp', 0, 0, tiled=True).sum(axis=0).astype(BF16)  6.62 us
    ppermute x9, waiting for transfers between devices, turn(): lax.ppermute(a, 'fsdp', [(z * INNER + x, (z + steps) % outer * INNER + x)...  6.17 us
    ppermute x1, starting transfers between devices, shards(): lax.ppermute(lax.dynamic_index_in_dim(dec, z % share ^ j, 0, False), ('fs...  3.25 us
    unnamed x18, local copies, waits for them, and re-layouts  3.07 us
  transfers between devices with their start and end apart: 21, of which 9 were waited for; matrix products, arithmetic and copies ran while one was open for 0% of the time, Pallas kernels for 24%

profile of v9, /device:TPU:17, one launch (start us, length us, event | category | flops | bytes accessed | tf_op | source)
XLA Modules:
  0.0 74.2 jit_solution(10562966580074688968)
XLA Ops:
  0.6 1.3 %collective-permute-start = (bf16[512,1024]{1,0:T(8,128)(2,1)}, bf16[512,1024]{1,0:T(8,128)(2,1)}, u32[]{:S(2)}, u32[]{:S(2)}) collective-permute-start(bf16[512,1024]{1,0:T(8,128)(2,1)} %refs_0_.6), channel_id=1, source_target_pairs={{0,4},{4,0},{8,12},{12,8},{16,20},{20,16},{24,28},{28,24},{1,5},{5... | collective-permute-start | bytes 3145736 | tf_op jit(solution)/shard_map/weight_x/ppermute | solution.py:22
  1.9 2.0 %cut.1 = (bf16[96,1024]{1,0:T(8,128)(2,1)}, bf16[96,1024]{1,0:T(8,128)(2,1)}, bf16[96,1024]{1,0:T(8,128)(2,1)}) custom-call(bf16[128,4096]{1,0:T(8,128)(2,1)} %refs_0_.5, bf16[128,1024]{1,0:T(8,128)(2,1)} %refs_2_.3), custom_call_target="tpu_custom_call" | custom-call | tf_op jit(solution)/shard_map/cut/pallas_call | solution.py:82
  3.9 1.3 %collective-permute-start.1 = (bf16[96,1024]{1,0:T(8,128)(2,1)}, bf16[96,1024]{1,0:T(8,128)(2,1)S(1)}, u32[]{:S(2)}, u32[]{:S(2)}) collective-permute-start(bf16[96,1024]{1,0:T(8,128)(2,1)} %get-tuple-element.31), channel_id=1, source_target_pairs={{0,8},{4,12},{8,16},{12,20},{16,24},{20,28},{24,0},{28,4},{1,9},{5... | collective-permute-start | bytes 589832 | tf_op jit(solution)/shard_map/first_z1/ppermute | solution.py:28
  5.2 0.1 collective-permute-start.2
  5.3 1.2 %collective-permute-start.3 = (bf16[96,1024]{1,0:T(8,128)(2,1)}, bf16[96,1024]{1,0:T(8,128)(2,1)S(1)}, u32[]{:S(2)}, u32[]{:S(2)}) collective-permute-start(bf16[96,1024]{1,0:T(8,128)(2,1)} %get-tuple-element.33), channel_id=1, source_target_pairs={{0,24},{4,28},{8,0},{12,4},{16,8},{20,12},{24,16},{28,20},{1,25},{... | collective-permute-start | bytes 589832 | tf_op jit(solution)/shard_map/first_z3/ppermute | solution.py:28
  7.1 3.4 %attend.1 = (f32[40,256]{1,0:T(8,128)}, f32[1,16,256]{2,1,0:T(8,128)}, f32[2,16,256]{2,1,0:T(8,128)}) custom-call(s32[1]{0:T(128)S(6)} %copy.26.refs_0_, bf16[1,2,4096]{2,1,0:T(2,128)(2,1)} %refs_1_.4, bf16[1,512,512]{2,1,0:T(8,128)(2,1)} %refs_2_.2, bf16[1,512,512]{2,1,0:T(8,128)(2,1)} %refs_3_.1, bf16[1,2,512]{2,1,0:T(2,128)(2,1)} %refs_4_.1, ...), custom_call_target="tpu_custom_call" | custom-call | tf_op jit(solution)/shard_map/attend/pallas_call | solution.py:82
  10.6 0.0 copy-start
  10.6 1.7 %collective-permute-start.5 = (f32[1,16,256]{2,1,0:T(8,128)}, f32[1,16,256]{2,1,0:T(8,128)S(1)}, u32[]{:S(2)}, u32[]{:S(2)}) collective-permute-start(f32[1,16,256]{2,1,0:T(8,128)} %get-tuple-element.36), channel_id=1, source_target_pairs={{0,1},{1,0},{2,3},{3,2},{4,5},{5,4},{6,7},{7,6},{8,9},{9,8},{10,11... | collective-permute-start | bytes 49160 | tf_op jit(solution)/shard_map/softmax_tp1/ppermute | solution.py:22
  12.3 1.0 %collective-permute-done.5.refs_1_ = f32[1,16,256]{2,1,0:T(8,128)S(1)} collective-permute-done((f32[1,16,256]{2,1,0:T(8,128)}, f32[1,16,256]{2,1,0:T(8,128)S(1)}, u32[]{:S(2)}, u32[]{:S(2)}) %collective-permute-start.5) | collective-permute-done | bytes 16416 | tf_op jit(solution)/shard_map/softmax_tp1/ppermute | solution.py:22
  13.4 1.2 %collective-permute-start.4 = (f32[2,16,256]{2,1,0:T(8,128)}, f32[2,16,256]{2,1,0:T(8,128)S(1)}, u32[]{:S(2)}, u32[]{:S(2)}) collective-permute-start(f32[2,16,256]{2,1,0:T(8,128)} %get-tuple-element.35), channel_id=1, source_target_pairs={{0,2},{1,3},{2,0},{3,1},{4,6},{5,7},{6,4},{7,5},{8,10},{9,11},{10,... | collective-permute-start | bytes 98312 | tf_op jit(solution)/shard_map/softmax_tp2/ppermute | solution.py:22
  14.6 2.1 %collective-permute-done.4.refs_0_ = f32[2,16,256]{2,1,0:T(8,128)S(1)} collective-permute-done((f32[2,16,256]{2,1,0:T(8,128)}, f32[2,16,256]{2,1,0:T(8,128)S(1)}, u32[]{:S(2)}, u32[]{:S(2)}) %collective-permute-start.4) | collective-permute-done | bytes 32800 | tf_op jit(solution)/shard_map/softmax_tp2/ppermute | solution.py:22
  16.8 1.1 %collective-permute-start.6 = (f32[2,16,256]{2,1,0:T(8,128)S(1)}, f32[2,16,256]{2,1,0:T(8,128)S(1)}, u32[]{:S(2)}, u32[]{:S(2)}) collective-permute-start(f32[2,16,256]{2,1,0:T(8,128)S(1)} %collective-permute-done.4.refs_0_), channel_id=1, source_target_pairs={{0,1},{1,0},{2,3},{3,2},{4,5},{5,4},{6,7},{7,6},{8,9},{9,8},{10,11... | collective-permute-start | bytes 98312 | tf_op jit(solution)/shard_map/softmax_tp1/ppermute | solution.py:22
  17.9 0.8 %copy-done.8 = f32[40,256]{1,0:T(8,128)S(1)} copy-done((f32[40,256]{1,0:T(8,128)S(1)}, f32[40,256]{1,0:T(8,128)}, u32[]{:S(2)}) %copy-start.8) | copy-done | bytes 40984
  18.6 0.1 collective-permute-done.6.refs_2_
  18.7 0.8 %combine.1.refs_3_.refs_2_ = bf16[104,1024]{1,0:T(8,128)(2,1)S(1)} custom-call(bf16[128,1024]{1,0:T(8,128)(2,1)S(1)} %copy-done.3, f32[40,256]{1,0:T(8,128)S(1)} %hold.1.own_ref, f32[2,16,256]{2,1,0:T(8,128)S(1)} %collective-permute-done.4.refs_0_, f32[1,16,256]{2,1,0:T(8,128)S(1)} %collective-permute-done.5.refs_1_, ...), custom_call_target="tpu_custom_call" | custom-call | tf_op jit(solution)/shard_map/combine/pallas_call | solution.py:442
  19.5 3.0 %collective-permute-done.3.refs_2_ = bf16[96,1024]{1,0:T(8,128)(2,1)S(1)} collective-permute-done((bf16[96,1024]{1,0:T(8,128)(2,1)}, bf16[96,1024]{1,0:T(8,128)(2,1)S(1)}, u32[]{:S(2)}, u32[]{:S(2)}) %collective-permute-start.3) | collective-permute-done | bytes 196640 | tf_op jit(solution)/shard_map/first_z3/ppermute | solution.py:28
  22.5 0.5 collective-permute-start.7
  23.0 0.0 collective-permute-start.8
  23.0 0.5 collective-permute-start.9
  23.5 2.3 %collective-permute-start.14 = (bf16[104,1024]{1,0:T(8,128)(2,1)S(1)}, bf16[104,1024]{1,0:T(8,128)(2,1)S(1)}, u32[]{:S(2)}, u32[]{:S(2)}) collective-permute-start(bf16[104,1024]{1,0:T(8,128)(2,1)S(1)} %combine.1.refs_3_.refs_2_), channel_id=1, source_target_pairs={{0,8},{4,12},{8,16},{12,20},{16,24},{20,28},{24,0},{28,4},{1,9},{5... | collective-permute-start | bytes 638984 | tf_op jit(solution)/shard_map/last_z1/ppermute | solution.py:28
  25.8 1.0 %collective-permute-start.13 = (bf16[104,1024]{1,0:T(8,128)(2,1)S(1)}, bf16[104,1024]{1,0:T(8,128)(2,1)S(1)}, u32[]{:S(2)}, u32[]{:S(2)}) collective-permute-start(bf16[104,1024]{1,0:T(8,128)(2,1)S(1)} %combine.1.refs_3_.refs_2_), channel_id=1, source_target_pairs={{0,16},{4,20},{8,24},{12,28},{16,0},{20,4},{24,8},{28,12},{1,17},{... | collective-permute-start | bytes 638984 | tf_op jit(solution)/shard_map/last_z2/ppermute | solution.py:28
  26.8 0.7 collective-permute-start.12
  27.6 0.0 copy-start.1
  27.6 1.2 %copy-done.1 = bf16[512,1024]{1,0:T(8,128)(2,1)S(1)} copy-done((bf16[512,1024]{1,0:T(8,128)(2,1)S(1)}, bf16[512,1024]{1,0:T(8,128)(2,1)}, u32[]{:S(2)}) %copy-start.1) | copy-done | bytes 1048600
  28.8 4.1 %middle.1 = (bf16[128,1024]{1,0:T(8,128)(2,1)}, bf16[128,1024]{1,0:T(8,128)(2,1)}, bf16[128,1024]{1,0:T(8,128)(2,1)}, f32[128,1024]{1,0:T(8,128)S(1)}, bf16[512,...) custom-call(bf16[128,4096]{1,0:T(8,128)(2,1)S(1)} %copy-done, ...), custom_call_target="tpu_custom_call" | custom-call | tf_op jit(solution)/shard_map/middle/pallas_call | solution.py:82
  32.9 0.0 copy-start.6
  32.9 0.0 copy-start.2
  33.0 0.3 collective-permute-start.10
  33.2 1.2 %collective-permute-start.11 = (bf16[128,512]{1,0:T(8,128)(2,1)S(1)}, bf16[128,512]{1,0:T(8,128)(2,1)S(1)}, u32[]{:S(2)}, u32[]{:S(2)}) collective-permute-start(bf16[128,512]{1,0:T(8,128)(2,1)S(1)} %get-tuple-element.45), channel_id=1, source_target_pairs={{0,4},{4,0},{8,12},{12,8},{16,20},{20,16},{24,28},{28,24},{1,5},{5... | collective-permute-start | bytes 393224 | tf_op jit(solution)/shard_map/cot_x/ppermute | solution.py:22
  34.5 2.6 %collective-permute-done.10.refs_0_ = bf16[128,512]{1,0:T(8,128)(2,1)S(1)} collective-permute-done((bf16[128,512]{1,0:T(8,128)(2,1)S(1)}, bf16[128,512]{1,0:T(8,128)(2,1)S(1)}, u32[]{:S(2)}, u32[]{:S(2)}) %collective-permute-start.10) | collective-permute-done | bytes 131104 | tf_op jit(solution)/shard_map/cot_x/ppermute | solution.py:22
  37.1 2.8 %collective-permute-done.11.refs_1_ = bf16[128,512]{1,0:T(8,128)(2,1)S(1)} collective-permute-done((bf16[128,512]{1,0:T(8,128)(2,1)S(1)}, bf16[128,512]{1,0:T(8,128)(2,1)S(1)}, u32[]{:S(2)}, u32[]{:S(2)}) %collective-permute-start.11) | collective-permute-done | bytes 131104 | tf_op jit(solution)/shard_map/cot_x/ppermute | solution.py:22
  39.9 1.2 %pack.1 = (bf16[256,512]{1,0:T(8,128)(2,1)S(1)}, bf16[512,1024]{1,0:T(8,128)(2,1)S(1)}) custom-call(bf16[128,512]{1,0:T(8,128)(2,1)S(1)} %collective-permute-done.10.refs_0_, bf16[128,512]{1,0:T(8,128)(2,1)S(1)} %collective-permute-done.11.refs_1_, bf16[128,1024]{1,0:T(8,128)(2,1)S(1)} %copy-done.3, bf16[96,1024]{1,0:T(8,128)(2,1)S(1)} %get-tuple-element.37.refs_3_, ...), custom_call_target="tpu_custom_call" | custom-call | tf_op jit(solution)/shard_map/pack/pallas_call | solution.py:82
  41.1 3.2 %collective-permute-done.12.refs_5_ = bf16[104,1024]{1,0:T(8,128)(2,1)S(1)} collective-permute-done((bf16[104,1024]{1,0:T(8,128)(2,1)S(1)}, bf16[104,1024]{1,0:T(8,128)(2,1)S(1)}, u32[]{:S(2)}, u32[]{:S(2)}) %collective-permute-start.12) | collective-permute-done | bytes 213024 | tf_op jit(solution)/shard_map/last_z3/ppermute | solution.py:28
  44.2 0.8 %gate.1 = (bf16[128,1024]{1,0:T(8,128)(2,1)}, bf16[128,1024]{1,0:T(8,128)(2,1)}, bf16[128,1024]{1,0:T(8,128)(2,1)}, bf16[512,1024]{1,0:T(8,128)(2,1)S(1)}) custom-call(bf16[128,1024]{1,0:T(8,128)(2,1)} %get-tuple-element.41.refs_0_, ...), custom_call_target="tpu_custom_call", output_to_operand_aliasing={{0}: (0, {}), {1}: (1, {}), {2}: (2, {}), {3}: (3, {})} | custom-call | tf_op jit(solution)/shard_map/gate/pallas_call | solution.py:490
  45.0 0.3 collective-permute-start.20
  45.3 0.8 %collective-permute-start.19 = (bf16[256,512]{1,0:T(8,128)(2,1)S(1)}, bf16[256,512]{1,0:T(8,128)(2,1)}, u32[]{:S(2)}, u32[]{:S(2)}) collective-permute-start(bf16[256,512]{1,0:T(8,128)(2,1)S(1)} %get-tuple-element.47.refs_4_.refs_2_), channel_id=1, source_target_pairs={{0,1},{1,0},{2,3},{3,2},{4,5},{5,4},{6,7},{7,6},{8,9},{9,8},{10,11... | collective-permute-start | bytes 786440 | tf_op jit(solution)/shard_map/cot_x_core/ppermute | solution.py:22
  46.1 2.0 %collective-permute-start.15 = (bf16[128,1024]{1,0:T(8,128)(2,1)}, bf16[128,1024]{1,0:T(8,128)(2,1)S(1)}, u32[]{:S(2)}, u32[]{:S(2)}) collective-permute-start(bf16[128,1024]{1,0:T(8,128)(2,1)} %get-tuple-element.48), channel_id=1, source_target_pairs={{0,8},{4,12},{8,16},{12,20},{16,24},{20,28},{24,0},{28,4},{1,9},{5... | collective-permute-start | bytes 786440 | tf_op jit(solution)/shard_map/sum_z3/ppermute | solution.py:28
  48.1 1.4 %collective-permute-start.16 = (bf16[128,1024]{1,0:T(8,128)(2,1)}, bf16[128,1024]{1,0:T(8,128)(2,1)S(1)}, u32[]{:S(2)}, u32[]{:S(2)}) collective-permute-start(bf16[128,1024]{1,0:T(8,128)(2,1)} %get-tuple-element.49), channel_id=1, source_target_pairs={{0,16},{4,20},{8,24},{12,28},{16,0},{20,4},{24,8},{28,12},{1,17},{... | collective-permute-start | bytes 786440 | tf_op jit(solution)/shard_map/sum_z2/ppermute | solution.py:28
  49.5 3.3 %decode.1 = f32[4,1,2,1024]{3,2,1,0:T(2,128)S(1)} custom-call(bf16[512,1024]{1,0:T(8,128)(2,1)S(1)} %copy-done.2, bf16[512,1024]{1,0:T(8,128)(2,1)} %collective-permute-done.refs_2_.refs_1_, bf16[104,1024]{1,0:T(8,128)(2,1)S(1)} %combine.1.refs_3_.refs_2_, bf16[104,1024]{1,0:T(8,128)(2,1)S(1)} %collective-permute-done.14.refs_7_.refs_3_, ...), custom_call_target="tpu_custom_call" | custom-call | tf_op jit(solution)/shard_map/decode/pallas_call | solution.py:82
  52.8 6.6 %all_to_all.5 = f32[4,1,2,1024]{3,2,1,0:T(2,128)S(1)} all-to-all(f32[4,1,2,1024]{3,2,1,0:T(2,128)S(1)} %decode.1), channel_id=1, replica_groups=mesh['fsdp'=8,'tp'=4] {'tp'}, dimensions={0} | all-to-all | bytes 65536 | tf_op jit(solution)/shard_map/dec_tp/all_to_all | solution.py:525
  59.5 3.2 %collective-permute-start.18 = (bf16[2,1024]{1,0:T(2,128)(2,1)S(1)}, bf16[2,1024]{1,0:T(2,128)(2,1)S(1)}, u32[]{:S(2)}, u32[]{:S(2)}) collective-permute-start(bf16[2,1024]{1,0:T(2,128)(2,1)S(1)} %reduce_sum.9), channel_id=1, source_target_pairs={{0,0},{1,8},{2,16},{3,24},{4,4},{5,12},{6,20},{7,28},{8,1},{9,9},{... | collective-permute-start | bytes 12296 | tf_op jit(solution)/shard_map/dec_place/ppermute | solution.py:535
  62.8 0.0 copy-start.7
  62.8 1.0 %copy-done.7 = bf16[512,512]{1,0:T(8,128)(2,1)S(1)} copy-done((bf16[512,512]{1,0:T(8,128)(2,1)S(1)}, bf16[512,512]{1,0:T(8,128)(2,1)}, u32[]{:S(2)}) %copy-start.7) | copy-done | bytes 524312
  63.8 1.5 %own.1 = (f32[512,1024]{1,0:T(8,128)S(1)}, bf16[512,512]{1,0:T(8,128)(2,1)S(1)}) custom-call(bf16[512,512]{1,0:T(8,128)(2,1)S(1)} %copy-done.7, bf16[512,1024]{1,0:T(8,128)(2,1)S(1)} %get-tuple-element.51.refs_6_.refs_1_, bf16[256,512]{1,0:T(8,128)(2,1)S(1)} %get-tuple-element.47.refs_4_.refs_2_, bf16[256,512]{1,0:T(8,128)(2,1)} %collective-permute-done.19.refs_3_), custom_call_target="tpu_custom_call" | custom-call | tf_op jit(solution)/shard_map/own/pallas_call | solution.py:82
  65.3 4.0 %collective-permute-done.20.refs_1_ = bf16[512,1024]{1,0:T(8,128)(2,1)S(1)} collective-permute-done((bf16[512,1024]{1,0:T(8,128)(2,1)S(1)}, bf16[512,1024]{1,0:T(8,128)(2,1)S(1)}, u32[]{:S(2)}, u32[]{:S(2)}) %collective-permute-start.20) | collective-permute-done | bytes 1048608 | tf_op jit(solution)/shard_map/attn_x/ppermute | solution.py:22
  69.3 1.8 %product.1 = (f32[512,1024]{1,0:T(8,128)}, f32[8,128]{1,0:T(8,128)S(1)}) custom-call(f32[512,1024]{1,0:T(8,128)S(1)} %get-tuple-element.53.refs_0_, bf16[512,1024]{1,0:T(8,128)(2,1)S(1)} %collective-permute-done.20.refs_1_, bf16[512,512]{1,0:T(8,128)(2,1)S(1)} %get-tuple-element.54.refs_2_), custom_call_target="tpu_custom_call" | custom-call | tf_op jit(solution)/shard_map/product/pallas_call | solution.py:82
  71.1 1.9 %collective-permute-done.18.refs_4_ = bf16[2,1024]{1,0:T(2,128)(2,1)S(1)} collective-permute-done((bf16[2,1024]{1,0:T(2,128)(2,1)S(1)}, bf16[2,1024]{1,0:T(2,128)(2,1)S(1)}, u32[]{:S(2)}, u32[]{:S(2)}) %collective-permute-start.18) | collective-permute-done | bytes 4128 | tf_op jit(solution)/shard_map/dec_place/ppermute | solution.py:535
  73.1 1.1 %sum.1 = (bf16[1,2,1024]{2,1,0:T(2,128)(2,1)}, bf16[128,1024]{1,0:T(8,128)(2,1)}) custom-call(f32[128,1024]{1,0:T(8,128)S(1)} %copy-done.5, bf16[128,1024]{1,0:T(8,128)(2,1)S(1)} %collective-permute-done.15.refs_1_, bf16[128,1024]{1,0:T(8,128)(2,1)S(1)} %collective-permute-done.16.refs_2_, bf16[128,1024]{1,0:T(8,128)(2,1)S(1)} %collective-permute-done.17.refs_3_, ...), custom_call_target="tpu_custom_call" | custom-call | tf_op jit(solution)/shard_map/sum/pallas_call | solution.py:82
  (26 shorter events, 0.1 us)
Async XLA Ops:
  0.6 18.1 %copy-start.3 = (bf16[128,1024]{1,0:T(8,128)(2,1)S(1)}, bf16[128,1024]{1,0:T(8,128)(2,1)}, u32[]{:S(2)}) copy-start(bf16[128,1024]{1,0:T(8,128)(2,1)} %refs_2_.3) | copy-start | bytes 786436
  0.6 26.9 %collective-permute-start = (bf16[512,1024]{1,0:T(8,128)(2,1)}, bf16[512,1024]{1,0:T(8,128)(2,1)}, u32[]{:S(2)}, u32[]{:S(2)}) collective-permute-start(bf16[512,1024]{1,0:T(8,128)(2,1)} %refs_0_.6), channel_id=1, source_target_pairs={{0,4},{4,0},{8,12},{12,8},{16,20},{20,16},{24,28},{28,24},{1,5},{5... | collective-permute-start | bytes 3145736 | tf_op jit(solution)/shard_map/weight_x/ppermute | solution.py:22
  3.9 15.6 %collective-permute-start.1 = (bf16[96,1024]{1,0:T(8,128)(2,1)}, bf16[96,1024]{1,0:T(8,128)(2,1)S(1)}, u32[]{:S(2)}, u32[]{:S(2)}) collective-permute-start(bf16[96,1024]{1,0:T(8,128)(2,1)} %get-tuple-element.31), channel_id=1, source_target_pairs={{0,8},{4,12},{8,16},{12,20},{16,24},{20,28},{24,0},{28,4},{1,9},{5... | collective-permute-start | bytes 589832 | tf_op jit(solution)/shard_map/first_z1/ppermute | solution.py:28
  5.2 14.3 %collective-permute-start.2 = (bf16[96,1024]{1,0:T(8,128)(2,1)}, bf16[96,1024]{1,0:T(8,128)(2,1)S(1)}, u32[]{:S(2)}, u32[]{:S(2)}) collective-permute-start(bf16[96,1024]{1,0:T(8,128)(2,1)} %get-tuple-element.32), channel_id=1, source_target_pairs={{0,16},{4,20},{8,24},{12,28},{16,0},{20,4},{24,8},{28,12},{1,17},{... | collective-permute-start | bytes 589832 | tf_op jit(solution)/shard_map/first_z2/ppermute | solution.py:28
  5.3 17.2 %collective-permute-start.3 = (bf16[96,1024]{1,0:T(8,128)(2,1)}, bf16[96,1024]{1,0:T(8,128)(2,1)S(1)}, u32[]{:S(2)}, u32[]{:S(2)}) collective-permute-start(bf16[96,1024]{1,0:T(8,128)(2,1)} %get-tuple-element.33), channel_id=1, source_target_pairs={{0,24},{4,28},{8,0},{12,4},{16,8},{20,12},{24,16},{28,20},{1,25},{... | collective-permute-start | bytes 589832 | tf_op jit(solution)/shard_map/first_z3/ppermute | solution.py:28
  10.6 17.0 %copy-start = (bf16[128,4096]{1,0:T(8,128)(2,1)S(1)}, bf16[128,4096]{1,0:T(8,128)(2,1)}, u32[]{:S(2)}) copy-start(bf16[128,4096]{1,0:T(8,128)(2,1)} %refs_0_.5) | copy-start | bytes 3145732
  10.6 2.8 %collective-permute-start.5 = (f32[1,16,256]{2,1,0:T(8,128)}, f32[1,16,256]{2,1,0:T(8,128)S(1)}, u32[]{:S(2)}, u32[]{:S(2)}) collective-permute-start(f32[1,16,256]{2,1,0:T(8,128)} %get-tuple-element.36), channel_id=1, source_target_pairs={{0,1},{1,0},{2,3},{3,2},{4,5},{5,4},{6,7},{7,6},{8,9},{9,8},{10,11... | collective-permute-start | bytes 49160 | tf_op jit(solution)/shard_map/softmax_tp1/ppermute | solution.py:22
  13.4 3.4 %collective-permute-start.4 = (f32[2,16,256]{2,1,0:T(8,128)}, f32[2,16,256]{2,1,0:T(8,128)S(1)}, u32[]{:S(2)}, u32[]{:S(2)}) collective-permute-start(f32[2,16,256]{2,1,0:T(8,128)} %get-tuple-element.35), channel_id=1, source_target_pairs={{0,2},{1,3},{2,0},{3,1},{4,6},{5,7},{6,4},{7,5},{8,10},{9,11},{10,... | collective-permute-start | bytes 98312 | tf_op jit(solution)/shard_map/softmax_tp2/ppermute | solution.py:22
  16.8 2.0 %collective-permute-start.6 = (f32[2,16,256]{2,1,0:T(8,128)S(1)}, f32[2,16,256]{2,1,0:T(8,128)S(1)}, u32[]{:S(2)}, u32[]{:S(2)}) collective-permute-start(f32[2,16,256]{2,1,0:T(8,128)S(1)} %collective-permute-done.4.refs_0_), channel_id=1, source_target_pairs={{0,1},{1,0},{2,3},{3,2},{4,5},{5,4},{6,7},{7,6},{8,9},{9,8},{10,11... | collective-permute-start | bytes 98312 | tf_op jit(solution)/shard_map/softmax_tp1/ppermute | solution.py:22
  17.9 0.8 %copy-start.8 = (f32[40,256]{1,0:T(8,128)S(1)}, f32[40,256]{1,0:T(8,128)}, u32[]{:S(2)}) copy-start(f32[40,256]{1,0:T(8,128)} %get-tuple-element.34.in_ref) | copy-start | bytes 122884
  22.5 3.3 %collective-permute-start.7 = (bf16[96,1024]{1,0:T(8,128)(2,1)S(1)}, bf16[96,1024]{1,0:T(8,128)(2,1)S(1)}, u32[]{:S(2)}, u32[]{:S(2)}) collective-permute-start(bf16[96,1024]{1,0:T(8,128)(2,1)S(1)} %get-tuple-element.37.refs_3_), channel_id=1, source_target_pairs={{0,1},{1,0},{2,3},{3,2},{4,5},{5,4},{6,7},{7,6},{8,9},{9,8},{10,11... | collective-permute-start | bytes 589832 | tf_op jit(solution)/shard_map/cot_core/ppermute | solution.py:22
  23.0 3.8 %collective-permute-start.8 = (bf16[96,1024]{1,0:T(8,128)(2,1)S(1)}, bf16[96,1024]{1,0:T(8,128)(2,1)S(1)}, u32[]{:S(2)}, u32[]{:S(2)}) collective-permute-start(bf16[96,1024]{1,0:T(8,128)(2,1)S(1)} %get-tuple-element.38.refs_4_), channel_id=1, source_target_pairs={{0,1},{1,0},{2,3},{3,2},{4,5},{5,4},{6,7},{7,6},{8,9},{9,8},{10,11... | collective-permute-start | bytes 589832 | tf_op jit(solution)/shard_map/cot_core/ppermute | solution.py:22
  23.0 4.5 %collective-permute-start.9 = (bf16[96,1024]{1,0:T(8,128)(2,1)S(1)}, bf16[96,1024]{1,0:T(8,128)(2,1)S(1)}, u32[]{:S(2)}, u32[]{:S(2)}) collective-permute-start(bf16[96,1024]{1,0:T(8,128)(2,1)S(1)} %get-tuple-element.39.refs_5_), channel_id=1, source_target_pairs={{0,1},{1,0},{2,3},{3,2},{4,5},{5,4},{6,7},{7,6},{8,9},{9,8},{10,11... | collective-permute-start | bytes 589832 | tf_op jit(solution)/shard_map/cot_core/ppermute | solution.py:22
  23.5 17.5 %collective-permute-start.14 = (bf16[104,1024]{1,0:T(8,128)(2,1)S(1)}, bf16[104,1024]{1,0:T(8,128)(2,1)S(1)}, u32[]{:S(2)}, u32[]{:S(2)}) collective-permute-start(bf16[104,1024]{1,0:T(8,128)(2,1)S(1)} %combine.1.refs_3_.refs_2_), channel_id=1, source_target_pairs={{0,8},{4,12},{8,16},{12,20},{16,24},{20,28},{24,0},{28,4},{1,9},{5... | collective-permute-start | bytes 638984 | tf_op jit(solution)/shard_map/last_z1/ppermute | solution.py:28
  25.8 15.3 %collective-permute-start.13 = (bf16[104,1024]{1,0:T(8,128)(2,1)S(1)}, bf16[104,1024]{1,0:T(8,128)(2,1)S(1)}, u32[]{:S(2)}, u32[]{:S(2)}) collective-permute-start(bf16[104,1024]{1,0:T(8,128)(2,1)S(1)} %combine.1.refs_3_.refs_2_), channel_id=1, source_target_pairs={{0,16},{4,20},{8,24},{12,28},{16,0},{20,4},{24,8},{28,12},{1,17},{... | collective-permute-start | bytes 638984 | tf_op jit(solution)/shard_map/last_z2/ppermute | solution.py:28
  26.8 17.4 %collective-permute-start.12 = (bf16[104,1024]{1,0:T(8,128)(2,1)S(1)}, bf16[104,1024]{1,0:T(8,128)(2,1)S(1)}, u32[]{:S(2)}, u32[]{:S(2)}) collective-permute-start(bf16[104,1024]{1,0:T(8,128)(2,1)S(1)} %combine.1.refs_3_.refs_2_), channel_id=1, source_target_pairs={{0,24},{4,28},{8,0},{12,4},{16,8},{20,12},{24,16},{28,20},{1,25},{... | collective-permute-start | bytes 638984 | tf_op jit(solution)/shard_map/last_z3/ppermute | solution.py:28
  27.6 1.2 %copy-start.1 = (bf16[512,1024]{1,0:T(8,128)(2,1)S(1)}, bf16[512,1024]{1,0:T(8,128)(2,1)}, u32[]{:S(2)}) copy-start(bf16[512,1024]{1,0:T(8,128)(2,1)} %refs_0_.6) | copy-start | bytes 3145732
  32.9 19.9 %copy-start.4 = (f32[128,1024]{1,0:T(8,128)}, f32[128,1024]{1,0:T(8,128)S(1)}, u32[]{:S(2)}) copy-start(f32[128,1024]{1,0:T(8,128)S(1)} %get-tuple-element.40.refs_0_) | copy-start | bytes 1572868
  32.9 19.9 %copy-start.6 = (bf16[512,512]{1,0:T(8,128)(2,1)}, bf16[512,512]{1,0:T(8,128)(2,1)S(1)}, u32[]{:S(2)}) copy-start(bf16[512,512]{1,0:T(8,128)(2,1)S(1)} %get-tuple-element.52.refs_0_) | copy-start | bytes 1572868
  32.9 16.5 %copy-start.2 = (bf16[512,1024]{1,0:T(8,128)(2,1)S(1)}, bf16[512,1024]{1,0:T(8,128)(2,1)}, u32[]{:S(2)}) copy-start(bf16[512,1024]{1,0:T(8,128)(2,1)} %refs_0_.6) | copy-start | bytes 3145732
  33.0 4.2 %collective-permute-start.10 = (bf16[128,512]{1,0:T(8,128)(2,1)S(1)}, bf16[128,512]{1,0:T(8,128)(2,1)S(1)}, u32[]{:S(2)}, u32[]{:S(2)}) collective-permute-start(bf16[128,512]{1,0:T(8,128)(2,1)S(1)} %get-tuple-element.44), channel_id=1, source_target_pairs={{0,4},{4,0},{8,12},{12,8},{16,20},{20,16},{24,28},{28,24},{1,5},{5... | collective-permute-start | bytes 393224 | tf_op jit(solution)/shard_map/cot_x/ppermute | solution.py:22
  33.2 6.6 %collective-permute-start.11 = (bf16[128,512]{1,0:T(8,128)(2,1)S(1)}, bf16[128,512]{1,0:T(8,128)(2,1)S(1)}, u32[]{:S(2)}, u32[]{:S(2)}) collective-permute-start(bf16[128,512]{1,0:T(8,128)(2,1)S(1)} %get-tuple-element.45), channel_id=1, source_target_pairs={{0,4},{4,0},{8,12},{12,8},{16,20},{20,16},{24,28},{28,24},{1,5},{5... | collective-permute-start | bytes 393224 | tf_op jit(solution)/shard_map/cot_x/ppermute | solution.py:22
  45.0 24.3 %collective-permute-start.20 = (bf16[512,1024]{1,0:T(8,128)(2,1)S(1)}, bf16[512,1024]{1,0:T(8,128)(2,1)S(1)}, u32[]{:S(2)}, u32[]{:S(2)}) collective-permute-start(bf16[512,1024]{1,0:T(8,128)(2,1)S(1)} %get-tuple-element.51.refs_6_.refs_1_), channel_id=1, source_target_pairs={{0,4},{4,0},{8,12},{12,8},{16,20},{20,16},{24,28},{28,24},{1,5},{5... | collective-permute-start | bytes 3145736 | tf_op jit(solution)/shard_map/attn_x/ppermute | solution.py:22
  45.3 14.2 %collective-permute-start.19 = (bf16[256,512]{1,0:T(8,128)(2,1)S(1)}, bf16[256,512]{1,0:T(8,128)(2,1)}, u32[]{:S(2)}, u32[]{:S(2)}) collective-permute-start(bf16[256,512]{1,0:T(8,128)(2,1)S(1)} %get-tuple-element.47.refs_4_.refs_2_), channel_id=1, source_target_pairs={{0,1},{1,0},{2,3},{3,2},{4,5},{5,4},{6,7},{7,6},{8,9},{9,8},{10,11... | collective-permute-start | bytes 786440 | tf_op jit(solution)/shard_map/cot_x_core/ppermute | solution.py:22
  46.1 27.0 %collective-permute-start.15 = (bf16[128,1024]{1,0:T(8,128)(2,1)}, bf16[128,1024]{1,0:T(8,128)(2,1)S(1)}, u32[]{:S(2)}, u32[]{:S(2)}) collective-permute-start(bf16[128,1024]{1,0:T(8,128)(2,1)} %get-tuple-element.48), channel_id=1, source_target_pairs={{0,8},{4,12},{8,16},{12,20},{16,24},{20,28},{24,0},{28,4},{1,9},{5... | collective-permute-start | bytes 786440 | tf_op jit(solution)/shard_map/sum_z3/ppermute | solution.py:28
  48.1 25.0 %collective-permute-start.16 = (bf16[128,1024]{1,0:T(8,128)(2,1)}, bf16[128,1024]{1,0:T(8,128)(2,1)S(1)}, u32[]{:S(2)}, u32[]{:S(2)}) collective-permute-start(bf16[128,1024]{1,0:T(8,128)(2,1)} %get-tuple-element.49), channel_id=1, source_target_pairs={{0,16},{4,20},{8,24},{12,28},{16,0},{20,4},{24,8},{28,12},{1,17},{... | collective-permute-start | bytes 786440 | tf_op jit(solution)/shard_map/sum_z2/ppermute | solution.py:28
  49.5 23.6 %collective-permute-start.17 = (bf16[128,1024]{1,0:T(8,128)(2,1)}, bf16[128,1024]{1,0:T(8,128)(2,1)S(1)}, u32[]{:S(2)}, u32[]{:S(2)}) collective-permute-start(bf16[128,1024]{1,0:T(8,128)(2,1)} %get-tuple-element.50), channel_id=1, source_target_pairs={{0,24},{4,28},{8,0},{12,4},{16,8},{20,12},{24,16},{28,20},{1,25},{... | collective-permute-start | bytes 786440 | tf_op jit(solution)/shard_map/sum_z1/ppermute | solution.py:28
  59.5 13.6 %collective-permute-start.18 = (bf16[2,1024]{1,0:T(2,128)(2,1)S(1)}, bf16[2,1024]{1,0:T(2,128)(2,1)S(1)}, u32[]{:S(2)}, u32[]{:S(2)}) collective-permute-start(bf16[2,1024]{1,0:T(2,128)(2,1)S(1)} %reduce_sum.9), channel_id=1, source_target_pairs={{0,0},{1,8},{2,16},{3,24},{4,4},{5,12},{6,20},{7,28},{8,1},{9,9},{... | collective-permute-start | bytes 12296 | tf_op jit(solution)/shard_map/dec_place/ppermute | solution.py:535
  62.8 1.0 %copy-start.7 = (bf16[512,512]{1,0:T(8,128)(2,1)S(1)}, bf16[512,512]{1,0:T(8,128)(2,1)}, u32[]{:S(2)}) copy-start(bf16[512,512]{1,0:T(8,128)(2,1)} %copy-done.6) | copy-start | bytes 1572868
  65.3 7.8 %copy-start.5 = (f32[128,1024]{1,0:T(8,128)S(1)}, f32[128,1024]{1,0:T(8,128)}, u32[]{:S(2)}) copy-start(f32[128,1024]{1,0:T(8,128)} %copy-done.4) | copy-start | bytes 1572868

commit v10 on v9

--- a/solution.py
+++ b/solution.py
@@ -318,33 +318,32 @@
 
 def sum_kernel(outer, share, mover, ins, outs, scratch):
     total_ref, *rest = ins
-    part_hbms, piece_refs = rest[: outer - 1], rest[outer - 1 :]
-    parts_ref, sum_ref = scratch
+    part_refs, piece_refs = rest[: outer - 1], rest[outer - 1 :]
+    (sum_ref,) = scratch
     _, _, z, _, _ = places()
     plane = piece_refs[0].shape[1]
-    arrive = [mover.start(hbm, parts_ref.at[i]) for i, hbm in enumerate(part_hbms)]
     for j in range(share):
         mover.start(piece_refs[j], outs[0].at[0, :, pl.ds(pl.multiple_of((z % share ^ j) * plane, plane), plane)])
-    mover.wait(*arrive)
-    total = total_ref[...]
-    for i in range(outer - 1):
-        total = total + parts_ref[i].astype(F32)
-    sum_ref[...] = total.astype(BF16)
-    mover.start(sum_ref, outs[1])
+    pieces = 2
+    step = sum_ref.shape[0] // pieces
+    for p in range(pieces):
+        here = slice(p * step, (p + 1) * step)
+        total = total_ref[here, :]
+        for part_ref in part_refs:
+            total = total + part_ref[here, :].astype(F32)
+        sum_ref[here, :] = total.astype(BF16)
+        mover.start(sum_ref.at[here], outs[1].at[here])
 
 
 def pack_kernel(early, skip, mover, ins, outs, scratch):
     low_hbm, high_hbm, own_hbm, *first_hbms = ins
     cots_ref, attn_out = outs
-    (attn_ref,) = scratch
     tokens, size = own_hbm.shape[0], low_hbm.shape[0]
     mover.start(low_hbm, cots_ref.at[:size])
     mover.start(high_hbm, cots_ref.at[size:])
-    parts = [(own_hbm, 0, tokens)] + [(hbm.at[skip:], (k + 1) * tokens, early) for k, hbm in enumerate(first_hbms)]
-    arrive = [mover.start(source, attn_ref.at[at : at + rows]) for source, at, rows in parts]
-    for copy, (_, at, rows) in zip(arrive, parts):
-        mover.wait(copy)
-        mover.start(attn_ref.at[at : at + rows], attn_out.at[at : at + rows])
+    mover.start(own_hbm, attn_out.at[:tokens])
+    for k, hbm in enumerate(first_hbms):
+        mover.start(hbm.at[skip:], attn_out.at[(k + 1) * tokens : (k + 1) * tokens + early])
 
 
 def gate_kernel(count, early, *refs):
@@ -352,7 +351,8 @@
     rest = refs[0].shape[0] - PAD
     tokens = rest + early
     copies = []
-    for k, ref in enumerate(refs[::-1]):
+    order = [*range(1, len(refs)), 0]
+    for k, ref in zip(order[::-1], refs):
         target = pack_out.at[(k + 1) * tokens + early : (k + 2) * tokens]
         copies.append(pltpu.make_async_copy(ref.at[:rest], target, sems.at[k]))
     for copy in copies:
@@ -483,7 +483,7 @@
         "pack",
         [*cots_x, train_attn, *(got if plane == cols else firsts)],
         [((outer * half, feats), BF16), ((outer * tokens, cols), BF16)],
-        [((outer * tokens, cols), BF16)],
+        [],
         fast=[0],
     )
 
@@ -499,7 +499,7 @@
         compiler_params=pltpu.CompilerParams(vmem_limit_bytes=12 << 20),
         cost_estimate=pl.CostEstimate(flops=0, bytes_accessed=0, transcendentals=0),
         name="gate",
-    )(*sent, pack, cots_x, *lasts[:0:-1])
+    )(*sent, pack, cots_x, *[lasts[k + 1] for k in [*range(1, len(far)), 0][::-1]])
     sent, pack = results[:-1], results[-1]
     sums = [turn(sent[k - 1], outer - k, f"sum_z{k}") for k in far]
     pack_x = flip(pack, "fsdp", 1, "attn_x")
@@ -556,9 +556,9 @@
         "sum",
         operands,
         [((rows, steps, share * plane), BF16), ((tokens, cols), BF16)],
-        [((len(far), tokens, cols), BF16), ((tokens, cols), BF16)],
+        [((tokens, cols), BF16)],
         waits=[mark],
-        near=[0, *range(outer, len(operands))],
+        near=range(len(operands)),
     )
     return dec_out, grad_attn, grad_weight
 

time: 75.6 us -> 75 us (level); the launches traced: 74.2 us -> 74.5 us
  waiting for transfers between devices: 20.8 us -> 24.8 us
  starting transfers between devices: 22.2 us -> 18.8 us
    ppermute x11, waiting for transfers between devices: 12.7 us -> 16 us  [flip(): return lax.ppermute(a, axis, [(i, i ^ bits) for i in range(size)])]
    ppermute x9, starting transfers between devices: 10 us -> 6.97 us  [turn(): lax.ppermute(a, 'fsdp', [(z * INNER + x, (z + steps) % outer * INNER + x)...]
    ppermute x9, waiting for transfers between devices: 6.17 us -> 7.77 us  [turn(): lax.ppermute(a, 'fsdp', [(z * INNER + x, (z + steps) % outer * INNER + x)...]
    ppermute x1, waiting for transfers between devices: 1.91 us -> 1.08 us  [shards(): lax.ppermute(lax.dynamic_index_in_dim(dec, z % share ^ j, 0, False), ('fs...]
  transfers between devices with their start and end apart: 21 -> 21, of which waited for: 9 -> 11; matrix products, arithmetic and copies ran while one was open for 0% -> 0% of each run, Pallas kernels for 24% -> 24%
where the time goes in v10:
time: 75 us; the launch traced here: 74.5 us
  waiting for transfers between devices  24.8 us (33%)
  Pallas kernels  19.6 us (26%)
  starting transfers between devices  18.8 us (25%)
  blocking collectives  6.62 us (9%)
  local copies, waits for them, and re-layouts  3.07 us (4%)
  between operations  1.53 us (2%)
    pallas_call x8, Pallas kernels, call(): pl.pallas_call(body, out_shape=[jax.ShapeDtypeStruct(shape, dtype) for sh...  18 us
    ppermute x11, waiting for transfers between devices, flip(): return lax.ppermute(a, axis, [(i, i ^ bits) for i in range(size)])  16 us
    ppermute x11, starting transfers between devices, flip(): return lax.ppermute(a, axis, [(i, i ^ bits) for i in range(size)])  8.93 us
    ppermute x9, waiting for transfers between devices, turn(): lax.ppermute(a, 'fsdp', [(z * INNER + x, (z + steps) % outer * INNER + x)...  7.77 us
    ppermute x9, starting transfers between devices, turn(): lax.ppermute(a, 'fsdp', [(z * INNER + x, (z + steps) % outer * INNER + x)...  6.97 us
    all_to_all x1, blocking collectives, shards(): dec = lax.all_to_all(dec, 'tp', 0, 0, tiled=True).sum(axis=0).astype(BF16)  6.62 us
    unnamed x18, local copies, waits for them, and re-layouts  3.07 us
    ppermute x1, starting transfers between devices, shards(): lax.ppermute(lax.dynamic_index_in_dim(dec, z % share ^ j, 0, False), ('fs...  2.9 us
  transfers between devices with their start and end apart: 21, of which 11 were waited for; matrix products, arithmetic and copies ran while one was open for 0% of the time, Pallas kernels for 24%

profile of v10, /device:TPU:17, one launch (start us, length us, event | category | flops | bytes accessed | tf_op | source)
XLA Modules:
  0.0 74.5 jit_solution(16951437734692191091)
XLA Ops:
  0.6 1.3 %collective-permute-start = (bf16[512,1024]{1,0:T(8,128)(2,1)}, bf16[512,1024]{1,0:T(8,128)(2,1)}, u32[]{:S(2)}, u32[]{:S(2)}) collective-permute-start(bf16[512,1024]{1,0:T(8,128)(2,1)} %refs_0_.6), channel_id=1, source_target_pairs={{0,4},{4,0},{8,12},{12,8},{16,20},{20,16},{24,28},{28,24},{1,5},{5... | collective-permute-start | bytes 3145736 | tf_op jit(solution)/shard_map/weight_x/ppermute | solution.py:22
  1.9 2.0 %cut.1 = (bf16[96,1024]{1,0:T(8,128)(2,1)}, bf16[96,1024]{1,0:T(8,128)(2,1)}, bf16[96,1024]{1,0:T(8,128)(2,1)}) custom-call(bf16[128,4096]{1,0:T(8,128)(2,1)} %refs_0_.5, bf16[128,1024]{1,0:T(8,128)(2,1)} %refs_2_.3), custom_call_target="tpu_custom_call" | custom-call | tf_op jit(solution)/shard_map/cut/pallas_call | solution.py:82
  3.9 1.3 %collective-permute-start.1 = (bf16[96,1024]{1,0:T(8,128)(2,1)}, bf16[96,1024]{1,0:T(8,128)(2,1)S(1)}, u32[]{:S(2)}, u32[]{:S(2)}) collective-permute-start(bf16[96,1024]{1,0:T(8,128)(2,1)} %get-tuple-element.31), channel_id=1, source_target_pairs={{0,8},{4,12},{8,16},{12,20},{16,24},{20,28},{24,0},{28,4},{1,9},{5... | collective-permute-start | bytes 589832 | tf_op jit(solution)/shard_map/first_z1/ppermute | solution.py:28
  5.2 0.1 collective-permute-start.2
  5.3 1.2 %collective-permute-start.3 = (bf16[96,1024]{1,0:T(8,128)(2,1)}, bf16[96,1024]{1,0:T(8,128)(2,1)S(1)}, u32[]{:S(2)}, u32[]{:S(2)}) collective-permute-start(bf16[96,1024]{1,0:T(8,128)(2,1)} %get-tuple-element.33), channel_id=1, source_target_pairs={{0,24},{4,28},{8,0},{12,4},{16,8},{20,12},{24,16},{28,20},{1,25},{... | collective-permute-start | bytes 589832 | tf_op jit(solution)/shard_map/first_z3/ppermute | solution.py:28
  7.1 3.4 %attend.1 = (f32[40,256]{1,0:T(8,128)}, f32[1,16,256]{2,1,0:T(8,128)}, f32[2,16,256]{2,1,0:T(8,128)}) custom-call(s32[1]{0:T(128)S(6)} %copy.26.refs_0_, bf16[1,2,4096]{2,1,0:T(2,128)(2,1)} %refs_1_.4, bf16[1,512,512]{2,1,0:T(8,128)(2,1)} %refs_2_.2, bf16[1,512,512]{2,1,0:T(8,128)(2,1)} %refs_3_.1, bf16[1,2,512]{2,1,0:T(2,128)(2,1)} %refs_4_.1, ...), custom_call_target="tpu_custom_call" | custom-call | tf_op jit(solution)/shard_map/attend/pallas_call | solution.py:82
  10.6 0.0 copy-start
  10.6 1.7 %collective-permute-start.5 = (f32[1,16,256]{2,1,0:T(8,128)}, f32[1,16,256]{2,1,0:T(8,128)S(1)}, u32[]{:S(2)}, u32[]{:S(2)}) collective-permute-start(f32[1,16,256]{2,1,0:T(8,128)} %get-tuple-element.36), channel_id=1, source_target_pairs={{0,1},{1,0},{2,3},{3,2},{4,5},{5,4},{6,7},{7,6},{8,9},{9,8},{10,11... | collective-permute-start | bytes 49160 | tf_op jit(solution)/shard_map/softmax_tp1/ppermute | solution.py:22
  12.3 1.0 %collective-permute-done.5.refs_1_ = f32[1,16,256]{2,1,0:T(8,128)S(1)} collective-permute-done((f32[1,16,256]{2,1,0:T(8,128)}, f32[1,16,256]{2,1,0:T(8,128)S(1)}, u32[]{:S(2)}, u32[]{:S(2)}) %collective-permute-start.5) | collective-permute-done | bytes 16416 | tf_op jit(solution)/shard_map/softmax_tp1/ppermute | solution.py:22
  13.4 1.2 %collective-permute-start.4 = (f32[2,16,256]{2,1,0:T(8,128)}, f32[2,16,256]{2,1,0:T(8,128)S(1)}, u32[]{:S(2)}, u32[]{:S(2)}) collective-permute-start(f32[2,16,256]{2,1,0:T(8,128)} %get-tuple-element.35), channel_id=1, source_target_pairs={{0,2},{1,3},{2,0},{3,1},{4,6},{5,7},{6,4},{7,5},{8,10},{9,11},{10,... | collective-permute-start | bytes 98312 | tf_op jit(solution)/shard_map/softmax_tp2/ppermute | solution.py:22
  14.6 2.1 %collective-permute-done.4.refs_0_ = f32[2,16,256]{2,1,0:T(8,128)S(1)} collective-permute-done((f32[2,16,256]{2,1,0:T(8,128)}, f32[2,16,256]{2,1,0:T(8,128)S(1)}, u32[]{:S(2)}, u32[]{:S(2)}) %collective-permute-start.4) | collective-permute-done | bytes 32800 | tf_op jit(solution)/shard_map/softmax_tp2/ppermute | solution.py:22
  16.8 1.1 %collective-permute-start.6 = (f32[2,16,256]{2,1,0:T(8,128)S(1)}, f32[2,16,256]{2,1,0:T(8,128)S(1)}, u32[]{:S(2)}, u32[]{:S(2)}) collective-permute-start(f32[2,16,256]{2,1,0:T(8,128)S(1)} %collective-permute-done.4.refs_0_), channel_id=1, source_target_pairs={{0,1},{1,0},{2,3},{3,2},{4,5},{5,4},{6,7},{7,6},{8,9},{9,8},{10,11... | collective-permute-start | bytes 98312 | tf_op jit(solution)/shard_map/softmax_tp1/ppermute | solution.py:22
  17.9 0.8 %copy-done.8 = f32[40,256]{1,0:T(8,128)S(1)} copy-done((f32[40,256]{1,0:T(8,128)S(1)}, f32[40,256]{1,0:T(8,128)}, u32[]{:S(2)}) %copy-start.8) | copy-done | bytes 40984
  18.6 0.1 collective-permute-done.6.refs_2_
  18.7 0.8 %combine.1.refs_3_.refs_2_ = bf16[104,1024]{1,0:T(8,128)(2,1)S(1)} custom-call(bf16[128,1024]{1,0:T(8,128)(2,1)S(1)} %copy-done.3, f32[40,256]{1,0:T(8,128)S(1)} %hold.1.own_ref, f32[2,16,256]{2,1,0:T(8,128)S(1)} %collective-permute-done.4.refs_0_, f32[1,16,256]{2,1,0:T(8,128)S(1)} %collective-permute-done.5.refs_1_, ...), custom_call_target="tpu_custom_call" | custom-call | tf_op jit(solution)/shard_map/combine/pallas_call | solution.py:442
  19.5 3.0 %collective-permute-done.3.refs_2_ = bf16[96,1024]{1,0:T(8,128)(2,1)S(1)} collective-permute-done((bf16[96,1024]{1,0:T(8,128)(2,1)}, bf16[96,1024]{1,0:T(8,128)(2,1)S(1)}, u32[]{:S(2)}, u32[]{:S(2)}) %collective-permute-start.3) | collective-permute-done | bytes 196640 | tf_op jit(solution)/shard_map/first_z3/ppermute | solution.py:28
  22.5 0.5 collective-permute-start.7
  23.0 0.0 collective-permute-start.8
  23.0 0.5 collective-permute-start.9
  23.5 0.6 collective-permute-done.7.refs_6_
  24.1 2.9 %collective-permute-start.13 = (bf16[104,1024]{1,0:T(8,128)(2,1)S(1)}, bf16[104,1024]{1,0:T(8,128)(2,1)S(1)}, u32[]{:S(2)}, u32[]{:S(2)}) collective-permute-start(bf16[104,1024]{1,0:T(8,128)(2,1)S(1)} %combine.1.refs_3_.refs_2_), channel_id=1, source_target_pairs={{0,24},{4,28},{8,0},{12,4},{16,8},{20,12},{24,16},{28,20},{1,25},{... | collective-permute-start | bytes 638984 | tf_op jit(solution)/shard_map/last_z3/ppermute | solution.py:28
  27.0 0.0 copy-start.1
  27.0 1.2 %copy-done.1 = bf16[512,1024]{1,0:T(8,128)(2,1)S(1)} copy-done((bf16[512,1024]{1,0:T(8,128)(2,1)S(1)}, bf16[512,1024]{1,0:T(8,128)(2,1)}, u32[]{:S(2)}) %copy-start.1) | copy-done | bytes 1048600
  28.2 4.1 %middle.1 = (bf16[128,1024]{1,0:T(8,128)(2,1)}, bf16[128,1024]{1,0:T(8,128)(2,1)}, bf16[128,1024]{1,0:T(8,128)(2,1)}, f32[128,1024]{1,0:T(8,128)S(1)}, bf16[512,...) custom-call(bf16[128,4096]{1,0:T(8,128)(2,1)S(1)} %copy-done, ...), custom_call_target="tpu_custom_call" | custom-call | tf_op jit(solution)/shard_map/middle/pallas_call | solution.py:82
  32.4 0.0 copy-start.6
  32.4 0.0 copy-start.2
  32.4 0.3 collective-permute-start.10
  32.7 1.2 %collective-permute-start.11 = (bf16[128,512]{1,0:T(8,128)(2,1)S(1)}, bf16[128,512]{1,0:T(8,128)(2,1)S(1)}, u32[]{:S(2)}, u32[]{:S(2)}) collective-permute-start(bf16[128,512]{1,0:T(8,128)(2,1)S(1)} %get-tuple-element.45), channel_id=1, source_target_pairs={{0,4},{4,0},{8,12},{12,8},{16,20},{20,16},{24,28},{28,24},{1,5},{5... | collective-permute-start | bytes 393224 | tf_op jit(solution)/shard_map/cot_x/ppermute | solution.py:22
  33.9 3.0 %collective-permute-done.10.refs_0_ = bf16[128,512]{1,0:T(8,128)(2,1)S(1)} collective-permute-done((bf16[128,512]{1,0:T(8,128)(2,1)S(1)}, bf16[128,512]{1,0:T(8,128)(2,1)S(1)}, u32[]{:S(2)}, u32[]{:S(2)}) %collective-permute-start.10) | collective-permute-done | bytes 131104 | tf_op jit(solution)/shard_map/cot_x/ppermute | solution.py:22
  36.9 2.8 %collective-permute-done.11.refs_1_ = bf16[128,512]{1,0:T(8,128)(2,1)S(1)} collective-permute-done((bf16[128,512]{1,0:T(8,128)(2,1)S(1)}, bf16[128,512]{1,0:T(8,128)(2,1)S(1)}, u32[]{:S(2)}, u32[]{:S(2)}) %collective-permute-start.11) | collective-permute-done | bytes 131104 | tf_op jit(solution)/shard_map/cot_x/ppermute | solution.py:22
  39.7 0.9 %pack.1 = (bf16[256,512]{1,0:T(8,128)(2,1)S(1)}, bf16[512,1024]{1,0:T(8,128)(2,1)S(1)}) custom-call(bf16[128,512]{1,0:T(8,128)(2,1)S(1)} %collective-permute-done.10.refs_0_, bf16[128,512]{1,0:T(8,128)(2,1)S(1)} %collective-permute-done.11.refs_1_, bf16[128,1024]{1,0:T(8,128)(2,1)S(1)} %copy-done.3, bf16[96,1024]{1,0:T(8,128)(2,1)S(1)} %get-tuple-element.37.refs_3_, ...), custom_call_target="tpu_custom_call" | custom-call | tf_op jit(solution)/shard_map/pack/pallas_call | solution.py:82
  40.6 1.5 %collective-permute-done.13.refs_6_.refs_5_ = bf16[104,1024]{1,0:T(8,128)(2,1)S(1)} collective-permute-done((bf16[104,1024]{1,0:T(8,128)(2,1)S(1)}, bf16[104,1024]{1,0:T(8,128)(2,1)S(1)}, u32[]{:S(2)}, u32[]{:S(2)}) %collective-permute-start.13) | collective-permute-done | bytes 213024 | tf_op jit(solution)/shard_map/last_z3/ppermute | solution.py:28
  42.1 3.3 %collective-permute-done.12.refs_5_.refs_3_ = bf16[104,1024]{1,0:T(8,128)(2,1)S(1)} collective-permute-done((bf16[104,1024]{1,0:T(8,128)(2,1)S(1)}, bf16[104,1024]{1,0:T(8,128)(2,1)S(1)}, u32[]{:S(2)}, u32[]{:S(2)}) %collective-permute-start.12) | collective-permute-done | bytes 213024 | tf_op jit(solution)/shard_map/last_z1/ppermute | solution.py:28
  45.4 0.8 %gate.1 = (bf16[128,1024]{1,0:T(8,128)(2,1)}, bf16[128,1024]{1,0:T(8,128)(2,1)}, bf16[128,1024]{1,0:T(8,128)(2,1)}, bf16[512,1024]{1,0:T(8,128)(2,1)S(1)}) custom-call(bf16[128,1024]{1,0:T(8,128)(2,1)} %get-tuple-element.41.refs_0_, ...), custom_call_target="tpu_custom_call", output_to_operand_aliasing={{0}: (0, {}), {1}: (1, {}), {2}: (2, {}), {3}: (3, {})} | custom-call | tf_op jit(solution)/shard_map/gate/pallas_call | solution.py:490
  46.2 0.3 collective-permute-start.20
  46.5 0.7 collective-permute-start.19
  47.2 0.5 collective-permute-start.16
  47.7 1.0 %collective-permute-start.17 = (bf16[128,1024]{1,0:T(8,128)(2,1)}, bf16[128,1024]{1,0:T(8,128)(2,1)S(1)}, u32[]{:S(2)}, u32[]{:S(2)}) collective-permute-start(bf16[128,1024]{1,0:T(8,128)(2,1)} %get-tuple-element.50), channel_id=1, source_target_pairs={{0,24},{4,28},{8,0},{12,4},{16,8},{20,12},{24,16},{28,20},{1,25},{... | collective-permute-start | bytes 786440 | tf_op jit(solution)/shard_map/sum_z1/ppermute | solution.py:28
  48.7 3.3 %decode.1 = f32[4,1,2,1024]{3,2,1,0:T(2,128)S(1)} custom-call(bf16[512,1024]{1,0:T(8,128)(2,1)S(1)} %copy-done.2, bf16[512,1024]{1,0:T(8,128)(2,1)} %collective-permute-done.refs_2_.refs_1_, bf16[104,1024]{1,0:T(8,128)(2,1)S(1)} %combine.1.refs_3_.refs_2_, bf16[104,1024]{1,0:T(8,128)(2,1)S(1)} %collective-permute-done.12.refs_5_.refs_3_, ...), custom_call_target="tpu_custom_call" | custom-call | tf_op jit(solution)/shard_map/decode/pallas_call | solution.py:82
  52.0 6.6 %all_to_all.5 = f32[4,1,2,1024]{3,2,1,0:T(2,128)S(1)} all-to-all(f32[4,1,2,1024]{3,2,1,0:T(2,128)S(1)} %decode.1), channel_id=1, replica_groups=mesh['fsdp'=8,'tp'=4] {'tp'}, dimensions={0} | all-to-all | bytes 65536 | tf_op jit(solution)/shard_map/dec_tp/all_to_all | solution.py:525
  58.7 2.9 %collective-permute-start.18 = (bf16[2,1024]{1,0:T(2,128)(2,1)S(1)}, bf16[2,1024]{1,0:T(2,128)(2,1)S(1)}, u32[]{:S(2)}, u32[]{:S(2)}) collective-permute-start(bf16[2,1024]{1,0:T(2,128)(2,1)S(1)} %reduce_sum.9), channel_id=1, source_target_pairs={{0,0},{1,8},{2,16},{3,24},{4,4},{5,12},{6,20},{7,28},{8,1},{9,9},{... | collective-permute-start | bytes 12296 | tf_op jit(solution)/shard_map/dec_place/ppermute | solution.py:535
  61.6 0.0 copy-start.7
  61.6 1.0 %copy-done.7 = bf16[512,512]{1,0:T(8,128)(2,1)S(1)} copy-done((bf16[512,512]{1,0:T(8,128)(2,1)S(1)}, bf16[512,512]{1,0:T(8,128)(2,1)}, u32[]{:S(2)}) %copy-start.7) | copy-done | bytes 524312
  62.6 1.5 %own.1 = (f32[512,1024]{1,0:T(8,128)S(1)}, bf16[512,512]{1,0:T(8,128)(2,1)S(1)}) custom-call(bf16[512,512]{1,0:T(8,128)(2,1)S(1)} %copy-done.7, bf16[512,1024]{1,0:T(8,128)(2,1)S(1)} %get-tuple-element.51.refs_6_.refs_1_, bf16[256,512]{1,0:T(8,128)(2,1)S(1)} %get-tuple-element.47.refs_4_.refs_2_, bf16[256,512]{1,0:T(8,128)(2,1)} %collective-permute-done.19.refs_3_), custom_call_target="tpu_custom_call" | custom-call | tf_op jit(solution)/shard_map/own/pallas_call | solution.py:82
  64.1 6.4 %collective-permute-done.20.refs_1_ = bf16[512,1024]{1,0:T(8,128)(2,1)S(1)} collective-permute-done((bf16[512,1024]{1,0:T(8,128)(2,1)S(1)}, bf16[512,1024]{1,0:T(8,128)(2,1)S(1)}, u32[]{:S(2)}, u32[]{:S(2)}) %collective-permute-start.20) | collective-permute-done | bytes 1048608 | tf_op jit(solution)/shard_map/attn_x/ppermute | solution.py:22
  70.5 1.8 %product.1 = (f32[512,1024]{1,0:T(8,128)}, f32[8,128]{1,0:T(8,128)S(1)}) custom-call(f32[512,1024]{1,0:T(8,128)S(1)} %get-tuple-element.53.refs_0_, bf16[512,1024]{1,0:T(8,128)(2,1)S(1)} %collective-permute-done.20.refs_1_, bf16[512,512]{1,0:T(8,128)(2,1)S(1)} %get-tuple-element.54.refs_2_), custom_call_target="tpu_custom_call" | custom-call | tf_op jit(solution)/shard_map/product/pallas_call | solution.py:82
  72.4 1.1 %collective-permute-done.18.refs_4_ = bf16[2,1024]{1,0:T(2,128)(2,1)S(1)} collective-permute-done((bf16[2,1024]{1,0:T(2,128)(2,1)S(1)}, bf16[2,1024]{1,0:T(2,128)(2,1)S(1)}, u32[]{:S(2)}, u32[]{:S(2)}) %collective-permute-start.18) | collective-permute-done | bytes 4128 | tf_op jit(solution)/shard_map/dec_place/ppermute | solution.py:535
  73.5 1.0 %sum.1 = (bf16[1,2,1024]{2,1,0:T(2,128)(2,1)}, bf16[128,1024]{1,0:T(8,128)(2,1)}) custom-call(f32[128,1024]{1,0:T(8,128)S(1)} %copy-done.5, bf16[128,1024]{1,0:T(8,128)(2,1)S(1)} %collective-permute-done.15.refs_1_, bf16[128,1024]{1,0:T(8,128)(2,1)S(1)} %collective-permute-done.16.refs_2_, bf16[128,1024]{1,0:T(8,128)(2,1)S(1)} %collective-permute-done.17.refs_3_, ...), custom_call_target="tpu_custom_call" | custom-call | tf_op jit(solution)/shard_map/sum/pallas_call | solution.py:82
  (26 shorter events, 0.1 us)
Async XLA Ops:
  0.6 18.1 %copy-start.3 = (bf16[128,1024]{1,0:T(8,128)(2,1)S(1)}, bf16[128,1024]{1,0:T(8,128)(2,1)}, u32[]{:S(2)}) copy-start(bf16[128,1024]{1,0:T(8,128)(2,1)} %refs_2_.3) | copy-start | bytes 786436
  0.6 26.4 %collective-permute-start = (bf16[512,1024]{1,0:T(8,128)(2,1)}, bf16[512,1024]{1,0:T(8,128)(2,1)}, u32[]{:S(2)}, u32[]{:S(2)}) collective-permute-start(bf16[512,1024]{1,0:T(8,128)(2,1)} %refs_0_.6), channel_id=1, source_target_pairs={{0,4},{4,0},{8,12},{12,8},{16,20},{20,16},{24,28},{28,24},{1,5},{5... | collective-permute-start | bytes 3145736 | tf_op jit(solution)/shard_map/weight_x/ppermute | solution.py:22
  3.9 15.6 %collective-permute-start.1 = (bf16[96,1024]{1,0:T(8,128)(2,1)}, bf16[96,1024]{1,0:T(8,128)(2,1)S(1)}, u32[]{:S(2)}, u32[]{:S(2)}) collective-permute-start(bf16[96,1024]{1,0:T(8,128)(2,1)} %get-tuple-element.31), channel_id=1, source_target_pairs={{0,8},{4,12},{8,16},{12,20},{16,24},{20,28},{24,0},{28,4},{1,9},{5... | collective-permute-start | bytes 589832 | tf_op jit(solution)/shard_map/first_z1/ppermute | solution.py:28
  5.2 14.3 %collective-permute-start.2 = (bf16[96,1024]{1,0:T(8,128)(2,1)}, bf16[96,1024]{1,0:T(8,128)(2,1)S(1)}, u32[]{:S(2)}, u32[]{:S(2)}) collective-permute-start(bf16[96,1024]{1,0:T(8,128)(2,1)} %get-tuple-element.32), channel_id=1, source_target_pairs={{0,16},{4,20},{8,24},{12,28},{16,0},{20,4},{24,8},{28,12},{1,17},{... | collective-permute-start | bytes 589832 | tf_op jit(solution)/shard_map/first_z2/ppermute | solution.py:28
  5.3 17.2 %collective-permute-start.3 = (bf16[96,1024]{1,0:T(8,128)(2,1)}, bf16[96,1024]{1,0:T(8,128)(2,1)S(1)}, u32[]{:S(2)}, u32[]{:S(2)}) collective-permute-start(bf16[96,1024]{1,0:T(8,128)(2,1)} %get-tuple-element.33), channel_id=1, source_target_pairs={{0,24},{4,28},{8,0},{12,4},{16,8},{20,12},{24,16},{28,20},{1,25},{... | collective-permute-start | bytes 589832 | tf_op jit(solution)/shard_map/first_z3/ppermute | solution.py:28
  10.6 16.4 %copy-start = (bf16[128,4096]{1,0:T(8,128)(2,1)S(1)}, bf16[128,4096]{1,0:T(8,128)(2,1)}, u32[]{:S(2)}) copy-start(bf16[128,4096]{1,0:T(8,128)(2,1)} %refs_0_.5) | copy-start | bytes 3145732
  10.6 2.8 %collective-permute-start.5 = (f32[1,16,256]{2,1,0:T(8,128)}, f32[1,16,256]{2,1,0:T(8,128)S(1)}, u32[]{:S(2)}, u32[]{:S(2)}) collective-permute-start(f32[1,16,256]{2,1,0:T(8,128)} %get-tuple-element.36), channel_id=1, source_target_pairs={{0,1},{1,0},{2,3},{3,2},{4,5},{5,4},{6,7},{7,6},{8,9},{9,8},{10,11... | collective-permute-start | bytes 49160 | tf_op jit(solution)/shard_map/softmax_tp1/ppermute | solution.py:22
  13.4 3.4 %collective-permute-start.4 = (f32[2,16,256]{2,1,0:T(8,128)}, f32[2,16,256]{2,1,0:T(8,128)S(1)}, u32[]{:S(2)}, u32[]{:S(2)}) collective-permute-start(f32[2,16,256]{2,1,0:T(8,128)} %get-tuple-element.35), channel_id=1, source_target_pairs={{0,2},{1,3},{2,0},{3,1},{4,6},{5,7},{6,4},{7,5},{8,10},{9,11},{10,... | collective-permute-start | bytes 98312 | tf_op jit(solution)/shard_map/softmax_tp2/ppermute | solution.py:22
  16.8 2.0 %collective-permute-start.6 = (f32[2,16,256]{2,1,0:T(8,128)S(1)}, f32[2,16,256]{2,1,0:T(8,128)S(1)}, u32[]{:S(2)}, u32[]{:S(2)}) collective-permute-start(f32[2,16,256]{2,1,0:T(8,128)S(1)} %collective-permute-done.4.refs_0_), channel_id=1, source_target_pairs={{0,1},{1,0},{2,3},{3,2},{4,5},{5,4},{6,7},{7,6},{8,9},{9,8},{10,11... | collective-permute-start | bytes 98312 | tf_op jit(solution)/shard_map/softmax_tp1/ppermute | solution.py:22
  17.9 0.8 %copy-start.8 = (f32[40,256]{1,0:T(8,128)S(1)}, f32[40,256]{1,0:T(8,128)}, u32[]{:S(2)}) copy-start(f32[40,256]{1,0:T(8,128)} %get-tuple-element.34.in_ref) | copy-start | bytes 122884
  22.5 1.6 %collective-permute-start.7 = (bf16[96,1024]{1,0:T(8,128)(2,1)S(1)}, bf16[96,1024]{1,0:T(8,128)(2,1)S(1)}, u32[]{:S(2)}, u32[]{:S(2)}) collective-permute-start(bf16[96,1024]{1,0:T(8,128)(2,1)S(1)} %get-tuple-element.37.refs_3_), channel_id=1, source_target_pairs={{0,1},{1,0},{2,3},{3,2},{4,5},{5,4},{6,7},{7,6},{8,9},{9,8},{10,11... | collective-permute-start | bytes 589832 | tf_op jit(solution)/shard_map/cot_core/ppermute | solution.py:22
  23.0 4.0 %collective-permute-start.8 = (bf16[96,1024]{1,0:T(8,128)(2,1)S(1)}, bf16[96,1024]{1,0:T(8,128)(2,1)S(1)}, u32[]{:S(2)}, u32[]{:S(2)}) collective-permute-start(bf16[96,1024]{1,0:T(8,128)(2,1)S(1)} %get-tuple-element.38.refs_4_), channel_id=1, source_target_pairs={{0,1},{1,0},{2,3},{3,2},{4,5},{5,4},{6,7},{7,6},{8,9},{9,8},{10,11... | collective-permute-start | bytes 589832 | tf_op jit(solution)/shard_map/cot_core/ppermute | solution.py:22
  23.0 4.0 %collective-permute-start.9 = (bf16[96,1024]{1,0:T(8,128)(2,1)S(1)}, bf16[96,1024]{1,0:T(8,128)(2,1)S(1)}, u32[]{:S(2)}, u32[]{:S(2)}) collective-permute-start(bf16[96,1024]{1,0:T(8,128)(2,1)S(1)} %get-tuple-element.39.refs_5_), channel_id=1, source_target_pairs={{0,1},{1,0},{2,3},{3,2},{4,5},{5,4},{6,7},{7,6},{8,9},{9,8},{10,11... | collective-permute-start | bytes 589832 | tf_op jit(solution)/shard_map/cot_core/ppermute | solution.py:22
  23.5 17.1 %collective-permute-start.14 = (bf16[104,1024]{1,0:T(8,128)(2,1)S(1)}, bf16[104,1024]{1,0:T(8,128)(2,1)S(1)}, u32[]{:S(2)}, u32[]{:S(2)}) collective-permute-start(bf16[104,1024]{1,0:T(8,128)(2,1)S(1)} %combine.1.refs_3_.refs_2_), channel_id=1, source_target_pairs={{0,16},{4,20},{8,24},{12,28},{16,0},{20,4},{24,8},{28,12},{1,17},{... | collective-permute-start | bytes 638984 | tf_op jit(solution)/shard_map/last_z2/ppermute | solution.py:28
  24.1 18.0 %collective-permute-start.13 = (bf16[104,1024]{1,0:T(8,128)(2,1)S(1)}, bf16[104,1024]{1,0:T(8,128)(2,1)S(1)}, u32[]{:S(2)}, u32[]{:S(2)}) collective-permute-start(bf16[104,1024]{1,0:T(8,128)(2,1)S(1)} %combine.1.refs_3_.refs_2_), channel_id=1, source_target_pairs={{0,24},{4,28},{8,0},{12,4},{16,8},{20,12},{24,16},{28,20},{1,25},{... | collective-permute-start | bytes 638984 | tf_op jit(solution)/shard_map/last_z3/ppermute | solution.py:28
  27.0 18.4 %collective-permute-start.12 = (bf16[104,1024]{1,0:T(8,128)(2,1)S(1)}, bf16[104,1024]{1,0:T(8,128)(2,1)S(1)}, u32[]{:S(2)}, u32[]{:S(2)}) collective-permute-start(bf16[104,1024]{1,0:T(8,128)(2,1)S(1)} %combine.1.refs_3_.refs_2_), channel_id=1, source_target_pairs={{0,8},{4,12},{8,16},{12,20},{16,24},{20,28},{24,0},{28,4},{1,9},{5... | collective-permute-start | bytes 638984 | tf_op jit(solution)/shard_map/last_z1/ppermute | solution.py:28
  27.0 1.2 %copy-start.1 = (bf16[512,1024]{1,0:T(8,128)(2,1)S(1)}, bf16[512,1024]{1,0:T(8,128)(2,1)}, u32[]{:S(2)}) copy-start(bf16[512,1024]{1,0:T(8,128)(2,1)} %refs_0_.6) | copy-start | bytes 3145732
  32.4 19.6 %copy-start.4 = (f32[128,1024]{1,0:T(8,128)}, f32[128,1024]{1,0:T(8,128)S(1)}, u32[]{:S(2)}) copy-start(f32[128,1024]{1,0:T(8,128)S(1)} %get-tuple-element.40.refs_0_) | copy-start | bytes 1572868
  32.4 19.6 %copy-start.6 = (bf16[512,512]{1,0:T(8,128)(2,1)}, bf16[512,512]{1,0:T(8,128)(2,1)S(1)}, u32[]{:S(2)}) copy-start(bf16[512,512]{1,0:T(8,128)(2,1)S(1)} %get-tuple-element.52.refs_0_) | copy-start | bytes 1572868
  32.4 16.3 %copy-start.2 = (bf16[512,1024]{1,0:T(8,128)(2,1)S(1)}, bf16[512,1024]{1,0:T(8,128)(2,1)}, u32[]{:S(2)}) copy-start(bf16[512,1024]{1,0:T(8,128)(2,1)} %refs_0_.6) | copy-start | bytes 3145732
  32.4 4.5 %collective-permute-start.10 = (bf16[128,512]{1,0:T(8,128)(2,1)S(1)}, bf16[128,512]{1,0:T(8,128)(2,1)S(1)}, u32[]{:S(2)}, u32[]{:S(2)}) collective-permute-start(bf16[128,512]{1,0:T(8,128)(2,1)S(1)} %get-tuple-element.44), channel_id=1, source_target_pairs={{0,4},{4,0},{8,12},{12,8},{16,20},{20,16},{24,28},{28,24},{1,5},{5... | collective-permute-start | bytes 393224 | tf_op jit(solution)/shard_map/cot_x/ppermute | solution.py:22
  32.7 7.0 %collective-permute-start.11 = (bf16[128,512]{1,0:T(8,128)(2,1)S(1)}, bf16[128,512]{1,0:T(8,128)(2,1)S(1)}, u32[]{:S(2)}, u32[]{:S(2)}) collective-permute-start(bf16[128,512]{1,0:T(8,128)(2,1)S(1)} %get-tuple-element.45), channel_id=1, source_target_pairs={{0,4},{4,0},{8,12},{12,8},{16,20},{20,16},{24,28},{28,24},{1,5},{5... | collective-permute-start | bytes 393224 | tf_op jit(solution)/shard_map/cot_x/ppermute | solution.py:22
  46.2 24.4 %collective-permute-start.20 = (bf16[512,1024]{1,0:T(8,128)(2,1)S(1)}, bf16[512,1024]{1,0:T(8,128)(2,1)S(1)}, u32[]{:S(2)}, u32[]{:S(2)}) collective-permute-start(bf16[512,1024]{1,0:T(8,128)(2,1)S(1)} %get-tuple-element.51.refs_6_.refs_1_), channel_id=1, source_target_pairs={{0,4},{4,0},{8,12},{12,8},{16,20},{20,16},{24,28},{28,24},{1,5},{5... | collective-permute-start | bytes 3145736 | tf_op jit(solution)/shard_map/attn_x/ppermute | solution.py:22
  46.5 12.2 %collective-permute-start.19 = (bf16[256,512]{1,0:T(8,128)(2,1)S(1)}, bf16[256,512]{1,0:T(8,128)(2,1)}, u32[]{:S(2)}, u32[]{:S(2)}) collective-permute-start(bf16[256,512]{1,0:T(8,128)(2,1)S(1)} %get-tuple-element.47.refs_4_.refs_2_), channel_id=1, source_target_pairs={{0,1},{1,0},{2,3},{3,2},{4,5},{5,4},{6,7},{7,6},{8,9},{9,8},{10,11... | collective-permute-start | bytes 786440 | tf_op jit(solution)/shard_map/cot_x_core/ppermute | solution.py:22
  47.2 26.2 %collective-permute-start.15 = (bf16[128,1024]{1,0:T(8,128)(2,1)}, bf16[128,1024]{1,0:T(8,128)(2,1)S(1)}, u32[]{:S(2)}, u32[]{:S(2)}) collective-permute-start(bf16[128,1024]{1,0:T(8,128)(2,1)} %get-tuple-element.48), channel_id=1, source_target_pairs={{0,8},{4,12},{8,16},{12,20},{16,24},{20,28},{24,0},{28,4},{1,9},{5... | collective-permute-start | bytes 786440 | tf_op jit(solution)/shard_map/sum_z3/ppermute | solution.py:28
  47.2 26.2 %collective-permute-start.16 = (bf16[128,1024]{1,0:T(8,128)(2,1)}, bf16[128,1024]{1,0:T(8,128)(2,1)S(1)}, u32[]{:S(2)}, u32[]{:S(2)}) collective-permute-start(bf16[128,1024]{1,0:T(8,128)(2,1)} %get-tuple-element.49), channel_id=1, source_target_pairs={{0,16},{4,20},{8,24},{12,28},{16,0},{20,4},{24,8},{28,12},{1,17},{... | collective-permute-start | bytes 786440 | tf_op jit(solution)/shard_map/sum_z2/ppermute | solution.py:28
  47.7 25.8 %collective-permute-start.17 = (bf16[128,1024]{1,0:T(8,128)(2,1)}, bf16[128,1024]{1,0:T(8,128)(2,1)S(1)}, u32[]{:S(2)}, u32[]{:S(2)}) collective-permute-start(bf16[128,1024]{1,0:T(8,128)(2,1)} %get-tuple-element.50), channel_id=1, source_target_pairs={{0,24},{4,28},{8,0},{12,4},{16,8},{20,12},{24,16},{28,20},{1,25},{... | collective-permute-start | bytes 786440 | tf_op jit(solution)/shard_map/sum_z1/ppermute | solution.py:28
  58.7 14.8 %collective-permute-start.18 = (bf16[2,1024]{1,0:T(2,128)(2,1)S(1)}, bf16[2,1024]{1,0:T(2,128)(2,1)S(1)}, u32[]{:S(2)}, u32[]{:S(2)}) collective-permute-start(bf16[2,1024]{1,0:T(2,128)(2,1)S(1)} %reduce_sum.9), channel_id=1, source_target_pairs={{0,0},{1,8},{2,16},{3,24},{4,4},{5,12},{6,20},{7,28},{8,1},{9,9},{... | collective-permute-start | bytes 12296 | tf_op jit(solution)/shard_map/dec_place/ppermute | solution.py:535
  61.6 1.0 %copy-start.7 = (bf16[512,512]{1,0:T(8,128)(2,1)S(1)}, bf16[512,512]{1,0:T(8,128)(2,1)}, u32[]{:S(2)}) copy-start(bf16[512,512]{1,0:T(8,128)(2,1)} %copy-done.6) | copy-start | bytes 1572868
  64.1 9.3 %copy-start.5 = (f32[128,1024]{1,0:T(8,128)S(1)}, f32[128,1024]{1,0:T(8,128)}, u32[]{:S(2)}) copy-start(f32[128,1024]{1,0:T(8,128)} %copy-done.4) | copy-start | bytes 1572868
